TPU v7x, 32 devices: a whole 2x2x4 slice. The times are simulated.
32 devices in a mesh: seq: 8 (over y, x, core), chan: 4 (over z).
Axes of the slice: x: 2, y: 2, z: 4, core: 2. Of those that a mesh axis runs over, the one named last changes fastest.
Arguments:
- out_grads: bfloat16 [1024, 4096], P(('seq', 'chan')), may hold values from -6 to 6
- layer_inputs: bfloat16 [1024, 4096], P('seq', 'chan'), may hold values from -0.046875 to 0.046875
- filters: bfloat16 [512, 256], P('seq', 'chan'), may hold values from -0.25 to 0.25
Outputs:
- input_grads: bfloat16 [1024, 4096], P('seq', 'chan')
- filter_grads: float32 [512, 256], P('seq', 'chan')
All inputs are finite; a program needn't handle non-finite values.
Results may differ from a plain program's by a relative error of at most 0.001.
Values may be sent and summed in bfloat16 or wider, within the bound.
No kernel may reach another device: no remote copies, remote signals or barrier semaphores. Data moves between devices by JAX's collectives and lax.ppermute only.
A program may use at most 64 MiB of HBM per device.

v0:
```python
import jax
import jax.numpy as jnp
from jax import lax
from jax.sharding import PartitionSpec as P


def shifted(value, axis, steps):
    count = lax.axis_size(axis)
    pairs = [(source, (source + steps) % count) for source in range(count)]
    return lax.ppermute(value, axis, pairs)


def skewed_sums(products):
    groups_here, length, _ = products.shape
    padded = jnp.pad(products, ((0, 0), (0, 0), (0, length)))
    flat = padded.reshape(groups_here, 2 * length * length)[:, : length * (2 * length - 1)]
    return flat.reshape(groups_here, length, 2 * length - 1).sum(axis=1)


def on_device(out_grads, layer_inputs, filters):
    local_grads = lax.all_to_all(out_grads, "chan", split_axis=1, concat_axis=0, tiled=True)
    taps_all = lax.all_gather(filters, "seq", axis=0, tiled=True)
    block_len = local_grads.shape[0]
    chan_width = local_grads.shape[1]
    groups_here = filters.shape[1]
    per_group = chan_width // groups_here
    taps_total = taps_all.shape[0]
    spread_blocks = taps_total // block_len
    filt_rows = taps_all.T
    x_reversed = layer_inputs[::-1].reshape(block_len, groups_here, per_group).transpose(1, 2, 0)
    offsets = lax.broadcasted_iota(jnp.int32, (block_len, block_len), 1) - lax.broadcasted_iota(
        jnp.int32, (block_len, block_len), 0
    )
    dx_total = jnp.zeros((groups_here, per_group, block_len), jnp.float32)
    lag_buffer = jnp.zeros((groups_here, (spread_blocks + 2) * block_len), jnp.float32)
    current = local_grads
    for lag_block in range(spread_blocks + 1):
        if lag_block > 0:
            current = shifted(local_grads, "seq", -lag_block)
        dy_grouped = current.reshape(block_len, groups_here, per_group).transpose(1, 2, 0)
        lag_index = lag_block * block_len + offsets
        inside = (lag_index >= 0) & (lag_index < taps_total)
        picked = jnp.take(filt_rows, jnp.clip(lag_index, 0, taps_total - 1), axis=1)
        toeplitz = jnp.where(inside[None], picked, jnp.zeros((), jnp.bfloat16))
        dx_total = dx_total + jnp.einsum(
            "guv,gkv->gku", toeplitz, dy_grouped, preferred_element_type=jnp.float32
        )
        products = jnp.einsum(
            "gku,gkv->guv", x_reversed, dy_grouped, preferred_element_type=jnp.float32
        )
        start = lag_block * block_len
        lag_buffer = lag_buffer.at[:, start : start + 2 * block_len - 1].add(skewed_sums(products))
    partial_dh = lag_buffer[:, block_len - 1 : block_len - 1 + taps_total].T
    filter_grads = lax.psum_scatter(partial_dh, "seq", scatter_dimension=0, tiled=True)
    input_grads = dx_total.transpose(2, 0, 1).reshape(block_len, chan_width).astype(jnp.bfloat16)
    return (input_grads, filter_grads)


def solution(mesh):
    in_specs = (P(("seq", "chan"), None), P("seq", "chan"), P("seq", "chan"))
    out_specs = (P("seq", "chan"), P("seq", "chan"))
    return jax.shard_map(
        on_device, mesh=mesh, in_specs=in_specs, out_specs=out_specs, check_vma=False
    )
```

profile of v0, /device:TPU:0, one launch (start us, length us, event | category | flops | bytes accessed | tf_op | source)
XLA Modules:
  0.0 570.7 jit_solution(14987402076204767617)
XLA Ops:
  8.8 6.3 %all-to-all-start = ((bf16[32,4,1024]{2,0,1:T(8,128)(2,1)}), bf16[32,4,1024]{2,0,1:T(8,128)(2,1)}, u32[]{:S(2)}, u32[]{:S(2)}) async-start(bf16[32,4,1024]{2,0,1:T(8,128)(2,1)} %bitcast.98), calls=%async_computation | async-start | bytes 524288 | tf_op jit(solution)/shard_map/all_to_all | solution.py:21
  16.5 9.4 %all_gather.3 = bf16[512,64]{1,0:T(8,128)(2,1)S(1)} all-gather(bf16[64,64]{1,0:T(8,128)(2,1)} %param.17), channel_id=1, replica_groups=mesh['seq'=8,'chan'=4] {'seq'}, dimensions={0}, use_global_device_ids=true | all-gather | bytes 73728 | tf_op jit(solution)/shard_map/all_gather | solution.py:22
  25.9 57.4 %gather_fusion.4 = bf16[16384,64]{1,0:T(8,128)(2,1)} fusion(bf16[64,512]{0,1:T(8,128)(2,1)S(1)} %bitcast.99, s32[16384]{0:T(1024)S(1)} %bitcast_clamp_fusion), kind=kCustom, calls=%fused_computation.4.clone | custom fusion | bytes 4259840 | tf_op jit(solution)/shard_map/jit(_take)/gather | solution.py:43
  83.3 5.6 copy.61
  89.0 57.4 %gather_fusion.3 = bf16[16384,64]{1,0:T(8,128)(2,1)} fusion(bf16[64,512]{0,1:T(8,128)(2,1)S(1)} %bitcast.100, s32[16384]{0:T(1024)S(1)} %bitcast_clamp_fusion.1), kind=kCustom, calls=%fused_computation.3.clone | custom fusion | bytes 4259840 | tf_op jit(solution)/shard_map/jit(_take)/gather | solution.py:43
  146.3 4.8 copy.59
  151.2 57.4 %gather_fusion.2 = bf16[16384,64]{1,0:T(8,128)(2,1)} fusion(bf16[64,512]{0,1:T(8,128)(2,1)S(1)} %bitcast.101, s32[16384]{0:T(1024)S(1)} %bitcast_clamp_fusion.2), kind=kCustom, calls=%fused_computation.2.clone | custom fusion | bytes 4259840 | tf_op jit(solution)/shard_map/jit(_take)/gather | solution.py:43
  208.6 5.6 copy.57
  214.2 57.4 %gather_fusion = bf16[16384,64]{1,0:T(8,128)(2,1)} fusion(bf16[64,512]{0,1:T(8,128)(2,1)S(1)} %bitcast.102, s32[16384]{0:T(1024)S(1)} %bitcast_clamp_fusion.4), kind=kCustom, calls=%fused_computation.clone | custom fusion | bytes 4259840 | tf_op jit(solution)/shard_map/jit(_take)/gather | solution.py:43
  271.6 5.6 copy.52
  277.2 57.4 %gather_fusion.1 = bf16[16384,64]{1,0:T(8,128)(2,1)} fusion(bf16[64,512]{0,1:T(8,128)(2,1)S(1)} %bitcast.103, s32[16384]{0:T(1024)S(1)} %bitcast_clamp_fusion.3), kind=kCustom, calls=%fused_computation.1.clone | custom fusion | bytes 4259840 | tf_op jit(solution)/shard_map/jit(_take)/gather | solution.py:43
  334.6 5.7 %copy.55 = bf16[128,128,64]{1,0,2:T(8,128)(2,1)} copy(bf16[128,128,64]{2,1,0:T(8,128)(2,1)} %bitcast.119) | data formatting | bytes 4194304 | tf_op jit(solution)/shard_map/jit(_take)/gather | solution.py:43
  356.0 4.7 copy.69
  364.4 16.3 %reshape.230 = f32[64,128,255]{2,1,0:T(8,128)} reshape(f32[64,32640]{1,0:T(8,128)} %slice.130) | data formatting | bytes 16711680 | tf_op jit(solution)/shard_map/reshape | solution.py:17
  392.6 4.7 copy.70
  401.1 16.1 %reshape.232 = f32[64,128,255]{2,1,0:T(8,128)} reshape(f32[64,32640]{1,0:T(8,128)} %slice.131) | data formatting | bytes 16711680 | tf_op jit(solution)/shard_map/reshape | solution.py:17
  433.1 16.1 %reshape.234 = f32[64,128,255]{2,1,0:T(8,128)} reshape(f32[64,32640]{1,0:T(8,128)} %slice.133) | data formatting | bytes 16711680 | tf_op jit(solution)/shard_map/reshape | solution.py:17
  456.6 4.7 copy.72
  465.1 16.2 %reshape.236 = f32[64,128,255]{2,1,0:T(8,128)} reshape(f32[64,32640]{1,0:T(8,128)} %slice.135) | data formatting | bytes 16711680 | tf_op jit(solution)/shard_map/reshape | solution.py:17
  481.3 5.0 reduce_sum.48
  490.9 4.7 copy.73
  499.4 15.9 %reshape.238 = f32[64,128,255]{2,1,0:T(8,128)} reshape(f32[64,32640]{1,0:T(8,128)} %slice.137) | data formatting | bytes 16711680 | tf_op jit(solution)/shard_map/reshape | solution.py:17
  515.3 5.1 reduce_sum.49
  537.2 26.2 %reduce-scatter.4.cloned.1.call-done = f32[64,64]{1,0:T(8,128)} async-done(((f32[512,64]{1,0:T(8,128)}), f32[64,64]{1,0:T(8,128)}) %reduce-scatter.4.cloned.1.call-update) | async-done | bytes 16400
  (96 shorter events, 89.8 us)
Async XLA Ops:
  8.8 336.9 %all-to-all-start = ((bf16[32,4,1024]{2,0,1:T(8,128)(2,1)}), bf16[32,4,1024]{2,0,1:T(8,128)(2,1)}, u32[]{:S(2)}, u32[]{:S(2)}) async-start(bf16[32,4,1024]{2,0,1:T(8,128)(2,1)} %bitcast.98), calls=%async_computation | async-start | bytes 524288 | tf_op jit(solution)/shard_map/all_to_all | solution.py:21
  15.2 548.2 %reduce-scatter.4.cloned.1.call-start = ((), (), s32[]{:S(2)}) async-start(), calls=%async_computation.2 | async-start | bytes 294912
  334.6 5.7 %copy-start.4 = (bf16[128,1024]{1,0:T(8,128)(2,1)S(1)}, bf16[128,1024]{1,0:T(8,128)(2,1)}, u32[]{:S(2)}) copy-start(bf16[128,1024]{1,0:T(8,128)(2,1)} %param.16) | copy-start | bytes 786436
  345.8 140.5 %collective-permute-start.3 = (bf16[128,1024]{1,0:T(8,128)(2,1)}, bf16[128,1024]{1,0:T(8,128)(2,1)}, u32[]{:S(2)}, u32[]{:S(2)}) collective-permute-start(bf16[128,1024]{1,0:T(8,128)(2,1)} %bitcast.9), channel_id=1, source_target_pairs={{0,16},{4,20},{8,24},{12,28},{16,0},{20,4},{24,8},{28,12},{1,17},{... | collective-permute-start | bytes 786440 | tf_op jit(solution)/shard_map/ppermute | solution.py:10
  347.1 106.5 %collective-permute-start.2 = (bf16[128,1024]{1,0:T(8,128)(2,1)}, bf16[128,1024]{1,0:T(8,128)(2,1)}, u32[]{:S(2)}, u32[]{:S(2)}) collective-permute-start(bf16[128,1024]{1,0:T(8,128)(2,1)} %bitcast.9), channel_id=1, source_target_pairs={{0,20},{4,24},{8,28},{12,0},{16,4},{20,8},{24,12},{28,16},{1,21},{... | collective-permute-start | bytes 786440 | tf_op jit(solution)/shard_map/ppermute | solution.py:10
  347.5 74.1 %collective-permute-start.1 = (bf16[128,1024]{1,0:T(8,128)(2,1)}, bf16[128,1024]{1,0:T(8,128)(2,1)}, u32[]{:S(2)}, u32[]{:S(2)}) collective-permute-start(bf16[128,1024]{1,0:T(8,128)(2,1)} %bitcast.9), channel_id=1, source_target_pairs={{0,24},{4,28},{8,0},{12,4},{16,8},{20,12},{24,16},{28,20},{1,25},{... | collective-permute-start | bytes 786440 | tf_op jit(solution)/shard_map/ppermute | solution.py:10
  348.9 40.7 %collective-permute-start = (bf16[128,1024]{1,0:T(8,128)(2,1)}, bf16[128,1024]{1,0:T(8,128)(2,1)}, u32[]{:S(2)}, u32[]{:S(2)}) collective-permute-start(bf16[128,1024]{1,0:T(8,128)(2,1)} %bitcast.9), channel_id=1, source_target_pairs={{0,28},{4,0},{8,4},{12,8},{16,12},{20,16},{24,20},{28,24},{1,29},{... | collective-permute-start | bytes 786440 | tf_op jit(solution)/shard_map/ppermute | solution.py:10
  380.8 5.2 copy-start.2
  515.3 13.9 %copy-start.3 = (bf16[128,1024]{0,1:T(8,128)(2,1)S(1)}, bf16[128,1024]{0,1:T(8,128)(2,1)}, u32[]{:S(2)}) copy-start(bf16[128,1024]{0,1:T(8,128)(2,1)} %copy.62) | copy-start | bytes 786436
  528.3 3.8 copy-start.5
  528.3 3.8 copy-start.6
  532.0 1.6 copy-start
  532.0 1.6 copy-start.7
  532.0 1.6 copy-start.8
  533.3 1.7 copy-start.1
  533.3 1.7 copy-start.9
  533.3 1.7 copy-start.10
  533.3 1.8 copy-start.11
Sparse Core Ops, SparseCore 0:
  529.4 33.9 reduce-scatter.3
where the time goes:
time: 577 us; the launch traced here: 571 us
  local copies, waits for them, and re-layouts  459 us (80%)
  other arithmetic  34.6 us (6%)
  waiting for transfers between devices  26.2 us (5%)
  matrix products  15.7 us (3%)
  between operations  15 us (3%)
  starting transfers between devices  10.9 us (2%)
  blocking collectives  9.38 us (2%)
    gather x10, local copies, waits for them, and re-layouts, on_device(): picked = jnp.take(filt_rows, jnp.clip(lag_index, 0, taps_total - 1), axis=1)  314 us
    reshape x5, local copies, waits for them, and re-layouts, skewed_sums(): return flat.reshape(groups_here, length, 2 * length - 1).sum(axis=1)  80.6 us
    unnamed x32, local copies, waits for them, and re-layouts  26.2 us
    unnamed x2, waiting for transfers between devices  26.2 us
    reduce_sum x5, other arithmetic, skewed_sums(): return flat.reshape(groups_here, length, 2 * length - 1).sum(axis=1)  23.4 us
    slice x5, local copies, waits for them, and re-layouts, skewed_sums(): padded.reshape(groups_here, 2 * length * length)  18.7 us
  transfers between devices with their start and end apart: 6, of which 1 were waited for; matrix products, arithmetic and copies ran while one was open for 81% of the time, Pallas kernels for 0%

commit v1 on v0

--- a/solution.py
+++ b/solution.py
@@ -1,7 +1,16 @@
+import functools
+
 import jax
 import jax.numpy as jnp
 from jax import lax
+from jax.experimental import pallas as pl
+from jax.experimental.pallas import tpu as pltpu
 from jax.sharding import PartitionSpec as P
+
+LANES = 128
+STEP = 32
+EXTRA = 16
+VMEM_LIMIT = 40 * 1024 * 1024
 
 
 def shifted(value, axis, steps):
@@ -17,7 +26,7 @@
     return flat.reshape(groups_here, length, 2 * length - 1).sum(axis=1)
 
 
-def on_device(out_grads, layer_inputs, filters):
+def by_tokens(out_grads, layer_inputs, filters):
     local_grads = lax.all_to_all(out_grads, "chan", split_axis=1, concat_axis=0, tiled=True)
     taps_all = lax.all_gather(filters, "seq", axis=0, tiled=True)
     block_len = local_grads.shape[0]
@@ -56,7 +65,202 @@
     return (input_grads, filter_grads)
 
 
+def roll_left(value, steps):
+    width = value.shape[-1]
+    return pltpu.roll(value, (width - steps) % width, value.ndim - 1)
+
+
+def pack_kernel(n_seq, n_chan, dy_ref, x_ref, f_ref, dyp_ref, xp_ref):
+    for seq in range(n_seq):
+        for chan in range(n_chan):
+            start = (chan * n_seq + seq) * LANES
+            dyp_ref[seq * n_chan + chan] = dy_ref[:, start : start + LANES]
+    block_len = x_ref.shape[0]
+    taps_here, groups_here = f_ref.shape
+    per_dest = groups_here // n_seq
+    by_group = f_ref[...].astype(jnp.float32).T
+    by_group = jnp.concatenate(
+        [by_group, jnp.zeros((groups_here, LANES - taps_here), jnp.float32)], axis=1
+    )
+    rest = jnp.zeros((EXTRA - per_dest, LANES), jnp.float32)
+    for seq in range(n_seq):
+        xp_ref[seq, :block_len, :] = x_ref[:, seq * LANES : (seq + 1) * LANES]
+        rows = by_group[seq * per_dest : (seq + 1) * per_dest]
+        xp_ref[seq, block_len:, :] = jnp.concatenate([rows, rest], axis=0).astype(jnp.bfloat16)
+
+
+def conv_kernel(n_seq, taps_here, dy_ref, xf_ref, out_ref, dye_ref, toep_ref, lag_ref):
+    tokens = dy_ref.shape[0]
+    block_len = tokens // n_seq
+    groups = toep_ref.shape[0] // STEP
+    taps = n_seq * taps_here
+    reach = taps + LANES
+    per_group = LANES // groups
+    tile_taps = LANES // taps_here
+
+    dye_ref[:tokens] = dy_ref[...]
+    dye_ref[tokens:] = dy_ref[:reach]
+
+    low = lax.broadcasted_iota(jnp.int32, (groups, LANES), 1) < taps_here
+    pieces = [xf_ref[seq, block_len:, :].astype(jnp.float32)[:groups] for seq in range(n_seq)]
+    tiles = []
+    for tile in range(n_seq // tile_taps):
+        first, second = pieces[tile * 2], pieces[tile * 2 + 1]
+        tiles.append(jnp.where(low, first, pltpu.roll(second, taps_here, 1)))
+    filt = jnp.concatenate(tiles + [jnp.zeros((groups, LANES), jnp.float32)], axis=1)
+    for group in range(groups):
+        rows = jnp.broadcast_to(filt[group : group + 1], (STEP, reach))
+        rows = pltpu.roll(rows, 0, 1, stride=1, stride_axis=0)
+        toep_ref[group * STEP : (group + 1) * STEP] = rows.astype(jnp.bfloat16)
+
+    lane2 = lax.broadcasted_iota(jnp.int32, (STEP, 2 * LANES), 1)
+    group2 = (lane2 % LANES) // per_group
+    lane1 = lax.broadcasted_iota(jnp.int32, (STEP, LANES), 1)
+    group1 = lane1 // per_group
+    toeplitz = toep_ref[...]
+    for pair in range(tokens // (2 * STEP)):
+        at = pair * 2 * STEP
+        window = jnp.concatenate(
+            [dye_ref[at : at + reach], dye_ref[at + STEP : at + STEP + reach]], axis=1
+        )
+        full = jnp.dot(toeplitz, window, preferred_element_type=jnp.float32)
+        total = jnp.zeros((STEP, 2 * LANES), jnp.float32)
+        for group in range(groups):
+            total = jnp.where(group2 == group, full[group * STEP : (group + 1) * STEP], total)
+        block, row = at // block_len, at % block_len
+        out_ref[block, row : row + STEP, :] = total[:, :LANES].astype(jnp.bfloat16)
+        out_ref[block, row + STEP : row + 2 * STEP, :] = total[:, LANES:].astype(jnp.bfloat16)
+        x_first = xf_ref[block, row : row + STEP, :]
+        x_second = xf_ref[block, row + STEP : row + 2 * STEP, :]
+        masked = jnp.concatenate(
+            [
+                jnp.concatenate(
+                    [
+                        jnp.where(group1 == group, x_first, jnp.zeros_like(x_first)),
+                        jnp.where(group1 == group, x_second, jnp.zeros_like(x_second)),
+                    ],
+                    axis=1,
+                )
+                for group in range(groups)
+            ],
+            axis=0,
+        )
+        part = lax.dot_general(
+            masked, window, (((1,), (1,)), ((), ())), preferred_element_type=jnp.float32
+        )
+        if pair == 0:
+            lag_ref[...] = part
+        else:
+            lag_ref[...] += part
+
+    eights = []
+    for group in range(groups):
+        at = group * STEP
+        rows = lag_ref[at : at + 8]
+        for high in range(1, STEP // 8):
+            rows = rows + roll_left(lag_ref[at + 8 * high : at + 8 * high + 8], 8 * high)
+        eights.append(rows)
+    skew = jnp.concatenate(eights, axis=0)
+    row_in = lax.broadcasted_iota(jnp.int32, skew.shape, 0) % 8
+    for bit in (1, 2, 4):
+        skew = jnp.where((row_in & bit) != 0, roll_left(skew, bit), skew)
+    dh = skew.reshape(groups, 8, reach).sum(axis=1)[:, :taps]
+
+    high = dh.astype(jnp.bfloat16).astype(jnp.float32)
+    left = dh - high
+    mid = left.astype(jnp.bfloat16).astype(jnp.float32)
+    least = left - mid
+    for seq in range(n_seq):
+        tile = (seq // tile_taps) * LANES
+        parts = [value[:, tile : tile + LANES] for value in (high, mid, least)]
+        turned = [pltpu.roll(value, taps_here, 1) for value in parts]
+        if seq % tile_taps == 0:
+            top, bottom = jnp.where(low, parts[0], turned[1]), parts[2]
+        else:
+            top, bottom = jnp.where(low, turned[0], parts[1]), turned[2]
+        out_ref[seq, block_len:, :] = jnp.concatenate([top, bottom], axis=0).astype(jnp.bfloat16)
+
+
+def unpack_kernel(n_seq, got_ref, dx_ref, dh_ref):
+    block_len = dx_ref.shape[0]
+    taps_here, groups_here = dh_ref.shape
+    groups = groups_here // n_seq
+    rows = []
+    for seq in range(n_seq):
+        dx_ref[:, seq * LANES : (seq + 1) * LANES] = got_ref[seq, :block_len, :]
+        extra = got_ref[seq, block_len:, :].astype(jnp.float32)
+        top, bottom = extra[:groups], extra[groups:]
+        rows.append(top + pltpu.roll(top, taps_here, 1) + bottom)
+    dh_ref[...] = jnp.concatenate(rows, axis=0).T[:taps_here]
+
+
+def by_channels(n_seq, n_chan, out_grads, layer_inputs, filters):
+    rows = out_grads.shape[0]
+    block_len = layer_inputs.shape[0]
+    taps_here, groups_here = filters.shape
+    groups = groups_here // n_seq
+    tokens = n_seq * block_len
+    taps = n_seq * taps_here
+    params = pltpu.CompilerParams(vmem_limit_bytes=VMEM_LIMIT)
+    whole = pl.BlockSpec(memory_space=pltpu.VMEM)
+    packed_shape = jax.ShapeDtypeStruct((n_seq, block_len + EXTRA, LANES), jnp.bfloat16)
+    dy_packed, x_packed = pl.pallas_call(
+        functools.partial(pack_kernel, n_seq, n_chan),
+        out_shape=(
+            jax.ShapeDtypeStruct((n_seq * n_chan, rows, LANES), jnp.bfloat16),
+            packed_shape,
+        ),
+        in_specs=[whole] * 3,
+        out_specs=(whole, whole),
+        compiler_params=params,
+        name="pack",
+    )(out_grads, layer_inputs, filters)
+    dy = lax.all_to_all(dy_packed, ("seq", "chan"), split_axis=0, concat_axis=0, tiled=True)
+    xf = lax.all_to_all(x_packed, "seq", split_axis=0, concat_axis=0, tiled=True)
+    result = pl.pallas_call(
+        functools.partial(conv_kernel, n_seq, taps_here),
+        out_shape=packed_shape,
+        in_specs=[whole] * 2,
+        out_specs=whole,
+        scratch_shapes=[
+            pltpu.VMEM((tokens + taps + LANES, LANES), jnp.bfloat16),
+            pltpu.VMEM((groups * STEP, taps + LANES), jnp.bfloat16),
+            pltpu.VMEM((groups * STEP, taps + LANES), jnp.float32),
+        ],
+        compiler_params=params,
+        name="conv",
+    )(dy.reshape(tokens, LANES), xf)
+    back = lax.all_to_all(result, "seq", split_axis=0, concat_axis=0, tiled=True)
+    return pl.pallas_call(
+        functools.partial(unpack_kernel, n_seq),
+        out_shape=(
+            jax.ShapeDtypeStruct((block_len, n_seq * LANES), jnp.bfloat16),
+            jax.ShapeDtypeStruct((taps_here, groups_here), jnp.float32),
+        ),
+        in_specs=[whole],
+        out_specs=(whole, whole),
+        compiler_params=params,
+        name="unpack",
+    )(back)
+
+
 def solution(mesh):
+    n_seq, n_chan = mesh.shape["seq"], mesh.shape["chan"]
+
+    def on_device(out_grads, layer_inputs, filters):
+        taps_here, groups_here = filters.shape
+        fits = (
+            layer_inputs.shape[1] == n_seq * LANES
+            and groups_here == 8 * n_seq
+            and 2 * taps_here == LANES
+            and out_grads.shape[0] % 16 == 0
+            and layer_inputs.shape[0] % (2 * STEP) == 0
+            and n_seq * taps_here + LANES <= n_seq * layer_inputs.shape[0]
+        )
+        if fits:
+            return by_channels(n_seq, n_chan, out_grads, layer_inputs, filters)
+        return by_tokens(out_grads, layer_inputs, filters)
+
     in_specs = (P(("seq", "chan"), None), P("seq", "chan"), P("seq", "chan"))
     out_specs = (P("seq", "chan"), P("seq", "chan"))
     return jax.shard_map(

time: 577 us -> 44.3 us (0.08); the launches traced: 571 us -> 44 us
  local copies, waits for them, and re-layouts: 459 us -> 2.61 us
  other arithmetic: 34.6 us -> 0 us
  blocking collectives: 9.38 us -> 35.9 us
  waiting for transfers between devices: 26.2 us -> 0 us
  matrix products: 15.7 us -> 0 us
  between operations: 15 us -> 0.65 us
  starting transfers between devices: 10.9 us -> 0 us
    gather x10 -> x0, local copies, waits for them, and re-layouts: 314 us -> none  [on_device(): picked = jnp.take(filt_rows, jnp.clip(lag_index, 0, taps_total - 1), axis=1)]
    reshape x6 -> x0, local copies, waits for them, and re-layouts: 81.9 us -> none  [the longest x5 80.6 us: skewed_sums(): return flat.reshape(groups_here, length, 2 * length - 1).sum(axis=1)]
    all_to_all x0 -> x3, blocking collectives: none -> 35.9 us  [the longest x1 14 us: by_channels(): lax.all_to_all(dy_packed, ('seq', 'chan'), split_axis=0, concat_axis=0, t...]
    unnamed x2 -> x0, waiting for transfers between devices: 26.2 us -> none
    unnamed x32 -> x6, local copies, waits for them, and re-layouts: 26.2 us -> 2.61 us
    reduce_sum x5 -> x0, other arithmetic: 23.4 us -> none  [skewed_sums(): return flat.reshape(groups_here, length, 2 * length - 1).sum(axis=1)]
    slice x5 -> x0, local copies, waits for them, and re-layouts: 18.7 us -> none  [skewed_sums(): padded.reshape(groups_here, 2 * length * length)]
    dot_general x10 -> x0, matrix products: 15.7 us -> none  [the longest x5 9.99 us: on_device(): jnp.einsum('guv,gkv->gku', toeplitz, dy_grouped, preferred_element_type=j...]
  transfers between devices with their start and end apart: 6 -> 0, of which waited for: 1 -> 0; matrix products, arithmetic and copies ran while one was open for 81% -> 0% of each run, Pallas kernels for 0% -> 0%
where the time goes in v1:
time: 44.3 us; the launch traced here: 44 us
  blocking collectives  35.9 us (81%)
  Pallas kernels  4.89 us (11%)
  local copies, waits for them, and re-layouts  2.61 us (6%)
  between operations  0.65 us (1%)
    all_to_all x1, blocking collectives, by_channels(): lax.all_to_all(dy_packed, ('seq', 'chan'), split_axis=0, concat_axis=0, t...  14 us
    all_to_all x1, blocking collectives, by_channels(): lax.all_to_all(x_packed, 'seq', split_axis=0, concat_axis=0, tiled=True)  12.3 us
    all_to_all x1, blocking collectives, by_channels(): lax.all_to_all(result, 'seq', split_axis=0, concat_axis=0, tiled=True)  9.66 us
    pallas_call x1, Pallas kernels, by_channels(): pl.pallas_call(functools.partial(conv_kernel, n_seq, taps_here), out_shap...  3.98 us
    unnamed x6, local copies, waits for them, and re-layouts  2.61 us

profile of v1, /device:TPU:0, one launch (start us, length us, event | category | flops | bytes accessed | tf_op | source)
XLA Modules:
  0.0 44.0 jit_solution(11427503625051079452)
XLA Ops:
  0.6 0.0 copy-start
  0.6 0.9 %copy-done = bf16[32,4096]{1,0:T(8,128)(2,1)S(1)} copy-done((bf16[32,4096]{1,0:T(8,128)(2,1)S(1)}, bf16[32,4096]{1,0:T(8,128)(2,1)}, u32[]{:S(2)}) %copy-start) | copy-done | bytes 262168
  1.6 0.0 copy-start.1
  1.6 0.9 %copy-done.1 = bf16[128,1024]{1,0:T(8,128)(2,1)S(1)} copy-done((bf16[128,1024]{1,0:T(8,128)(2,1)S(1)}, bf16[128,1024]{1,0:T(8,128)(2,1)}, u32[]{:S(2)}) %copy-start.1) | copy-done | bytes 262168
  2.5 0.0 copy-start.2
  2.5 0.7 %copy-done.2 = bf16[64,64]{1,0:T(8,128)(2,1)S(1)} copy-done((bf16[64,64]{1,0:T(8,128)(2,1)S(1)}, bf16[64,64]{1,0:T(8,128)(2,1)}, u32[]{:S(2)}) %copy-start.2) | copy-done | bytes 8216
  3.2 0.1 pack.1
  3.3 12.3 %all_to_all.15.xf_ref = bf16[8,144,128]{2,1,0:T(8,128)(2,1)S(1)} all-to-all(bf16[8,144,128]{2,1,0:T(8,128)(2,1)S(1)} %get-tuple-element.5), channel_id=1, replica_groups=mesh['seq'=8,'chan'=4] {'seq'}, dimensions={0} | all-to-all | bytes 589824 | tf_op jit(solution)/shard_map/all_to_all | solution.py:219
  15.6 14.0 %all_to_all.16 = bf16[32,32,128]{2,1,0:T(8,128)(2,1)S(1)} all-to-all(bf16[32,32,128]{2,1,0:T(8,128)(2,1)S(1)} %get-tuple-element.4), channel_id=1, replica_groups=mesh['seq'=8,'chan'=4] {'seq','chan'}, dimensions={0} | all-to-all | bytes 524288 | tf_op jit(solution)/shard_map/all_to_all | solution.py:218
  29.6 4.0 %conv.1 = bf16[8,144,128]{2,1,0:T(8,128)(2,1)S(1)} custom-call(bf16[1024,128]{1,0:T(8,128)(2,1)S(1)} %bitcast.1, bf16[8,144,128]{2,1,0:T(8,128)(2,1)S(1)} %all_to_all.15.xf_ref), custom_call_target="tpu_custom_call" | custom-call | tf_op jit(solution)/shard_map/conv/pallas_call | solution.py:220
  33.5 9.7 %all_to_all.17.got_ref = bf16[8,144,128]{2,1,0:T(8,128)(2,1)S(1)} all-to-all(bf16[8,144,128]{2,1,0:T(8,128)(2,1)S(1)} %conv.1), channel_id=1, replica_groups=mesh['seq'=8,'chan'=4] {'seq'}, dimensions={0} | all-to-all | bytes 589824 | tf_op jit(solution)/shard_map/all_to_all | solution.py:233
  43.2 0.8 %unpack.1 = (bf16[128,1024]{1,0:T(8,128)(2,1)}, f32[64,64]{1,0:T(8,128)}) custom-call(bf16[8,144,128]{2,1,0:T(8,128)(2,1)S(1)} %all_to_all.17.got_ref), custom_call_target="tpu_custom_call" | custom-call | tf_op jit(solution)/shard_map/unpack/pallas_call | solution.py:234
Async XLA Ops:
  0.6 1.0 %copy-start = (bf16[32,4096]{1,0:T(8,128)(2,1)S(1)}, bf16[32,4096]{1,0:T(8,128)(2,1)}, u32[]{:S(2)}) copy-start(bf16[32,4096]{1,0:T(8,128)(2,1)} %dy_ref.1) | copy-start | bytes 786436
  1.6 0.9 %copy-start.1 = (bf16[128,1024]{1,0:T(8,128)(2,1)S(1)}, bf16[128,1024]{1,0:T(8,128)(2,1)}, u32[]{:S(2)}) copy-start(bf16[128,1024]{1,0:T(8,128)(2,1)} %x_ref.1) | copy-start | bytes 786436
  2.5 0.7 %copy-start.2 = (bf16[64,64]{1,0:T(8,128)(2,1)S(1)}, bf16[64,64]{1,0:T(8,128)(2,1)}, u32[]{:S(2)}) copy-start(bf16[64,64]{1,0:T(8,128)(2,1)} %f_ref.1) | copy-start | bytes 24580

commit v2 on v1

--- a/solution.py
+++ b/solution.py
@@ -70,11 +70,13 @@
     return pltpu.roll(value, (width - steps) % width, value.ndim - 1)
 
 
-def pack_kernel(n_seq, n_chan, dy_ref, x_ref, f_ref, dyp_ref, xp_ref):
-    for seq in range(n_seq):
-        for chan in range(n_chan):
-            start = (chan * n_seq + seq) * LANES
-            dyp_ref[seq * n_chan + chan] = dy_ref[:, start : start + LANES]
+def split_kernel(dy_ref, out_ref):
+    n_chan, _, width = out_ref.shape
+    for chan in range(n_chan):
+        out_ref[chan] = dy_ref[:, chan * width : (chan + 1) * width]
+
+
+def pack_kernel(n_seq, dy_ref, x_ref, f_ref, out_ref):
     block_len = x_ref.shape[0]
     taps_here, groups_here = f_ref.shape
     per_dest = groups_here // n_seq
@@ -84,25 +86,28 @@
     )
     rest = jnp.zeros((EXTRA - per_dest, LANES), jnp.float32)
     for seq in range(n_seq):
-        xp_ref[seq, :block_len, :] = x_ref[:, seq * LANES : (seq + 1) * LANES]
+        columns = slice(seq * LANES, (seq + 1) * LANES)
+        out_ref[seq, :block_len, :] = dy_ref[:, columns]
+        out_ref[seq, block_len : 2 * block_len, :] = x_ref[:, columns]
         rows = by_group[seq * per_dest : (seq + 1) * per_dest]
-        xp_ref[seq, block_len:, :] = jnp.concatenate([rows, rest], axis=0).astype(jnp.bfloat16)
-
-
-def conv_kernel(n_seq, taps_here, dy_ref, xf_ref, out_ref, dye_ref, toep_ref, lag_ref):
-    tokens = dy_ref.shape[0]
-    block_len = tokens // n_seq
+        out_ref[seq, 2 * block_len :, :] = jnp.concatenate([rows, rest], axis=0).astype(jnp.bfloat16)
+
+
+def conv_kernel(n_seq, taps_here, in_ref, out_ref, dye_ref, toep_ref, lag_ref):
+    block_len = out_ref.shape[1] - EXTRA
+    tokens = n_seq * block_len
     groups = toep_ref.shape[0] // STEP
     taps = n_seq * taps_here
     reach = taps + LANES
     per_group = LANES // groups
     tile_taps = LANES // taps_here
 
-    dye_ref[:tokens] = dy_ref[...]
-    dye_ref[tokens:] = dy_ref[:reach]
+    for start in range(0, tokens + reach, block_len):
+        rows = min(block_len, tokens + reach - start)
+        dye_ref[start : start + rows] = in_ref[start // block_len % n_seq, :rows, :]
 
     low = lax.broadcasted_iota(jnp.int32, (groups, LANES), 1) < taps_here
-    pieces = [xf_ref[seq, block_len:, :].astype(jnp.float32)[:groups] for seq in range(n_seq)]
+    pieces = [in_ref[seq, 2 * block_len :, :].astype(jnp.float32)[:groups] for seq in range(n_seq)]
     tiles = []
     for tile in range(n_seq // tile_taps):
         first, second = pieces[tile * 2], pieces[tile * 2 + 1]
@@ -130,8 +135,8 @@
         block, row = at // block_len, at % block_len
         out_ref[block, row : row + STEP, :] = total[:, :LANES].astype(jnp.bfloat16)
         out_ref[block, row + STEP : row + 2 * STEP, :] = total[:, LANES:].astype(jnp.bfloat16)
-        x_first = xf_ref[block, row : row + STEP, :]
-        x_second = xf_ref[block, row + STEP : row + 2 * STEP, :]
+        x_first = in_ref[block, block_len + row : block_len + row + STEP, :]
+        x_second = in_ref[block, block_len + row + STEP : block_len + row + 2 * STEP, :]
         masked = jnp.concatenate(
             [
                 jnp.concatenate(
@@ -203,24 +208,28 @@
     taps = n_seq * taps_here
     params = pltpu.CompilerParams(vmem_limit_bytes=VMEM_LIMIT)
     whole = pl.BlockSpec(memory_space=pltpu.VMEM)
-    packed_shape = jax.ShapeDtypeStruct((n_seq, block_len + EXTRA, LANES), jnp.bfloat16)
-    dy_packed, x_packed = pl.pallas_call(
-        functools.partial(pack_kernel, n_seq, n_chan),
-        out_shape=(
-            jax.ShapeDtypeStruct((n_seq * n_chan, rows, LANES), jnp.bfloat16),
-            packed_shape,
-        ),
+    dy_split = pl.pallas_call(
+        split_kernel,
+        out_shape=jax.ShapeDtypeStruct((n_chan, rows, n_seq * LANES), jnp.bfloat16),
+        in_specs=[whole],
+        out_specs=whole,
+        compiler_params=params,
+        name="split",
+    )(out_grads)
+    dy = lax.all_to_all(dy_split, "chan", split_axis=0, concat_axis=0, tiled=True)
+    packed = pl.pallas_call(
+        functools.partial(pack_kernel, n_seq),
+        out_shape=jax.ShapeDtypeStruct((n_seq, 2 * block_len + EXTRA, LANES), jnp.bfloat16),
         in_specs=[whole] * 3,
-        out_specs=(whole, whole),
+        out_specs=whole,
         compiler_params=params,
         name="pack",
-    )(out_grads, layer_inputs, filters)
-    dy = lax.all_to_all(dy_packed, ("seq", "chan"), split_axis=0, concat_axis=0, tiled=True)
-    xf = lax.all_to_all(x_packed, "seq", split_axis=0, concat_axis=0, tiled=True)
+    )(dy.reshape(block_len, n_seq * LANES), layer_inputs, filters)
+    packed = lax.all_to_all(packed, "seq", split_axis=0, concat_axis=0, tiled=True)
     result = pl.pallas_call(
         functools.partial(conv_kernel, n_seq, taps_here),
-        out_shape=packed_shape,
-        in_specs=[whole] * 2,
+        out_shape=jax.ShapeDtypeStruct((n_seq, block_len + EXTRA, LANES), jnp.bfloat16),
+        in_specs=[whole],
         out_specs=whole,
         scratch_shapes=[
             pltpu.VMEM((tokens + taps + LANES, LANES), jnp.bfloat16),
@@ -229,7 +238,7 @@
         ],
         compiler_params=params,
         name="conv",
-    )(dy.reshape(tokens, LANES), xf)
+    )(packed)
     back = lax.all_to_all(result, "seq", split_axis=0, concat_axis=0, tiled=True)
     return pl.pallas_call(
         functools.partial(unpack_kernel, n_seq),

time: 44.3 us -> 45.2 us (1.020)
  blocking collectives: 35.9 us -> 38.4 us
  local copies, waits for them, and re-layouts: 2.61 us -> 0.96 us
    all_to_all x2, blocking collectives: 26.2 us -> 28.7 us  [the longest x1 15.1 us: by_channels(): lax.all_to_all(dy_split, 'chan', split_axis=0, concat_axis=0, tiled=True)]
    unnamed x6, local copies, waits for them, and re-layouts: 2.61 us -> 0.96 us
where the time goes in v2:
time: 45.2 us; the launch traced here: 44.9 us
  blocking collectives  38.4 us (85%)
  Pallas kernels  4.91 us (11%)
  local copies, waits for them, and re-layouts  0.96 us (2%)
  between operations  0.67 us (1%)
    all_to_all x1, blocking collectives, by_channels(): lax.all_to_all(dy_split, 'chan', split_axis=0, concat_axis=0, tiled=True)  15.1 us
    all_to_all x1, blocking collectives, by_channels(): lax.all_to_all(packed, 'seq', split_axis=0, concat_axis=0, tiled=True)  13.6 us
    all_to_all x1, blocking collectives, by_channels(): lax.all_to_all(result, 'seq', split_axis=0, concat_axis=0, tiled=True)  9.66 us
    pallas_call x1, Pallas kernels, by_channels(): pl.pallas_call(functools.partial(conv_kernel, n_seq, taps_here), out_shap...  3.97 us
    unnamed x6, local copies, waits for them, and re-layouts  0.96 us

profile of v2, /device:TPU:0, one launch (start us, length us, event | category | flops | bytes accessed | tf_op | source)
XLA Modules:
  0.0 44.9 jit_solution(914896252303517855)
XLA Ops:
  0.6 0.0 copy-start
  0.6 0.9 %copy-done = bf16[32,4096]{1,0:T(8,128)(2,1)S(1)} copy-done((bf16[32,4096]{1,0:T(8,128)(2,1)S(1)}, bf16[32,4096]{1,0:T(8,128)(2,1)}, u32[]{:S(2)}) %copy-start) | copy-done | bytes 262168
  1.6 0.0 copy-start.1
  1.6 0.0 copy-start.2
  1.6 15.1 %all_to_all.15 = bf16[4,32,1024]{2,1,0:T(8,128)(2,1)S(1)} all-to-all(bf16[4,32,1024]{2,1,0:T(8,128)(2,1)S(1)} %split.1), channel_id=1, replica_groups=mesh['seq'=8,'chan'=4] {'chan'}, dimensions={0} | all-to-all | bytes 524288 | tf_op jit(solution)/shard_map/all_to_all | solution.py:219
  16.7 0.0 copy-done.1
  16.8 0.0 copy-done.2
  16.8 0.1 pack.1
  16.9 13.6 %all_to_all.16.in_ref = bf16[8,272,128]{2,1,0:T(8,128)(2,1)S(1)} all-to-all(bf16[8,272,128]{2,1,0:T(8,128)(2,1)S(1)} %pack.1), channel_id=1, replica_groups=mesh['seq'=8,'chan'=4] {'seq'}, dimensions={0} | all-to-all | bytes 1114112 | tf_op jit(solution)/shard_map/all_to_all | solution.py:228
  30.5 4.0 %conv.1 = bf16[8,144,128]{2,1,0:T(8,128)(2,1)S(1)} custom-call(bf16[8,272,128]{2,1,0:T(8,128)(2,1)S(1)} %all_to_all.16.in_ref), custom_call_target="tpu_custom_call" | custom-call | tf_op jit(solution)/shard_map/conv/pallas_call | solution.py:229
  34.5 9.7 %all_to_all.17.got_ref = bf16[8,144,128]{2,1,0:T(8,128)(2,1)S(1)} all-to-all(bf16[8,144,128]{2,1,0:T(8,128)(2,1)S(1)} %conv.1), channel_id=1, replica_groups=mesh['seq'=8,'chan'=4] {'seq'}, dimensions={0} | all-to-all | bytes 589824 | tf_op jit(solution)/shard_map/all_to_all | solution.py:242
  44.1 0.8 %unpack.1 = (bf16[128,1024]{1,0:T(8,128)(2,1)}, f32[64,64]{1,0:T(8,128)}) custom-call(bf16[8,144,128]{2,1,0:T(8,128)(2,1)S(1)} %all_to_all.17.got_ref), custom_call_target="tpu_custom_call" | custom-call | tf_op jit(solution)/shard_map/unpack/pallas_call | solution.py:243
  (1 shorter events, 0.0 us)
Async XLA Ops:
  0.6 1.0 %copy-start = (bf16[32,4096]{1,0:T(8,128)(2,1)S(1)}, bf16[32,4096]{1,0:T(8,128)(2,1)}, u32[]{:S(2)}) copy-start(bf16[32,4096]{1,0:T(8,128)(2,1)} %dy_ref.1) | copy-start | bytes 786436
  1.6 15.1 %copy-start.1 = (bf16[128,1024]{1,0:T(8,128)(2,1)S(1)}, bf16[128,1024]{1,0:T(8,128)(2,1)}, u32[]{:S(2)}) copy-start(bf16[128,1024]{1,0:T(8,128)(2,1)} %x_ref.1) | copy-start | bytes 786436
  1.6 15.1 %copy-start.2 = (bf16[64,64]{1,0:T(8,128)(2,1)S(1)}, bf16[64,64]{1,0:T(8,128)(2,1)}, u32[]{:S(2)}) copy-start(bf16[64,64]{1,0:T(8,128)(2,1)} %f_ref.1) | copy-start | bytes 24580

commit v3 on v1

--- a/solution.py
+++ b/solution.py
@@ -65,16 +65,29 @@
     return (input_grads, filter_grads)
 
 
+def xor_permute(value, axis, bits):
+    pairs = [(source, source ^ bits) for source in range(lax.axis_size(axis))]
+    return lax.ppermute(value, axis, pairs)
+
+
 def roll_left(value, steps):
     width = value.shape[-1]
     return pltpu.roll(value, (width - steps) % width, value.ndim - 1)
 
 
-def pack_kernel(n_seq, n_chan, dy_ref, x_ref, f_ref, dyp_ref, xp_ref):
-    for seq in range(n_seq):
-        for chan in range(n_chan):
-            start = (chan * n_seq + seq) * LANES
-            dyp_ref[seq * n_chan + chan] = dy_ref[:, start : start + LANES]
+def place():
+    seq = lax.axis_index("seq")
+    return seq // 2, seq % 2, lax.axis_index("chan")
+
+
+def rows_at(index, size):
+    return pl.ds(pl.multiple_of(index * size, 16), size)
+
+
+def split_kernel(n_seq, n_chan, dy_ref, x_ref, f_ref, keep_ref, send_ref):
+    _, core, _ = place()
+    chips = n_seq // 2
+    rows = dy_ref.shape[0]
     block_len = x_ref.shape[0]
     taps_here, groups_here = f_ref.shape
     per_dest = groups_here // n_seq
@@ -83,30 +96,86 @@
         [by_group, jnp.zeros((groups_here, LANES - taps_here), jnp.float32)], axis=1
     )
     rest = jnp.zeros((EXTRA - per_dest, LANES), jnp.float32)
-    for seq in range(n_seq):
-        xp_ref[seq, :block_len, :] = x_ref[:, seq * LANES : (seq + 1) * LANES]
-        rows = by_group[seq * per_dest : (seq + 1) * per_dest]
-        xp_ref[seq, block_len:, :] = jnp.concatenate([rows, rest], axis=0).astype(jnp.bfloat16)
-
-
-def conv_kernel(n_seq, taps_here, dy_ref, xf_ref, out_ref, dye_ref, toep_ref, lag_ref):
-    tokens = dy_ref.shape[0]
-    block_len = tokens // n_seq
+    for flip, out_ref in ((0, keep_ref), (1, send_ref)):
+        to_core = core ^ flip
+        for chan in range(n_chan):
+            for chip in range(chips):
+                column = (chan * n_seq + 2 * chip + to_core) * LANES
+                at = (chan * chips + chip) * rows
+                out_ref[at : at + rows] = dy_ref[:, pl.ds(pl.multiple_of(column, LANES), LANES)]
+        base = n_chan * chips * rows
+        for chip in range(chips):
+            column = (2 * chip + to_core) * LANES
+            at = base + chip * (block_len + EXTRA)
+            out_ref[at : at + block_len] = x_ref[:, pl.ds(pl.multiple_of(column, LANES), LANES)]
+            first = 2 * chip * per_dest
+            taps = jnp.where(
+                to_core == 0,
+                by_group[first : first + per_dest],
+                by_group[first + per_dest : first + 2 * per_dest],
+            )
+            out_ref[at + block_len : at + block_len + EXTRA] = jnp.concatenate(
+                [taps, rest], axis=0
+            ).astype(jnp.bfloat16)
+
+
+def fan_kernel(n_chan, rows, keep_ref, got_ref, *out_refs):
+    chip, _, chan = place()
+    chips = len(out_refs) - n_chan
+    size = chips * rows
+    base = n_chan * size
+    for bits in range(n_chan):
+        out_refs[bits][:size] = keep_ref[rows_at(chan ^ bits, size)]
+        out_refs[bits][size:] = got_ref[rows_at(chan ^ bits, size)]
+    for bits in range(chips):
+        out_ref = out_refs[n_chan + bits]
+        size = out_ref.shape[0] // 2
+        source = pl.ds(pl.multiple_of(base + (chip ^ bits) * size, 16), size)
+        out_ref[:size] = keep_ref[source]
+        out_ref[size:] = got_ref[source]
+
+
+def regroup_kernel(rows, n_chan, *refs):
+    chip, _, chan = place()
+    in_refs, out_refs = refs[:n_chan], refs[n_chan:]
+    chips = len(out_refs)
+    for to_bits in range(chips):
+        for from_bits in range(n_chan):
+            for core in range(2):
+                out_refs[to_bits][rows_at(core * n_chan + (chan ^ from_bits), rows)] = in_refs[
+                    from_bits
+                ][rows_at(core * chips + (chip ^ to_bits), rows)]
+
+
+def conv_kernel(n_seq, taps_here, *refs):
+    chips = n_seq // 2
+    dy_refs, x_refs = refs[:chips], refs[chips : 2 * chips]
+    keep_ref, send_ref, dye_ref, x_ref, filt_ref, toep_ref, lag_ref, out_ref = refs[2 * chips :]
+    block_len = out_ref.shape[1] - EXTRA
+    tokens = n_seq * block_len
     groups = toep_ref.shape[0] // STEP
     taps = n_seq * taps_here
     reach = taps + LANES
     per_group = LANES // groups
-    tile_taps = LANES // taps_here
-
-    dye_ref[:tokens] = dy_ref[...]
-    dye_ref[tokens:] = dy_ref[:reach]
+    chip, core, _ = place()
 
     low = lax.broadcasted_iota(jnp.int32, (groups, LANES), 1) < taps_here
-    pieces = [xf_ref[seq, block_len:, :].astype(jnp.float32)[:groups] for seq in range(n_seq)]
-    tiles = []
-    for tile in range(n_seq // tile_taps):
-        first, second = pieces[tile * 2], pieces[tile * 2 + 1]
-        tiles.append(jnp.where(low, first, pltpu.roll(second, taps_here, 1)))
+    for bits in range(chips):
+        pieces = []
+        for flip in range(2):
+            source = (chip ^ bits) * 2 + (core ^ flip)
+            at = flip * block_len
+            dye_ref[rows_at(source, block_len)] = dy_refs[bits][at : at + block_len]
+            at = flip * (block_len + EXTRA)
+            x_ref[rows_at(source, block_len)] = x_refs[bits][at : at + block_len]
+            at += block_len
+            pieces.append(x_refs[bits][at : at + EXTRA].astype(jnp.float32)[:groups])
+        first = jnp.where(core == 0, pieces[0], pieces[1])
+        second = jnp.where(core == 0, pieces[1], pieces[0])
+        filt_ref[chip ^ bits] = jnp.where(low, first, pltpu.roll(second, taps_here, 1))
+    dye_ref[tokens:] = dye_ref[:reach]
+
+    tiles = [filt_ref[tile] for tile in range(chips)]
     filt = jnp.concatenate(tiles + [jnp.zeros((groups, LANES), jnp.float32)], axis=1)
     for group in range(groups):
         rows = jnp.broadcast_to(filt[group : group + 1], (STEP, reach))
@@ -130,8 +199,8 @@
         block, row = at // block_len, at % block_len
         out_ref[block, row : row + STEP, :] = total[:, :LANES].astype(jnp.bfloat16)
         out_ref[block, row + STEP : row + 2 * STEP, :] = total[:, LANES:].astype(jnp.bfloat16)
-        x_first = xf_ref[block, row : row + STEP, :]
-        x_second = xf_ref[block, row + STEP : row + 2 * STEP, :]
+        x_first = x_ref[at : at + STEP]
+        x_second = x_ref[at + STEP : at + 2 * STEP]
         masked = jnp.concatenate(
             [
                 jnp.concatenate(
@@ -171,27 +240,57 @@
     mid = left.astype(jnp.bfloat16).astype(jnp.float32)
     least = left - mid
     for seq in range(n_seq):
-        tile = (seq // tile_taps) * LANES
+        tile = (seq // 2) * LANES
         parts = [value[:, tile : tile + LANES] for value in (high, mid, least)]
         turned = [pltpu.roll(value, taps_here, 1) for value in parts]
-        if seq % tile_taps == 0:
+        if seq % 2 == 0:
             top, bottom = jnp.where(low, parts[0], turned[1]), parts[2]
         else:
             top, bottom = jnp.where(low, turned[0], parts[1]), turned[2]
         out_ref[seq, block_len:, :] = jnp.concatenate([top, bottom], axis=0).astype(jnp.bfloat16)
 
-
-def unpack_kernel(n_seq, got_ref, dx_ref, dh_ref):
+    for to_chip in range(chips):
+        keep_ref[to_chip] = out_ref[to_chip * 2 + core]
+        send_ref[to_chip] = out_ref[to_chip * 2 + (1 - core)]
+
+
+def back_kernel(keep_ref, got_ref, *out_refs):
+    chip, _, _ = place()
+    for bits, out_ref in enumerate(out_refs):
+        out_ref[0] = keep_ref[chip ^ bits]
+        out_ref[1] = got_ref[chip ^ bits]
+
+
+def unpack_kernel(*refs):
+    *got_refs, dx_ref, dh_ref, rows_ref = refs
+    chip, core, _ = place()
     block_len = dx_ref.shape[0]
     taps_here, groups_here = dh_ref.shape
-    groups = groups_here // n_seq
-    rows = []
-    for seq in range(n_seq):
-        dx_ref[:, seq * LANES : (seq + 1) * LANES] = got_ref[seq, :block_len, :]
-        extra = got_ref[seq, block_len:, :].astype(jnp.float32)
-        top, bottom = extra[:groups], extra[groups:]
-        rows.append(top + pltpu.roll(top, taps_here, 1) + bottom)
-    dh_ref[...] = jnp.concatenate(rows, axis=0).T[:taps_here]
+    groups = groups_here // (2 * len(got_refs))
+    for bits, got_ref in enumerate(got_refs):
+        for flip in range(2):
+            source = (chip ^ bits) * 2 + (core ^ flip)
+            columns = pl.ds(pl.multiple_of(source * LANES, LANES), LANES)
+            dx_ref[:, columns] = got_ref[flip, :block_len, :]
+            extra = got_ref[flip, block_len:, :].astype(jnp.float32)
+            top, bottom = extra[:groups], extra[groups:]
+            rows_ref[pl.ds(pl.multiple_of(source * groups, 8), groups)] = (
+                top + pltpu.roll(top, taps_here, 1) + bottom
+            )
+    dh_ref[...] = rows_ref[...].T[:taps_here]
+
+
+def local_call(kernel, out_shape, operands, name, scratch=()):
+    whole = pl.BlockSpec(memory_space=pltpu.VMEM)
+    return pl.pallas_call(
+        kernel,
+        out_shape=out_shape,
+        in_specs=[whole] * len(operands),
+        out_specs=[whole] * len(out_shape),
+        scratch_shapes=scratch,
+        compiler_params=pltpu.CompilerParams(vmem_limit_bytes=VMEM_LIMIT),
+        name=name,
+    )(*operands)
 
 
 def by_channels(n_seq, n_chan, out_grads, layer_inputs, filters):
@@ -201,47 +300,62 @@
     groups = groups_here // n_seq
     tokens = n_seq * block_len
     taps = n_seq * taps_here
-    params = pltpu.CompilerParams(vmem_limit_bytes=VMEM_LIMIT)
-    whole = pl.BlockSpec(memory_space=pltpu.VMEM)
-    packed_shape = jax.ShapeDtypeStruct((n_seq, block_len + EXTRA, LANES), jnp.bfloat16)
-    dy_packed, x_packed = pl.pallas_call(
-        functools.partial(pack_kernel, n_seq, n_chan),
-        out_shape=(
-            jax.ShapeDtypeStruct((n_seq * n_chan, rows, LANES), jnp.bfloat16),
-            packed_shape,
-        ),
-        in_specs=[whole] * 3,
-        out_specs=(whole, whole),
-        compiler_params=params,
-        name="pack",
-    )(out_grads, layer_inputs, filters)
-    dy = lax.all_to_all(dy_packed, ("seq", "chan"), split_axis=0, concat_axis=0, tiled=True)
-    xf = lax.all_to_all(x_packed, "seq", split_axis=0, concat_axis=0, tiled=True)
-    result = pl.pallas_call(
+    chips = n_seq // 2
+
+    def half(*shape):
+        return jax.ShapeDtypeStruct(shape, jnp.bfloat16)
+
+    unit = block_len + EXTRA
+    keep, send = local_call(
+        functools.partial(split_kernel, n_seq, n_chan),
+        [half(chips * (n_chan * rows + unit), LANES)] * 2,
+        (out_grads, layer_inputs, filters),
+        "split",
+    )
+    got = xor_permute(send, "seq", 1)
+    pieces = local_call(
+        functools.partial(fan_kernel, n_chan, rows),
+        [half(2 * chips * rows, LANES)] * n_chan + [half(2 * unit, LANES)] * chips,
+        (keep, got),
+        "fan",
+    )
+    dy = [pieces[0]] + [xor_permute(pieces[k], "chan", k) for k in range(1, n_chan)]
+    pieces = pieces[n_chan:]
+    x = [pieces[0]] + [xor_permute(pieces[k], "seq", 2 * k) for k in range(1, chips)]
+    pieces = local_call(
+        functools.partial(regroup_kernel, rows, n_chan),
+        [half(2 * n_chan * rows, LANES)] * chips,
+        dy,
+        "regroup",
+    )
+    dy = [pieces[0]] + [xor_permute(pieces[k], "seq", 2 * k) for k in range(1, chips)]
+    keep, send = local_call(
         functools.partial(conv_kernel, n_seq, taps_here),
-        out_shape=packed_shape,
-        in_specs=[whole] * 2,
-        out_specs=whole,
-        scratch_shapes=[
+        [half(chips, unit, LANES)] * 2,
+        (*dy, *x),
+        "conv",
+        [
             pltpu.VMEM((tokens + taps + LANES, LANES), jnp.bfloat16),
+            pltpu.VMEM((tokens, LANES), jnp.bfloat16),
+            pltpu.VMEM((chips, groups, LANES), jnp.float32),
             pltpu.VMEM((groups * STEP, taps + LANES), jnp.bfloat16),
             pltpu.VMEM((groups * STEP, taps + LANES), jnp.float32),
+            pltpu.VMEM((n_seq, unit, LANES), jnp.bfloat16),
         ],
-        compiler_params=params,
-        name="conv",
-    )(dy.reshape(tokens, LANES), xf)
-    back = lax.all_to_all(result, "seq", split_axis=0, concat_axis=0, tiled=True)
-    return pl.pallas_call(
-        functools.partial(unpack_kernel, n_seq),
-        out_shape=(
-            jax.ShapeDtypeStruct((block_len, n_seq * LANES), jnp.bfloat16),
+    )
+    got = xor_permute(send, "seq", 1)
+    pieces = local_call(back_kernel, [half(2, unit, LANES)] * chips, (keep, got), "back")
+    back = [pieces[0]] + [xor_permute(pieces[k], "seq", 2 * k) for k in range(1, chips)]
+    return local_call(
+        unpack_kernel,
+        [
+            half(block_len, n_seq * LANES),
             jax.ShapeDtypeStruct((taps_here, groups_here), jnp.float32),
-        ),
-        in_specs=[whole],
-        out_specs=(whole, whole),
-        compiler_params=params,
-        name="unpack",
-    )(back)
+        ],
+        back,
+        "unpack",
+        [pltpu.VMEM((groups_here, LANES), jnp.float32)],
+    )
 
 
 def solution(mesh):
@@ -250,7 +364,9 @@
     def on_device(out_grads, layer_inputs, filters):
         taps_here, groups_here = filters.shape
         fits = (
-            layer_inputs.shape[1] == n_seq * LANES
+            n_seq in (2, 4, 8, 16, 32)
+            and n_chan in (2, 4, 8, 16, 32)
+            and layer_inputs.shape[1] == n_seq * LANES
             and groups_here == 8 * n_seq
             and 2 * taps_here == LANES
             and out_grads.shape[0] % 16 == 0
@@ -258,7 +374,7 @@
             and n_seq * taps_here + LANES <= n_seq * layer_inputs.shape[0]
         )
         if fits:
-            return by_channels(n_seq, n_chan, out_grads, layer_inputs, filters)
+            return tuple(by_channels(n_seq, n_chan, out_grads, layer_inputs, filters))
         return by_tokens(out_grads, layer_inputs, filters)
 
     in_specs = (P(("seq", "chan"), None), P("seq", "chan"), P("seq", "chan"))

time: 44.3 us -> 39.6 us (0.89)
  blocking collectives: 35.9 us -> 0 us
  starting transfers between devices: 0 us -> 16.8 us
  waiting for transfers between devices: 0 us -> 14.3 us
    all_to_all x3 -> x0, blocking collectives: 35.9 us -> none  [the longest x1 14 us: by_channels(): lax.all_to_all(dy_packed, ('seq', 'chan'), split_axis=0, concat_axis=0, t...]
    ppermute x0 -> x14, starting transfers between devices: none -> 16.8 us  [xor_permute(): return lax.ppermute(value, axis, pairs)]
    ppermute x0 -> x14, waiting for transfers between devices: none -> 14.3 us  [xor_permute(): return lax.ppermute(value, axis, pairs)]
    pallas_call x3 -> x6, Pallas kernels: 4.89 us -> 5.01 us  [local_call(): pl.pallas_call(kernel, out_shape=out_shape, in_specs=[whole] * len(operan...]
  transfers between devices with their start and end apart: 0 -> 14, of which waited for: 0 -> 9; matrix products, arithmetic and copies ran while one was open for 0% -> 0% of each run, Pallas kernels for 0% -> 0%
where the time goes in v3:
time: 39.6 us; the launch traced here: 39.4 us
  starting transfers between devices  16.8 us (42%)
  waiting for transfers between devices  14.3 us (36%)
  Pallas kernels  5.01 us (13%)
  local copies, waits for them, and re-layouts  2.61 us (7%)
  between operations  0.68 us (2%)
    ppermute x14, starting transfers between devices, xor_permute(): return lax.ppermute(value, axis, pairs)  16.8 us
    ppermute x14, waiting for transfers between devices, xor_permute(): return lax.ppermute(value, axis, pairs)  14.3 us
    pallas_call x6, Pallas kernels, local_call(): pl.pallas_call(kernel, out_shape=out_shape, in_specs=[whole] * len(operan...  5.01 us
    unnamed x6, local copies, waits for them, and re-layouts  2.61 us
  transfers between devices with their start and end apart: 14, of which 9 were waited for; matrix products, arithmetic and copies ran while one was open for 0% of the time, Pallas kernels for 0%

profile of v3, /device:TPU:0, one launch (start us, length us, event | category | flops | bytes accessed | tf_op | source)
XLA Modules:
  0.0 39.4 jit_solution(17612136675485310799)
XLA Ops:
  0.6 0.9 %copy-done = bf16[32,4096]{1,0:T(8,128)(2,1)S(1)} copy-done((bf16[32,4096]{1,0:T(8,128)(2,1)S(1)}, bf16[32,4096]{1,0:T(8,128)(2,1)}, u32[]{:S(2)}) %copy-start) | copy-done | bytes 262168
  1.6 0.9 %copy-done.1 = bf16[128,1024]{1,0:T(8,128)(2,1)S(1)} copy-done((bf16[128,1024]{1,0:T(8,128)(2,1)S(1)}, bf16[128,1024]{1,0:T(8,128)(2,1)}, u32[]{:S(2)}) %copy-start.1) | copy-done | bytes 262168
  2.5 0.7 %copy-done.2 = bf16[64,64]{1,0:T(8,128)(2,1)S(1)} copy-done((bf16[64,64]{1,0:T(8,128)(2,1)S(1)}, bf16[64,64]{1,0:T(8,128)(2,1)}, u32[]{:S(2)}) %copy-start.2) | copy-done | bytes 8216
  3.4 0.5 %collective-permute-start = (bf16[1088,128]{1,0:T(8,128)(2,1)S(1)}, bf16[1088,128]{1,0:T(8,128)(2,1)S(1)}, u32[]{:S(2)}, u32[]{:S(2)}) collective-permute-start(bf16[1088,128]{1,0:T(8,128)(2,1)S(1)} %get-tuple-element.23), channel_id=1, source_target_pairs={{0,4},{4,0},{8,12},{12,8},{16,20},{20,16},{24,28},{28,24},{1,5},{5... | collective-permute-start | bytes 835592 | tf_op jit(solution)/shard_map/ppermute | solution.py:70
  3.9 1.2 %collective-permute-done.got_ref = bf16[1088,128]{1,0:T(8,128)(2,1)S(1)} collective-permute-done((bf16[1088,128]{1,0:T(8,128)(2,1)S(1)}, bf16[1088,128]{1,0:T(8,128)(2,1)S(1)}, u32[]{:S(2)}, u32[]{:S(2)}) %collective-permute-start) | collective-permute-done | bytes 278560 | tf_op jit(solution)/shard_map/ppermute | solution.py:70
  5.2 3.0 %collective-permute-start.1 = (bf16[256,128]{1,0:T(8,128)(2,1)S(1)}, bf16[256,128]{1,0:T(8,128)(2,1)S(1)}, u32[]{:S(2)}, u32[]{:S(2)}) collective-permute-start(bf16[256,128]{1,0:T(8,128)(2,1)S(1)} %get-tuple-element.25), channel_id=1, source_target_pairs={{0,1},{1,0},{2,3},{3,2},{4,5},{5,4},{6,7},{7,6},{8,9},{9,8},{10,11... | collective-permute-start | bytes 196616 | tf_op jit(solution)/shard_map/ppermute | solution.py:70
  8.2 1.5 %collective-permute-start.7 = (bf16[288,128]{1,0:T(8,128)(2,1)S(1)}, bf16[288,128]{1,0:T(8,128)(2,1)S(1)}, u32[]{:S(2)}, u32[]{:S(2)}) collective-permute-start(bf16[288,128]{1,0:T(8,128)(2,1)S(1)} %get-tuple-element.33), channel_id=1, source_target_pairs={{0,8},{4,12},{8,0},{12,4},{16,24},{20,28},{24,16},{28,20},{1,9},{5... | collective-permute-start | bytes 221192 | tf_op jit(solution)/shard_map/ppermute | solution.py:70
  9.7 2.6 %collective-permute-start.2 = (bf16[256,128]{1,0:T(8,128)(2,1)S(1)}, bf16[256,128]{1,0:T(8,128)(2,1)S(1)}, u32[]{:S(2)}, u32[]{:S(2)}) collective-permute-start(bf16[256,128]{1,0:T(8,128)(2,1)S(1)} %get-tuple-element.26), channel_id=1, source_target_pairs={{0,2},{1,3},{2,0},{3,1},{4,6},{5,7},{6,4},{7,5},{8,10},{9,11},{10,... | collective-permute-start | bytes 196616 | tf_op jit(solution)/shard_map/ppermute | solution.py:70
  12.5 1.5 %collective-permute-start.8 = (bf16[288,128]{1,0:T(8,128)(2,1)S(1)}, bf16[288,128]{1,0:T(8,128)(2,1)S(1)}, u32[]{:S(2)}, u32[]{:S(2)}) collective-permute-start(bf16[288,128]{1,0:T(8,128)(2,1)S(1)} %get-tuple-element.34), channel_id=1, source_target_pairs={{0,16},{4,20},{8,24},{12,28},{16,0},{20,4},{24,8},{28,12},{1,17},{... | collective-permute-start | bytes 221192 | tf_op jit(solution)/shard_map/ppermute | solution.py:70
  14.3 2.6 %collective-permute-done.2.refs_2_ = bf16[256,128]{1,0:T(8,128)(2,1)S(1)} collective-permute-done((bf16[256,128]{1,0:T(8,128)(2,1)S(1)}, bf16[256,128]{1,0:T(8,128)(2,1)S(1)}, u32[]{:S(2)}, u32[]{:S(2)}) %collective-permute-start.2) | collective-permute-done | bytes 65568 | tf_op jit(solution)/shard_map/ppermute | solution.py:70
  16.8 1.5 %collective-permute-done.3.refs_3_ = bf16[256,128]{1,0:T(8,128)(2,1)S(1)} collective-permute-done((bf16[256,128]{1,0:T(8,128)(2,1)S(1)}, bf16[256,128]{1,0:T(8,128)(2,1)S(1)}, u32[]{:S(2)}, u32[]{:S(2)}) %collective-permute-start.3) | collective-permute-done | bytes 65568 | tf_op jit(solution)/shard_map/ppermute | solution.py:70
  18.3 0.7 %collective-permute-start.4 = (bf16[256,128]{1,0:T(8,128)(2,1)S(1)}, bf16[256,128]{1,0:T(8,128)(2,1)S(1)}, u32[]{:S(2)}, u32[]{:S(2)}) collective-permute-start(bf16[256,128]{1,0:T(8,128)(2,1)S(1)} %get-tuple-element.29), channel_id=1, source_target_pairs={{0,8},{4,12},{8,0},{12,4},{16,24},{20,28},{24,16},{28,20},{1,9},{5... | collective-permute-start | bytes 196616 | tf_op jit(solution)/shard_map/ppermute | solution.py:70
  19.0 1.5 %collective-permute-start.5 = (bf16[256,128]{1,0:T(8,128)(2,1)S(1)}, bf16[256,128]{1,0:T(8,128)(2,1)S(1)}, u32[]{:S(2)}, u32[]{:S(2)}) collective-permute-start(bf16[256,128]{1,0:T(8,128)(2,1)S(1)} %get-tuple-element.30), channel_id=1, source_target_pairs={{0,16},{4,20},{8,24},{12,28},{16,0},{20,4},{24,8},{28,12},{1,17},{... | collective-permute-start | bytes 196616 | tf_op jit(solution)/shard_map/ppermute | solution.py:70
  20.5 1.4 %collective-permute-start.6 = (bf16[256,128]{1,0:T(8,128)(2,1)S(1)}, bf16[256,128]{1,0:T(8,128)(2,1)S(1)}, u32[]{:S(2)}, u32[]{:S(2)}) collective-permute-start(bf16[256,128]{1,0:T(8,128)(2,1)S(1)} %get-tuple-element.31), channel_id=1, source_target_pairs={{0,24},{4,28},{8,16},{12,20},{16,8},{20,12},{24,0},{28,4},{1,25},{... | collective-permute-start | bytes 196616 | tf_op jit(solution)/shard_map/ppermute | solution.py:70
  21.9 0.8 %collective-permute-done.4.refs_1_ = bf16[256,128]{1,0:T(8,128)(2,1)S(1)} collective-permute-done((bf16[256,128]{1,0:T(8,128)(2,1)S(1)}, bf16[256,128]{1,0:T(8,128)(2,1)S(1)}, u32[]{:S(2)}, u32[]{:S(2)}) %collective-permute-start.4) | collective-permute-done | bytes 65568 | tf_op jit(solution)/shard_map/ppermute | solution.py:70
  22.7 0.6 %collective-permute-done.5.refs_2_ = bf16[256,128]{1,0:T(8,128)(2,1)S(1)} collective-permute-done((bf16[256,128]{1,0:T(8,128)(2,1)S(1)}, bf16[256,128]{1,0:T(8,128)(2,1)S(1)}, u32[]{:S(2)}, u32[]{:S(2)}) %collective-permute-start.5) | collective-permute-done | bytes 65568 | tf_op jit(solution)/shard_map/ppermute | solution.py:70
  23.3 2.4 %collective-permute-done.6.refs_3_ = bf16[256,128]{1,0:T(8,128)(2,1)S(1)} collective-permute-done((bf16[256,128]{1,0:T(8,128)(2,1)S(1)}, bf16[256,128]{1,0:T(8,128)(2,1)S(1)}, u32[]{:S(2)}, u32[]{:S(2)}) %collective-permute-start.6) | collective-permute-done | bytes 65568 | tf_op jit(solution)/shard_map/ppermute | solution.py:70
  25.7 4.0 %conv.1 = (bf16[4,144,128]{2,1,0:T(8,128)(2,1)S(1)}, bf16[4,144,128]{2,1,0:T(8,128)(2,1)S(1)}) custom-call(bf16[256,128]{1,0:T(8,128)(2,1)S(1)} %get-tuple-element.28.refs_0_, bf16[256,128]{1,0:T(8,128)(2,1)S(1)} %collective-permute-done.4.refs_1_, bf16[256,128]{1,0:T(8,128)(2,1)S(1)} %collective-permute-done.5.refs_2_, ...), custom_call_target="tpu_custom_call" | custom-call | tf_op jit(solution)/shard_map/conv/pallas_call | solution.py:285
  29.8 1.4 %collective-permute-done.10.got_ref = bf16[4,144,128]{2,1,0:T(8,128)(2,1)S(1)} collective-permute-done((bf16[4,144,128]{2,1,0:T(8,128)(2,1)S(1)}, bf16[4,144,128]{2,1,0:T(8,128)(2,1)S(1)}, u32[]{:S(2)}, u32[]{:S(2)}) %collective-permute-start.10) | collective-permute-done | bytes 147488 | tf_op jit(solution)/shard_map/ppermute | solution.py:70
  31.1 1.5 %collective-permute-start.11 = (bf16[2,144,128]{2,1,0:T(8,128)(2,1)S(1)}, bf16[2,144,128]{2,1,0:T(8,128)(2,1)S(1)}, u32[]{:S(2)}, u32[]{:S(2)}) collective-permute-start(bf16[2,144,128]{2,1,0:T(8,128)(2,1)S(1)} %get-tuple-element.39), channel_id=1, source_target_pairs={{0,8},{4,12},{8,0},{12,4},{16,24},{20,28},{24,16},{28,20},{1,9},{5... | collective-permute-start | bytes 221192 | tf_op jit(solution)/shard_map/ppermute | solution.py:70
  33.1 1.6 %collective-permute-start.13 = (bf16[2,144,128]{2,1,0:T(8,128)(2,1)S(1)}, bf16[2,144,128]{2,1,0:T(8,128)(2,1)S(1)}, u32[]{:S(2)}, u32[]{:S(2)}) collective-permute-start(bf16[2,144,128]{2,1,0:T(8,128)(2,1)S(1)} %get-tuple-element.41), channel_id=1, source_target_pairs={{0,24},{4,28},{8,16},{12,20},{16,8},{20,12},{24,0},{28,4},{1,25},{... | collective-permute-start | bytes 221192 | tf_op jit(solution)/shard_map/ppermute | solution.py:70
  34.7 0.9 %collective-permute-done.11.refs_1_ = bf16[2,144,128]{2,1,0:T(8,128)(2,1)S(1)} collective-permute-done((bf16[2,144,128]{2,1,0:T(8,128)(2,1)S(1)}, bf16[2,144,128]{2,1,0:T(8,128)(2,1)S(1)}, u32[]{:S(2)}, u32[]{:S(2)}) %collective-permute-start.11) | collective-permute-done | bytes 73760 | tf_op jit(solution)/shard_map/ppermute | solution.py:70
  35.6 3.0 %collective-permute-done.12.refs_2_ = bf16[2,144,128]{2,1,0:T(8,128)(2,1)S(1)} collective-permute-done((bf16[2,144,128]{2,1,0:T(8,128)(2,1)S(1)}, bf16[2,144,128]{2,1,0:T(8,128)(2,1)S(1)}, u32[]{:S(2)}, u32[]{:S(2)}) %collective-permute-start.12) | collective-permute-done | bytes 73760 | tf_op jit(solution)/shard_map/ppermute | solution.py:70
  38.6 0.8 %unpack.1 = (bf16[128,1024]{1,0:T(8,128)(2,1)}, f32[64,64]{1,0:T(8,128)}) custom-call(bf16[2,144,128]{2,1,0:T(8,128)(2,1)S(1)} %get-tuple-element.38.refs_0_, bf16[2,144,128]{2,1,0:T(8,128)(2,1)S(1)} %collective-permute-done.11.refs_1_, bf16[2,144,128]{2,1,0:T(8,128)(2,1)S(1)} %collective-permute-done.12.refs_2_, ...), custom_call_target="tpu_custom_call" | custom-call | tf_op jit(solution)/shard_map/unpack/pallas_call | solution.py:285
  (16 shorter events, 1.3 us)
Async XLA Ops:
  0.6 1.0 %copy-start = (bf16[32,4096]{1,0:T(8,128)(2,1)S(1)}, bf16[32,4096]{1,0:T(8,128)(2,1)}, u32[]{:S(2)}) copy-start(bf16[32,4096]{1,0:T(8,128)(2,1)} %dy_ref.1) | copy-start | bytes 786436
  1.6 0.9 %copy-start.1 = (bf16[128,1024]{1,0:T(8,128)(2,1)S(1)}, bf16[128,1024]{1,0:T(8,128)(2,1)}, u32[]{:S(2)}) copy-start(bf16[128,1024]{1,0:T(8,128)(2,1)} %x_ref.1) | copy-start | bytes 786436
  2.5 0.7 %copy-start.2 = (bf16[64,64]{1,0:T(8,128)(2,1)S(1)}, bf16[64,64]{1,0:T(8,128)(2,1)}, u32[]{:S(2)}) copy-start(bf16[64,64]{1,0:T(8,128)(2,1)} %f_ref.1) | copy-start | bytes 24580
  3.4 1.7 %collective-permute-start = (bf16[1088,128]{1,0:T(8,128)(2,1)S(1)}, bf16[1088,128]{1,0:T(8,128)(2,1)S(1)}, u32[]{:S(2)}, u32[]{:S(2)}) collective-permute-start(bf16[1088,128]{1,0:T(8,128)(2,1)S(1)} %get-tuple-element.23), channel_id=1, source_target_pairs={{0,4},{4,0},{8,12},{12,8},{16,20},{20,16},{24,28},{28,24},{1,5},{5... | collective-permute-start | bytes 835592 | tf_op jit(solution)/shard_map/ppermute | solution.py:70
  5.2 8.8 %collective-permute-start.1 = (bf16[256,128]{1,0:T(8,128)(2,1)S(1)}, bf16[256,128]{1,0:T(8,128)(2,1)S(1)}, u32[]{:S(2)}, u32[]{:S(2)}) collective-permute-start(bf16[256,128]{1,0:T(8,128)(2,1)S(1)} %get-tuple-element.25), channel_id=1, source_target_pairs={{0,1},{1,0},{2,3},{3,2},{4,5},{5,4},{6,7},{7,6},{8,9},{9,8},{10,11... | collective-permute-start | bytes 196616 | tf_op jit(solution)/shard_map/ppermute | solution.py:70
  8.2 12.4 %collective-permute-start.7 = (bf16[288,128]{1,0:T(8,128)(2,1)S(1)}, bf16[288,128]{1,0:T(8,128)(2,1)S(1)}, u32[]{:S(2)}, u32[]{:S(2)}) collective-permute-start(bf16[288,128]{1,0:T(8,128)(2,1)S(1)} %get-tuple-element.33), channel_id=1, source_target_pairs={{0,8},{4,12},{8,0},{12,4},{16,24},{20,28},{24,16},{28,20},{1,9},{5... | collective-permute-start | bytes 221192 | tf_op jit(solution)/shard_map/ppermute | solution.py:70
  9.7 7.2 %collective-permute-start.2 = (bf16[256,128]{1,0:T(8,128)(2,1)S(1)}, bf16[256,128]{1,0:T(8,128)(2,1)S(1)}, u32[]{:S(2)}, u32[]{:S(2)}) collective-permute-start(bf16[256,128]{1,0:T(8,128)(2,1)S(1)} %get-tuple-element.26), channel_id=1, source_target_pairs={{0,2},{1,3},{2,0},{3,1},{4,6},{5,7},{6,4},{7,5},{8,10},{9,11},{10,... | collective-permute-start | bytes 196616 | tf_op jit(solution)/shard_map/ppermute | solution.py:70
  12.2 6.1 %collective-permute-start.3 = (bf16[256,128]{1,0:T(8,128)(2,1)S(1)}, bf16[256,128]{1,0:T(8,128)(2,1)S(1)}, u32[]{:S(2)}, u32[]{:S(2)}) collective-permute-start(bf16[256,128]{1,0:T(8,128)(2,1)S(1)} %get-tuple-element.27), channel_id=1, source_target_pairs={{0,3},{1,2},{2,1},{3,0},{4,7},{5,6},{6,5},{7,4},{8,11},{9,10},{10,... | collective-permute-start | bytes 196616 | tf_op jit(solution)/shard_map/ppermute | solution.py:70
  12.5 9.4 %collective-permute-start.8 = (bf16[288,128]{1,0:T(8,128)(2,1)S(1)}, bf16[288,128]{1,0:T(8,128)(2,1)S(1)}, u32[]{:S(2)}, u32[]{:S(2)}) collective-permute-start(bf16[288,128]{1,0:T(8,128)(2,1)S(1)} %get-tuple-element.34), channel_id=1, source_target_pairs={{0,16},{4,20},{8,24},{12,28},{16,0},{20,4},{24,8},{28,12},{1,17},{... | collective-permute-start | bytes 221192 | tf_op jit(solution)/shard_map/ppermute | solution.py:70
  14.0 7.9 %collective-permute-start.9 = (bf16[288,128]{1,0:T(8,128)(2,1)S(1)}, bf16[288,128]{1,0:T(8,128)(2,1)S(1)}, u32[]{:S(2)}, u32[]{:S(2)}) collective-permute-start(bf16[288,128]{1,0:T(8,128)(2,1)S(1)} %get-tuple-element.35), channel_id=1, source_target_pairs={{0,24},{4,28},{8,16},{12,20},{16,8},{20,12},{24,0},{28,4},{1,25},{... | collective-permute-start | bytes 221192 | tf_op jit(solution)/shard_map/ppermute | solution.py:70
  18.3 4.3 %collective-permute-start.4 = (bf16[256,128]{1,0:T(8,128)(2,1)S(1)}, bf16[256,128]{1,0:T(8,128)(2,1)S(1)}, u32[]{:S(2)}, u32[]{:S(2)}) collective-permute-start(bf16[256,128]{1,0:T(8,128)(2,1)S(1)} %get-tuple-element.29), channel_id=1, source_target_pairs={{0,8},{4,12},{8,0},{12,4},{16,24},{20,28},{24,16},{28,20},{1,9},{5... | collective-permute-start | bytes 196616 | tf_op jit(solution)/shard_map/ppermute | solution.py:70
  19.0 4.3 %collective-permute-start.5 = (bf16[256,128]{1,0:T(8,128)(2,1)S(1)}, bf16[256,128]{1,0:T(8,128)(2,1)S(1)}, u32[]{:S(2)}, u32[]{:S(2)}) collective-permute-start(bf16[256,128]{1,0:T(8,128)(2,1)S(1)} %get-tuple-element.30), channel_id=1, source_target_pairs={{0,16},{4,20},{8,24},{12,28},{16,0},{20,4},{24,8},{28,12},{1,17},{... | collective-permute-start | bytes 196616 | tf_op jit(solution)/shard_map/ppermute | solution.py:70
  20.5 5.2 %collective-permute-start.6 = (bf16[256,128]{1,0:T(8,128)(2,1)S(1)}, bf16[256,128]{1,0:T(8,128)(2,1)S(1)}, u32[]{:S(2)}, u32[]{:S(2)}) collective-permute-start(bf16[256,128]{1,0:T(8,128)(2,1)S(1)} %get-tuple-element.31), channel_id=1, source_target_pairs={{0,24},{4,28},{8,16},{12,20},{16,8},{20,12},{24,0},{28,4},{1,25},{... | collective-permute-start | bytes 196616 | tf_op jit(solution)/shard_map/ppermute | solution.py:70
  29.7 1.4 %collective-permute-start.10 = (bf16[4,144,128]{2,1,0:T(8,128)(2,1)S(1)}, bf16[4,144,128]{2,1,0:T(8,128)(2,1)S(1)}, u32[]{:S(2)}, u32[]{:S(2)}) collective-permute-start(bf16[4,144,128]{2,1,0:T(8,128)(2,1)S(1)} %get-tuple-element.37), channel_id=1, source_target_pairs={{0,4},{4,0},{8,12},{12,8},{16,20},{20,16},{24,28},{28,24},{1,5},{5... | collective-permute-start | bytes 442376 | tf_op jit(solution)/shard_map/ppermute | solution.py:70
  31.1 4.4 %collective-permute-start.11 = (bf16[2,144,128]{2,1,0:T(8,128)(2,1)S(1)}, bf16[2,144,128]{2,1,0:T(8,128)(2,1)S(1)}, u32[]{:S(2)}, u32[]{:S(2)}) collective-permute-start(bf16[2,144,128]{2,1,0:T(8,128)(2,1)S(1)} %get-tuple-element.39), channel_id=1, source_target_pairs={{0,8},{4,12},{8,0},{12,4},{16,24},{20,28},{24,16},{28,20},{1,9},{5... | collective-permute-start | bytes 221192 | tf_op jit(solution)/shard_map/ppermute | solution.py:70
  32.6 5.9 %collective-permute-start.12 = (bf16[2,144,128]{2,1,0:T(8,128)(2,1)S(1)}, bf16[2,144,128]{2,1,0:T(8,128)(2,1)S(1)}, u32[]{:S(2)}, u32[]{:S(2)}) collective-permute-start(bf16[2,144,128]{2,1,0:T(8,128)(2,1)S(1)} %get-tuple-element.40), channel_id=1, source_target_pairs={{0,16},{4,20},{8,24},{12,28},{16,0},{20,4},{24,8},{28,12},{1,17},{... | collective-permute-start | bytes 221192 | tf_op jit(solution)/shard_map/ppermute | solution.py:70
  33.1 5.4 %collective-permute-start.13 = (bf16[2,144,128]{2,1,0:T(8,128)(2,1)S(1)}, bf16[2,144,128]{2,1,0:T(8,128)(2,1)S(1)}, u32[]{:S(2)}, u32[]{:S(2)}) collective-permute-start(bf16[2,144,128]{2,1,0:T(8,128)(2,1)S(1)} %get-tuple-element.41), channel_id=1, source_target_pairs={{0,24},{4,28},{8,16},{12,20},{16,8},{20,12},{24,0},{28,4},{1,25},{... | collective-permute-start | bytes 221192 | tf_op jit(solution)/shard_map/ppermute | solution.py:70

commit v4 on v3

--- a/solution.py
+++ b/solution.py
@@ -70,6 +70,15 @@
     return lax.ppermute(value, axis, pairs)
 
 
+def partners(count):
+    return [(count - step) % count for step in range(count)]
+
+
+def fan_out(pieces, axis, unit):
+    masks = partners(len(pieces))[1:]
+    return [pieces[0]] + [xor_permute(p, axis, m * unit) for p, m in zip(pieces[1:], masks)]
+
+
 def roll_left(value, steps):
     width = value.shape[-1]
     return pltpu.roll(value, (width - steps) % width, value.ndim - 1)
@@ -84,92 +93,113 @@
     return pl.ds(pl.multiple_of(index * size, 16), size)
 
 
-def split_kernel(n_seq, n_chan, dy_ref, x_ref, f_ref, keep_ref, send_ref):
-    _, core, _ = place()
-    chips = n_seq // 2
-    rows = dy_ref.shape[0]
-    block_len = x_ref.shape[0]
-    taps_here, groups_here = f_ref.shape
-    per_dest = groups_here // n_seq
-    by_group = f_ref[...].astype(jnp.float32).T
-    by_group = jnp.concatenate(
-        [by_group, jnp.zeros((groups_here, LANES - taps_here), jnp.float32)], axis=1
-    )
-    rest = jnp.zeros((EXTRA - per_dest, LANES), jnp.float32)
-    for flip, out_ref in ((0, keep_ref), (1, send_ref)):
-        to_core = core ^ flip
-        for chan in range(n_chan):
-            for chip in range(chips):
-                column = (chan * n_seq + 2 * chip + to_core) * LANES
-                at = (chan * chips + chip) * rows
-                out_ref[at : at + rows] = dy_ref[:, pl.ds(pl.multiple_of(column, LANES), LANES)]
-        base = n_chan * chips * rows
-        for chip in range(chips):
-            column = (2 * chip + to_core) * LANES
-            at = base + chip * (block_len + EXTRA)
-            out_ref[at : at + block_len] = x_ref[:, pl.ds(pl.multiple_of(column, LANES), LANES)]
-            first = 2 * chip * per_dest
-            taps = jnp.where(
-                to_core == 0,
-                by_group[first : first + per_dest],
-                by_group[first + per_dest : first + 2 * per_dest],
-            )
+def own_grads_kernel(n_seq, in_ref, out_ref):
+    _, core, chan = place()
+    n_chan, size, _ = out_ref.shape
+    rows = in_ref.shape[0]
+    for index, bits in enumerate(partners(n_chan)):
+        for chip in range(size // rows):
+            column = ((chan ^ bits) * n_seq + 2 * chip + core) * LANES
+            out_ref[index, chip * rows : (chip + 1) * rows] = in_ref[
+                :, pl.ds(pl.multiple_of(column, LANES), LANES)
+            ]
+
+
+def fan_grads_kernel(n_seq, own_ref, other_ref, *out_refs):
+    _, core, chan = place()
+    rows = other_ref.shape[0]
+    size = own_ref.shape[1]
+    for index, bits in enumerate(partners(len(out_refs))):
+        out_refs[index][:size] = own_ref[index]
+        for chip in range(size // rows):
+            column = ((chan ^ bits) * n_seq + 2 * chip + core) * LANES
+            at = size + chip * rows
+            out_refs[index][at : at + rows] = other_ref[
+                :, pl.ds(pl.multiple_of(column, LANES), LANES)
+            ]
+
+
+def fan_inputs_kernel(x_own_ref, x_other_ref, f_own_ref, f_other_ref, *refs):
+    *out_refs, taps_ref = refs
+    chip, core, _ = place()
+    block_len = x_own_ref.shape[0]
+    taps_here, groups_here = f_own_ref.shape
+    groups = groups_here // (2 * len(out_refs))
+    rest = jnp.zeros((EXTRA - groups, LANES), jnp.float32)
+    for flip, (x_ref, f_ref) in enumerate(((x_own_ref, f_own_ref), (x_other_ref, f_other_ref))):
+        taps_ref[flip] = jnp.concatenate(
+            [
+                f_ref[...].astype(jnp.float32).T,
+                jnp.zeros((groups_here, LANES - taps_here), jnp.float32),
+            ],
+            axis=1,
+        )
+        for bits, out_ref in zip(partners(len(out_refs)), out_refs):
+            target = 2 * (chip ^ bits) + core
+            at = flip * (block_len + EXTRA)
+            out_ref[at : at + block_len] = x_ref[
+                :, pl.ds(pl.multiple_of(target * LANES, LANES), LANES)
+            ]
+            taps = taps_ref[flip, pl.ds(pl.multiple_of(target * groups, groups), groups)]
             out_ref[at + block_len : at + block_len + EXTRA] = jnp.concatenate(
                 [taps, rest], axis=0
             ).astype(jnp.bfloat16)
-
-
-def fan_kernel(n_chan, rows, keep_ref, got_ref, *out_refs):
-    chip, _, chan = place()
-    chips = len(out_refs) - n_chan
-    size = chips * rows
-    base = n_chan * size
-    for bits in range(n_chan):
-        out_refs[bits][:size] = keep_ref[rows_at(chan ^ bits, size)]
-        out_refs[bits][size:] = got_ref[rows_at(chan ^ bits, size)]
-    for bits in range(chips):
-        out_ref = out_refs[n_chan + bits]
-        size = out_ref.shape[0] // 2
-        source = pl.ds(pl.multiple_of(base + (chip ^ bits) * size, 16), size)
-        out_ref[:size] = keep_ref[source]
-        out_ref[size:] = got_ref[source]
 
 
 def regroup_kernel(rows, n_chan, *refs):
     chip, _, chan = place()
     in_refs, out_refs = refs[:n_chan], refs[n_chan:]
     chips = len(out_refs)
-    for to_bits in range(chips):
-        for from_bits in range(n_chan):
+    for to_bits, out_ref in zip(partners(chips), out_refs):
+        for from_bits, in_ref in zip(partners(n_chan), in_refs):
             for core in range(2):
-                out_refs[to_bits][rows_at(core * n_chan + (chan ^ from_bits), rows)] = in_refs[
-                    from_bits
-                ][rows_at(core * chips + (chip ^ to_bits), rows)]
-
-
-def conv_kernel(n_seq, taps_here, *refs):
+                out_ref[rows_at(core * n_chan + (chan ^ from_bits), rows)] = in_ref[
+                    rows_at(core * chips + (chip ^ to_bits), rows)
+                ]
+
+
+def group_of_lane(width, groups):
+    lane = lax.broadcasted_iota(jnp.int32, (STEP, width), 1)
+    return (lane % LANES) // (LANES // groups)
+
+
+def window_at(dye_ref, at, reach):
+    return jnp.concatenate(
+        [dye_ref[at : at + reach], dye_ref[at + STEP : at + STEP + reach]], axis=1
+    )
+
+
+def filtered(toeplitz, window, groups):
+    full = jnp.dot(toeplitz, window, preferred_element_type=jnp.float32)
+    group2 = group_of_lane(2 * LANES, groups)
+    total = full[:STEP]
+    for group in range(1, groups):
+        total = jnp.where(group2 == group, full[group * STEP : (group + 1) * STEP], total)
+    return jnp.concatenate([total[:, :LANES], total[:, LANES:]], axis=0).astype(jnp.bfloat16)
+
+
+def first_kernel(n_seq, taps_here, *refs):
     chips = n_seq // 2
     dy_refs, x_refs = refs[:chips], refs[chips : 2 * chips]
-    keep_ref, send_ref, dye_ref, x_ref, filt_ref, toep_ref, lag_ref, out_ref = refs[2 * chips :]
-    block_len = out_ref.shape[1] - EXTRA
+    send_ref, taps_ref, dye_ref, toep_ref, x_ref, filt_ref, lag_ref, parts_ref = refs[2 * chips :]
+    block_len = x_ref.shape[0] // n_seq
     tokens = n_seq * block_len
     groups = toep_ref.shape[0] // STEP
     taps = n_seq * taps_here
     reach = taps + LANES
-    per_group = LANES // groups
     chip, core, _ = place()
 
     low = lax.broadcasted_iota(jnp.int32, (groups, LANES), 1) < taps_here
-    for bits in range(chips):
+    for bits, dy_piece_ref, x_piece_ref in zip(partners(chips), dy_refs, x_refs):
         pieces = []
         for flip in range(2):
-            source = (chip ^ bits) * 2 + (core ^ flip)
+            block = (2 * (chip ^ bits) + (core ^ flip) - core + n_seq) % n_seq
             at = flip * block_len
-            dye_ref[rows_at(source, block_len)] = dy_refs[bits][at : at + block_len]
+            dye_ref[rows_at(block, block_len)] = dy_piece_ref[at : at + block_len]
             at = flip * (block_len + EXTRA)
-            x_ref[rows_at(source, block_len)] = x_refs[bits][at : at + block_len]
+            x_ref[rows_at(block, block_len)] = x_piece_ref[at : at + block_len]
             at += block_len
-            pieces.append(x_refs[bits][at : at + EXTRA].astype(jnp.float32)[:groups])
+            pieces.append(x_piece_ref[at : at + EXTRA].astype(jnp.float32)[:groups])
         first = jnp.where(core == 0, pieces[0], pieces[1])
         second = jnp.where(core == 0, pieces[1], pieces[0])
         filt_ref[chip ^ bits] = jnp.where(low, first, pltpu.roll(second, taps_here, 1))
@@ -182,42 +212,26 @@
         rows = pltpu.roll(rows, 0, 1, stride=1, stride_axis=0)
         toep_ref[group * STEP : (group + 1) * STEP] = rows.astype(jnp.bfloat16)
 
-    lane2 = lax.broadcasted_iota(jnp.int32, (STEP, 2 * LANES), 1)
-    group2 = (lane2 % LANES) // per_group
-    lane1 = lax.broadcasted_iota(jnp.int32, (STEP, LANES), 1)
-    group1 = lane1 // per_group
+    group2 = group_of_lane(2 * LANES, groups)
     toeplitz = toep_ref[...]
-    for pair in range(tokens // (2 * STEP)):
-        at = pair * 2 * STEP
-        window = jnp.concatenate(
-            [dye_ref[at : at + reach], dye_ref[at + STEP : at + STEP + reach]], axis=1
-        )
-        full = jnp.dot(toeplitz, window, preferred_element_type=jnp.float32)
-        total = jnp.zeros((STEP, 2 * LANES), jnp.float32)
-        for group in range(groups):
-            total = jnp.where(group2 == group, full[group * STEP : (group + 1) * STEP], total)
+    for at in range(0, tokens, 2 * STEP):
+        window = window_at(dye_ref, at, reach)
         block, row = at // block_len, at % block_len
-        out_ref[block, row : row + STEP, :] = total[:, :LANES].astype(jnp.bfloat16)
-        out_ref[block, row + STEP : row + 2 * STEP, :] = total[:, LANES:].astype(jnp.bfloat16)
-        x_first = x_ref[at : at + STEP]
-        x_second = x_ref[at + STEP : at + 2 * STEP]
+        if block % 2 == 1:
+            send_ref[(block // 2 + core) % chips, row : row + 2 * STEP, :] = filtered(
+                toeplitz, window, groups
+            )
+        inputs = jnp.concatenate(
+            [x_ref[at : at + STEP], x_ref[at + STEP : at + 2 * STEP]], axis=1
+        )
         masked = jnp.concatenate(
-            [
-                jnp.concatenate(
-                    [
-                        jnp.where(group1 == group, x_first, jnp.zeros_like(x_first)),
-                        jnp.where(group1 == group, x_second, jnp.zeros_like(x_second)),
-                    ],
-                    axis=1,
-                )
-                for group in range(groups)
-            ],
+            [jnp.where(group2 == group, inputs, jnp.zeros_like(inputs)) for group in range(groups)],
             axis=0,
         )
         part = lax.dot_general(
             masked, window, (((1,), (1,)), ((), ())), preferred_element_type=jnp.float32
         )
-        if pair == 0:
+        if at == 0:
             lag_ref[...] = part
         else:
             lag_ref[...] += part
@@ -247,17 +261,29 @@
             top, bottom = jnp.where(low, parts[0], turned[1]), parts[2]
         else:
             top, bottom = jnp.where(low, turned[0], parts[1]), turned[2]
-        out_ref[seq, block_len:, :] = jnp.concatenate([top, bottom], axis=0).astype(jnp.bfloat16)
-
+        parts_ref[seq] = jnp.concatenate([top, bottom], axis=0).astype(jnp.bfloat16)
     for to_chip in range(chips):
-        keep_ref[to_chip] = out_ref[to_chip * 2 + core]
-        send_ref[to_chip] = out_ref[to_chip * 2 + (1 - core)]
-
-
-def back_kernel(keep_ref, got_ref, *out_refs):
+        taps_ref[to_chip] = parts_ref[2 * to_chip + core]
+        send_ref[to_chip, block_len:, :] = parts_ref[2 * to_chip + 1 - core]
+
+
+def second_kernel(dye_ref, toep_ref, out_ref):
+    chips, block_len, _ = out_ref.shape
+    groups = toep_ref.shape[0] // STEP
+    reach = toep_ref.shape[1]
+    toeplitz = toep_ref[...]
+    for to_chip in range(chips):
+        for row in range(0, block_len, 2 * STEP):
+            window = window_at(dye_ref, 2 * to_chip * block_len + row, reach)
+            out_ref[to_chip, row : row + 2 * STEP, :] = filtered(toeplitz, window, groups)
+
+
+def back_kernel(keep_ref, taps_ref, got_ref, *out_refs):
     chip, _, _ = place()
-    for bits, out_ref in enumerate(out_refs):
-        out_ref[0] = keep_ref[chip ^ bits]
+    block_len = keep_ref.shape[1]
+    for bits, out_ref in zip(partners(len(out_refs)), out_refs):
+        out_ref[0, :block_len, :] = keep_ref[chip ^ bits]
+        out_ref[0, block_len:, :] = taps_ref[chip ^ bits]
         out_ref[1] = got_ref[chip ^ bits]
 
 
@@ -267,7 +293,7 @@
     block_len = dx_ref.shape[0]
     taps_here, groups_here = dh_ref.shape
     groups = groups_here // (2 * len(got_refs))
-    for bits, got_ref in enumerate(got_refs):
+    for bits, got_ref in zip(partners(len(got_refs)), got_refs):
         for flip in range(2):
             source = (chip ^ bits) * 2 + (core ^ flip)
             columns = pl.ds(pl.multiple_of(source * LANES, LANES), LANES)
@@ -306,53 +332,68 @@
         return jax.ShapeDtypeStruct(shape, jnp.bfloat16)
 
     unit = block_len + EXTRA
-    keep, send = local_call(
-        functools.partial(split_kernel, n_seq, n_chan),
-        [half(chips * (n_chan * rows + unit), LANES)] * 2,
-        (out_grads, layer_inputs, filters),
-        "split",
-    )
-    got = xor_permute(send, "seq", 1)
+    dy_other = xor_permute(out_grads, "seq", 1)
+    x_other = xor_permute(layer_inputs, "seq", 1)
+    f_other = xor_permute(filters, "seq", 1)
+    (own,) = local_call(
+        functools.partial(own_grads_kernel, n_seq),
+        [half(n_chan, chips * rows, LANES)],
+        (out_grads,),
+        "own_grads",
+    )
     pieces = local_call(
-        functools.partial(fan_kernel, n_chan, rows),
-        [half(2 * chips * rows, LANES)] * n_chan + [half(2 * unit, LANES)] * chips,
-        (keep, got),
-        "fan",
-    )
-    dy = [pieces[0]] + [xor_permute(pieces[k], "chan", k) for k in range(1, n_chan)]
-    pieces = pieces[n_chan:]
-    x = [pieces[0]] + [xor_permute(pieces[k], "seq", 2 * k) for k in range(1, chips)]
+        functools.partial(fan_grads_kernel, n_seq),
+        [half(2 * chips * rows, LANES)] * n_chan,
+        (own, dy_other),
+        "fan_grads",
+    )
+    dy = fan_out(pieces, "chan", 1)
+    pieces = local_call(
+        fan_inputs_kernel,
+        [half(2 * unit, LANES)] * chips,
+        (layer_inputs, x_other, filters, f_other),
+        "fan_inputs",
+        [pltpu.VMEM((2, groups_here, LANES), jnp.float32)],
+    )
+    x = fan_out(pieces, "seq", 2)
     pieces = local_call(
         functools.partial(regroup_kernel, rows, n_chan),
         [half(2 * n_chan * rows, LANES)] * chips,
         dy,
         "regroup",
     )
-    dy = [pieces[0]] + [xor_permute(pieces[k], "seq", 2 * k) for k in range(1, chips)]
-    keep, send = local_call(
-        functools.partial(conv_kernel, n_seq, taps_here),
-        [half(chips, unit, LANES)] * 2,
+    dy = fan_out(pieces, "seq", 2)
+    send, tap_parts, dye, toeplitz = local_call(
+        functools.partial(first_kernel, n_seq, taps_here),
+        [
+            half(chips, unit, LANES),
+            half(chips, EXTRA, LANES),
+            half(tokens + taps + LANES, LANES),
+            half(groups * STEP, taps + LANES),
+        ],
         (*dy, *x),
-        "conv",
+        "first",
         [
-            pltpu.VMEM((tokens + taps + LANES, LANES), jnp.bfloat16),
             pltpu.VMEM((tokens, LANES), jnp.bfloat16),
             pltpu.VMEM((chips, groups, LANES), jnp.float32),
-            pltpu.VMEM((groups * STEP, taps + LANES), jnp.bfloat16),
             pltpu.VMEM((groups * STEP, taps + LANES), jnp.float32),
-            pltpu.VMEM((n_seq, unit, LANES), jnp.bfloat16),
+            pltpu.VMEM((n_seq, EXTRA, LANES), jnp.bfloat16),
         ],
     )
     got = xor_permute(send, "seq", 1)
-    pieces = local_call(back_kernel, [half(2, unit, LANES)] * chips, (keep, got), "back")
-    back = [pieces[0]] + [xor_permute(pieces[k], "seq", 2 * k) for k in range(1, chips)]
+    (keep,) = local_call(
+        second_kernel, [half(chips, block_len, LANES)], (dye, toeplitz), "second"
+    )
+    pieces = local_call(
+        back_kernel, [half(2, unit, LANES)] * chips, (keep, tap_parts, got), "back"
+    )
     return local_call(
         unpack_kernel,
         [
             half(block_len, n_seq * LANES),
             jax.ShapeDtypeStruct((taps_here, groups_here), jnp.float32),
         ],
-        back,
+        fan_out(pieces, "seq", 2),
         "unpack",
         [pltpu.VMEM((groups_here, LANES), jnp.float32)],
     )

time: 39.6 us -> 34.9 us (0.88)
  waiting for transfers between devices: 14.3 us -> 10.1 us
  local copies, waits for them, and re-layouts: 2.61 us -> 0.96 us
  starting transfers between devices: 16.8 us -> 17.8 us
    ppermute x14 -> x16, waiting for transfers between devices: 14.3 us -> 10.1 us  [xor_permute(): return lax.ppermute(value, axis, pairs)]
    unnamed x6, local copies, waits for them, and re-layouts: 2.61 us -> 0.96 us
    ppermute x14 -> x16, starting transfers between devices: 16.8 us -> 17.8 us  [xor_permute(): return lax.ppermute(value, axis, pairs)]
    pallas_call x6 -> x8, Pallas kernels: 5.01 us -> 5.13 us  [local_call(): pl.pallas_call(kernel, out_shape=out_shape, in_specs=[whole] * len(operan...]
  transfers between devices with their start and end apart: 14 -> 16, of which waited for: 9 -> 8; matrix products, arithmetic and copies ran while one was open for 0% -> 0% of each run, Pallas kernels for 0% -> 3%
where the time goes in v4:
time: 34.9 us; the launch traced here: 34.7 us
  starting transfers between devices  17.8 us (51%)
  waiting for transfers between devices  10.1 us (29%)
  Pallas kernels  5.13 us (15%)
  local copies, waits for them, and re-layouts  0.96 us (3%)
  between operations  0.72 us (2%)
    ppermute x16, starting transfers between devices, xor_permute(): return lax.ppermute(value, axis, pairs)  17.8 us
    ppermute x16, waiting for transfers between devices, xor_permute(): return lax.ppermute(value, axis, pairs)  10.1 us
    pallas_call x8, Pallas kernels, local_call(): pl.pallas_call(kernel, out_shape=out_shape, in_specs=[whole] * len(operan...  5.13 us
    unnamed x6, local copies, waits for them, and re-layouts  0.96 us
  transfers between devices with their start and end apart: 16, of which 8 were waited for; matrix products, arithmetic and copies ran while one was open for 0% of the time, Pallas kernels for 3%

profile of v4, /device:TPU:0, one launch (start us, length us, event | category | flops | bytes accessed | tf_op | source)
XLA Modules:
  0.0 34.7 jit_solution(2250822976601949278)
XLA Ops:
  0.6 0.5 %collective-permute-start = (bf16[32,4096]{1,0:T(8,128)(2,1)}, bf16[32,4096]{1,0:T(8,128)(2,1)S(1)}, u32[]{:S(2)}, u32[]{:S(2)}) collective-permute-start(bf16[32,4096]{1,0:T(8,128)(2,1)} %in_ref.1), channel_id=1, source_target_pairs={{0,4},{4,0},{8,12},{12,8},{16,20},{20,16},{24,28},{28,24},{1,5},{5... | collective-permute-start | bytes 786440 | tf_op jit(solution)/shard_map/ppermute | solution.py:70
  1.2 0.4 %collective-permute-start.8 = (bf16[64,64]{1,0:T(8,128)(2,1)}, bf16[64,64]{1,0:T(8,128)(2,1)S(1)}, u32[]{:S(2)}, u32[]{:S(2)}) collective-permute-start(bf16[64,64]{1,0:T(8,128)(2,1)} %f_own_ref.1), channel_id=1, source_target_pairs={{0,4},{4,0},{8,12},{12,8},{16,20},{20,16},{24,28},{28,24},{1,5},{5... | collective-permute-start | bytes 24584 | tf_op jit(solution)/shard_map/ppermute | solution.py:70
  1.7 0.9 %copy-done = bf16[32,4096]{1,0:T(8,128)(2,1)S(1)} copy-done((bf16[32,4096]{1,0:T(8,128)(2,1)S(1)}, bf16[32,4096]{1,0:T(8,128)(2,1)}, u32[]{:S(2)}) %copy-start) | copy-done | bytes 262168
  2.7 4.9 %collective-permute-start.1 = (bf16[256,128]{1,0:T(8,128)(2,1)S(1)}, bf16[256,128]{1,0:T(8,128)(2,1)S(1)}, u32[]{:S(2)}, u32[]{:S(2)}) collective-permute-start(bf16[256,128]{1,0:T(8,128)(2,1)S(1)} %get-tuple-element.23), channel_id=1, source_target_pairs={{0,3},{1,2},{2,1},{3,0},{4,7},{5,6},{6,5},{7,4},{8,11},{9,10},{10,... | collective-permute-start | bytes 196616 | tf_op jit(solution)/shard_map/ppermute | solution.py:70
  7.7 2.5 %collective-permute-start.9 = (bf16[288,128]{1,0:T(8,128)(2,1)S(1)}, bf16[288,128]{1,0:T(8,128)(2,1)S(1)}, u32[]{:S(2)}, u32[]{:S(2)}) collective-permute-start(bf16[288,128]{1,0:T(8,128)(2,1)S(1)} %get-tuple-element.31), channel_id=1, source_target_pairs={{0,24},{4,28},{8,16},{12,20},{16,8},{20,12},{24,0},{28,4},{1,25},{... | collective-permute-start | bytes 221192 | tf_op jit(solution)/shard_map/ppermute | solution.py:70
  10.3 1.2 %collective-permute-start.3 = (bf16[256,128]{1,0:T(8,128)(2,1)S(1)}, bf16[256,128]{1,0:T(8,128)(2,1)S(1)}, u32[]{:S(2)}, u32[]{:S(2)}) collective-permute-start(bf16[256,128]{1,0:T(8,128)(2,1)S(1)} %get-tuple-element.25), channel_id=1, source_target_pairs={{0,1},{1,0},{2,3},{3,2},{4,5},{5,4},{6,7},{7,6},{8,9},{9,8},{10,11... | collective-permute-start | bytes 196616 | tf_op jit(solution)/shard_map/ppermute | solution.py:70
  11.5 0.5 %collective-permute-start.10 = (bf16[288,128]{1,0:T(8,128)(2,1)S(1)}, bf16[288,128]{1,0:T(8,128)(2,1)S(1)}, u32[]{:S(2)}, u32[]{:S(2)}) collective-permute-start(bf16[288,128]{1,0:T(8,128)(2,1)S(1)} %get-tuple-element.32), channel_id=1, source_target_pairs={{0,16},{4,20},{8,24},{12,28},{16,0},{20,4},{24,8},{28,12},{1,17},{... | collective-permute-start | bytes 221192 | tf_op jit(solution)/shard_map/ppermute | solution.py:70
  12.0 0.5 %collective-permute-start.11 = (bf16[288,128]{1,0:T(8,128)(2,1)S(1)}, bf16[288,128]{1,0:T(8,128)(2,1)S(1)}, u32[]{:S(2)}, u32[]{:S(2)}) collective-permute-start(bf16[288,128]{1,0:T(8,128)(2,1)S(1)} %get-tuple-element.33), channel_id=1, source_target_pairs={{0,8},{4,12},{8,0},{12,4},{16,24},{20,28},{24,16},{28,20},{1,9},{5... | collective-permute-start | bytes 221192 | tf_op jit(solution)/shard_map/ppermute | solution.py:70
  12.5 3.1 %collective-permute-done.2.refs_2_ = bf16[256,128]{1,0:T(8,128)(2,1)S(1)} collective-permute-done((bf16[256,128]{1,0:T(8,128)(2,1)S(1)}, bf16[256,128]{1,0:T(8,128)(2,1)S(1)}, u32[]{:S(2)}, u32[]{:S(2)}) %collective-permute-start.2) | collective-permute-done | bytes 65568 | tf_op jit(solution)/shard_map/ppermute | solution.py:70
  15.7 0.5 %collective-permute-start.4 = (bf16[256,128]{1,0:T(8,128)(2,1)S(1)}, bf16[256,128]{1,0:T(8,128)(2,1)S(1)}, u32[]{:S(2)}, u32[]{:S(2)}) collective-permute-start(bf16[256,128]{1,0:T(8,128)(2,1)S(1)} %get-tuple-element.27), channel_id=1, source_target_pairs={{0,24},{4,28},{8,16},{12,20},{16,8},{20,12},{24,0},{28,4},{1,25},{... | collective-permute-start | bytes 196616 | tf_op jit(solution)/shard_map/ppermute | solution.py:70
  16.2 1.5 %collective-permute-start.5 = (bf16[256,128]{1,0:T(8,128)(2,1)S(1)}, bf16[256,128]{1,0:T(8,128)(2,1)S(1)}, u32[]{:S(2)}, u32[]{:S(2)}) collective-permute-start(bf16[256,128]{1,0:T(8,128)(2,1)S(1)} %get-tuple-element.28), channel_id=1, source_target_pairs={{0,16},{4,20},{8,24},{12,28},{16,0},{20,4},{24,8},{28,12},{1,17},{... | collective-permute-start | bytes 196616 | tf_op jit(solution)/shard_map/ppermute | solution.py:70
  17.7 1.5 %collective-permute-start.6 = (bf16[256,128]{1,0:T(8,128)(2,1)S(1)}, bf16[256,128]{1,0:T(8,128)(2,1)S(1)}, u32[]{:S(2)}, u32[]{:S(2)}) collective-permute-start(bf16[256,128]{1,0:T(8,128)(2,1)S(1)} %get-tuple-element.29), channel_id=1, source_target_pairs={{0,8},{4,12},{8,0},{12,4},{16,24},{20,28},{24,16},{28,20},{1,9},{5... | collective-permute-start | bytes 196616 | tf_op jit(solution)/shard_map/ppermute | solution.py:70
  19.2 1.8 %collective-permute-done.4.refs_1_ = bf16[256,128]{1,0:T(8,128)(2,1)S(1)} collective-permute-done((bf16[256,128]{1,0:T(8,128)(2,1)S(1)}, bf16[256,128]{1,0:T(8,128)(2,1)S(1)}, u32[]{:S(2)}, u32[]{:S(2)}) %collective-permute-start.4) | collective-permute-done | bytes 65568 | tf_op jit(solution)/shard_map/ppermute | solution.py:70
  21.2 0.8 %collective-permute-done.6.refs_3_ = bf16[256,128]{1,0:T(8,128)(2,1)S(1)} collective-permute-done((bf16[256,128]{1,0:T(8,128)(2,1)S(1)}, bf16[256,128]{1,0:T(8,128)(2,1)S(1)}, u32[]{:S(2)}, u32[]{:S(2)}) %collective-permute-start.6) | collective-permute-done | bytes 65568 | tf_op jit(solution)/shard_map/ppermute | solution.py:70
  22.0 3.1 %first.1 = (bf16[4,144,128]{2,1,0:T(8,128)(2,1)S(1)}, bf16[4,16,128]{2,1,0:T(8,128)(2,1)S(1)}, bf16[1664,128]{1,0:T(8,128)(2,1)S(1)}, bf16[256,640]{1,0:T(8,128)(2,1)S(1)}) custom-call(bf16[256,128]{1,0:T(8,128)(2,1)S(1)} %get-tuple-element.26.refs_0_, bf16[256,128]{1,0:T(8,128)(2,1)S(1)} %collective-permute-done.4.refs_1_, ...), custom_call_target="tpu_custom_call" | custom-call | tf_op jit(solution)/shard_map/first/pallas_call | solution.py:311
  25.2 1.0 %second.1.keep_ref = bf16[4,128,128]{2,1,0:T(8,128)(2,1)S(1)} custom-call(bf16[1664,128]{1,0:T(8,128)(2,1)S(1)} %get-tuple-element.34.dye_ref, bf16[256,640]{1,0:T(8,128)(2,1)S(1)} %get-tuple-element.35.toep_ref), custom_call_target="tpu_custom_call" | custom-call | tf_op jit(solution)/shard_map/second/pallas_call | solution.py:311
  26.2 0.4 %collective-permute-done.12.got_ref = bf16[4,144,128]{2,1,0:T(8,128)(2,1)S(1)} collective-permute-done((bf16[4,144,128]{2,1,0:T(8,128)(2,1)S(1)}, bf16[4,144,128]{2,1,0:T(8,128)(2,1)S(1)}, u32[]{:S(2)}, u32[]{:S(2)}) %collective-permute-start.12) | collective-permute-done | bytes 147488 | tf_op jit(solution)/shard_map/ppermute | solution.py:70
  26.6 1.5 %collective-permute-start.13 = (bf16[2,144,128]{2,1,0:T(8,128)(2,1)S(1)}, bf16[2,144,128]{2,1,0:T(8,128)(2,1)S(1)}, u32[]{:S(2)}, u32[]{:S(2)}) collective-permute-start(bf16[2,144,128]{2,1,0:T(8,128)(2,1)S(1)} %get-tuple-element.39), channel_id=1, source_target_pairs={{0,24},{4,28},{8,16},{12,20},{16,8},{20,12},{24,0},{28,4},{1,25},{... | collective-permute-start | bytes 221192 | tf_op jit(solution)/shard_map/ppermute | solution.py:70
  28.1 1.5 %collective-permute-start.14 = (bf16[2,144,128]{2,1,0:T(8,128)(2,1)S(1)}, bf16[2,144,128]{2,1,0:T(8,128)(2,1)S(1)}, u32[]{:S(2)}, u32[]{:S(2)}) collective-permute-start(bf16[2,144,128]{2,1,0:T(8,128)(2,1)S(1)} %get-tuple-element.40), channel_id=1, source_target_pairs={{0,16},{4,20},{8,24},{12,28},{16,0},{20,4},{24,8},{28,12},{1,17},{... | collective-permute-start | bytes 221192 | tf_op jit(solution)/shard_map/ppermute | solution.py:70
  29.6 0.5 %collective-permute-start.15 = (bf16[2,144,128]{2,1,0:T(8,128)(2,1)S(1)}, bf16[2,144,128]{2,1,0:T(8,128)(2,1)S(1)}, u32[]{:S(2)}, u32[]{:S(2)}) collective-permute-start(bf16[2,144,128]{2,1,0:T(8,128)(2,1)S(1)} %get-tuple-element.41), channel_id=1, source_target_pairs={{0,8},{4,12},{8,0},{12,4},{16,24},{20,28},{24,16},{28,20},{1,9},{5... | collective-permute-start | bytes 221192 | tf_op jit(solution)/shard_map/ppermute | solution.py:70
  30.1 2.0 %collective-permute-done.13.refs_1_ = bf16[2,144,128]{2,1,0:T(8,128)(2,1)S(1)} collective-permute-done((bf16[2,144,128]{2,1,0:T(8,128)(2,1)S(1)}, bf16[2,144,128]{2,1,0:T(8,128)(2,1)S(1)}, u32[]{:S(2)}, u32[]{:S(2)}) %collective-permute-start.13) | collective-permute-done | bytes 73760 | tf_op jit(solution)/shard_map/ppermute | solution.py:70
  32.1 1.3 %collective-permute-done.14.refs_2_ = bf16[2,144,128]{2,1,0:T(8,128)(2,1)S(1)} collective-permute-done((bf16[2,144,128]{2,1,0:T(8,128)(2,1)S(1)}, bf16[2,144,128]{2,1,0:T(8,128)(2,1)S(1)}, u32[]{:S(2)}, u32[]{:S(2)}) %collective-permute-start.14) | collective-permute-done | bytes 73760 | tf_op jit(solution)/shard_map/ppermute | solution.py:70
  33.4 0.5 %collective-permute-done.15.refs_3_ = bf16[2,144,128]{2,1,0:T(8,128)(2,1)S(1)} collective-permute-done((bf16[2,144,128]{2,1,0:T(8,128)(2,1)S(1)}, bf16[2,144,128]{2,1,0:T(8,128)(2,1)S(1)}, u32[]{:S(2)}, u32[]{:S(2)}) %collective-permute-start.15) | collective-permute-done | bytes 73760 | tf_op jit(solution)/shard_map/ppermute | solution.py:70
  33.9 0.8 %unpack.1 = (bf16[128,1024]{1,0:T(8,128)(2,1)}, f32[64,64]{1,0:T(8,128)}) custom-call(bf16[2,144,128]{2,1,0:T(8,128)(2,1)S(1)} %get-tuple-element.38.refs_0_, bf16[2,144,128]{2,1,0:T(8,128)(2,1)S(1)} %collective-permute-done.13.refs_1_, bf16[2,144,128]{2,1,0:T(8,128)(2,1)S(1)} %collective-permute-done.14.refs_2_, ...), custom_call_target="tpu_custom_call" | custom-call | tf_op jit(solution)/shard_map/unpack/pallas_call | solution.py:311
  (22 shorter events, 0.6 us)
Async XLA Ops:
  0.6 2.0 %collective-permute-start = (bf16[32,4096]{1,0:T(8,128)(2,1)}, bf16[32,4096]{1,0:T(8,128)(2,1)S(1)}, u32[]{:S(2)}, u32[]{:S(2)}) collective-permute-start(bf16[32,4096]{1,0:T(8,128)(2,1)} %in_ref.1), channel_id=1, source_target_pairs={{0,4},{4,0},{8,12},{12,8},{16,20},{20,16},{24,28},{28,24},{1,5},{5... | collective-permute-start | bytes 786440 | tf_op jit(solution)/shard_map/ppermute | solution.py:70
  1.1 6.5 %collective-permute-start.7 = (bf16[128,1024]{1,0:T(8,128)(2,1)}, bf16[128,1024]{1,0:T(8,128)(2,1)S(1)}, u32[]{:S(2)}, u32[]{:S(2)}) collective-permute-start(bf16[128,1024]{1,0:T(8,128)(2,1)} %x_own_ref.1), channel_id=1, source_target_pairs={{0,4},{4,0},{8,12},{12,8},{16,20},{20,16},{24,28},{28,24},{1,5},{5... | collective-permute-start | bytes 786440 | tf_op jit(solution)/shard_map/ppermute | solution.py:70
  1.2 6.4 %collective-permute-start.8 = (bf16[64,64]{1,0:T(8,128)(2,1)}, bf16[64,64]{1,0:T(8,128)(2,1)S(1)}, u32[]{:S(2)}, u32[]{:S(2)}) collective-permute-start(bf16[64,64]{1,0:T(8,128)(2,1)} %f_own_ref.1), channel_id=1, source_target_pairs={{0,4},{4,0},{8,12},{12,8},{16,20},{20,16},{24,28},{28,24},{1,5},{5... | collective-permute-start | bytes 24584 | tf_op jit(solution)/shard_map/ppermute | solution.py:70
  1.7 0.9 %copy-start = (bf16[32,4096]{1,0:T(8,128)(2,1)S(1)}, bf16[32,4096]{1,0:T(8,128)(2,1)}, u32[]{:S(2)}) copy-start(bf16[32,4096]{1,0:T(8,128)(2,1)} %in_ref.1) | copy-start | bytes 786436
  2.6 5.0 %copy-start.1 = (bf16[128,1024]{1,0:T(8,128)(2,1)S(1)}, bf16[128,1024]{1,0:T(8,128)(2,1)}, u32[]{:S(2)}) copy-start(bf16[128,1024]{1,0:T(8,128)(2,1)} %x_own_ref.1) | copy-start | bytes 786436
  2.7 5.0 %copy-start.2 = (bf16[64,64]{1,0:T(8,128)(2,1)S(1)}, bf16[64,64]{1,0:T(8,128)(2,1)}, u32[]{:S(2)}) copy-start(bf16[64,64]{1,0:T(8,128)(2,1)} %f_own_ref.1) | copy-start | bytes 24580
  2.7 9.2 %collective-permute-start.1 = (bf16[256,128]{1,0:T(8,128)(2,1)S(1)}, bf16[256,128]{1,0:T(8,128)(2,1)S(1)}, u32[]{:S(2)}, u32[]{:S(2)}) collective-permute-start(bf16[256,128]{1,0:T(8,128)(2,1)S(1)} %get-tuple-element.23), channel_id=1, source_target_pairs={{0,3},{1,2},{2,1},{3,0},{4,7},{5,6},{6,5},{7,4},{8,11},{9,10},{10,... | collective-permute-start | bytes 196616 | tf_op jit(solution)/shard_map/ppermute | solution.py:70
  7.7 10.0 %collective-permute-start.9 = (bf16[288,128]{1,0:T(8,128)(2,1)S(1)}, bf16[288,128]{1,0:T(8,128)(2,1)S(1)}, u32[]{:S(2)}, u32[]{:S(2)}) collective-permute-start(bf16[288,128]{1,0:T(8,128)(2,1)S(1)} %get-tuple-element.31), channel_id=1, source_target_pairs={{0,24},{4,28},{8,16},{12,20},{16,8},{20,12},{24,0},{28,4},{1,25},{... | collective-permute-start | bytes 221192 | tf_op jit(solution)/shard_map/ppermute | solution.py:70
  10.3 5.4 %collective-permute-start.2 = (bf16[256,128]{1,0:T(8,128)(2,1)S(1)}, bf16[256,128]{1,0:T(8,128)(2,1)S(1)}, u32[]{:S(2)}, u32[]{:S(2)}) collective-permute-start(bf16[256,128]{1,0:T(8,128)(2,1)S(1)} %get-tuple-element.24), channel_id=1, source_target_pairs={{0,2},{1,3},{2,0},{3,1},{4,6},{5,7},{6,4},{7,5},{8,10},{9,11},{10,... | collective-permute-start | bytes 196616 | tf_op jit(solution)/shard_map/ppermute | solution.py:70
  10.3 5.4 %collective-permute-start.3 = (bf16[256,128]{1,0:T(8,128)(2,1)S(1)}, bf16[256,128]{1,0:T(8,128)(2,1)S(1)}, u32[]{:S(2)}, u32[]{:S(2)}) collective-permute-start(bf16[256,128]{1,0:T(8,128)(2,1)S(1)} %get-tuple-element.25), channel_id=1, source_target_pairs={{0,1},{1,0},{2,3},{3,2},{4,5},{5,4},{6,7},{7,6},{8,9},{9,8},{10,11... | collective-permute-start | bytes 196616 | tf_op jit(solution)/shard_map/ppermute | solution.py:70
  11.5 7.8 %collective-permute-start.10 = (bf16[288,128]{1,0:T(8,128)(2,1)S(1)}, bf16[288,128]{1,0:T(8,128)(2,1)S(1)}, u32[]{:S(2)}, u32[]{:S(2)}) collective-permute-start(bf16[288,128]{1,0:T(8,128)(2,1)S(1)} %get-tuple-element.32), channel_id=1, source_target_pairs={{0,16},{4,20},{8,24},{12,28},{16,0},{20,4},{24,8},{28,12},{1,17},{... | collective-permute-start | bytes 221192 | tf_op jit(solution)/shard_map/ppermute | solution.py:70
  12.0 7.3 %collective-permute-start.11 = (bf16[288,128]{1,0:T(8,128)(2,1)S(1)}, bf16[288,128]{1,0:T(8,128)(2,1)S(1)}, u32[]{:S(2)}, u32[]{:S(2)}) collective-permute-start(bf16[288,128]{1,0:T(8,128)(2,1)S(1)} %get-tuple-element.33), channel_id=1, source_target_pairs={{0,8},{4,12},{8,0},{12,4},{16,24},{20,28},{24,16},{28,20},{1,9},{5... | collective-permute-start | bytes 221192 | tf_op jit(solution)/shard_map/ppermute | solution.py:70
  15.7 5.3 %collective-permute-start.4 = (bf16[256,128]{1,0:T(8,128)(2,1)S(1)}, bf16[256,128]{1,0:T(8,128)(2,1)S(1)}, u32[]{:S(2)}, u32[]{:S(2)}) collective-permute-start(bf16[256,128]{1,0:T(8,128)(2,1)S(1)} %get-tuple-element.27), channel_id=1, source_target_pairs={{0,24},{4,28},{8,16},{12,20},{16,8},{20,12},{24,0},{28,4},{1,25},{... | collective-permute-start | bytes 196616 | tf_op jit(solution)/shard_map/ppermute | solution.py:70
  16.2 5.0 %collective-permute-start.5 = (bf16[256,128]{1,0:T(8,128)(2,1)S(1)}, bf16[256,128]{1,0:T(8,128)(2,1)S(1)}, u32[]{:S(2)}, u32[]{:S(2)}) collective-permute-start(bf16[256,128]{1,0:T(8,128)(2,1)S(1)} %get-tuple-element.28), channel_id=1, source_target_pairs={{0,16},{4,20},{8,24},{12,28},{16,0},{20,4},{24,8},{28,12},{1,17},{... | collective-permute-start | bytes 196616 | tf_op jit(solution)/shard_map/ppermute | solution.py:70
  17.7 4.3 %collective-permute-start.6 = (bf16[256,128]{1,0:T(8,128)(2,1)S(1)}, bf16[256,128]{1,0:T(8,128)(2,1)S(1)}, u32[]{:S(2)}, u32[]{:S(2)}) collective-permute-start(bf16[256,128]{1,0:T(8,128)(2,1)S(1)} %get-tuple-element.29), channel_id=1, source_target_pairs={{0,8},{4,12},{8,0},{12,4},{16,24},{20,28},{24,16},{28,20},{1,9},{5... | collective-permute-start | bytes 196616 | tf_op jit(solution)/shard_map/ppermute | solution.py:70
  25.1 1.4 %collective-permute-start.12 = (bf16[4,144,128]{2,1,0:T(8,128)(2,1)S(1)}, bf16[4,144,128]{2,1,0:T(8,128)(2,1)S(1)}, u32[]{:S(2)}, u32[]{:S(2)}) collective-permute-start(bf16[4,144,128]{2,1,0:T(8,128)(2,1)S(1)} %get-tuple-element.37), channel_id=1, source_target_pairs={{0,4},{4,0},{8,12},{12,8},{16,20},{20,16},{24,28},{28,24},{1,5},{5... | collective-permute-start | bytes 442376 | tf_op jit(solution)/shard_map/ppermute | solution.py:70
  26.6 5.5 %collective-permute-start.13 = (bf16[2,144,128]{2,1,0:T(8,128)(2,1)S(1)}, bf16[2,144,128]{2,1,0:T(8,128)(2,1)S(1)}, u32[]{:S(2)}, u32[]{:S(2)}) collective-permute-start(bf16[2,144,128]{2,1,0:T(8,128)(2,1)S(1)} %get-tuple-element.39), channel_id=1, source_target_pairs={{0,24},{4,28},{8,16},{12,20},{16,8},{20,12},{24,0},{28,4},{1,25},{... | collective-permute-start | bytes 221192 | tf_op jit(solution)/shard_map/ppermute | solution.py:70
  28.1 5.4 %collective-permute-start.14 = (bf16[2,144,128]{2,1,0:T(8,128)(2,1)S(1)}, bf16[2,144,128]{2,1,0:T(8,128)(2,1)S(1)}, u32[]{:S(2)}, u32[]{:S(2)}) collective-permute-start(bf16[2,144,128]{2,1,0:T(8,128)(2,1)S(1)} %get-tuple-element.40), channel_id=1, source_target_pairs={{0,16},{4,20},{8,24},{12,28},{16,0},{20,4},{24,8},{28,12},{1,17},{... | collective-permute-start | bytes 221192 | tf_op jit(solution)/shard_map/ppermute | solution.py:70
  29.6 4.4 %collective-permute-start.15 = (bf16[2,144,128]{2,1,0:T(8,128)(2,1)S(1)}, bf16[2,144,128]{2,1,0:T(8,128)(2,1)S(1)}, u32[]{:S(2)}, u32[]{:S(2)}) collective-permute-start(bf16[2,144,128]{2,1,0:T(8,128)(2,1)S(1)} %get-tuple-element.41), channel_id=1, source_target_pairs={{0,8},{4,12},{8,0},{12,4},{16,24},{20,28},{24,16},{28,20},{1,9},{5... | collective-permute-start | bytes 221192 | tf_op jit(solution)/shard_map/ppermute | solution.py:70

commit v5 on v4

--- a/solution.py
+++ b/solution.py
@@ -93,30 +93,12 @@
     return pl.ds(pl.multiple_of(index * size, 16), size)
 
 
-def own_grads_kernel(n_seq, in_ref, out_ref):
-    _, core, chan = place()
-    n_chan, size, _ = out_ref.shape
-    rows = in_ref.shape[0]
-    for index, bits in enumerate(partners(n_chan)):
-        for chip in range(size // rows):
-            column = ((chan ^ bits) * n_seq + 2 * chip + core) * LANES
-            out_ref[index, chip * rows : (chip + 1) * rows] = in_ref[
-                :, pl.ds(pl.multiple_of(column, LANES), LANES)
-            ]
-
-
-def fan_grads_kernel(n_seq, own_ref, other_ref, *out_refs):
-    _, core, chan = place()
-    rows = other_ref.shape[0]
-    size = own_ref.shape[1]
-    for index, bits in enumerate(partners(len(out_refs))):
-        out_refs[index][:size] = own_ref[index]
-        for chip in range(size // rows):
-            column = ((chan ^ bits) * n_seq + 2 * chip + core) * LANES
-            at = size + chip * rows
-            out_refs[index][at : at + rows] = other_ref[
-                :, pl.ds(pl.multiple_of(column, LANES), LANES)
-            ]
+def fan_grads_kernel(n_seq, in_ref, out_ref):
+    n_chan = out_ref.shape[0] // n_seq
+    for seq in range(n_seq):
+        for chan in range(n_chan):
+            start = (chan * n_seq + seq) * LANES
+            out_ref[seq * n_chan + chan] = in_ref[:, start : start + LANES]
 
 
 def fan_inputs_kernel(x_own_ref, x_other_ref, f_own_ref, f_other_ref, *refs):
@@ -146,16 +128,32 @@
             ).astype(jnp.bfloat16)
 
 
-def regroup_kernel(rows, n_chan, *refs):
-    chip, _, chan = place()
-    in_refs, out_refs = refs[:n_chan], refs[n_chan:]
-    chips = len(out_refs)
-    for to_bits, out_ref in zip(partners(chips), out_refs):
-        for from_bits, in_ref in zip(partners(n_chan), in_refs):
-            for core in range(2):
-                out_ref[rows_at(core * n_chan + (chan ^ from_bits), rows)] = in_ref[
-                    rows_at(core * chips + (chip ^ to_bits), rows)
-                ]
+def toeplitz_kernel(n_seq, taps_here, *refs):
+    chips = n_seq // 2
+    in_refs = refs[:chips]
+    toep_ref, x_ref, filt_ref = refs[chips:]
+    block_len = x_ref.shape[0] // n_seq
+    groups = toep_ref.shape[0] // STEP
+    reach = toep_ref.shape[1]
+    chip, core, _ = place()
+    low = lax.broadcasted_iota(jnp.int32, (groups, LANES), 1) < taps_here
+    for bits, in_ref in zip(partners(chips), in_refs):
+        pieces = []
+        for flip in range(2):
+            block = (2 * (chip ^ bits) + (core ^ flip) - core + n_seq) % n_seq
+            at = flip * (block_len + EXTRA)
+            x_ref[rows_at(block, block_len)] = in_ref[at : at + block_len]
+            at += block_len
+            pieces.append(in_ref[at : at + EXTRA].astype(jnp.float32)[:groups])
+        first = jnp.where(core == 0, pieces[0], pieces[1])
+        second = jnp.where(core == 0, pieces[1], pieces[0])
+        filt_ref[chip ^ bits] = jnp.where(low, first, pltpu.roll(second, taps_here, 1))
+    tiles = [filt_ref[tile] for tile in range(chips)]
+    filt = jnp.concatenate(tiles + [jnp.zeros((groups, LANES), jnp.float32)], axis=1)
+    for group in range(groups):
+        rows = jnp.broadcast_to(filt[group : group + 1], (STEP, reach))
+        rows = pltpu.roll(rows, 0, 1, stride=1, stride_axis=0)
+        toep_ref[group * STEP : (group + 1) * STEP] = rows.astype(jnp.bfloat16)
 
 
 def group_of_lane(width, groups):
@@ -178,39 +176,23 @@
     return jnp.concatenate([total[:, :LANES], total[:, LANES:]], axis=0).astype(jnp.bfloat16)
 
 
-def first_kernel(n_seq, taps_here, *refs):
+def first_kernel(
+    n_seq, taps_here, dy_ref, x_ref, toep_ref, send_ref, taps_ref, dye_ref, lag_ref, parts_ref
+):
     chips = n_seq // 2
-    dy_refs, x_refs = refs[:chips], refs[chips : 2 * chips]
-    send_ref, taps_ref, dye_ref, toep_ref, x_ref, filt_ref, lag_ref, parts_ref = refs[2 * chips :]
-    block_len = x_ref.shape[0] // n_seq
-    tokens = n_seq * block_len
+    tokens = dy_ref.shape[0]
+    block_len = tokens // n_seq
     groups = toep_ref.shape[0] // STEP
     taps = n_seq * taps_here
     reach = taps + LANES
-    chip, core, _ = place()
-
+    _, core, _ = place()
     low = lax.broadcasted_iota(jnp.int32, (groups, LANES), 1) < taps_here
-    for bits, dy_piece_ref, x_piece_ref in zip(partners(chips), dy_refs, x_refs):
-        pieces = []
-        for flip in range(2):
-            block = (2 * (chip ^ bits) + (core ^ flip) - core + n_seq) % n_seq
-            at = flip * block_len
-            dye_ref[rows_at(block, block_len)] = dy_piece_ref[at : at + block_len]
-            at = flip * (block_len + EXTRA)
-            x_ref[rows_at(block, block_len)] = x_piece_ref[at : at + block_len]
-            at += block_len
-            pieces.append(x_piece_ref[at : at + EXTRA].astype(jnp.float32)[:groups])
-        first = jnp.where(core == 0, pieces[0], pieces[1])
-        second = jnp.where(core == 0, pieces[1], pieces[0])
-        filt_ref[chip ^ bits] = jnp.where(low, first, pltpu.roll(second, taps_here, 1))
+
+    for block in range(n_seq):
+        dye_ref[block * block_len : (block + 1) * block_len] = dy_ref[
+            rows_at((block + core) % n_seq, block_len)
+        ]
     dye_ref[tokens:] = dye_ref[:reach]
-
-    tiles = [filt_ref[tile] for tile in range(chips)]
-    filt = jnp.concatenate(tiles + [jnp.zeros((groups, LANES), jnp.float32)], axis=1)
-    for group in range(groups):
-        rows = jnp.broadcast_to(filt[group : group + 1], (STEP, reach))
-        rows = pltpu.roll(rows, 0, 1, stride=1, stride_axis=0)
-        toep_ref[group * STEP : (group + 1) * STEP] = rows.astype(jnp.bfloat16)
 
     group2 = group_of_lane(2 * LANES, groups)
     toeplitz = toep_ref[...]
@@ -332,22 +314,15 @@
         return jax.ShapeDtypeStruct(shape, jnp.bfloat16)
 
     unit = block_len + EXTRA
-    dy_other = xor_permute(out_grads, "seq", 1)
     x_other = xor_permute(layer_inputs, "seq", 1)
     f_other = xor_permute(filters, "seq", 1)
-    (own,) = local_call(
-        functools.partial(own_grads_kernel, n_seq),
-        [half(n_chan, chips * rows, LANES)],
+    (dy,) = local_call(
+        functools.partial(fan_grads_kernel, n_seq),
+        [half(n_seq * n_chan, rows, LANES)],
         (out_grads,),
-        "own_grads",
-    )
-    pieces = local_call(
-        functools.partial(fan_grads_kernel, n_seq),
-        [half(2 * chips * rows, LANES)] * n_chan,
-        (own, dy_other),
         "fan_grads",
     )
-    dy = fan_out(pieces, "chan", 1)
+    dy = lax.all_to_all(dy, ("seq", "chan"), split_axis=0, concat_axis=0, tiled=True)
     pieces = local_call(
         fan_inputs_kernel,
         [half(2 * unit, LANES)] * chips,
@@ -355,27 +330,23 @@
         "fan_inputs",
         [pltpu.VMEM((2, groups_here, LANES), jnp.float32)],
     )
-    x = fan_out(pieces, "seq", 2)
-    pieces = local_call(
-        functools.partial(regroup_kernel, rows, n_chan),
-        [half(2 * n_chan * rows, LANES)] * chips,
-        dy,
-        "regroup",
-    )
-    dy = fan_out(pieces, "seq", 2)
-    send, tap_parts, dye, toeplitz = local_call(
+    toeplitz, x = local_call(
+        functools.partial(toeplitz_kernel, n_seq, taps_here),
+        [half(groups * STEP, taps + LANES), half(tokens, LANES)],
+        fan_out(pieces, "seq", 2),
+        "toeplitz",
+        [pltpu.VMEM((chips, groups, LANES), jnp.float32)],
+    )
+    send, tap_parts, dye = local_call(
         functools.partial(first_kernel, n_seq, taps_here),
         [
             half(chips, unit, LANES),
             half(chips, EXTRA, LANES),
             half(tokens + taps + LANES, LANES),
-            half(groups * STEP, taps + LANES),
         ],
-        (*dy, *x),
+        (dy.reshape(tokens, LANES), x, toeplitz),
         "first",
         [
-            pltpu.VMEM((tokens, LANES), jnp.bfloat16),
-            pltpu.VMEM((chips, groups, LANES), jnp.float32),
             pltpu.VMEM((groups * STEP, taps + LANES), jnp.float32),
             pltpu.VMEM((n_seq, EXTRA, LANES), jnp.bfloat16),
         ],

time: 34.9 us -> 32.8 us (0.940)
  starting transfers between devices: 17.8 us -> 15.2 us
  Pallas kernels: 5.13 us -> 5.97 us
  waiting for transfers between devices: 10.1 us -> 9.68 us
    ppermute x16 -> x9, starting transfers between devices: 17.8 us -> 7.94 us  [xor_permute(): return lax.ppermute(value, axis, pairs)]
    all_to_all x0 -> x1, starting transfers between devices: none -> 7.3 us  [by_channels(): lax.all_to_all(dy, ('seq', 'chan'), split_axis=0, concat_axis=0, tiled=True)]
    pallas_call x8 -> x7, Pallas kernels: 5.13 us -> 5.97 us  [local_call(): pl.pallas_call(kernel, out_shape=out_shape, in_specs=[whole] * len(operan...]
    ppermute x16 -> x9, waiting for transfers between devices: 10.1 us -> 9.68 us  [xor_permute(): return lax.ppermute(value, axis, pairs)]
  transfers between devices with their start and end apart: 16 -> 10, of which waited for: 8 -> 7; matrix products, arithmetic and copies ran while one was open for 0% -> 0% of each run, Pallas kernels for 3% -> 4%
where the time goes in v5:
time: 32.8 us; the launch traced here: 32.5 us
  starting transfers between devices  15.2 us (46%)
  waiting for transfers between devices  9.68 us (30%)
  Pallas kernels  5.97 us (18%)
  local copies, waits for them, and re-layouts  0.95 us (3%)
  between operations  0.69 us (2%)
    ppermute x9, waiting for transfers between devices, xor_permute(): return lax.ppermute(value, axis, pairs)  9.68 us
    ppermute x9, starting transfers between devices, xor_permute(): return lax.ppermute(value, axis, pairs)  7.94 us
    all_to_all x1, starting transfers between devices, by_channels(): lax.all_to_all(dy, ('seq', 'chan'), split_axis=0, concat_axis=0, tiled=True)  7.3 us
    pallas_call x7, Pallas kernels, local_call(): pl.pallas_call(kernel, out_shape=out_shape, in_specs=[whole] * len(operan...  5.97 us
    unnamed x6, local copies, waits for them, and re-layouts  0.95 us
  transfers between devices with their start and end apart: 10, of which 7 were waited for; matrix products, arithmetic and copies ran while one was open for 0% of the time, Pallas kernels for 4%

profile of v5, /device:TPU:0, one launch (start us, length us, event | category | flops | bytes accessed | tf_op | source)
XLA Modules:
  0.0 32.5 jit_solution(8085660450447477221)
XLA Ops:
  0.6 0.9 %copy-done = bf16[32,4096]{1,0:T(8,128)(2,1)S(1)} copy-done((bf16[32,4096]{1,0:T(8,128)(2,1)S(1)}, bf16[32,4096]{1,0:T(8,128)(2,1)}, u32[]{:S(2)}) %copy-start) | copy-done | bytes 262168
  1.6 0.7 %fan_grads.1 = bf16[32,32,128]{2,1,0:T(8,128)(2,1)} custom-call(bf16[32,4096]{1,0:T(8,128)(2,1)S(1)} %copy-done), custom_call_target="tpu_custom_call" | custom-call | tf_op jit(solution)/shard_map/fan_grads/pallas_call | solution.py:293
  2.3 7.3 %all-to-all-start = ((bf16[32,32,128]{2,1,0:T(8,128)(2,1)}), bf16[32,32,128]{2,1,0:T(8,128)(2,1)S(1)}, u32[]{:S(2)}, u32[]{:S(2)}) async-start(bf16[32,32,128]{2,1,0:T(8,128)(2,1)} %fan_grads.1), calls=%async_computation | async-start | bytes 524288 | tf_op jit(solution)/shard_map/all_to_all | solution.py:325
  9.6 0.3 collective-permute-start
  10.0 0.3 collective-permute-start.1
  10.2 1.0 %collective-permute-done.1.f_other_ref = bf16[64,64]{1,0:T(8,128)(2,1)S(1)} collective-permute-done((bf16[64,64]{1,0:T(8,128)(2,1)S(1)}, bf16[64,64]{1,0:T(8,128)(2,1)S(1)}, u32[]{:S(2)}, u32[]{:S(2)}) %collective-permute-start.1) | collective-permute-done | bytes 8224 | tf_op jit(solution)/shard_map/ppermute | solution.py:70
  11.3 0.1 fan_inputs.1
  11.4 2.7 %collective-permute-start.2 = (bf16[288,128]{1,0:T(8,128)(2,1)S(1)}, bf16[288,128]{1,0:T(8,128)(2,1)S(1)}, u32[]{:S(2)}, u32[]{:S(2)}) collective-permute-start(bf16[288,128]{1,0:T(8,128)(2,1)S(1)} %get-tuple-element.16), channel_id=1, source_target_pairs={{0,24},{4,28},{8,16},{12,20},{16,8},{20,12},{24,0},{28,4},{1,25},{... | collective-permute-start | bytes 221192 | tf_op jit(solution)/shard_map/ppermute | solution.py:70
  14.1 0.6 %collective-permute-start.3 = (bf16[288,128]{1,0:T(8,128)(2,1)S(1)}, bf16[288,128]{1,0:T(8,128)(2,1)S(1)}, u32[]{:S(2)}, u32[]{:S(2)}) collective-permute-start(bf16[288,128]{1,0:T(8,128)(2,1)S(1)} %get-tuple-element.17), channel_id=1, source_target_pairs={{0,16},{4,20},{8,24},{12,28},{16,0},{20,4},{24,8},{28,12},{1,17},{... | collective-permute-start | bytes 221192 | tf_op jit(solution)/shard_map/ppermute | solution.py:70
  14.7 0.3 collective-permute-start.4
  14.9 2.9 %collective-permute-done.2.refs_1_ = bf16[288,128]{1,0:T(8,128)(2,1)S(1)} collective-permute-done((bf16[288,128]{1,0:T(8,128)(2,1)S(1)}, bf16[288,128]{1,0:T(8,128)(2,1)S(1)}, u32[]{:S(2)}, u32[]{:S(2)}) %collective-permute-start.2) | collective-permute-done | bytes 73760 | tf_op jit(solution)/shard_map/ppermute | solution.py:70
  17.8 1.9 %collective-permute-done.3.refs_2_ = bf16[288,128]{1,0:T(8,128)(2,1)S(1)} collective-permute-done((bf16[288,128]{1,0:T(8,128)(2,1)S(1)}, bf16[288,128]{1,0:T(8,128)(2,1)S(1)}, u32[]{:S(2)}, u32[]{:S(2)}) %collective-permute-start.3) | collective-permute-done | bytes 73760 | tf_op jit(solution)/shard_map/ppermute | solution.py:70
  19.8 0.2 toeplitz.1
  20.0 3.1 %first.1 = (bf16[4,144,128]{2,1,0:T(8,128)(2,1)S(1)}, bf16[4,16,128]{2,1,0:T(8,128)(2,1)S(1)}, bf16[1664,128]{1,0:T(8,128)(2,1)S(1)}) custom-call(bf16[1024,128]{1,0:T(8,128)(2,1)S(1)} %bitcast.1, bf16[1024,128]{1,0:T(8,128)(2,1)S(1)} %get-tuple-element.19.x_ref, bf16[256,640]{1,0:T(8,128)(2,1)S(1)} %get-tuple-element.20.toep_ref), custom_call_target="tpu_custom_call" | custom-call | tf_op jit(solution)/shard_map/first/pallas_call | solution.py:293
  23.1 0.3 collective-permute-start.5
  23.4 1.0 %second.1.keep_ref = bf16[4,128,128]{2,1,0:T(8,128)(2,1)S(1)} custom-call(bf16[1664,128]{1,0:T(8,128)(2,1)S(1)} %get-tuple-element.21.dye_ref, bf16[256,640]{1,0:T(8,128)(2,1)S(1)} %get-tuple-element.20.toep_ref), custom_call_target="tpu_custom_call" | custom-call | tf_op jit(solution)/shard_map/second/pallas_call | solution.py:293
  24.4 0.2 collective-permute-done.5.got_ref
  24.6 1.5 %collective-permute-start.6 = (bf16[2,144,128]{2,1,0:T(8,128)(2,1)S(1)}, bf16[2,144,128]{2,1,0:T(8,128)(2,1)S(1)}, u32[]{:S(2)}, u32[]{:S(2)}) collective-permute-start(bf16[2,144,128]{2,1,0:T(8,128)(2,1)S(1)} %get-tuple-element.25), channel_id=1, source_target_pairs={{0,24},{4,28},{8,16},{12,20},{16,8},{20,12},{24,0},{28,4},{1,25},{... | collective-permute-start | bytes 221192 | tf_op jit(solution)/shard_map/ppermute | solution.py:70
  26.1 1.3 %collective-permute-start.7 = (bf16[2,144,128]{2,1,0:T(8,128)(2,1)S(1)}, bf16[2,144,128]{2,1,0:T(8,128)(2,1)S(1)}, u32[]{:S(2)}, u32[]{:S(2)}) collective-permute-start(bf16[2,144,128]{2,1,0:T(8,128)(2,1)S(1)} %get-tuple-element.26), channel_id=1, source_target_pairs={{0,16},{4,20},{8,24},{12,28},{16,0},{20,4},{24,8},{28,12},{1,17},{... | collective-permute-start | bytes 221192 | tf_op jit(solution)/shard_map/ppermute | solution.py:70
  27.4 0.7 %collective-permute-start.8 = (bf16[2,144,128]{2,1,0:T(8,128)(2,1)S(1)}, bf16[2,144,128]{2,1,0:T(8,128)(2,1)S(1)}, u32[]{:S(2)}, u32[]{:S(2)}) collective-permute-start(bf16[2,144,128]{2,1,0:T(8,128)(2,1)S(1)} %get-tuple-element.27), channel_id=1, source_target_pairs={{0,8},{4,12},{8,0},{12,4},{16,24},{20,28},{24,16},{28,20},{1,9},{5... | collective-permute-start | bytes 221192 | tf_op jit(solution)/shard_map/ppermute | solution.py:70
  28.1 2.0 %collective-permute-done.6.refs_1_ = bf16[2,144,128]{2,1,0:T(8,128)(2,1)S(1)} collective-permute-done((bf16[2,144,128]{2,1,0:T(8,128)(2,1)S(1)}, bf16[2,144,128]{2,1,0:T(8,128)(2,1)S(1)}, u32[]{:S(2)}, u32[]{:S(2)}) %collective-permute-start.6) | collective-permute-done | bytes 73760 | tf_op jit(solution)/shard_map/ppermute | solution.py:70
  30.1 1.3 %collective-permute-done.7.refs_2_ = bf16[2,144,128]{2,1,0:T(8,128)(2,1)S(1)} collective-permute-done((bf16[2,144,128]{2,1,0:T(8,128)(2,1)S(1)}, bf16[2,144,128]{2,1,0:T(8,128)(2,1)S(1)}, u32[]{:S(2)}, u32[]{:S(2)}) %collective-permute-start.7) | collective-permute-done | bytes 73760 | tf_op jit(solution)/shard_map/ppermute | solution.py:70
  31.5 0.3 collective-permute-done.8.refs_3_
  31.7 0.8 %unpack.1 = (bf16[128,1024]{1,0:T(8,128)(2,1)}, f32[64,64]{1,0:T(8,128)}) custom-call(bf16[2,144,128]{2,1,0:T(8,128)(2,1)S(1)} %get-tuple-element.24.refs_0_, bf16[2,144,128]{2,1,0:T(8,128)(2,1)S(1)} %collective-permute-done.6.refs_1_, bf16[2,144,128]{2,1,0:T(8,128)(2,1)S(1)} %collective-permute-done.7.refs_2_, ...), custom_call_target="tpu_custom_call" | custom-call | tf_op jit(solution)/shard_map/unpack/pallas_call | solution.py:293
  (9 shorter events, 0.0 us)
Async XLA Ops:
  0.6 1.0 %copy-start = (bf16[32,4096]{1,0:T(8,128)(2,1)S(1)}, bf16[32,4096]{1,0:T(8,128)(2,1)}, u32[]{:S(2)}) copy-start(bf16[32,4096]{1,0:T(8,128)(2,1)} %in_ref.1) | copy-start | bytes 786436
  2.3 7.3 %copy-start.1 = (bf16[128,1024]{1,0:T(8,128)(2,1)S(1)}, bf16[128,1024]{1,0:T(8,128)(2,1)}, u32[]{:S(2)}) copy-start(bf16[128,1024]{1,0:T(8,128)(2,1)} %x_own_ref.1) | copy-start | bytes 786436
  2.3 7.6 %copy-start.2 = (bf16[64,64]{1,0:T(8,128)(2,1)S(1)}, bf16[64,64]{1,0:T(8,128)(2,1)}, u32[]{:S(2)}) copy-start(bf16[64,64]{1,0:T(8,128)(2,1)} %f_own_ref.1) | copy-start | bytes 24580
  2.3 17.7 %all-to-all-start = ((bf16[32,32,128]{2,1,0:T(8,128)(2,1)}), bf16[32,32,128]{2,1,0:T(8,128)(2,1)S(1)}, u32[]{:S(2)}, u32[]{:S(2)}) async-start(bf16[32,32,128]{2,1,0:T(8,128)(2,1)} %fan_grads.1), calls=%async_computation | async-start | bytes 524288 | tf_op jit(solution)/shard_map/all_to_all | solution.py:325
  9.6 1.6 %collective-permute-start = (bf16[128,1024]{1,0:T(8,128)(2,1)S(1)}, bf16[128,1024]{1,0:T(8,128)(2,1)S(1)}, u32[]{:S(2)}, u32[]{:S(2)}) collective-permute-start(bf16[128,1024]{1,0:T(8,128)(2,1)S(1)} %copy-done.1), channel_id=1, source_target_pairs={{0,4},{4,0},{8,12},{12,8},{16,20},{20,16},{24,28},{28,24},{1,5},{5... | collective-permute-start | bytes 786440 | tf_op jit(solution)/shard_map/ppermute | solution.py:70
  10.0 1.3 %collective-permute-start.1 = (bf16[64,64]{1,0:T(8,128)(2,1)S(1)}, bf16[64,64]{1,0:T(8,128)(2,1)S(1)}, u32[]{:S(2)}, u32[]{:S(2)}) collective-permute-start(bf16[64,64]{1,0:T(8,128)(2,1)S(1)} %copy-done.2), channel_id=1, source_target_pairs={{0,4},{4,0},{8,12},{12,8},{16,20},{20,16},{24,28},{28,24},{1,5},{5... | collective-permute-start | bytes 24584 | tf_op jit(solution)/shard_map/ppermute | solution.py:70
  11.4 6.5 %collective-permute-start.2 = (bf16[288,128]{1,0:T(8,128)(2,1)S(1)}, bf16[288,128]{1,0:T(8,128)(2,1)S(1)}, u32[]{:S(2)}, u32[]{:S(2)}) collective-permute-start(bf16[288,128]{1,0:T(8,128)(2,1)S(1)} %get-tuple-element.16), channel_id=1, source_target_pairs={{0,24},{4,28},{8,16},{12,20},{16,8},{20,12},{24,0},{28,4},{1,25},{... | collective-permute-start | bytes 221192 | tf_op jit(solution)/shard_map/ppermute | solution.py:70
  14.1 5.7 %collective-permute-start.3 = (bf16[288,128]{1,0:T(8,128)(2,1)S(1)}, bf16[288,128]{1,0:T(8,128)(2,1)S(1)}, u32[]{:S(2)}, u32[]{:S(2)}) collective-permute-start(bf16[288,128]{1,0:T(8,128)(2,1)S(1)} %get-tuple-element.17), channel_id=1, source_target_pairs={{0,16},{4,20},{8,24},{12,28},{16,0},{20,4},{24,8},{28,12},{1,17},{... | collective-permute-start | bytes 221192 | tf_op jit(solution)/shard_map/ppermute | solution.py:70
  14.7 5.1 %collective-permute-start.4 = (bf16[288,128]{1,0:T(8,128)(2,1)S(1)}, bf16[288,128]{1,0:T(8,128)(2,1)S(1)}, u32[]{:S(2)}, u32[]{:S(2)}) collective-permute-start(bf16[288,128]{1,0:T(8,128)(2,1)S(1)} %get-tuple-element.18), channel_id=1, source_target_pairs={{0,8},{4,12},{8,0},{12,4},{16,24},{20,28},{24,16},{28,20},{1,9},{5... | collective-permute-start | bytes 221192 | tf_op jit(solution)/shard_map/ppermute | solution.py:70
  23.1 1.4 %collective-permute-start.5 = (bf16[4,144,128]{2,1,0:T(8,128)(2,1)S(1)}, bf16[4,144,128]{2,1,0:T(8,128)(2,1)S(1)}, u32[]{:S(2)}, u32[]{:S(2)}) collective-permute-start(bf16[4,144,128]{2,1,0:T(8,128)(2,1)S(1)} %get-tuple-element.23), channel_id=1, source_target_pairs={{0,4},{4,0},{8,12},{12,8},{16,20},{20,16},{24,28},{28,24},{1,5},{5... | collective-permute-start | bytes 442376 | tf_op jit(solution)/shard_map/ppermute | solution.py:70
  24.6 5.6 %collective-permute-start.6 = (bf16[2,144,128]{2,1,0:T(8,128)(2,1)S(1)}, bf16[2,144,128]{2,1,0:T(8,128)(2,1)S(1)}, u32[]{:S(2)}, u32[]{:S(2)}) collective-permute-start(bf16[2,144,128]{2,1,0:T(8,128)(2,1)S(1)} %get-tuple-element.25), channel_id=1, source_target_pairs={{0,24},{4,28},{8,16},{12,20},{16,8},{20,12},{24,0},{28,4},{1,25},{... | collective-permute-start | bytes 221192 | tf_op jit(solution)/shard_map/ppermute | solution.py:70
  26.1 5.4 %collective-permute-start.7 = (bf16[2,144,128]{2,1,0:T(8,128)(2,1)S(1)}, bf16[2,144,128]{2,1,0:T(8,128)(2,1)S(1)}, u32[]{:S(2)}, u32[]{:S(2)}) collective-permute-start(bf16[2,144,128]{2,1,0:T(8,128)(2,1)S(1)} %get-tuple-element.26), channel_id=1, source_target_pairs={{0,16},{4,20},{8,24},{12,28},{16,0},{20,4},{24,8},{28,12},{1,17},{... | collective-permute-start | bytes 221192 | tf_op jit(solution)/shard_map/ppermute | solution.py:70
  27.4 4.4 %collective-permute-start.8 = (bf16[2,144,128]{2,1,0:T(8,128)(2,1)S(1)}, bf16[2,144,128]{2,1,0:T(8,128)(2,1)S(1)}, u32[]{:S(2)}, u32[]{:S(2)}) collective-permute-start(bf16[2,144,128]{2,1,0:T(8,128)(2,1)S(1)} %get-tuple-element.27), channel_id=1, source_target_pairs={{0,8},{4,12},{8,0},{12,4},{16,24},{20,28},{24,16},{28,20},{1,9},{5... | collective-permute-start | bytes 221192 | tf_op jit(solution)/shard_map/ppermute | solution.py:70

commit v6 on v5

v6 whole, which is shorter than its diff:
```python
import functools

import jax
import jax.numpy as jnp
from jax import lax
from jax.experimental import pallas as pl
from jax.experimental.pallas import tpu as pltpu
from jax.sharding import PartitionSpec as P

LANES = 128
STEP = 32
EXTRA = 16
DEPTH = 1024
VMEM_LIMIT = 40 * 1024 * 1024


def shifted(value, axis, steps):
    count = lax.axis_size(axis)
    pairs = [(source, (source + steps) % count) for source in range(count)]
    return lax.ppermute(value, axis, pairs)


def skewed_sums(products):
    groups_here, length, _ = products.shape
    padded = jnp.pad(products, ((0, 0), (0, 0), (0, length)))
    flat = padded.reshape(groups_here, 2 * length * length)[:, : length * (2 * length - 1)]
    return flat.reshape(groups_here, length, 2 * length - 1).sum(axis=1)


def by_tokens(out_grads, layer_inputs, filters):
    local_grads = lax.all_to_all(out_grads, "chan", split_axis=1, concat_axis=0, tiled=True)
    taps_all = lax.all_gather(filters, "seq", axis=0, tiled=True)
    block_len = local_grads.shape[0]
    chan_width = local_grads.shape[1]
    groups_here = filters.shape[1]
    per_group = chan_width // groups_here
    taps_total = taps_all.shape[0]
    spread_blocks = taps_total // block_len
    filt_rows = taps_all.T
    x_reversed = layer_inputs[::-1].reshape(block_len, groups_here, per_group).transpose(1, 2, 0)
    offsets = lax.broadcasted_iota(jnp.int32, (block_len, block_len), 1) - lax.broadcasted_iota(
        jnp.int32, (block_len, block_len), 0
    )
    dx_total = jnp.zeros((groups_here, per_group, block_len), jnp.float32)
    lag_buffer = jnp.zeros((groups_here, (spread_blocks + 2) * block_len), jnp.float32)
    current = local_grads
    for lag_block in range(spread_blocks + 1):
        if lag_block > 0:
            current = shifted(local_grads, "seq", -lag_block)
        dy_grouped = current.reshape(block_len, groups_here, per_group).transpose(1, 2, 0)
        lag_index = lag_block * block_len + offsets
        inside = (lag_index >= 0) & (lag_index < taps_total)
        picked = jnp.take(filt_rows, jnp.clip(lag_index, 0, taps_total - 1), axis=1)
        toeplitz = jnp.where(inside[None], picked, jnp.zeros((), jnp.bfloat16))
        dx_total = dx_total + jnp.einsum(
            "guv,gkv->gku", toeplitz, dy_grouped, preferred_element_type=jnp.float32
        )
        products = jnp.einsum(
            "gku,gkv->guv", x_reversed, dy_grouped, preferred_element_type=jnp.float32
        )
        start = lag_block * block_len
        lag_buffer = lag_buffer.at[:, start : start + 2 * block_len - 1].add(skewed_sums(products))
    partial_dh = lag_buffer[:, block_len - 1 : block_len - 1 + taps_total].T
    filter_grads = lax.psum_scatter(partial_dh, "seq", scatter_dimension=0, tiled=True)
    input_grads = dx_total.transpose(2, 0, 1).reshape(block_len, chan_width).astype(jnp.bfloat16)
    return (input_grads, filter_grads)


def xor_permute(value, axis, bits):
    pairs = [(source, source ^ bits) for source in range(lax.axis_size(axis))]
    return lax.ppermute(value, axis, pairs)


def partners(count):
    return [(count - step) % count for step in range(count)]


def fan_out(pieces, axis, unit):
    masks = partners(len(pieces))[1:]
    return [pieces[0]] + [xor_permute(p, axis, m * unit) for p, m in zip(pieces[1:], masks)]


def roll_left(value, steps):
    width = value.shape[-1]
    return pltpu.roll(value, (width - steps) % width, value.ndim - 1)


def place():
    seq = lax.axis_index("seq")
    return seq // 2, seq % 2, lax.axis_index("chan")


def rows_at(index, size):
    return pl.ds(pl.multiple_of(index * size, 16), size)


def fan_grads_kernel(n_seq, in_ref, out_ref, sems):
    n_chan = out_ref.shape[0] // n_seq
    copies = []
    for chan in reversed(range(n_chan)):
        for seq in range(n_seq):
            start = (chan * n_seq + seq) * LANES
            to = seq * n_chan + chan
            copies.append(
                pltpu.make_async_copy(
                    in_ref.at[:, start : start + LANES], out_ref.at[to], sems.at[to]
                )
            )
    for copy in copies:
        copy.start()
    for copy in copies:
        copy.wait()


def fan_inputs_kernel(x_own_ref, x_other_ref, f_own_ref, f_other_ref, *refs):
    *out_refs, taps_ref = refs
    chip, core, _ = place()
    block_len = x_own_ref.shape[0]
    taps_here, groups_here = f_own_ref.shape
    groups = groups_here // (2 * len(out_refs))
    rest = jnp.zeros((groups_here, LANES - taps_here), jnp.float32)
    for flip, f_ref in enumerate((f_own_ref, f_other_ref)):
        taps_ref[flip] = jnp.concatenate([f_ref[...].astype(jnp.float32).T, rest], axis=1)
    for bits, out_ref in zip(partners(len(out_refs)), out_refs):
        target = 2 * (chip ^ bits) + core
        columns = pl.ds(pl.multiple_of(target * LANES, LANES), LANES)
        out_ref[:block_len] = x_own_ref[:, columns]
        out_ref[block_len : 2 * block_len] = x_other_ref[:, columns]
        rows = pl.ds(pl.multiple_of(target * groups, groups), groups)
        taps = jnp.concatenate([taps_ref[0, rows], taps_ref[1, rows]], axis=0)
        out_ref[2 * block_len :] = taps.astype(jnp.bfloat16)


def toeplitz_kernel(n_seq, taps_here, *refs):
    chips = n_seq // 2
    in_refs = refs[:chips]
    toep_ref, x_ref, filt_ref = refs[chips:]
    block_len = x_ref.shape[0] // n_seq
    groups = toep_ref.shape[0] // STEP
    reach = toep_ref.shape[1]
    chip, core, _ = place()
    low = lax.broadcasted_iota(jnp.int32, (groups, LANES), 1) < taps_here
    for bits, in_ref in zip(partners(chips), in_refs):
        for flip in range(2):
            block = 2 * (chip ^ bits) + (core ^ flip)
            x_ref[rows_at(block, block_len)] = in_ref[flip * block_len : (flip + 1) * block_len]
        taps = in_ref[2 * block_len :].astype(jnp.float32)
        first = jnp.where(core == 0, taps[:groups], taps[groups:])
        second = jnp.where(core == 0, taps[groups:], taps[:groups])
        filt_ref[chip ^ bits] = jnp.where(low, first, pltpu.roll(second, taps_here, 1))
    tiles = [filt_ref[tile] for tile in range(chips)]
    filt = jnp.concatenate(tiles + [jnp.zeros((groups, LANES), jnp.float32)], axis=1)
    for group in range(groups):
        rows = jnp.broadcast_to(filt[group : group + 1], (STEP, reach))
        rows = pltpu.roll(rows, 0, 1, stride=1, stride_axis=0)
        toep_ref[group * STEP : (group + 1) * STEP] = rows.astype(jnp.bfloat16)


def group_of_lane(rows, width, groups):
    lane = lax.broadcasted_iota(jnp.int32, (rows, width), 1)
    return (lane % LANES) // (LANES // groups)


def filtered(dye_ref, start, toeplitz, groups):
    reach = toeplitz.shape[1]
    window = jnp.concatenate(
        [
            dye_ref[pl.ds(pl.multiple_of(start, STEP), reach)],
            dye_ref[pl.ds(pl.multiple_of(start + STEP, STEP), reach)],
        ],
        axis=1,
    )
    full = jnp.dot(toeplitz, window, preferred_element_type=jnp.float32)
    group2 = group_of_lane(STEP, 2 * LANES, groups)
    total = full[:STEP]
    for group in range(1, groups):
        total = jnp.where(group2 == group, full[group * STEP : (group + 1) * STEP], total)
    return jnp.concatenate([total[:, :LANES], total[:, LANES:]], axis=0).astype(jnp.bfloat16)


def results_for(to_chip, core, dye_ref, toep_ref, taps_ref, out_ref):
    block_len = (out_ref.shape[0] - taps_ref.shape[1]) // 2
    toeplitz = toep_ref[...]
    groups = toeplitz.shape[0] // STEP
    for flip in range(2):
        start = (2 * to_chip + (core ^ flip)) * block_len
        for row in range(0, block_len, 2 * STEP):
            at = flip * block_len + row
            out_ref[at : at + 2 * STEP] = filtered(dye_ref, start + row, toeplitz, groups)
    out_ref[2 * block_len :] = taps_ref[to_chip]


def first_kernel(
    n_seq, taps_here, far, dy_ref, x_ref, toep_ref, dye_ref, taps_ref, out_ref, lag_ref
):
    chips = n_seq // 2
    tokens = dy_ref.shape[0]
    groups = toep_ref.shape[0] // STEP
    taps = n_seq * taps_here
    reach = taps + LANES
    chip, core, _ = place()

    dye_ref[:tokens] = dy_ref[...]
    dye_ref[tokens:] = dy_ref[:reach]

    deep = DEPTH // LANES
    group_in = group_of_lane(STEP, DEPTH, groups)
    for at in range(0, tokens, STEP * deep):
        starts = range(at, at + STEP * deep, STEP)
        windows = jnp.concatenate([dye_ref[row : row + reach] for row in starts], axis=1)
        inputs = jnp.concatenate([x_ref[row : row + STEP] for row in starts], axis=1)
        masked = jnp.concatenate(
            [jnp.where(group_in == group, inputs, jnp.zeros_like(inputs)) for group in range(groups)],
            axis=0,
        )
        part = lax.dot_general(
            masked, windows, (((1,), (1,)), ((), ())), preferred_element_type=jnp.float32
        )
        if at == 0:
            lag_ref[...] = part
        else:
            lag_ref[...] += part

    eights = []
    for group in range(groups):
        at = group * STEP
        rows = lag_ref[at : at + 8]
        for high in range(1, STEP // 8):
            rows = rows + roll_left(lag_ref[at + 8 * high : at + 8 * high + 8], 8 * high)
        eights.append(rows)
    skew = jnp.concatenate(eights, axis=0)
    row_in = lax.broadcasted_iota(jnp.int32, skew.shape, 0) % 8
    for bit in (1, 2, 4):
        skew = jnp.where((row_in & bit) != 0, roll_left(skew, bit), skew)
    dh = skew.reshape(groups, 8, reach).sum(axis=1)[:, :taps]

    high = dh.astype(jnp.bfloat16).astype(jnp.float32)
    rest = dh - high
    low = lax.broadcasted_iota(jnp.int32, (groups, LANES), 1) < taps_here
    for to_chip in range(chips):
        columns = slice(to_chip * LANES, (to_chip + 1) * LANES)
        top, bottom = high[:, columns], rest[:, columns]
        even = jnp.where(low, top, pltpu.roll(bottom, taps_here, 1))
        odd = jnp.where(low, pltpu.roll(top, taps_here, 1), bottom)
        mine = jnp.where(core == 0, even, odd)
        other = jnp.where(core == 0, odd, even)
        taps_ref[to_chip] = jnp.concatenate([mine, other], axis=0).astype(jnp.bfloat16)

    results_for(chip ^ far, core, dye_ref, toep_ref, taps_ref, out_ref)


def more_kernel(masks, dye_ref, toep_ref, taps_ref, *out_refs):
    chip, core, _ = place()
    for bits, out_ref in zip(masks, out_refs):
        results_for(chip ^ bits, core, dye_ref, toep_ref, taps_ref, out_ref)


def swap_kernel(*refs):
    *got_refs, out_ref = refs
    groups = EXTRA // 2
    block_len = (got_refs[0].shape[0] - EXTRA) // 2
    taps = []
    for index, got_ref in enumerate(got_refs):
        out_ref[index * block_len : (index + 1) * block_len] = got_ref[block_len : 2 * block_len]
        taps.append(got_ref[2 * block_len :].astype(jnp.float32)[groups:])
    out_ref[len(got_refs) * block_len :] = jnp.concatenate(taps, axis=0).astype(jnp.bfloat16)


def unpack_kernel(*refs):
    *got_refs, swapped_ref, dx_ref, dh_ref, rows_ref = refs
    chips = len(got_refs)
    chip, core, _ = place()
    block_len = dx_ref.shape[0]
    taps_here, groups_here = dh_ref.shape
    groups = groups_here // (2 * chips)
    other_taps = swapped_ref[chips * block_len :].astype(jnp.float32)
    for index, (bits, got_ref) in enumerate(zip(partners(chips), got_refs)):
        mine_taps = got_ref[2 * block_len :].astype(jnp.float32)[:groups]
        for flip, tokens, taps in (
            (0, got_ref[:block_len], mine_taps),
            (
                1,
                swapped_ref[index * block_len : (index + 1) * block_len],
                other_taps[index * groups : (index + 1) * groups],
            ),
        ):
            source = (chip ^ bits) * 2 + (core ^ flip)
            dx_ref[:, pl.ds(pl.multiple_of(source * LANES, LANES), LANES)] = tokens
            rows_ref[pl.ds(pl.multiple_of(source * groups, groups), groups)] = taps + pltpu.roll(
                taps, taps_here, 1
            )
    dh_ref[...] = rows_ref[...].T[:taps_here]


def local_call(kernel, out_shape, operands, name, scratch=()):
    whole = pl.BlockSpec(memory_space=pltpu.VMEM)
    return pl.pallas_call(
        kernel,
        out_shape=out_shape,
        in_specs=[whole] * len(operands),
        out_specs=[whole] * len(out_shape),
        scratch_shapes=scratch,
        compiler_params=pltpu.CompilerParams(vmem_limit_bytes=VMEM_LIMIT),
        name=name,
    )(*operands)


def by_channels(n_seq, n_chan, out_grads, layer_inputs, filters):
    rows = out_grads.shape[0]
    block_len = layer_inputs.shape[0]
    taps_here, groups_here = filters.shape
    groups = groups_here // n_seq
    tokens = n_seq * block_len
    taps = n_seq * taps_here
    chips = n_seq // 2
    masks = partners(chips)

    def half(*shape):
        return jax.ShapeDtypeStruct(shape, jnp.bfloat16)

    unit = half(2 * block_len + EXTRA, LANES)
    x_other = xor_permute(layer_inputs, "seq", 1)
    f_other = xor_permute(filters, "seq", 1)
    dy = pl.pallas_call(
        functools.partial(fan_grads_kernel, n_seq),
        out_shape=half(n_seq * n_chan, rows, LANES),
        in_specs=[pl.BlockSpec(memory_space=pltpu.HBM)],
        out_specs=pl.BlockSpec(memory_space=pltpu.HBM),
        scratch_shapes=[pltpu.SemaphoreType.DMA((n_seq * n_chan,))],
        name="fan_grads",
    )(out_grads)
    dy, x_other, f_other = lax.optimization_barrier((dy, x_other, f_other))
    dy = lax.all_to_all(dy, ("seq", "chan"), split_axis=0, concat_axis=0, tiled=True)
    pieces = local_call(
        fan_inputs_kernel,
        [unit] * chips,
        (layer_inputs, x_other, filters, f_other),
        "fan_inputs",
        [pltpu.VMEM((2, groups_here, LANES), jnp.float32)],
    )
    toeplitz, x = local_call(
        functools.partial(toeplitz_kernel, n_seq, taps_here),
        [half(groups * STEP, taps + LANES), half(tokens, LANES)],
        fan_out(pieces, "seq", 2),
        "toeplitz",
        [pltpu.VMEM((chips, groups, LANES), jnp.float32)],
    )
    dye, tap_parts, far = local_call(
        functools.partial(first_kernel, n_seq, taps_here, masks[1]),
        [half(tokens + taps + LANES, LANES), half(chips, EXTRA, LANES), unit],
        (dy.reshape(tokens, LANES), x, toeplitz),
        "first",
        [pltpu.VMEM((groups * STEP, taps + LANES), jnp.float32)],
    )
    results = [xor_permute(far, "seq", 2 * masks[1])]
    if masks[2:]:
        near = local_call(
            functools.partial(more_kernel, masks[2:]),
            [unit] * len(masks[2:]),
            (dye, toeplitz, tap_parts),
            "near",
        )
        results += [xor_permute(p, "seq", 2 * m) for p, m in zip(near, masks[2:])]
    results[0], tap_parts = lax.optimization_barrier((results[0], tap_parts))
    (own,) = local_call(
        functools.partial(more_kernel, masks[:1]), [unit], (dye, toeplitz, tap_parts), "own"
    )
    results = [own] + results
    (send,) = local_call(
        swap_kernel, [half(chips * (block_len + EXTRA // 2), LANES)], results, "swap"
    )
    return local_call(
        unpack_kernel,
        [
            half(block_len, n_seq * LANES),
            jax.ShapeDtypeStruct((taps_here, groups_here), jnp.float32),
        ],
        (*results, xor_permute(send, "seq", 1)),
        "unpack",
        [pltpu.VMEM((groups_here, LANES), jnp.float32)],
    )


def solution(mesh):
    n_seq, n_chan = mesh.shape["seq"], mesh.shape["chan"]

    def on_device(out_grads, layer_inputs, filters):
        taps_here, groups_here = filters.shape
        fits = (
            n_seq in (4, 8, 16, 32)
            and n_chan in (2, 4, 8, 16, 32)
            and layer_inputs.shape[1] == n_seq * LANES
            and groups_here == 8 * n_seq
            and 2 * taps_here == LANES
            and out_grads.shape[0] % 16 == 0
            and layer_inputs.shape[0] % (2 * STEP) == 0
            and n_seq * layer_inputs.shape[0] % (STEP * DEPTH // LANES) == 0
            and n_seq * taps_here + LANES <= n_seq * layer_inputs.shape[0]
        )
        if fits:
            return tuple(by_channels(n_seq, n_chan, out_grads, layer_inputs, filters))
        return by_tokens(out_grads, layer_inputs, filters)

    in_specs = (P(("seq", "chan"), None), P("seq", "chan"), P("seq", "chan"))
    out_specs = (P("seq", "chan"), P("seq", "chan"))
    return jax.shard_map(
        on_device, mesh=mesh, in_specs=in_specs, out_specs=out_specs, check_vma=False
    )
```

time: 32.8 us -> 41.1 us (1.25)
  Pallas kernels: 5.97 us -> 14.7 us
  local copies, waits for them, and re-layouts: 0.95 us -> 0.01 us
  waiting for transfers between devices: 9.68 us -> 10.3 us
    pallas_call x0 -> x1, Pallas kernels: none -> 9.33 us  [by_channels(): pl.pallas_call(functools.partial(fan_grads_kernel, n_seq), out_shape=half...]
    all_to_all x1, waiting for transfers between devices: 0.01 us -> 1.05 us  [by_channels(): lax.all_to_all(dy, ('seq', 'chan'), split_axis=0, concat_axis=0, tiled=True)]
    unnamed x6 -> x4, local copies, waits for them, and re-layouts: 0.95 us -> 0.01 us
    pallas_call x7, Pallas kernels: 5.97 us -> 5.39 us  [local_call(): pl.pallas_call(kernel, out_shape=out_shape, in_specs=[whole] * len(operan...]
    ppermute x9, waiting for transfers between devices: 9.68 us -> 9.26 us  [xor_permute(): return lax.ppermute(value, axis, pairs)]
  transfers between devices with their start and end apart: 10 -> 10, of which waited for: 7 -> 7; matrix products, arithmetic and copies ran while one was open for 0% -> 0% of each run, Pallas kernels for 4% -> 28%
where the time goes in v6:
time: 41.1 us; the launch traced here: 40.9 us
  starting transfers between devices  15.1 us (37%)
  Pallas kernels  14.7 us (36%)
  waiting for transfers between devices  10.3 us (25%)
  between operations  0.74 us (2%)
    pallas_call x1, Pallas kernels, by_channels(): pl.pallas_call(functools.partial(fan_grads_kernel, n_seq), out_shape=half...  9.33 us
    ppermute x9, waiting for transfers between devices, xor_permute(): return lax.ppermute(value, axis, pairs)  9.26 us
    ppermute x9, starting transfers between devices, xor_permute(): return lax.ppermute(value, axis, pairs)  7.82 us
    all_to_all x1, starting transfers between devices, by_channels(): lax.all_to_all(dy, ('seq', 'chan'), split_axis=0, concat_axis=0, tiled=True)  7.28 us
    pallas_call x7, Pallas kernels, local_call(): pl.pallas_call(kernel, out_shape=out_shape, in_specs=[whole] * len(operan...  5.39 us
    all_to_all x1, waiting for transfers between devices, by_channels(): lax.all_to_all(dy, ('seq', 'chan'), split_axis=0, concat_axis=0, tiled=True)  1.05 us
  transfers between devices with their start and end apart: 10, of which 7 were waited for; matrix products, arithmetic and copies ran while one was open for 0% of the time, Pallas kernels for 28%

profile of v6, /device:TPU:0, one launch (start us, length us, event | category | flops | bytes accessed | tf_op | source)
XLA Modules:
  0.0 40.9 jit_solution(17172953421495395383)
XLA Ops:
  0.6 0.5 %collective-permute-start = (bf16[128,1024]{1,0:T(8,128)(2,1)}, bf16[128,1024]{1,0:T(8,128)(2,1)S(1)}, u32[]{:S(2)}, u32[]{:S(2)}) collective-permute-start(bf16[128,1024]{1,0:T(8,128)(2,1)} %x_own_ref.1), channel_id=1, source_target_pairs={{0,4},{4,0},{8,12},{12,8},{16,20},{20,16},{24,28},{28,24},{1,5},{5... | collective-permute-start | bytes 786440 | tf_op jit(solution)/shard_map/ppermute | solution.py:71
  1.1 0.1 collective-permute-start.1
  1.2 9.3 %fan_grads.1 = bf16[32,32,128]{2,1,0:T(8,128)(2,1)} custom-call(bf16[32,4096]{1,0:T(8,128)(2,1)} %in_ref.1), custom_call_target="tpu_custom_call" | custom-call | tf_op jit(solution)/shard_map/fan_grads/pallas_call | solution.py:324
  10.6 7.3 %all-to-all-start = ((bf16[32,32,128]{2,1,0:T(8,128)(2,1)}), bf16[32,32,128]{2,1,0:T(8,128)(2,1)S(1)}, u32[]{:S(2)}, u32[]{:S(2)}) async-start(bf16[32,32,128]{2,1,0:T(8,128)(2,1)} %fan_grads.1), calls=%async_computation | async-start | bytes 524288 | tf_op jit(solution)/shard_map/all_to_all | solution.py:333
  17.9 0.1 fan_inputs.1
  18.0 2.7 %collective-permute-start.2 = (bf16[272,128]{1,0:T(8,128)(2,1)S(1)}, bf16[272,128]{1,0:T(8,128)(2,1)S(1)}, u32[]{:S(2)}, u32[]{:S(2)}) collective-permute-start(bf16[272,128]{1,0:T(8,128)(2,1)S(1)} %get-tuple-element.22), channel_id=1, source_target_pairs={{0,24},{4,28},{8,16},{12,20},{16,8},{20,12},{24,0},{28,4},{1,25},{... | collective-permute-start | bytes 208904 | tf_op jit(solution)/shard_map/ppermute | solution.py:71
  20.8 0.6 %collective-permute-start.3 = (bf16[272,128]{1,0:T(8,128)(2,1)S(1)}, bf16[272,128]{1,0:T(8,128)(2,1)S(1)}, u32[]{:S(2)}, u32[]{:S(2)}) collective-permute-start(bf16[272,128]{1,0:T(8,128)(2,1)S(1)} %get-tuple-element.23), channel_id=1, source_target_pairs={{0,16},{4,20},{8,24},{12,28},{16,0},{20,4},{24,8},{28,12},{1,17},{... | collective-permute-start | bytes 208904 | tf_op jit(solution)/shard_map/ppermute | solution.py:71
  21.3 0.3 collective-permute-start.4
  21.6 3.8 %collective-permute-done.2.refs_1_ = bf16[272,128]{1,0:T(8,128)(2,1)S(1)} collective-permute-done((bf16[272,128]{1,0:T(8,128)(2,1)S(1)}, bf16[272,128]{1,0:T(8,128)(2,1)S(1)}, u32[]{:S(2)}, u32[]{:S(2)}) %collective-permute-start.2) | collective-permute-done | bytes 69664 | tf_op jit(solution)/shard_map/ppermute | solution.py:71
  25.4 1.4 %collective-permute-done.3.refs_2_ = bf16[272,128]{1,0:T(8,128)(2,1)S(1)} collective-permute-done((bf16[272,128]{1,0:T(8,128)(2,1)S(1)}, bf16[272,128]{1,0:T(8,128)(2,1)S(1)}, u32[]{:S(2)}, u32[]{:S(2)}) %collective-permute-start.3) | collective-permute-done | bytes 69664 | tf_op jit(solution)/shard_map/ppermute | solution.py:71
  26.8 0.2 toeplitz.1
  27.1 1.0 %all-to-all-done = bf16[32,32,128]{2,1,0:T(8,128)(2,1)S(1)} async-done(((bf16[32,32,128]{2,1,0:T(8,128)(2,1)}), bf16[32,32,128]{2,1,0:T(8,128)(2,1)S(1)}, u32[]{:S(2)}, u32[]{:S(2)}) %all-to-all-start) | async-done | bytes 262176 | tf_op jit(solution)/shard_map/all_to_all | solution.py:333
  28.1 2.6 %first.1 = (bf16[1664,128]{1,0:T(8,128)(2,1)S(1)}, bf16[4,16,128]{2,1,0:T(8,128)(2,1)S(1)}, bf16[272,128]{1,0:T(8,128)(2,1)S(1)}) custom-call(bf16[1024,128]{1,0:T(8,128)(2,1)S(1)} %bitcast.1, bf16[1024,128]{1,0:T(8,128)(2,1)S(1)} %get-tuple-element.25.x_ref, bf16[256,640]{1,0:T(8,128)(2,1)S(1)} %get-tuple-element.26.toep_ref), custom_call_target="tpu_custom_call" | custom-call | tf_op jit(solution)/shard_map/first/pallas_call | solution.py:297
  30.7 1.0 %collective-permute-start.5 = (bf16[272,128]{1,0:T(8,128)(2,1)S(1)}, bf16[272,128]{1,0:T(8,128)(2,1)S(1)}, u32[]{:S(2)}, u32[]{:S(2)}) collective-permute-start(bf16[272,128]{1,0:T(8,128)(2,1)S(1)} %get-tuple-element.28), channel_id=1, source_target_pairs={{0,24},{4,28},{8,16},{12,20},{16,8},{20,12},{24,0},{28,4},{1,25},{... | collective-permute-start | bytes 208904 | tf_op jit(solution)/shard_map/ppermute | solution.py:71
  31.8 1.0 %near.1 = (bf16[272,128]{1,0:T(8,128)(2,1)S(1)}, bf16[272,128]{1,0:T(8,128)(2,1)S(1)}) custom-call(bf16[1664,128]{1,0:T(8,128)(2,1)S(1)} %get-tuple-element.27.dye_ref, bf16[256,640]{1,0:T(8,128)(2,1)S(1)} %get-tuple-element.26.toep_ref, bf16[4,16,128]{2,1,0:T(8,128)(2,1)S(1)} %get-tuple-element.30.taps_ref), custom_call_target="tpu_custom_call" | custom-call | tf_op jit(solution)/shard_map/near/pallas_call | solution.py:297
  32.8 1.6 %collective-permute-start.6 = (bf16[272,128]{1,0:T(8,128)(2,1)S(1)}, bf16[272,128]{1,0:T(8,128)(2,1)S(1)}, u32[]{:S(2)}, u32[]{:S(2)}) collective-permute-start(bf16[272,128]{1,0:T(8,128)(2,1)S(1)} %get-tuple-element.32), channel_id=1, source_target_pairs={{0,16},{4,20},{8,24},{12,28},{16,0},{20,4},{24,8},{28,12},{1,17},{... | collective-permute-start | bytes 208904 | tf_op jit(solution)/shard_map/ppermute | solution.py:71
  34.4 1.0 %collective-permute-start.7 = (bf16[272,128]{1,0:T(8,128)(2,1)S(1)}, bf16[272,128]{1,0:T(8,128)(2,1)S(1)}, u32[]{:S(2)}, u32[]{:S(2)}) collective-permute-start(bf16[272,128]{1,0:T(8,128)(2,1)S(1)} %get-tuple-element.33), channel_id=1, source_target_pairs={{0,8},{4,12},{8,0},{12,4},{16,24},{20,28},{24,16},{28,20},{1,9},{5... | collective-permute-start | bytes 208904 | tf_op jit(solution)/shard_map/ppermute | solution.py:71
  35.4 0.8 %collective-permute-done.5.refs_1_ = bf16[272,128]{1,0:T(8,128)(2,1)S(1)} collective-permute-done((bf16[272,128]{1,0:T(8,128)(2,1)S(1)}, bf16[272,128]{1,0:T(8,128)(2,1)S(1)}, u32[]{:S(2)}, u32[]{:S(2)}) %collective-permute-start.5) | collective-permute-done | bytes 69664 | tf_op jit(solution)/shard_map/ppermute | solution.py:71
  36.2 0.6 %own.1.refs_0_ = bf16[272,128]{1,0:T(8,128)(2,1)S(1)} custom-call(bf16[1664,128]{1,0:T(8,128)(2,1)S(1)} %get-tuple-element.27.dye_ref, bf16[256,640]{1,0:T(8,128)(2,1)S(1)} %get-tuple-element.26.toep_ref, bf16[4,16,128]{2,1,0:T(8,128)(2,1)S(1)} %get-tuple-element.30.taps_ref), custom_call_target="tpu_custom_call" | custom-call | tf_op jit(solution)/shard_map/own/pallas_call | solution.py:297
  36.8 0.8 %collective-permute-done.6.refs_2_ = bf16[272,128]{1,0:T(8,128)(2,1)S(1)} collective-permute-done((bf16[272,128]{1,0:T(8,128)(2,1)S(1)}, bf16[272,128]{1,0:T(8,128)(2,1)S(1)}, u32[]{:S(2)}, u32[]{:S(2)}) %collective-permute-start.6) | collective-permute-done | bytes 69664 | tf_op jit(solution)/shard_map/ppermute | solution.py:71
  37.6 1.0 %collective-permute-done.7.refs_3_ = bf16[272,128]{1,0:T(8,128)(2,1)S(1)} collective-permute-done((bf16[272,128]{1,0:T(8,128)(2,1)S(1)}, bf16[272,128]{1,0:T(8,128)(2,1)S(1)}, u32[]{:S(2)}, u32[]{:S(2)}) %collective-permute-start.7) | collective-permute-done | bytes 69664 | tf_op jit(solution)/shard_map/ppermute | solution.py:71
  38.7 0.1 collective-permute-start.8
  38.8 1.3 %collective-permute-done.8.refs_4_ = bf16[544,128]{1,0:T(8,128)(2,1)S(1)} collective-permute-done((bf16[544,128]{1,0:T(8,128)(2,1)S(1)}, bf16[544,128]{1,0:T(8,128)(2,1)S(1)}, u32[]{:S(2)}, u32[]{:S(2)}) %collective-permute-start.8) | collective-permute-done | bytes 139296 | tf_op jit(solution)/shard_map/ppermute | solution.py:71
  40.1 0.8 %unpack.1 = (bf16[128,1024]{1,0:T(8,128)(2,1)}, f32[64,64]{1,0:T(8,128)}) custom-call(bf16[272,128]{1,0:T(8,128)(2,1)S(1)} %own.1.refs_0_, bf16[272,128]{1,0:T(8,128)(2,1)S(1)} %collective-permute-done.5.refs_1_, bf16[272,128]{1,0:T(8,128)(2,1)S(1)} %collective-permute-done.6.refs_2_, bf16[272,128]{1,0:T(8,128)(2,1)S(1)} %collective-permute-done.7.refs_3_, ...), custom_call_target="tpu_custom_call" | custom-call | tf_op jit(solution)/shard_map/unpack/pallas_call | solution.py:297
  (8 shorter events, 0.0 us)
Async XLA Ops:
  0.6 10.0 %collective-permute-start = (bf16[128,1024]{1,0:T(8,128)(2,1)}, bf16[128,1024]{1,0:T(8,128)(2,1)S(1)}, u32[]{:S(2)}, u32[]{:S(2)}) collective-permute-start(bf16[128,1024]{1,0:T(8,128)(2,1)} %x_own_ref.1), channel_id=1, source_target_pairs={{0,4},{4,0},{8,12},{12,8},{16,20},{20,16},{24,28},{28,24},{1,5},{5... | collective-permute-start | bytes 786440 | tf_op jit(solution)/shard_map/ppermute | solution.py:71
  1.1 9.4 %collective-permute-start.1 = (bf16[64,64]{1,0:T(8,128)(2,1)}, bf16[64,64]{1,0:T(8,128)(2,1)S(1)}, u32[]{:S(2)}, u32[]{:S(2)}) collective-permute-start(bf16[64,64]{1,0:T(8,128)(2,1)} %f_own_ref.1), channel_id=1, source_target_pairs={{0,4},{4,0},{8,12},{12,8},{16,20},{20,16},{24,28},{28,24},{1,5},{5... | collective-permute-start | bytes 24584 | tf_op jit(solution)/shard_map/ppermute | solution.py:71
  10.6 7.3 %copy-start = (bf16[128,1024]{1,0:T(8,128)(2,1)S(1)}, bf16[128,1024]{1,0:T(8,128)(2,1)}, u32[]{:S(2)}) copy-start(bf16[128,1024]{1,0:T(8,128)(2,1)} %x_own_ref.1) | copy-start | bytes 786436
  10.6 7.3 %copy-start.1 = (bf16[64,64]{1,0:T(8,128)(2,1)S(1)}, bf16[64,64]{1,0:T(8,128)(2,1)}, u32[]{:S(2)}) copy-start(bf16[64,64]{1,0:T(8,128)(2,1)} %f_own_ref.1) | copy-start | bytes 24580
  10.6 17.5 %all-to-all-start = ((bf16[32,32,128]{2,1,0:T(8,128)(2,1)}), bf16[32,32,128]{2,1,0:T(8,128)(2,1)S(1)}, u32[]{:S(2)}, u32[]{:S(2)}) async-start(bf16[32,32,128]{2,1,0:T(8,128)(2,1)} %fan_grads.1), calls=%async_computation | async-start | bytes 524288 | tf_op jit(solution)/shard_map/all_to_all | solution.py:333
  18.0 7.3 %collective-permute-start.2 = (bf16[272,128]{1,0:T(8,128)(2,1)S(1)}, bf16[272,128]{1,0:T(8,128)(2,1)S(1)}, u32[]{:S(2)}, u32[]{:S(2)}) collective-permute-start(bf16[272,128]{1,0:T(8,128)(2,1)S(1)} %get-tuple-element.22), channel_id=1, source_target_pairs={{0,24},{4,28},{8,16},{12,20},{16,8},{20,12},{24,0},{28,4},{1,25},{... | collective-permute-start | bytes 208904 | tf_op jit(solution)/shard_map/ppermute | solution.py:71
  20.8 6.0 %collective-permute-start.3 = (bf16[272,128]{1,0:T(8,128)(2,1)S(1)}, bf16[272,128]{1,0:T(8,128)(2,1)S(1)}, u32[]{:S(2)}, u32[]{:S(2)}) collective-permute-start(bf16[272,128]{1,0:T(8,128)(2,1)S(1)} %get-tuple-element.23), channel_id=1, source_target_pairs={{0,16},{4,20},{8,24},{12,28},{16,0},{20,4},{24,8},{28,12},{1,17},{... | collective-permute-start | bytes 208904 | tf_op jit(solution)/shard_map/ppermute | solution.py:71
  21.3 5.5 %collective-permute-start.4 = (bf16[272,128]{1,0:T(8,128)(2,1)S(1)}, bf16[272,128]{1,0:T(8,128)(2,1)S(1)}, u32[]{:S(2)}, u32[]{:S(2)}) collective-permute-start(bf16[272,128]{1,0:T(8,128)(2,1)S(1)} %get-tuple-element.24), channel_id=1, source_target_pairs={{0,8},{4,12},{8,0},{12,4},{16,24},{20,28},{24,16},{28,20},{1,9},{5... | collective-permute-start | bytes 208904 | tf_op jit(solution)/shard_map/ppermute | solution.py:71
  30.7 5.5 %collective-permute-start.5 = (bf16[272,128]{1,0:T(8,128)(2,1)S(1)}, bf16[272,128]{1,0:T(8,128)(2,1)S(1)}, u32[]{:S(2)}, u32[]{:S(2)}) collective-permute-start(bf16[272,128]{1,0:T(8,128)(2,1)S(1)} %get-tuple-element.28), channel_id=1, source_target_pairs={{0,24},{4,28},{8,16},{12,20},{16,8},{20,12},{24,0},{28,4},{1,25},{... | collective-permute-start | bytes 208904 | tf_op jit(solution)/shard_map/ppermute | solution.py:71
  32.8 4.8 %collective-permute-start.6 = (bf16[272,128]{1,0:T(8,128)(2,1)S(1)}, bf16[272,128]{1,0:T(8,128)(2,1)S(1)}, u32[]{:S(2)}, u32[]{:S(2)}) collective-permute-start(bf16[272,128]{1,0:T(8,128)(2,1)S(1)} %get-tuple-element.32), channel_id=1, source_target_pairs={{0,16},{4,20},{8,24},{12,28},{16,0},{20,4},{24,8},{28,12},{1,17},{... | collective-permute-start | bytes 208904 | tf_op jit(solution)/shard_map/ppermute | solution.py:71
  34.4 4.3 %collective-permute-start.7 = (bf16[272,128]{1,0:T(8,128)(2,1)S(1)}, bf16[272,128]{1,0:T(8,128)(2,1)S(1)}, u32[]{:S(2)}, u32[]{:S(2)}) collective-permute-start(bf16[272,128]{1,0:T(8,128)(2,1)S(1)} %get-tuple-element.33), channel_id=1, source_target_pairs={{0,8},{4,12},{8,0},{12,4},{16,24},{20,28},{24,16},{28,20},{1,9},{5... | collective-permute-start | bytes 208904 | tf_op jit(solution)/shard_map/ppermute | solution.py:71
  38.7 1.4 %collective-permute-start.8 = (bf16[544,128]{1,0:T(8,128)(2,1)S(1)}, bf16[544,128]{1,0:T(8,128)(2,1)S(1)}, u32[]{:S(2)}, u32[]{:S(2)}) collective-permute-start(bf16[544,128]{1,0:T(8,128)(2,1)S(1)} %swap.1), channel_id=1, source_target_pairs={{0,4},{4,0},{8,12},{12,8},{16,20},{20,16},{24,28},{28,24},{1,5},{5... | collective-permute-start | bytes 417800 | tf_op jit(solution)/shard_map/ppermute | solution.py:71

commit v7 on v6

--- a/solution.py
+++ b/solution.py
@@ -71,6 +71,11 @@
     return lax.ppermute(value, axis, pairs)
 
 
+def turned_permute(value, axis, masks):
+    pairs = [(source, source ^ masks[source % 2]) for source in range(lax.axis_size(axis))]
+    return lax.ppermute(value, axis, pairs)
+
+
 def partners(count):
     return [(count - step) % count for step in range(count)]
 
@@ -94,22 +99,12 @@
     return pl.ds(pl.multiple_of(index * size, 16), size)
 
 
-def fan_grads_kernel(n_seq, in_ref, out_ref, sems):
+def fan_grads_kernel(n_seq, in_ref, out_ref):
     n_chan = out_ref.shape[0] // n_seq
-    copies = []
-    for chan in reversed(range(n_chan)):
-        for seq in range(n_seq):
+    for seq in range(n_seq):
+        for chan in range(n_chan):
             start = (chan * n_seq + seq) * LANES
-            to = seq * n_chan + chan
-            copies.append(
-                pltpu.make_async_copy(
-                    in_ref.at[:, start : start + LANES], out_ref.at[to], sems.at[to]
-                )
-            )
-    for copy in copies:
-        copy.start()
-    for copy in copies:
-        copy.wait()
+            out_ref[seq * n_chan + chan] = in_ref[:, start : start + LANES]
 
 
 def fan_inputs_kernel(x_own_ref, x_other_ref, f_own_ref, f_other_ref, *refs):
@@ -178,16 +173,13 @@
     return jnp.concatenate([total[:, :LANES], total[:, LANES:]], axis=0).astype(jnp.bfloat16)
 
 
-def results_for(to_chip, core, dye_ref, toep_ref, taps_ref, out_ref):
-    block_len = (out_ref.shape[0] - taps_ref.shape[1]) // 2
+def tokens_of(seq, dye_ref, toep_ref, out_ref, at, block_len):
     toeplitz = toep_ref[...]
     groups = toeplitz.shape[0] // STEP
-    for flip in range(2):
-        start = (2 * to_chip + (core ^ flip)) * block_len
-        for row in range(0, block_len, 2 * STEP):
-            at = flip * block_len + row
-            out_ref[at : at + 2 * STEP] = filtered(dye_ref, start + row, toeplitz, groups)
-    out_ref[2 * block_len :] = taps_ref[to_chip]
+    for row in range(0, block_len, 2 * STEP):
+        out_ref[at + row : at + row + 2 * STEP] = filtered(
+            dye_ref, seq * block_len + row, toeplitz, groups
+        )
 
 
 def first_kernel(
@@ -246,49 +238,97 @@
         other = jnp.where(core == 0, odd, even)
         taps_ref[to_chip] = jnp.concatenate([mine, other], axis=0).astype(jnp.bfloat16)
 
-    results_for(chip ^ far, core, dye_ref, toep_ref, taps_ref, out_ref)
-
-
-def more_kernel(masks, dye_ref, toep_ref, taps_ref, *out_refs):
-    chip, core, _ = place()
-    for bits, out_ref in zip(masks, out_refs):
-        results_for(chip ^ bits, core, dye_ref, toep_ref, taps_ref, out_ref)
+    block_len = (out_ref.shape[0] - EXTRA) // 2
+    for flip in range(2):
+        seq = 2 * (chip ^ far) + (core ^ flip)
+        tokens_of(seq, dye_ref, toep_ref, out_ref, flip * block_len, block_len)
+    out_ref[2 * block_len :] = taps_ref[chip ^ far]
+
+
+def half_of(taps, flip):
+    groups = EXTRA // 2
+    return taps.astype(jnp.float32)[flip * groups : (flip + 1) * groups]
+
+
+def stacked(rows):
+    return jnp.concatenate(rows, axis=0).astype(jnp.bfloat16)
+
+
+def near_kernel(masks, flip, dye_ref, toep_ref, taps_ref, out_ref):
+    chip, core, _ = place()
+    block_len = (out_ref.shape[0] - len(masks) * EXTRA // 2) // len(masks)
+    for index, bits in enumerate(masks):
+        seq = 2 * (chip ^ bits) + (core ^ flip)
+        tokens_of(seq, dye_ref, toep_ref, out_ref, index * block_len, block_len)
+    out_ref[len(masks) * block_len :] = stacked(
+        [half_of(taps_ref[chip ^ bits], flip) for bits in masks]
+    )
+
+
+def near_pieces_kernel(keep_ref, got_ref, *out_refs):
+    _, core, _ = place()
+    count = len(out_refs)
+    block_len = (out_refs[0].shape[0] - EXTRA) // 2
+    groups = EXTRA // 2
+    keep_taps = keep_ref[count * block_len :].astype(jnp.float32)
+    got_taps = got_ref[count * block_len :].astype(jnp.float32)
+    taps = [
+        stacked(
+            [value[index * groups : (index + 1) * groups] for value in (keep_taps, got_taps)]
+        )
+        for index in range(count)
+    ]
+    for index, out_ref in enumerate(out_refs):
+        other = (index + 1) % count
+        out_ref[:block_len] = keep_ref[rows_at((index + core) % count, block_len)]
+        out_ref[block_len : 2 * block_len] = got_ref[rows_at((index + core) % count, block_len)]
+        out_ref[2 * block_len :] = jnp.where(core == 0, taps[index], taps[other])
+
+
+def own_kernel(dye_ref, toep_ref, taps_ref, out_ref):
+    chip, core, _ = place()
+    block_len = (out_ref.shape[0] - EXTRA) // 2
+    for flip in range(2):
+        seq = 2 * chip + (core ^ flip)
+        tokens_of(seq, dye_ref, toep_ref, out_ref, flip * block_len, block_len)
+    out_ref[2 * block_len :] = taps_ref[chip]
 
 
 def swap_kernel(*refs):
-    *got_refs, out_ref = refs
-    groups = EXTRA // 2
-    block_len = (got_refs[0].shape[0] - EXTRA) // 2
-    taps = []
-    for index, got_ref in enumerate(got_refs):
-        out_ref[index * block_len : (index + 1) * block_len] = got_ref[block_len : 2 * block_len]
-        taps.append(got_ref[2 * block_len :].astype(jnp.float32)[groups:])
-    out_ref[len(got_refs) * block_len :] = jnp.concatenate(taps, axis=0).astype(jnp.bfloat16)
-
-
-def unpack_kernel(*refs):
-    *got_refs, swapped_ref, dx_ref, dh_ref, rows_ref = refs
-    chips = len(got_refs)
+    *in_refs, out_ref = refs
+    block_len = (in_refs[0].shape[0] - EXTRA) // 2
+    for index, in_ref in enumerate(in_refs):
+        out_ref[index * block_len : (index + 1) * block_len] = in_ref[block_len : 2 * block_len]
+    out_ref[len(in_refs) * block_len :] = stacked(
+        [half_of(in_ref[2 * block_len :], 1) for in_ref in in_refs]
+    )
+
+
+def unpack_kernel(masks, *refs):
+    own_ref, far_ref, swapped_ref, *near_refs, dx_ref, dh_ref, rows_ref = refs
     chip, core, _ = place()
     block_len = dx_ref.shape[0]
     taps_here, groups_here = dh_ref.shape
-    groups = groups_here // (2 * chips)
-    other_taps = swapped_ref[chips * block_len :].astype(jnp.float32)
-    for index, (bits, got_ref) in enumerate(zip(partners(chips), got_refs)):
-        mine_taps = got_ref[2 * block_len :].astype(jnp.float32)[:groups]
-        for flip, tokens, taps in (
-            (0, got_ref[:block_len], mine_taps),
-            (
-                1,
-                swapped_ref[index * block_len : (index + 1) * block_len],
-                other_taps[index * groups : (index + 1) * groups],
-            ),
-        ):
-            source = (chip ^ bits) * 2 + (core ^ flip)
-            dx_ref[:, pl.ds(pl.multiple_of(source * LANES, LANES), LANES)] = tokens
-            rows_ref[pl.ds(pl.multiple_of(source * groups, groups), groups)] = taps + pltpu.roll(
-                taps, taps_here, 1
-            )
+    groups = EXTRA // 2
+
+    def put(from_chip, flip, tokens, taps):
+        source = 2 * from_chip + (core ^ flip)
+        dx_ref[:, pl.ds(pl.multiple_of(source * LANES, LANES), LANES)] = tokens
+        rows_ref[pl.ds(pl.multiple_of(source * groups, groups), groups)] = taps + pltpu.roll(
+            taps, taps_here, 1
+        )
+
+    swapped_taps = swapped_ref[2 * block_len :]
+    for index, ref in enumerate((own_ref, far_ref)):
+        put(chip ^ masks[index], 0, ref[:block_len], half_of(ref[2 * block_len :], 0))
+        rows = swapped_ref[index * block_len : (index + 1) * block_len]
+        put(chip ^ masks[index], 1, rows, half_of(swapped_taps, index))
+    near = masks[2:]
+    for index, ref in enumerate(near_refs):
+        bits = jnp.where(core == 0, near[index], near[(index + 1) % len(near)])
+        for flip in range(2):
+            rows = ref[flip * block_len : (flip + 1) * block_len]
+            put(chip ^ bits, flip, rows, half_of(ref[2 * block_len :], flip))
     dh_ref[...] = rows_ref[...].T[:taps_here]
 
 
@@ -321,15 +361,12 @@
     unit = half(2 * block_len + EXTRA, LANES)
     x_other = xor_permute(layer_inputs, "seq", 1)
     f_other = xor_permute(filters, "seq", 1)
-    dy = pl.pallas_call(
+    (dy,) = local_call(
         functools.partial(fan_grads_kernel, n_seq),
-        out_shape=half(n_seq * n_chan, rows, LANES),
-        in_specs=[pl.BlockSpec(memory_space=pltpu.HBM)],
-        out_specs=pl.BlockSpec(memory_space=pltpu.HBM),
-        scratch_shapes=[pltpu.SemaphoreType.DMA((n_seq * n_chan,))],
-        name="fan_grads",
-    )(out_grads)
-    dy, x_other, f_other = lax.optimization_barrier((dy, x_other, f_other))
+        [half(n_seq * n_chan, rows, LANES)],
+        (out_grads,),
+        "fan_grads",
+    )
     dy = lax.all_to_all(dy, ("seq", "chan"), split_axis=0, concat_axis=0, tiled=True)
     pieces = local_call(
         fan_inputs_kernel,
@@ -352,30 +389,33 @@
         "first",
         [pltpu.VMEM((groups * STEP, taps + LANES), jnp.float32)],
     )
-    results = [xor_permute(far, "seq", 2 * masks[1])]
-    if masks[2:]:
-        near = local_call(
-            functools.partial(more_kernel, masks[2:]),
-            [unit] * len(masks[2:]),
-            (dye, toeplitz, tap_parts),
-            "near",
-        )
-        results += [xor_permute(p, "seq", 2 * m) for p, m in zip(near, masks[2:])]
-    results[0], tap_parts = lax.optimization_barrier((results[0], tap_parts))
-    (own,) = local_call(
-        functools.partial(more_kernel, masks[:1]), [unit], (dye, toeplitz, tap_parts), "own"
-    )
-    results = [own] + results
+    far = xor_permute(far, "seq", 2 * masks[1])
+    near = masks[2:]
+    near_shape = half(len(near) * (block_len + EXTRA // 2), LANES)
     (send,) = local_call(
-        swap_kernel, [half(chips * (block_len + EXTRA // 2), LANES)], results, "swap"
+        functools.partial(near_kernel, near, 1), [near_shape], (dye, toeplitz, tap_parts), "near_swap"
+    )
+    got = xor_permute(send, "seq", 1)
+    (keep,) = local_call(
+        functools.partial(near_kernel, near, 0), [near_shape], (dye, toeplitz, tap_parts), "near_keep"
+    )
+    pieces = local_call(near_pieces_kernel, [unit] * len(near), (keep, got), "near_pieces")
+    pieces = [
+        turned_permute(piece, "seq", [2 * bits for bits in near[index:] + near[:index]])
+        for index, piece in enumerate(pieces)
+    ]
+    far, tap_parts = lax.optimization_barrier((far, tap_parts))
+    (own,) = local_call(own_kernel, [unit], (dye, toeplitz, tap_parts), "own")
+    (send,) = local_call(
+        swap_kernel, [half(2 * block_len + EXTRA, LANES)], (own, far), "swap"
     )
     return local_call(
-        unpack_kernel,
+        functools.partial(unpack_kernel, masks),
         [
             half(block_len, n_seq * LANES),
             jax.ShapeDtypeStruct((taps_here, groups_here), jnp.float32),
         ],
-        (*results, xor_permute(send, "seq", 1)),
+        (own, far, xor_permute(send, "seq", 1), *pieces),
         "unpack",
         [pltpu.VMEM((groups_here, LANES), jnp.float32)],
     )
@@ -387,8 +427,8 @@
     def on_device(out_grads, layer_inputs, filters):
         taps_here, groups_here = filters.shape
         fits = (
-            n_seq in (4, 8, 16, 32)
-            and n_chan in (2, 4, 8, 16, 32)
+            n_seq == 8
+            and n_chan in (2, 4, 8)
             and layer_inputs.shape[1] == n_seq * LANES
             and groups_here == 8 * n_seq
             and 2 * taps_here == LANES

time: 41.1 us -> 31.9 us (0.78)
  Pallas kernels: 14.7 us -> 6.29 us
  waiting for transfers between devices: 10.3 us -> 8.27 us
  local copies, waits for them, and re-layouts: 0.01 us -> 0.95 us
    pallas_call x1 -> x0, Pallas kernels: 9.33 us -> none  [by_channels(): pl.pallas_call(functools.partial(fan_grads_kernel, n_seq), out_shape=half...]
    ppermute x9 -> x8, waiting for transfers between devices: 9.26 us -> 6.63 us  [xor_permute(): return lax.ppermute(value, axis, pairs)]
    ppermute x0 -> x2, starting transfers between devices: none -> 2.52 us  [turned_permute(): return lax.ppermute(value, axis, pairs)]
    ppermute x9 -> x8, starting transfers between devices: 7.82 us -> 5.63 us  [xor_permute(): return lax.ppermute(value, axis, pairs)]
    ppermute x0 -> x2, waiting for transfers between devices: none -> 1.48 us  [turned_permute(): return lax.ppermute(value, axis, pairs)]
    unnamed x4 -> x6, local copies, waits for them, and re-layouts: 0.01 us -> 0.95 us
    pallas_call x7 -> x10, Pallas kernels: 5.39 us -> 6.29 us  [local_call(): pl.pallas_call(kernel, out_shape=out_shape, in_specs=[whole] * len(operan...]
    all_to_all x1, waiting for transfers between devices: 1.05 us -> 0.15 us  [by_channels(): lax.all_to_all(dy, ('seq', 'chan'), split_axis=0, concat_axis=0, tiled=True)]
  transfers between devices with their start and end apart: 10 -> 11, of which waited for: 7 -> 7; matrix products, arithmetic and copies ran while one was open for 0% -> 0% of each run, Pallas kernels for 28% -> 5%
where the time goes in v7:
time: 31.9 us; the launch traced here: 31.7 us
  starting transfers between devices  15.4 us (48%)
  waiting for transfers between devices  8.27 us (26%)
  Pallas kernels  6.29 us (20%)
  local copies, waits for them, and re-layouts  0.95 us (3%)
  between operations  0.73 us (2%)
    all_to_all x1, starting transfers between devices, by_channels(): lax.all_to_all(dy, ('seq', 'chan'), split_axis=0, concat_axis=0, tiled=True)  7.3 us
    ppermute x8, waiting for transfers between devices, xor_permute(): return lax.ppermute(value, axis, pairs)  6.63 us
    pallas_call x10, Pallas kernels, local_call(): pl.pallas_call(kernel, out_shape=out_shape, in_specs=[whole] * len(operan...  6.29 us
    ppermute x8, starting transfers between devices, xor_permute(): return lax.ppermute(value, axis, pairs)  5.63 us
    ppermute x2, starting transfers between devices, turned_permute(): return lax.ppermute(value, axis, pairs)  2.52 us
    ppermute x2, waiting for transfers between devices, turned_permute(): return lax.ppermute(value, axis, pairs)  1.48 us
    unnamed x6, local copies, waits for them, and re-layouts  0.95 us
  transfers between devices with their start and end apart: 11, of which 7 were waited for; matrix products, arithmetic and copies ran while one was open for 0% of the time, Pallas kernels for 5%

profile of v7, /device:TPU:0, one launch (start us, length us, event | category | flops | bytes accessed | tf_op | source)
XLA Modules:
  0.0 31.7 jit_solution(10312840690735531842)
XLA Ops:
  0.6 0.9 %copy-done = bf16[32,4096]{1,0:T(8,128)(2,1)S(1)} copy-done((bf16[32,4096]{1,0:T(8,128)(2,1)S(1)}, bf16[32,4096]{1,0:T(8,128)(2,1)}, u32[]{:S(2)}) %copy-start) | copy-done | bytes 262168
  1.6 0.7 %fan_grads.1 = bf16[32,32,128]{2,1,0:T(8,128)(2,1)} custom-call(bf16[32,4096]{1,0:T(8,128)(2,1)S(1)} %copy-done), custom_call_target="tpu_custom_call" | custom-call | tf_op jit(solution)/shard_map/fan_grads/pallas_call | solution.py:337
  2.3 7.3 %all-to-all-start = ((bf16[32,32,128]{2,1,0:T(8,128)(2,1)}), bf16[32,32,128]{2,1,0:T(8,128)(2,1)S(1)}, u32[]{:S(2)}, u32[]{:S(2)}) async-start(bf16[32,32,128]{2,1,0:T(8,128)(2,1)} %fan_grads.1), calls=%async_computation | async-start | bytes 524288 | tf_op jit(solution)/shard_map/all_to_all | solution.py:370
  9.6 0.3 collective-permute-start
  10.0 0.3 collective-permute-start.1
  10.2 1.0 %collective-permute-done.1.f_other_ref = bf16[64,64]{1,0:T(8,128)(2,1)S(1)} collective-permute-done((bf16[64,64]{1,0:T(8,128)(2,1)S(1)}, bf16[64,64]{1,0:T(8,128)(2,1)S(1)}, u32[]{:S(2)}, u32[]{:S(2)}) %collective-permute-start.1) | collective-permute-done | bytes 8224 | tf_op jit(solution)/shard_map/ppermute | solution.py:71
  11.4 2.7 %collective-permute-start.2 = (bf16[272,128]{1,0:T(8,128)(2,1)S(1)}, bf16[272,128]{1,0:T(8,128)(2,1)S(1)}, u32[]{:S(2)}, u32[]{:S(2)}) collective-permute-start(bf16[272,128]{1,0:T(8,128)(2,1)S(1)} %get-tuple-element.16), channel_id=1, source_target_pairs={{0,24},{4,28},{8,16},{12,20},{16,8},{20,12},{24,0},{28,4},{1,25},{... | collective-permute-start | bytes 208904 | tf_op jit(solution)/shard_map/ppermute | solution.py:71
  14.1 0.6 %collective-permute-start.3 = (bf16[272,128]{1,0:T(8,128)(2,1)S(1)}, bf16[272,128]{1,0:T(8,128)(2,1)S(1)}, u32[]{:S(2)}, u32[]{:S(2)}) collective-permute-start(bf16[272,128]{1,0:T(8,128)(2,1)S(1)} %get-tuple-element.17), channel_id=1, source_target_pairs={{0,16},{4,20},{8,24},{12,28},{16,0},{20,4},{24,8},{28,12},{1,17},{... | collective-permute-start | bytes 208904 | tf_op jit(solution)/shard_map/ppermute | solution.py:71
  14.7 0.3 collective-permute-start.4
  14.9 2.8 %collective-permute-done.2.refs_1_ = bf16[272,128]{1,0:T(8,128)(2,1)S(1)} collective-permute-done((bf16[272,128]{1,0:T(8,128)(2,1)S(1)}, bf16[272,128]{1,0:T(8,128)(2,1)S(1)}, u32[]{:S(2)}, u32[]{:S(2)}) %collective-permute-start.2) | collective-permute-done | bytes 69664 | tf_op jit(solution)/shard_map/ppermute | solution.py:71
  17.8 1.7 %collective-permute-done.3.refs_2_ = bf16[272,128]{1,0:T(8,128)(2,1)S(1)} collective-permute-done((bf16[272,128]{1,0:T(8,128)(2,1)S(1)}, bf16[272,128]{1,0:T(8,128)(2,1)S(1)}, u32[]{:S(2)}, u32[]{:S(2)}) %collective-permute-start.3) | collective-permute-done | bytes 69664 | tf_op jit(solution)/shard_map/ppermute | solution.py:71
  19.5 0.2 toeplitz.1
  19.9 2.6 %first.1 = (bf16[1664,128]{1,0:T(8,128)(2,1)S(1)}, bf16[4,16,128]{2,1,0:T(8,128)(2,1)S(1)}, bf16[272,128]{1,0:T(8,128)(2,1)S(1)}) custom-call(bf16[1024,128]{1,0:T(8,128)(2,1)S(1)} %bitcast.1, bf16[1024,128]{1,0:T(8,128)(2,1)S(1)} %get-tuple-element.19.x_ref, bf16[256,640]{1,0:T(8,128)(2,1)S(1)} %get-tuple-element.20.toep_ref), custom_call_target="tpu_custom_call" | custom-call | tf_op jit(solution)/shard_map/first/pallas_call | solution.py:337
  22.5 0.6 %near_swap.1 = bf16[272,128]{1,0:T(8,128)(2,1)S(1)} custom-call(bf16[1664,128]{1,0:T(8,128)(2,1)S(1)} %get-tuple-element.21.dye_ref, bf16[256,640]{1,0:T(8,128)(2,1)S(1)} %get-tuple-element.20.toep_ref, bf16[4,16,128]{2,1,0:T(8,128)(2,1)S(1)} %get-tuple-element.24.taps_ref), custom_call_target="tpu_custom_call" | custom-call | tf_op jit(solution)/shard_map/near_swap/pallas_call | solution.py:337
  23.1 0.4 %collective-permute-start.7 = (bf16[272,128]{1,0:T(8,128)(2,1)S(1)}, bf16[272,128]{1,0:T(8,128)(2,1)S(1)}, u32[]{:S(2)}, u32[]{:S(2)}) collective-permute-start(bf16[272,128]{1,0:T(8,128)(2,1)S(1)} %near_swap.1), channel_id=1, source_target_pairs={{0,4},{4,0},{8,12},{12,8},{16,20},{20,16},{24,28},{28,24},{1,5},{5... | collective-permute-start | bytes 208904 | tf_op jit(solution)/shard_map/ppermute | solution.py:71
  23.5 1.0 %collective-permute-start.5 = (bf16[272,128]{1,0:T(8,128)(2,1)S(1)}, bf16[272,128]{1,0:T(8,128)(2,1)S(1)}, u32[]{:S(2)}, u32[]{:S(2)}) collective-permute-start(bf16[272,128]{1,0:T(8,128)(2,1)S(1)} %get-tuple-element.22), channel_id=1, source_target_pairs={{0,24},{4,28},{8,16},{12,20},{16,8},{20,12},{24,0},{28,4},{1,25},{... | collective-permute-start | bytes 208904 | tf_op jit(solution)/shard_map/ppermute | solution.py:71
  24.6 0.6 %near_keep.1.keep_ref = bf16[272,128]{1,0:T(8,128)(2,1)S(1)} custom-call(bf16[1664,128]{1,0:T(8,128)(2,1)S(1)} %get-tuple-element.21.dye_ref, bf16[256,640]{1,0:T(8,128)(2,1)S(1)} %get-tuple-element.20.toep_ref, bf16[4,16,128]{2,1,0:T(8,128)(2,1)S(1)} %get-tuple-element.24.taps_ref), custom_call_target="tpu_custom_call" | custom-call | tf_op jit(solution)/shard_map/near_keep/pallas_call | solution.py:337
  25.2 1.4 %collective-permute-start.8 = (bf16[272,128]{1,0:T(8,128)(2,1)S(1)}, bf16[272,128]{1,0:T(8,128)(2,1)S(1)}, u32[]{:S(2)}, u32[]{:S(2)}) collective-permute-start(bf16[272,128]{1,0:T(8,128)(2,1)S(1)} %get-tuple-element.26), channel_id=1, source_target_pairs={{0,16},{4,12},{8,24},{12,4},{16,0},{20,28},{24,8},{28,20},{1,17},{... | collective-permute-start | bytes 208904 | tf_op jit(solution)/shard_map/ppermute | solution.py:76
  26.6 1.1 %collective-permute-start.9 = (bf16[272,128]{1,0:T(8,128)(2,1)S(1)}, bf16[272,128]{1,0:T(8,128)(2,1)S(1)}, u32[]{:S(2)}, u32[]{:S(2)}) collective-permute-start(bf16[272,128]{1,0:T(8,128)(2,1)S(1)} %get-tuple-element.27), channel_id=1, source_target_pairs={{0,8},{4,20},{8,0},{12,28},{16,24},{20,4},{24,16},{28,12},{1,9},{5... | collective-permute-start | bytes 208904 | tf_op jit(solution)/shard_map/ppermute | solution.py:76
  27.7 1.0 %collective-permute-done.5.refs_1_ = bf16[272,128]{1,0:T(8,128)(2,1)S(1)} collective-permute-done((bf16[272,128]{1,0:T(8,128)(2,1)S(1)}, bf16[272,128]{1,0:T(8,128)(2,1)S(1)}, u32[]{:S(2)}, u32[]{:S(2)}) %collective-permute-start.5) | collective-permute-done | bytes 69664 | tf_op jit(solution)/shard_map/ppermute | solution.py:71
  28.7 0.6 %own.1.refs_0_ = bf16[272,128]{1,0:T(8,128)(2,1)S(1)} custom-call(bf16[1664,128]{1,0:T(8,128)(2,1)S(1)} %get-tuple-element.21.dye_ref, bf16[256,640]{1,0:T(8,128)(2,1)S(1)} %get-tuple-element.20.toep_ref, bf16[4,16,128]{2,1,0:T(8,128)(2,1)S(1)} %get-tuple-element.24.taps_ref), custom_call_target="tpu_custom_call" | custom-call | tf_op jit(solution)/shard_map/own/pallas_call | solution.py:337
  29.4 0.8 %collective-permute-done.8.refs_3_ = bf16[272,128]{1,0:T(8,128)(2,1)S(1)} collective-permute-done((bf16[272,128]{1,0:T(8,128)(2,1)S(1)}, bf16[272,128]{1,0:T(8,128)(2,1)S(1)}, u32[]{:S(2)}, u32[]{:S(2)}) %collective-permute-start.8) | collective-permute-done | bytes 69664 | tf_op jit(solution)/shard_map/ppermute | solution.py:76
  30.2 0.7 %collective-permute-done.9.refs_4_ = bf16[272,128]{1,0:T(8,128)(2,1)S(1)} collective-permute-done((bf16[272,128]{1,0:T(8,128)(2,1)S(1)}, bf16[272,128]{1,0:T(8,128)(2,1)S(1)}, u32[]{:S(2)}, u32[]{:S(2)}) %collective-permute-start.9) | collective-permute-done | bytes 69664 | tf_op jit(solution)/shard_map/ppermute | solution.py:76
  30.9 0.8 %unpack.1 = (bf16[128,1024]{1,0:T(8,128)(2,1)}, f32[64,64]{1,0:T(8,128)}) custom-call(bf16[272,128]{1,0:T(8,128)(2,1)S(1)} %own.1.refs_0_, bf16[272,128]{1,0:T(8,128)(2,1)S(1)} %collective-permute-done.5.refs_1_, bf16[272,128]{1,0:T(8,128)(2,1)S(1)} %collective-permute-done.6.refs_2_, bf16[272,128]{1,0:T(8,128)(2,1)S(1)} %collective-permute-done.8.refs_3_, ...), custom_call_target="tpu_custom_call" | custom-call | tf_op jit(solution)/shard_map/unpack/pallas_call | solution.py:337
  (14 shorter events, 0.4 us)
Async XLA Ops:
  0.6 1.0 %copy-start = (bf16[32,4096]{1,0:T(8,128)(2,1)S(1)}, bf16[32,4096]{1,0:T(8,128)(2,1)}, u32[]{:S(2)}) copy-start(bf16[32,4096]{1,0:T(8,128)(2,1)} %in_ref.1) | copy-start | bytes 786436
  2.3 7.3 %copy-start.1 = (bf16[128,1024]{1,0:T(8,128)(2,1)S(1)}, bf16[128,1024]{1,0:T(8,128)(2,1)}, u32[]{:S(2)}) copy-start(bf16[128,1024]{1,0:T(8,128)(2,1)} %x_own_ref.1) | copy-start | bytes 786436
  2.3 7.6 %copy-start.2 = (bf16[64,64]{1,0:T(8,128)(2,1)S(1)}, bf16[64,64]{1,0:T(8,128)(2,1)}, u32[]{:S(2)}) copy-start(bf16[64,64]{1,0:T(8,128)(2,1)} %f_own_ref.1) | copy-start | bytes 24580
  2.3 17.6 %all-to-all-start = ((bf16[32,32,128]{2,1,0:T(8,128)(2,1)}), bf16[32,32,128]{2,1,0:T(8,128)(2,1)S(1)}, u32[]{:S(2)}, u32[]{:S(2)}) async-start(bf16[32,32,128]{2,1,0:T(8,128)(2,1)} %fan_grads.1), calls=%async_computation | async-start | bytes 524288 | tf_op jit(solution)/shard_map/all_to_all | solution.py:370
  9.6 1.6 %collective-permute-start = (bf16[128,1024]{1,0:T(8,128)(2,1)S(1)}, bf16[128,1024]{1,0:T(8,128)(2,1)S(1)}, u32[]{:S(2)}, u32[]{:S(2)}) collective-permute-start(bf16[128,1024]{1,0:T(8,128)(2,1)S(1)} %copy-done.1), channel_id=1, source_target_pairs={{0,4},{4,0},{8,12},{12,8},{16,20},{20,16},{24,28},{28,24},{1,5},{5... | collective-permute-start | bytes 786440 | tf_op jit(solution)/shard_map/ppermute | solution.py:71
  10.0 1.3 %collective-permute-start.1 = (bf16[64,64]{1,0:T(8,128)(2,1)S(1)}, bf16[64,64]{1,0:T(8,128)(2,1)S(1)}, u32[]{:S(2)}, u32[]{:S(2)}) collective-permute-start(bf16[64,64]{1,0:T(8,128)(2,1)S(1)} %copy-done.2), channel_id=1, source_target_pairs={{0,4},{4,0},{8,12},{12,8},{16,20},{20,16},{24,28},{28,24},{1,5},{5... | collective-permute-start | bytes 24584 | tf_op jit(solution)/shard_map/ppermute | solution.py:71
  11.4 6.4 %collective-permute-start.2 = (bf16[272,128]{1,0:T(8,128)(2,1)S(1)}, bf16[272,128]{1,0:T(8,128)(2,1)S(1)}, u32[]{:S(2)}, u32[]{:S(2)}) collective-permute-start(bf16[272,128]{1,0:T(8,128)(2,1)S(1)} %get-tuple-element.16), channel_id=1, source_target_pairs={{0,24},{4,28},{8,16},{12,20},{16,8},{20,12},{24,0},{28,4},{1,25},{... | collective-permute-start | bytes 208904 | tf_op jit(solution)/shard_map/ppermute | solution.py:71
  14.1 5.4 %collective-permute-start.3 = (bf16[272,128]{1,0:T(8,128)(2,1)S(1)}, bf16[272,128]{1,0:T(8,128)(2,1)S(1)}, u32[]{:S(2)}, u32[]{:S(2)}) collective-permute-start(bf16[272,128]{1,0:T(8,128)(2,1)S(1)} %get-tuple-element.17), channel_id=1, source_target_pairs={{0,16},{4,20},{8,24},{12,28},{16,0},{20,4},{24,8},{28,12},{1,17},{... | collective-permute-start | bytes 208904 | tf_op jit(solution)/shard_map/ppermute | solution.py:71
  14.7 4.8 %collective-permute-start.4 = (bf16[272,128]{1,0:T(8,128)(2,1)S(1)}, bf16[272,128]{1,0:T(8,128)(2,1)S(1)}, u32[]{:S(2)}, u32[]{:S(2)}) collective-permute-start(bf16[272,128]{1,0:T(8,128)(2,1)S(1)} %get-tuple-element.18), channel_id=1, source_target_pairs={{0,8},{4,12},{8,0},{12,4},{16,24},{20,28},{24,16},{28,20},{1,9},{5... | collective-permute-start | bytes 208904 | tf_op jit(solution)/shard_map/ppermute | solution.py:71
  23.1 2.0 %collective-permute-start.7 = (bf16[272,128]{1,0:T(8,128)(2,1)S(1)}, bf16[272,128]{1,0:T(8,128)(2,1)S(1)}, u32[]{:S(2)}, u32[]{:S(2)}) collective-permute-start(bf16[272,128]{1,0:T(8,128)(2,1)S(1)} %near_swap.1), channel_id=1, source_target_pairs={{0,4},{4,0},{8,12},{12,8},{16,20},{20,16},{24,28},{28,24},{1,5},{5... | collective-permute-start | bytes 208904 | tf_op jit(solution)/shard_map/ppermute | solution.py:71
  23.5 5.2 %collective-permute-start.5 = (bf16[272,128]{1,0:T(8,128)(2,1)S(1)}, bf16[272,128]{1,0:T(8,128)(2,1)S(1)}, u32[]{:S(2)}, u32[]{:S(2)}) collective-permute-start(bf16[272,128]{1,0:T(8,128)(2,1)S(1)} %get-tuple-element.22), channel_id=1, source_target_pairs={{0,24},{4,28},{8,16},{12,20},{16,8},{20,12},{24,0},{28,4},{1,25},{... | collective-permute-start | bytes 208904 | tf_op jit(solution)/shard_map/ppermute | solution.py:71
  25.2 5.0 %collective-permute-start.8 = (bf16[272,128]{1,0:T(8,128)(2,1)S(1)}, bf16[272,128]{1,0:T(8,128)(2,1)S(1)}, u32[]{:S(2)}, u32[]{:S(2)}) collective-permute-start(bf16[272,128]{1,0:T(8,128)(2,1)S(1)} %get-tuple-element.26), channel_id=1, source_target_pairs={{0,16},{4,12},{8,24},{12,4},{16,0},{20,28},{24,8},{28,20},{1,17},{... | collective-permute-start | bytes 208904 | tf_op jit(solution)/shard_map/ppermute | solution.py:76
  26.6 4.3 %collective-permute-start.9 = (bf16[272,128]{1,0:T(8,128)(2,1)S(1)}, bf16[272,128]{1,0:T(8,128)(2,1)S(1)}, u32[]{:S(2)}, u32[]{:S(2)}) collective-permute-start(bf16[272,128]{1,0:T(8,128)(2,1)S(1)} %get-tuple-element.27), channel_id=1, source_target_pairs={{0,8},{4,20},{8,0},{12,28},{16,24},{20,4},{24,16},{28,12},{1,9},{5... | collective-permute-start | bytes 208904 | tf_op jit(solution)/shard_map/ppermute | solution.py:76
  29.3 1.6 %collective-permute-start.6 = (bf16[272,128]{1,0:T(8,128)(2,1)S(1)}, bf16[272,128]{1,0:T(8,128)(2,1)S(1)}, u32[]{:S(2)}, u32[]{:S(2)}) collective-permute-start(bf16[272,128]{1,0:T(8,128)(2,1)S(1)} %swap.1), channel_id=1, source_target_pairs={{0,4},{4,0},{8,12},{12,8},{16,20},{20,16},{24,28},{28,24},{1,5},{5... | collective-permute-start | bytes 208904 | tf_op jit(solution)/shard_map/ppermute | solution.py:71

commit v8 on v7

--- a/solution.py
+++ b/solution.py
@@ -9,6 +9,7 @@
 
 LANES = 128
 STEP = 32
+SLAB = 64
 EXTRA = 16
 DEPTH = 1024
 VMEM_LIMIT = 40 * 1024 * 1024
@@ -131,7 +132,7 @@
     in_refs = refs[:chips]
     toep_ref, x_ref, filt_ref = refs[chips:]
     block_len = x_ref.shape[0] // n_seq
-    groups = toep_ref.shape[0] // STEP
+    groups = toep_ref.shape[0] // SLAB
     reach = toep_ref.shape[1]
     chip, core, _ = place()
     low = lax.broadcasted_iota(jnp.int32, (groups, LANES), 1) < taps_here
@@ -146,9 +147,9 @@
     tiles = [filt_ref[tile] for tile in range(chips)]
     filt = jnp.concatenate(tiles + [jnp.zeros((groups, LANES), jnp.float32)], axis=1)
     for group in range(groups):
-        rows = jnp.broadcast_to(filt[group : group + 1], (STEP, reach))
+        rows = jnp.broadcast_to(filt[group : group + 1], (SLAB, reach))
         rows = pltpu.roll(rows, 0, 1, stride=1, stride_axis=0)
-        toep_ref[group * STEP : (group + 1) * STEP] = rows.astype(jnp.bfloat16)
+        toep_ref[group * SLAB : (group + 1) * SLAB] = rows.astype(jnp.bfloat16)
 
 
 def group_of_lane(rows, width, groups):
@@ -160,24 +161,24 @@
     reach = toeplitz.shape[1]
     window = jnp.concatenate(
         [
-            dye_ref[pl.ds(pl.multiple_of(start, STEP), reach)],
-            dye_ref[pl.ds(pl.multiple_of(start + STEP, STEP), reach)],
+            dye_ref[pl.ds(pl.multiple_of(start, SLAB), reach)],
+            dye_ref[pl.ds(pl.multiple_of(start + SLAB, SLAB), reach)],
         ],
         axis=1,
     )
     full = jnp.dot(toeplitz, window, preferred_element_type=jnp.float32)
-    group2 = group_of_lane(STEP, 2 * LANES, groups)
-    total = full[:STEP]
+    group2 = group_of_lane(SLAB, 2 * LANES, groups)
+    total = full[:SLAB]
     for group in range(1, groups):
-        total = jnp.where(group2 == group, full[group * STEP : (group + 1) * STEP], total)
+        total = jnp.where(group2 == group, full[group * SLAB : (group + 1) * SLAB], total)
     return jnp.concatenate([total[:, :LANES], total[:, LANES:]], axis=0).astype(jnp.bfloat16)
 
 
 def tokens_of(seq, dye_ref, toep_ref, out_ref, at, block_len):
     toeplitz = toep_ref[...]
-    groups = toeplitz.shape[0] // STEP
-    for row in range(0, block_len, 2 * STEP):
-        out_ref[at + row : at + row + 2 * STEP] = filtered(
+    groups = toeplitz.shape[0] // SLAB
+    for row in range(0, block_len, 2 * SLAB):
+        out_ref[at + row : at + row + 2 * SLAB] = filtered(
             dye_ref, seq * block_len + row, toeplitz, groups
         )
 
@@ -187,7 +188,7 @@
 ):
     chips = n_seq // 2
     tokens = dy_ref.shape[0]
-    groups = toep_ref.shape[0] // STEP
+    groups = toep_ref.shape[0] // SLAB
     taps = n_seq * taps_here
     reach = taps + LANES
     chip, core, _ = place()
@@ -206,19 +207,20 @@
             axis=0,
         )
         part = lax.dot_general(
-            masked, windows, (((1,), (1,)), ((), ())), preferred_element_type=jnp.float32
+            windows, masked, (((1,), (1,)), ((), ())), preferred_element_type=jnp.float32
         )
         if at == 0:
             lag_ref[...] = part
         else:
             lag_ref[...] += part
 
+    lags = lag_ref[...].T
     eights = []
     for group in range(groups):
         at = group * STEP
-        rows = lag_ref[at : at + 8]
+        rows = lags[at : at + 8]
         for high in range(1, STEP // 8):
-            rows = rows + roll_left(lag_ref[at + 8 * high : at + 8 * high + 8], 8 * high)
+            rows = rows + roll_left(lags[at + 8 * high : at + 8 * high + 8], 8 * high)
         eights.append(rows)
     skew = jnp.concatenate(eights, axis=0)
     row_in = lax.broadcasted_iota(jnp.int32, skew.shape, 0) % 8
@@ -377,7 +379,7 @@
     )
     toeplitz, x = local_call(
         functools.partial(toeplitz_kernel, n_seq, taps_here),
-        [half(groups * STEP, taps + LANES), half(tokens, LANES)],
+        [half(groups * SLAB, taps + LANES), half(tokens, LANES)],
         fan_out(pieces, "seq", 2),
         "toeplitz",
         [pltpu.VMEM((chips, groups, LANES), jnp.float32)],
@@ -387,7 +389,7 @@
         [half(tokens + taps + LANES, LANES), half(chips, EXTRA, LANES), unit],
         (dy.reshape(tokens, LANES), x, toeplitz),
         "first",
-        [pltpu.VMEM((groups * STEP, taps + LANES), jnp.float32)],
+        [pltpu.VMEM((taps + LANES, groups * STEP), jnp.float32)],
     )
     far = xor_permute(far, "seq", 2 * masks[1])
     near = masks[2:]
@@ -433,7 +435,7 @@
             and groups_here == 8 * n_seq
             and 2 * taps_here == LANES
             and out_grads.shape[0] % 16 == 0
-            and layer_inputs.shape[0] % (2 * STEP) == 0
+            and layer_inputs.shape[0] % (2 * SLAB) == 0
             and n_seq * layer_inputs.shape[0] % (STEP * DEPTH // LANES) == 0
             and n_seq * taps_here + LANES <= n_seq * layer_inputs.shape[0]
         )

time: 31.9 us -> 32 us (level)
  no operation moved by 1% of the time
where the time goes in v8:
time: 32 us; the launch traced here: 31.8 us
  starting transfers between devices  15.4 us (48%)
  waiting for transfers between devices  8.3 us (26%)
  Pallas kernels  6.38 us (20%)
  local copies, waits for them, and re-layouts  0.95 us (3%)
  between operations  0.73 us (2%)
    all_to_all x1, starting transfers between devices, by_channels(): lax.all_to_all(dy, ('seq', 'chan'), split_axis=0, concat_axis=0, tiled=True)  7.3 us
    ppermute x8, waiting for transfers between devices, xor_permute(): return lax.ppermute(value, axis, pairs)  6.64 us
    pallas_call x10, Pallas kernels, local_call(): pl.pallas_call(kernel, out_shape=out_shape, in_specs=[whole] * len(operan...  6.38 us
    ppermute x8, starting transfers between devices, xor_permute(): return lax.ppermute(value, axis, pairs)  5.72 us
    ppermute x2, starting transfers between devices, turned_permute(): return lax.ppermute(value, axis, pairs)  2.42 us
    ppermute x2, waiting for transfers between devices, turned_permute(): return lax.ppermute(value, axis, pairs)  1.59 us
    unnamed x6, local copies, waits for them, and re-layouts  0.95 us
  transfers between devices with their start and end apart: 11, of which 7 were waited for; matrix products, arithmetic and copies ran while one was open for 0% of the time, Pallas kernels for 5%

profile of v8, /device:TPU:0, one launch (start us, length us, event | category | flops | bytes accessed | tf_op | source)
XLA Modules:
  0.0 31.8 jit_solution(477977525763785773)
XLA Ops:
  0.6 0.9 %copy-done = bf16[32,4096]{1,0:T(8,128)(2,1)S(1)} copy-done((bf16[32,4096]{1,0:T(8,128)(2,1)S(1)}, bf16[32,4096]{1,0:T(8,128)(2,1)}, u32[]{:S(2)}) %copy-start) | copy-done | bytes 262168
  1.6 0.7 %fan_grads.1 = bf16[32,32,128]{2,1,0:T(8,128)(2,1)} custom-call(bf16[32,4096]{1,0:T(8,128)(2,1)S(1)} %copy-done), custom_call_target="tpu_custom_call" | custom-call | tf_op jit(solution)/shard_map/fan_grads/pallas_call | solution.py:339
  2.3 7.3 %all-to-all-start = ((bf16[32,32,128]{2,1,0:T(8,128)(2,1)}), bf16[32,32,128]{2,1,0:T(8,128)(2,1)S(1)}, u32[]{:S(2)}, u32[]{:S(2)}) async-start(bf16[32,32,128]{2,1,0:T(8,128)(2,1)} %fan_grads.1), calls=%async_computation | async-start | bytes 524288 | tf_op jit(solution)/shard_map/all_to_all | solution.py:372
  9.6 0.3 collective-permute-start
  10.0 0.3 collective-permute-start.1
  10.2 1.0 %collective-permute-done.1.f_other_ref = bf16[64,64]{1,0:T(8,128)(2,1)S(1)} collective-permute-done((bf16[64,64]{1,0:T(8,128)(2,1)S(1)}, bf16[64,64]{1,0:T(8,128)(2,1)S(1)}, u32[]{:S(2)}, u32[]{:S(2)}) %collective-permute-start.1) | collective-permute-done | bytes 8224 | tf_op jit(solution)/shard_map/ppermute | solution.py:72
  11.4 2.7 %collective-permute-start.2 = (bf16[272,128]{1,0:T(8,128)(2,1)S(1)}, bf16[272,128]{1,0:T(8,128)(2,1)S(1)}, u32[]{:S(2)}, u32[]{:S(2)}) collective-permute-start(bf16[272,128]{1,0:T(8,128)(2,1)S(1)} %get-tuple-element.16), channel_id=1, source_target_pairs={{0,24},{4,28},{8,16},{12,20},{16,8},{20,12},{24,0},{28,4},{1,25},{... | collective-permute-start | bytes 208904 | tf_op jit(solution)/shard_map/ppermute | solution.py:72
  14.1 0.6 %collective-permute-start.3 = (bf16[272,128]{1,0:T(8,128)(2,1)S(1)}, bf16[272,128]{1,0:T(8,128)(2,1)S(1)}, u32[]{:S(2)}, u32[]{:S(2)}) collective-permute-start(bf16[272,128]{1,0:T(8,128)(2,1)S(1)} %get-tuple-element.17), channel_id=1, source_target_pairs={{0,16},{4,20},{8,24},{12,28},{16,0},{20,4},{24,8},{28,12},{1,17},{... | collective-permute-start | bytes 208904 | tf_op jit(solution)/shard_map/ppermute | solution.py:72
  14.7 0.3 collective-permute-start.4
  14.9 2.8 %collective-permute-done.2.refs_1_ = bf16[272,128]{1,0:T(8,128)(2,1)S(1)} collective-permute-done((bf16[272,128]{1,0:T(8,128)(2,1)S(1)}, bf16[272,128]{1,0:T(8,128)(2,1)S(1)}, u32[]{:S(2)}, u32[]{:S(2)}) %collective-permute-start.2) | collective-permute-done | bytes 69664 | tf_op jit(solution)/shard_map/ppermute | solution.py:72
  17.8 1.7 %collective-permute-done.3.refs_2_ = bf16[272,128]{1,0:T(8,128)(2,1)S(1)} collective-permute-done((bf16[272,128]{1,0:T(8,128)(2,1)S(1)}, bf16[272,128]{1,0:T(8,128)(2,1)S(1)}, u32[]{:S(2)}, u32[]{:S(2)}) %collective-permute-start.3) | collective-permute-done | bytes 69664 | tf_op jit(solution)/shard_map/ppermute | solution.py:72
  19.5 0.3 %toeplitz.1 = (bf16[512,640]{1,0:T(8,128)(2,1)S(1)}, bf16[1024,128]{1,0:T(8,128)(2,1)S(1)}) custom-call(bf16[272,128]{1,0:T(8,128)(2,1)S(1)} %get-tuple-element.15.refs_0_, bf16[272,128]{1,0:T(8,128)(2,1)S(1)} %collective-permute-done.2.refs_1_, bf16[272,128]{1,0:T(8,128)(2,1)S(1)} %collective-permute-done.3.refs_2_, ...), custom_call_target="tpu_custom_call" | custom-call | tf_op jit(solution)/shard_map/toeplitz/pallas_call | solution.py:339
  19.9 2.6 %first.1 = (bf16[1664,128]{1,0:T(8,128)(2,1)S(1)}, bf16[4,16,128]{2,1,0:T(8,128)(2,1)S(1)}, bf16[272,128]{1,0:T(8,128)(2,1)S(1)}) custom-call(bf16[1024,128]{1,0:T(8,128)(2,1)S(1)} %bitcast.1, bf16[1024,128]{1,0:T(8,128)(2,1)S(1)} %get-tuple-element.19.x_ref, bf16[512,640]{1,0:T(8,128)(2,1)S(1)} %get-tuple-element.20.toep_ref), custom_call_target="tpu_custom_call" | custom-call | tf_op jit(solution)/shard_map/first/pallas_call | solution.py:339
  22.5 0.6 %near_swap.1 = bf16[272,128]{1,0:T(8,128)(2,1)S(1)} custom-call(bf16[1664,128]{1,0:T(8,128)(2,1)S(1)} %get-tuple-element.21.dye_ref, bf16[512,640]{1,0:T(8,128)(2,1)S(1)} %get-tuple-element.20.toep_ref, bf16[4,16,128]{2,1,0:T(8,128)(2,1)S(1)} %get-tuple-element.24.taps_ref), custom_call_target="tpu_custom_call" | custom-call | tf_op jit(solution)/shard_map/near_swap/pallas_call | solution.py:339
  23.1 0.4 %collective-permute-start.7 = (bf16[272,128]{1,0:T(8,128)(2,1)S(1)}, bf16[272,128]{1,0:T(8,128)(2,1)S(1)}, u32[]{:S(2)}, u32[]{:S(2)}) collective-permute-start(bf16[272,128]{1,0:T(8,128)(2,1)S(1)} %near_swap.1), channel_id=1, source_target_pairs={{0,4},{4,0},{8,12},{12,8},{16,20},{20,16},{24,28},{28,24},{1,5},{5... | collective-permute-start | bytes 208904 | tf_op jit(solution)/shard_map/ppermute | solution.py:72
  23.5 1.1 %collective-permute-start.5 = (bf16[272,128]{1,0:T(8,128)(2,1)S(1)}, bf16[272,128]{1,0:T(8,128)(2,1)S(1)}, u32[]{:S(2)}, u32[]{:S(2)}) collective-permute-start(bf16[272,128]{1,0:T(8,128)(2,1)S(1)} %get-tuple-element.22), channel_id=1, source_target_pairs={{0,24},{4,28},{8,16},{12,20},{16,8},{20,12},{24,0},{28,4},{1,25},{... | collective-permute-start | bytes 208904 | tf_op jit(solution)/shard_map/ppermute | solution.py:72
  24.7 0.6 %near_keep.1.keep_ref = bf16[272,128]{1,0:T(8,128)(2,1)S(1)} custom-call(bf16[1664,128]{1,0:T(8,128)(2,1)S(1)} %get-tuple-element.21.dye_ref, bf16[512,640]{1,0:T(8,128)(2,1)S(1)} %get-tuple-element.20.toep_ref, bf16[4,16,128]{2,1,0:T(8,128)(2,1)S(1)} %get-tuple-element.24.taps_ref), custom_call_target="tpu_custom_call" | custom-call | tf_op jit(solution)/shard_map/near_keep/pallas_call | solution.py:339
  25.3 1.4 %collective-permute-start.8 = (bf16[272,128]{1,0:T(8,128)(2,1)S(1)}, bf16[272,128]{1,0:T(8,128)(2,1)S(1)}, u32[]{:S(2)}, u32[]{:S(2)}) collective-permute-start(bf16[272,128]{1,0:T(8,128)(2,1)S(1)} %get-tuple-element.26), channel_id=1, source_target_pairs={{0,16},{4,12},{8,24},{12,4},{16,0},{20,28},{24,8},{28,20},{1,17},{... | collective-permute-start | bytes 208904 | tf_op jit(solution)/shard_map/ppermute | solution.py:77
  26.7 1.0 %collective-permute-start.9 = (bf16[272,128]{1,0:T(8,128)(2,1)S(1)}, bf16[272,128]{1,0:T(8,128)(2,1)S(1)}, u32[]{:S(2)}, u32[]{:S(2)}) collective-permute-start(bf16[272,128]{1,0:T(8,128)(2,1)S(1)} %get-tuple-element.27), channel_id=1, source_target_pairs={{0,8},{4,20},{8,0},{12,28},{16,24},{20,4},{24,16},{28,12},{1,9},{5... | collective-permute-start | bytes 208904 | tf_op jit(solution)/shard_map/ppermute | solution.py:77
  27.7 1.0 %collective-permute-done.5.refs_1_ = bf16[272,128]{1,0:T(8,128)(2,1)S(1)} collective-permute-done((bf16[272,128]{1,0:T(8,128)(2,1)S(1)}, bf16[272,128]{1,0:T(8,128)(2,1)S(1)}, u32[]{:S(2)}, u32[]{:S(2)}) %collective-permute-start.5) | collective-permute-done | bytes 69664 | tf_op jit(solution)/shard_map/ppermute | solution.py:72
  28.7 0.6 %own.1.refs_0_ = bf16[272,128]{1,0:T(8,128)(2,1)S(1)} custom-call(bf16[1664,128]{1,0:T(8,128)(2,1)S(1)} %get-tuple-element.21.dye_ref, bf16[512,640]{1,0:T(8,128)(2,1)S(1)} %get-tuple-element.20.toep_ref, bf16[4,16,128]{2,1,0:T(8,128)(2,1)S(1)} %get-tuple-element.24.taps_ref), custom_call_target="tpu_custom_call" | custom-call | tf_op jit(solution)/shard_map/own/pallas_call | solution.py:339
  29.4 0.9 %collective-permute-done.8.refs_3_ = bf16[272,128]{1,0:T(8,128)(2,1)S(1)} collective-permute-done((bf16[272,128]{1,0:T(8,128)(2,1)S(1)}, bf16[272,128]{1,0:T(8,128)(2,1)S(1)}, u32[]{:S(2)}, u32[]{:S(2)}) %collective-permute-start.8) | collective-permute-done | bytes 69664 | tf_op jit(solution)/shard_map/ppermute | solution.py:77
  30.3 0.7 %collective-permute-done.9.refs_4_ = bf16[272,128]{1,0:T(8,128)(2,1)S(1)} collective-permute-done((bf16[272,128]{1,0:T(8,128)(2,1)S(1)}, bf16[272,128]{1,0:T(8,128)(2,1)S(1)}, u32[]{:S(2)}, u32[]{:S(2)}) %collective-permute-start.9) | collective-permute-done | bytes 69664 | tf_op jit(solution)/shard_map/ppermute | solution.py:77
  31.0 0.8 %unpack.1 = (bf16[128,1024]{1,0:T(8,128)(2,1)}, f32[64,64]{1,0:T(8,128)}) custom-call(bf16[272,128]{1,0:T(8,128)(2,1)S(1)} %own.1.refs_0_, bf16[272,128]{1,0:T(8,128)(2,1)S(1)} %collective-permute-done.5.refs_1_, bf16[272,128]{1,0:T(8,128)(2,1)S(1)} %collective-permute-done.6.refs_2_, bf16[272,128]{1,0:T(8,128)(2,1)S(1)} %collective-permute-done.8.refs_3_, ...), custom_call_target="tpu_custom_call" | custom-call | tf_op jit(solution)/shard_map/unpack/pallas_call | solution.py:339
  (14 shorter events, 0.3 us)
Async XLA Ops:
  0.6 1.0 %copy-start = (bf16[32,4096]{1,0:T(8,128)(2,1)S(1)}, bf16[32,4096]{1,0:T(8,128)(2,1)}, u32[]{:S(2)}) copy-start(bf16[32,4096]{1,0:T(8,128)(2,1)} %in_ref.1) | copy-start | bytes 786436
  2.3 7.3 %copy-start.1 = (bf16[128,1024]{1,0:T(8,128)(2,1)S(1)}, bf16[128,1024]{1,0:T(8,128)(2,1)}, u32[]{:S(2)}) copy-start(bf16[128,1024]{1,0:T(8,128)(2,1)} %x_own_ref.1) | copy-start | bytes 786436
  2.3 7.6 %copy-start.2 = (bf16[64,64]{1,0:T(8,128)(2,1)S(1)}, bf16[64,64]{1,0:T(8,128)(2,1)}, u32[]{:S(2)}) copy-start(bf16[64,64]{1,0:T(8,128)(2,1)} %f_own_ref.1) | copy-start | bytes 24580
  2.3 17.6 %all-to-all-start = ((bf16[32,32,128]{2,1,0:T(8,128)(2,1)}), bf16[32,32,128]{2,1,0:T(8,128)(2,1)S(1)}, u32[]{:S(2)}, u32[]{:S(2)}) async-start(bf16[32,32,128]{2,1,0:T(8,128)(2,1)} %fan_grads.1), calls=%async_computation | async-start | bytes 524288 | tf_op jit(solution)/shard_map/all_to_all | solution.py:372
  9.6 1.6 %collective-permute-start = (bf16[128,1024]{1,0:T(8,128)(2,1)S(1)}, bf16[128,1024]{1,0:T(8,128)(2,1)S(1)}, u32[]{:S(2)}, u32[]{:S(2)}) collective-permute-start(bf16[128,1024]{1,0:T(8,128)(2,1)S(1)} %copy-done.1), channel_id=1, source_target_pairs={{0,4},{4,0},{8,12},{12,8},{16,20},{20,16},{24,28},{28,24},{1,5},{5... | collective-permute-start | bytes 786440 | tf_op jit(solution)/shard_map/ppermute | solution.py:72
  10.0 1.3 %collective-permute-start.1 = (bf16[64,64]{1,0:T(8,128)(2,1)S(1)}, bf16[64,64]{1,0:T(8,128)(2,1)S(1)}, u32[]{:S(2)}, u32[]{:S(2)}) collective-permute-start(bf16[64,64]{1,0:T(8,128)(2,1)S(1)} %copy-done.2), channel_id=1, source_target_pairs={{0,4},{4,0},{8,12},{12,8},{16,20},{20,16},{24,28},{28,24},{1,5},{5... | collective-permute-start | bytes 24584 | tf_op jit(solution)/shard_map/ppermute | solution.py:72
  11.4 6.4 %collective-permute-start.2 = (bf16[272,128]{1,0:T(8,128)(2,1)S(1)}, bf16[272,128]{1,0:T(8,128)(2,1)S(1)}, u32[]{:S(2)}, u32[]{:S(2)}) collective-permute-start(bf16[272,128]{1,0:T(8,128)(2,1)S(1)} %get-tuple-element.16), channel_id=1, source_target_pairs={{0,24},{4,28},{8,16},{12,20},{16,8},{20,12},{24,0},{28,4},{1,25},{... | collective-permute-start | bytes 208904 | tf_op jit(solution)/shard_map/ppermute | solution.py:72
  14.1 5.4 %collective-permute-start.3 = (bf16[272,128]{1,0:T(8,128)(2,1)S(1)}, bf16[272,128]{1,0:T(8,128)(2,1)S(1)}, u32[]{:S(2)}, u32[]{:S(2)}) collective-permute-start(bf16[272,128]{1,0:T(8,128)(2,1)S(1)} %get-tuple-element.17), channel_id=1, source_target_pairs={{0,16},{4,20},{8,24},{12,28},{16,0},{20,4},{24,8},{28,12},{1,17},{... | collective-permute-start | bytes 208904 | tf_op jit(solution)/shard_map/ppermute | solution.py:72
  14.7 4.8 %collective-permute-start.4 = (bf16[272,128]{1,0:T(8,128)(2,1)S(1)}, bf16[272,128]{1,0:T(8,128)(2,1)S(1)}, u32[]{:S(2)}, u32[]{:S(2)}) collective-permute-start(bf16[272,128]{1,0:T(8,128)(2,1)S(1)} %get-tuple-element.18), channel_id=1, source_target_pairs={{0,8},{4,12},{8,0},{12,4},{16,24},{20,28},{24,16},{28,20},{1,9},{5... | collective-permute-start | bytes 208904 | tf_op jit(solution)/shard_map/ppermute | solution.py:72
  23.1 2.1 %collective-permute-start.7 = (bf16[272,128]{1,0:T(8,128)(2,1)S(1)}, bf16[272,128]{1,0:T(8,128)(2,1)S(1)}, u32[]{:S(2)}, u32[]{:S(2)}) collective-permute-start(bf16[272,128]{1,0:T(8,128)(2,1)S(1)} %near_swap.1), channel_id=1, source_target_pairs={{0,4},{4,0},{8,12},{12,8},{16,20},{20,16},{24,28},{28,24},{1,5},{5... | collective-permute-start | bytes 208904 | tf_op jit(solution)/shard_map/ppermute | solution.py:72
  23.5 5.2 %collective-permute-start.5 = (bf16[272,128]{1,0:T(8,128)(2,1)S(1)}, bf16[272,128]{1,0:T(8,128)(2,1)S(1)}, u32[]{:S(2)}, u32[]{:S(2)}) collective-permute-start(bf16[272,128]{1,0:T(8,128)(2,1)S(1)} %get-tuple-element.22), channel_id=1, source_target_pairs={{0,24},{4,28},{8,16},{12,20},{16,8},{20,12},{24,0},{28,4},{1,25},{... | collective-permute-start | bytes 208904 | tf_op jit(solution)/shard_map/ppermute | solution.py:72
  25.3 5.0 %collective-permute-start.8 = (bf16[272,128]{1,0:T(8,128)(2,1)S(1)}, bf16[272,128]{1,0:T(8,128)(2,1)S(1)}, u32[]{:S(2)}, u32[]{:S(2)}) collective-permute-start(bf16[272,128]{1,0:T(8,128)(2,1)S(1)} %get-tuple-element.26), channel_id=1, source_target_pairs={{0,16},{4,12},{8,24},{12,4},{16,0},{20,28},{24,8},{28,20},{1,17},{... | collective-permute-start | bytes 208904 | tf_op jit(solution)/shard_map/ppermute | solution.py:77
  26.7 4.3 %collective-permute-start.9 = (bf16[272,128]{1,0:T(8,128)(2,1)S(1)}, bf16[272,128]{1,0:T(8,128)(2,1)S(1)}, u32[]{:S(2)}, u32[]{:S(2)}) collective-permute-start(bf16[272,128]{1,0:T(8,128)(2,1)S(1)} %get-tuple-element.27), channel_id=1, source_target_pairs={{0,8},{4,20},{8,0},{12,28},{16,24},{20,4},{24,16},{28,12},{1,9},{5... | collective-permute-start | bytes 208904 | tf_op jit(solution)/shard_map/ppermute | solution.py:77
  29.3 1.7 %collective-permute-start.6 = (bf16[272,128]{1,0:T(8,128)(2,1)S(1)}, bf16[272,128]{1,0:T(8,128)(2,1)S(1)}, u32[]{:S(2)}, u32[]{:S(2)}) collective-permute-start(bf16[272,128]{1,0:T(8,128)(2,1)S(1)} %swap.1), channel_id=1, source_target_pairs={{0,4},{4,0},{8,12},{12,8},{16,20},{20,16},{24,28},{28,24},{1,5},{5... | collective-permute-start | bytes 208904 | tf_op jit(solution)/shard_map/ppermute | solution.py:72

commit v9 on v8

--- a/solution.py
+++ b/solution.py
@@ -127,16 +127,12 @@
         out_ref[2 * block_len :] = taps.astype(jnp.bfloat16)
 
 
-def toeplitz_kernel(n_seq, taps_here, *refs):
-    chips = n_seq // 2
-    in_refs = refs[:chips]
-    toep_ref, x_ref, filt_ref = refs[chips:]
-    block_len = x_ref.shape[0] // n_seq
-    groups = toep_ref.shape[0] // SLAB
-    reach = toep_ref.shape[1]
+def place_inputs(in_refs, taps_here, x_ref, filt_ref):
+    block_len = (in_refs[0].shape[0] - EXTRA) // 2
+    groups = EXTRA // 2
     chip, core, _ = place()
     low = lax.broadcasted_iota(jnp.int32, (groups, LANES), 1) < taps_here
-    for bits, in_ref in zip(partners(chips), in_refs):
+    for bits, in_ref in zip(partners(len(in_refs)), in_refs):
         for flip in range(2):
             block = 2 * (chip ^ bits) + (core ^ flip)
             x_ref[rows_at(block, block_len)] = in_ref[flip * block_len : (flip + 1) * block_len]
@@ -144,6 +140,11 @@
         first = jnp.where(core == 0, taps[:groups], taps[groups:])
         second = jnp.where(core == 0, taps[groups:], taps[:groups])
         filt_ref[chip ^ bits] = jnp.where(low, first, pltpu.roll(second, taps_here, 1))
+
+
+def toeplitz_rows(filt_ref, toep_ref):
+    chips, groups, _ = filt_ref.shape
+    reach = toep_ref.shape[1]
     tiles = [filt_ref[tile] for tile in range(chips)]
     filt = jnp.concatenate(tiles + [jnp.zeros((groups, LANES), jnp.float32)], axis=1)
     for group in range(groups):
@@ -183,24 +184,27 @@
         )
 
 
-def first_kernel(
-    n_seq, taps_here, far, dy_ref, x_ref, toep_ref, dye_ref, taps_ref, out_ref, lag_ref
-):
+def first_kernel(n_seq, taps_here, far, dy_ref, *refs):
     chips = n_seq // 2
+    in_refs = refs[:chips]
+    dye_ref, taps_ref, toep_ref, out_ref, x_ref, filt_ref, lag_ref = refs[chips:]
     tokens = dy_ref.shape[0]
-    groups = toep_ref.shape[0] // SLAB
+    groups = EXTRA // 2
     taps = n_seq * taps_here
     reach = taps + LANES
     chip, core, _ = place()
 
+    place_inputs(in_refs, taps_here, x_ref, filt_ref)
     dye_ref[:tokens] = dy_ref[...]
     dye_ref[tokens:] = dy_ref[:reach]
 
+    rows = taps + STEP
     deep = DEPTH // LANES
     group_in = group_of_lane(STEP, DEPTH, groups)
+    lag_ref[rows:] = jnp.zeros((reach - rows, groups * STEP), jnp.float32)
     for at in range(0, tokens, STEP * deep):
         starts = range(at, at + STEP * deep, STEP)
-        windows = jnp.concatenate([dye_ref[row : row + reach] for row in starts], axis=1)
+        windows = jnp.concatenate([dye_ref[row : row + rows] for row in starts], axis=1)
         inputs = jnp.concatenate([x_ref[row : row + STEP] for row in starts], axis=1)
         masked = jnp.concatenate(
             [jnp.where(group_in == group, inputs, jnp.zeros_like(inputs)) for group in range(groups)],
@@ -210,9 +214,11 @@
             windows, masked, (((1,), (1,)), ((), ())), preferred_element_type=jnp.float32
         )
         if at == 0:
-            lag_ref[...] = part
+            lag_ref[:rows] = part
         else:
-            lag_ref[...] += part
+            lag_ref[:rows] += part
+        if at == 0:
+            toeplitz_rows(filt_ref, toep_ref)
 
     lags = lag_ref[...].T
     eights = []
@@ -377,29 +383,37 @@
         "fan_inputs",
         [pltpu.VMEM((2, groups_here, LANES), jnp.float32)],
     )
-    toeplitz, x = local_call(
-        functools.partial(toeplitz_kernel, n_seq, taps_here),
-        [half(groups * SLAB, taps + LANES), half(tokens, LANES)],
-        fan_out(pieces, "seq", 2),
-        "toeplitz",
-        [pltpu.VMEM((chips, groups, LANES), jnp.float32)],
-    )
-    dye, tap_parts, far = local_call(
+    dye, tap_parts, toeplitz, far = local_call(
         functools.partial(first_kernel, n_seq, taps_here, masks[1]),
-        [half(tokens + taps + LANES, LANES), half(chips, EXTRA, LANES), unit],
-        (dy.reshape(tokens, LANES), x, toeplitz),
+        [
+            half(tokens + taps + LANES, LANES),
+            half(chips, EXTRA, LANES),
+            half(groups * SLAB, taps + LANES),
+            unit,
+        ],
+        (dy.reshape(tokens, LANES), *fan_out(pieces, "seq", 2)),
         "first",
-        [pltpu.VMEM((taps + LANES, groups * STEP), jnp.float32)],
+        [
+            pltpu.VMEM((tokens, LANES), jnp.bfloat16),
+            pltpu.VMEM((chips, groups, LANES), jnp.float32),
+            pltpu.VMEM((taps + LANES, groups * STEP), jnp.float32),
+        ],
     )
     far = xor_permute(far, "seq", 2 * masks[1])
     near = masks[2:]
     near_shape = half(len(near) * (block_len + EXTRA // 2), LANES)
     (send,) = local_call(
-        functools.partial(near_kernel, near, 1), [near_shape], (dye, toeplitz, tap_parts), "near_swap"
+        functools.partial(near_kernel, near, 1),
+        [near_shape],
+        (dye, toeplitz, tap_parts),
+        "near_swap",
     )
     got = xor_permute(send, "seq", 1)
     (keep,) = local_call(
-        functools.partial(near_kernel, near, 0), [near_shape], (dye, toeplitz, tap_parts), "near_keep"
+        functools.partial(near_kernel, near, 0),
+        [near_shape],
+        (dye, toeplitz, tap_parts),
+        "near_keep",
     )
     pieces = local_call(near_pieces_kernel, [unit] * len(near), (keep, got), "near_pieces")
     pieces = [

time: 32 us -> 31.8 us (level)
  Pallas kernels: 6.38 us -> 5.91 us
    pallas_call x10 -> x9, Pallas kernels: 6.38 us -> 5.91 us  [local_call(): pl.pallas_call(kernel, out_shape=out_shape, in_specs=[whole] * len(operan...]
    all_to_all x1, waiting for transfers between devices: 0.07 us -> 0.41 us  [by_channels(): lax.all_to_all(dy, ('seq', 'chan'), split_axis=0, concat_axis=0, tiled=True)]
  transfers between devices with their start and end apart: 11 -> 11, of which waited for: 7 -> 7; matrix products, arithmetic and copies ran while one was open for 0% -> 0% of each run, Pallas kernels for 5% -> 4%
where the time goes in v9:
time: 31.8 us; the launch traced here: 31.6 us
  starting transfers between devices  15.4 us (48%)
  waiting for transfers between devices  8.52 us (27%)
  Pallas kernels  5.91 us (19%)
  local copies, waits for them, and re-layouts  0.95 us (3%)
  between operations  0.73 us (2%)
    all_to_all x1, starting transfers between devices, by_channels(): lax.all_to_all(dy, ('seq', 'chan'), split_axis=0, concat_axis=0, tiled=True)  7.3 us
    ppermute x8, waiting for transfers between devices, xor_permute(): return lax.ppermute(value, axis, pairs)  6.83 us
    pallas_call x9, Pallas kernels, local_call(): pl.pallas_call(kernel, out_shape=out_shape, in_specs=[whole] * len(operan...  5.91 us
    ppermute x8, starting transfers between devices, xor_permute(): return lax.ppermute(value, axis, pairs)  5.48 us
    ppermute x2, starting transfers between devices, turned_permute(): return lax.ppermute(value, axis, pairs)  2.66 us
    ppermute x2, waiting for transfers between devices, turned_permute(): return lax.ppermute(value, axis, pairs)  1.29 us
    unnamed x6, local copies, waits for them, and re-layouts  0.95 us
  transfers between devices with their start and end apart: 11, of which 7 were waited for; matrix products, arithmetic and copies ran while one was open for 0% of the time, Pallas kernels for 4%

profile of v9, /device:TPU:0, one launch (start us, length us, event | category | flops | bytes accessed | tf_op | source)
XLA Modules:
  0.0 31.6 jit_solution(12757917122492293877)
XLA Ops:
  0.6 0.9 %copy-done = bf16[32,4096]{1,0:T(8,128)(2,1)S(1)} copy-done((bf16[32,4096]{1,0:T(8,128)(2,1)S(1)}, bf16[32,4096]{1,0:T(8,128)(2,1)}, u32[]{:S(2)}) %copy-start) | copy-done | bytes 262168
  1.6 0.7 %fan_grads.1 = bf16[32,32,128]{2,1,0:T(8,128)(2,1)} custom-call(bf16[32,4096]{1,0:T(8,128)(2,1)S(1)} %copy-done), custom_call_target="tpu_custom_call" | custom-call | tf_op jit(solution)/shard_map/fan_grads/pallas_call | solution.py:345
  2.3 7.3 %all-to-all-start = ((bf16[32,32,128]{2,1,0:T(8,128)(2,1)}), bf16[32,32,128]{2,1,0:T(8,128)(2,1)S(1)}, u32[]{:S(2)}, u32[]{:S(2)}) async-start(bf16[32,32,128]{2,1,0:T(8,128)(2,1)} %fan_grads.1), calls=%async_computation | async-start | bytes 524288 | tf_op jit(solution)/shard_map/all_to_all | solution.py:378
  9.6 0.3 %collective-permute-start = (bf16[128,1024]{1,0:T(8,128)(2,1)S(1)}, bf16[128,1024]{1,0:T(8,128)(2,1)S(1)}, u32[]{:S(2)}, u32[]{:S(2)}) collective-permute-start(bf16[128,1024]{1,0:T(8,128)(2,1)S(1)} %copy-done.1), channel_id=1, source_target_pairs={{0,4},{4,0},{8,12},{12,8},{16,20},{20,16},{24,28},{28,24},{1,5},{5... | collective-permute-start | bytes 786440 | tf_op jit(solution)/shard_map/ppermute | solution.py:72
  10.0 0.3 collective-permute-start.1
  10.2 1.0 %collective-permute-done.1.f_other_ref = bf16[64,64]{1,0:T(8,128)(2,1)S(1)} collective-permute-done((bf16[64,64]{1,0:T(8,128)(2,1)S(1)}, bf16[64,64]{1,0:T(8,128)(2,1)S(1)}, u32[]{:S(2)}, u32[]{:S(2)}) %collective-permute-start.1) | collective-permute-done | bytes 8224 | tf_op jit(solution)/shard_map/ppermute | solution.py:72
  11.4 2.7 %collective-permute-start.2 = (bf16[272,128]{1,0:T(8,128)(2,1)S(1)}, bf16[272,128]{1,0:T(8,128)(2,1)S(1)}, u32[]{:S(2)}, u32[]{:S(2)}) collective-permute-start(bf16[272,128]{1,0:T(8,128)(2,1)S(1)} %get-tuple-element.15), channel_id=1, source_target_pairs={{0,24},{4,28},{8,16},{12,20},{16,8},{20,12},{24,0},{28,4},{1,25},{... | collective-permute-start | bytes 208904 | tf_op jit(solution)/shard_map/ppermute | solution.py:72
  14.1 0.6 %collective-permute-start.3 = (bf16[272,128]{1,0:T(8,128)(2,1)S(1)}, bf16[272,128]{1,0:T(8,128)(2,1)S(1)}, u32[]{:S(2)}, u32[]{:S(2)}) collective-permute-start(bf16[272,128]{1,0:T(8,128)(2,1)S(1)} %get-tuple-element.16), channel_id=1, source_target_pairs={{0,16},{4,20},{8,24},{12,28},{16,0},{20,4},{24,8},{28,12},{1,17},{... | collective-permute-start | bytes 208904 | tf_op jit(solution)/shard_map/ppermute | solution.py:72
  14.7 0.3 collective-permute-start.4
  14.9 2.8 %collective-permute-done.2.refs_1_ = bf16[272,128]{1,0:T(8,128)(2,1)S(1)} collective-permute-done((bf16[272,128]{1,0:T(8,128)(2,1)S(1)}, bf16[272,128]{1,0:T(8,128)(2,1)S(1)}, u32[]{:S(2)}, u32[]{:S(2)}) %collective-permute-start.2) | collective-permute-done | bytes 69664 | tf_op jit(solution)/shard_map/ppermute | solution.py:72
  17.8 1.7 %collective-permute-done.3.refs_2_ = bf16[272,128]{1,0:T(8,128)(2,1)S(1)} collective-permute-done((bf16[272,128]{1,0:T(8,128)(2,1)S(1)}, bf16[272,128]{1,0:T(8,128)(2,1)S(1)}, u32[]{:S(2)}, u32[]{:S(2)}) %collective-permute-start.3) | collective-permute-done | bytes 69664 | tf_op jit(solution)/shard_map/ppermute | solution.py:72
  19.5 0.4 %all-to-all-done = bf16[32,32,128]{2,1,0:T(8,128)(2,1)S(1)} async-done(((bf16[32,32,128]{2,1,0:T(8,128)(2,1)}), bf16[32,32,128]{2,1,0:T(8,128)(2,1)S(1)}, u32[]{:S(2)}, u32[]{:S(2)}) %all-to-all-start) | async-done | bytes 262176 | tf_op jit(solution)/shard_map/all_to_all | solution.py:378
  19.9 2.5 %first.1 = (bf16[1664,128]{1,0:T(8,128)(2,1)S(1)}, bf16[4,16,128]{2,1,0:T(8,128)(2,1)S(1)}, bf16[512,640]{1,0:T(8,128)(2,1)S(1)}, bf16[272,128]{1,0:T(8,128)(2,1)S(1)}) custom-call(bf16[1024,128]{1,0:T(8,128)(2,1)S(1)} %bitcast.1, bf16[272,128]{1,0:T(8,128)(2,1)S(1)} %get-tuple-element.14.refs_0_, bf16[272,128]{1,0:T(8,128)(2,1)S(1)} %collective-permute-done.2.refs_1_, ...), custom_call_target="tpu_custom_call" | custom-call | tf_op jit(solution)/shard_map/first/pallas_call | solution.py:345
  22.4 0.6 %near_swap.1 = bf16[272,128]{1,0:T(8,128)(2,1)S(1)} custom-call(bf16[1664,128]{1,0:T(8,128)(2,1)S(1)} %get-tuple-element.18.dye_ref, bf16[512,640]{1,0:T(8,128)(2,1)S(1)} %get-tuple-element.19.toep_ref, bf16[4,16,128]{2,1,0:T(8,128)(2,1)S(1)} %get-tuple-element.22.taps_ref), custom_call_target="tpu_custom_call" | custom-call | tf_op jit(solution)/shard_map/near_swap/pallas_call | solution.py:345
  23.0 0.4 %collective-permute-start.7 = (bf16[272,128]{1,0:T(8,128)(2,1)S(1)}, bf16[272,128]{1,0:T(8,128)(2,1)S(1)}, u32[]{:S(2)}, u32[]{:S(2)}) collective-permute-start(bf16[272,128]{1,0:T(8,128)(2,1)S(1)} %near_swap.1), channel_id=1, source_target_pairs={{0,4},{4,0},{8,12},{12,8},{16,20},{20,16},{24,28},{28,24},{1,5},{5... | collective-permute-start | bytes 208904 | tf_op jit(solution)/shard_map/ppermute | solution.py:72
  23.4 0.9 %collective-permute-start.5 = (bf16[272,128]{1,0:T(8,128)(2,1)S(1)}, bf16[272,128]{1,0:T(8,128)(2,1)S(1)}, u32[]{:S(2)}, u32[]{:S(2)}) collective-permute-start(bf16[272,128]{1,0:T(8,128)(2,1)S(1)} %get-tuple-element.20), channel_id=1, source_target_pairs={{0,24},{4,28},{8,16},{12,20},{16,8},{20,12},{24,0},{28,4},{1,25},{... | collective-permute-start | bytes 208904 | tf_op jit(solution)/shard_map/ppermute | solution.py:72
  24.3 0.6 %near_keep.1.keep_ref = bf16[272,128]{1,0:T(8,128)(2,1)S(1)} custom-call(bf16[1664,128]{1,0:T(8,128)(2,1)S(1)} %get-tuple-element.18.dye_ref, bf16[512,640]{1,0:T(8,128)(2,1)S(1)} %get-tuple-element.19.toep_ref, bf16[4,16,128]{2,1,0:T(8,128)(2,1)S(1)} %get-tuple-element.22.taps_ref), custom_call_target="tpu_custom_call" | custom-call | tf_op jit(solution)/shard_map/near_keep/pallas_call | solution.py:345
  24.9 1.5 %collective-permute-start.8 = (bf16[272,128]{1,0:T(8,128)(2,1)S(1)}, bf16[272,128]{1,0:T(8,128)(2,1)S(1)}, u32[]{:S(2)}, u32[]{:S(2)}) collective-permute-start(bf16[272,128]{1,0:T(8,128)(2,1)S(1)} %get-tuple-element.24), channel_id=1, source_target_pairs={{0,16},{4,12},{8,24},{12,4},{16,0},{20,28},{24,8},{28,20},{1,17},{... | collective-permute-start | bytes 208904 | tf_op jit(solution)/shard_map/ppermute | solution.py:77
  26.4 1.1 %collective-permute-start.9 = (bf16[272,128]{1,0:T(8,128)(2,1)S(1)}, bf16[272,128]{1,0:T(8,128)(2,1)S(1)}, u32[]{:S(2)}, u32[]{:S(2)}) collective-permute-start(bf16[272,128]{1,0:T(8,128)(2,1)S(1)} %get-tuple-element.25), channel_id=1, source_target_pairs={{0,8},{4,20},{8,0},{12,28},{16,24},{20,4},{24,16},{28,12},{1,9},{5... | collective-permute-start | bytes 208904 | tf_op jit(solution)/shard_map/ppermute | solution.py:77
  27.6 1.2 %collective-permute-done.5.refs_1_ = bf16[272,128]{1,0:T(8,128)(2,1)S(1)} collective-permute-done((bf16[272,128]{1,0:T(8,128)(2,1)S(1)}, bf16[272,128]{1,0:T(8,128)(2,1)S(1)}, u32[]{:S(2)}, u32[]{:S(2)}) %collective-permute-start.5) | collective-permute-done | bytes 69664 | tf_op jit(solution)/shard_map/ppermute | solution.py:72
  28.8 0.6 %own.1.refs_0_ = bf16[272,128]{1,0:T(8,128)(2,1)S(1)} custom-call(bf16[1664,128]{1,0:T(8,128)(2,1)S(1)} %get-tuple-element.18.dye_ref, bf16[512,640]{1,0:T(8,128)(2,1)S(1)} %get-tuple-element.19.toep_ref, bf16[4,16,128]{2,1,0:T(8,128)(2,1)S(1)} %get-tuple-element.22.taps_ref), custom_call_target="tpu_custom_call" | custom-call | tf_op jit(solution)/shard_map/own/pallas_call | solution.py:345
  29.5 0.6 %collective-permute-done.8.refs_3_ = bf16[272,128]{1,0:T(8,128)(2,1)S(1)} collective-permute-done((bf16[272,128]{1,0:T(8,128)(2,1)S(1)}, bf16[272,128]{1,0:T(8,128)(2,1)S(1)}, u32[]{:S(2)}, u32[]{:S(2)}) %collective-permute-start.8) | collective-permute-done | bytes 69664 | tf_op jit(solution)/shard_map/ppermute | solution.py:77
  30.1 0.7 %collective-permute-done.9.refs_4_ = bf16[272,128]{1,0:T(8,128)(2,1)S(1)} collective-permute-done((bf16[272,128]{1,0:T(8,128)(2,1)S(1)}, bf16[272,128]{1,0:T(8,128)(2,1)S(1)}, u32[]{:S(2)}, u32[]{:S(2)}) %collective-permute-start.9) | collective-permute-done | bytes 69664 | tf_op jit(solution)/shard_map/ppermute | solution.py:77
  30.8 0.8 %unpack.1 = (bf16[128,1024]{1,0:T(8,128)(2,1)}, f32[64,64]{1,0:T(8,128)}) custom-call(bf16[272,128]{1,0:T(8,128)(2,1)S(1)} %own.1.refs_0_, bf16[272,128]{1,0:T(8,128)(2,1)S(1)} %collective-permute-done.5.refs_1_, bf16[272,128]{1,0:T(8,128)(2,1)S(1)} %collective-permute-done.6.refs_2_, bf16[272,128]{1,0:T(8,128)(2,1)S(1)} %collective-permute-done.8.refs_3_, ...), custom_call_target="tpu_custom_call" | custom-call | tf_op jit(solution)/shard_map/unpack/pallas_call | solution.py:345
  (13 shorter events, 0.2 us)
Async XLA Ops:
  0.6 1.0 %copy-start = (bf16[32,4096]{1,0:T(8,128)(2,1)S(1)}, bf16[32,4096]{1,0:T(8,128)(2,1)}, u32[]{:S(2)}) copy-start(bf16[32,4096]{1,0:T(8,128)(2,1)} %in_ref.1) | copy-start | bytes 786436
  2.3 7.3 %copy-start.1 = (bf16[128,1024]{1,0:T(8,128)(2,1)S(1)}, bf16[128,1024]{1,0:T(8,128)(2,1)}, u32[]{:S(2)}) copy-start(bf16[128,1024]{1,0:T(8,128)(2,1)} %x_own_ref.1) | copy-start | bytes 786436
  2.3 7.6 %copy-start.2 = (bf16[64,64]{1,0:T(8,128)(2,1)S(1)}, bf16[64,64]{1,0:T(8,128)(2,1)}, u32[]{:S(2)}) copy-start(bf16[64,64]{1,0:T(8,128)(2,1)} %f_own_ref.1) | copy-start | bytes 24580
  2.3 17.6 %all-to-all-start = ((bf16[32,32,128]{2,1,0:T(8,128)(2,1)}), bf16[32,32,128]{2,1,0:T(8,128)(2,1)S(1)}, u32[]{:S(2)}, u32[]{:S(2)}) async-start(bf16[32,32,128]{2,1,0:T(8,128)(2,1)} %fan_grads.1), calls=%async_computation | async-start | bytes 524288 | tf_op jit(solution)/shard_map/all_to_all | solution.py:378
  9.6 1.6 %collective-permute-start = (bf16[128,1024]{1,0:T(8,128)(2,1)S(1)}, bf16[128,1024]{1,0:T(8,128)(2,1)S(1)}, u32[]{:S(2)}, u32[]{:S(2)}) collective-permute-start(bf16[128,1024]{1,0:T(8,128)(2,1)S(1)} %copy-done.1), channel_id=1, source_target_pairs={{0,4},{4,0},{8,12},{12,8},{16,20},{20,16},{24,28},{28,24},{1,5},{5... | collective-permute-start | bytes 786440 | tf_op jit(solution)/shard_map/ppermute | solution.py:72
  10.0 1.3 %collective-permute-start.1 = (bf16[64,64]{1,0:T(8,128)(2,1)S(1)}, bf16[64,64]{1,0:T(8,128)(2,1)S(1)}, u32[]{:S(2)}, u32[]{:S(2)}) collective-permute-start(bf16[64,64]{1,0:T(8,128)(2,1)S(1)} %copy-done.2), channel_id=1, source_target_pairs={{0,4},{4,0},{8,12},{12,8},{16,20},{20,16},{24,28},{28,24},{1,5},{5... | collective-permute-start | bytes 24584 | tf_op jit(solution)/shard_map/ppermute | solution.py:72
  11.4 6.4 %collective-permute-start.2 = (bf16[272,128]{1,0:T(8,128)(2,1)S(1)}, bf16[272,128]{1,0:T(8,128)(2,1)S(1)}, u32[]{:S(2)}, u32[]{:S(2)}) collective-permute-start(bf16[272,128]{1,0:T(8,128)(2,1)S(1)} %get-tuple-element.15), channel_id=1, source_target_pairs={{0,24},{4,28},{8,16},{12,20},{16,8},{20,12},{24,0},{28,4},{1,25},{... | collective-permute-start | bytes 208904 | tf_op jit(solution)/shard_map/ppermute | solution.py:72
  14.1 5.4 %collective-permute-start.3 = (bf16[272,128]{1,0:T(8,128)(2,1)S(1)}, bf16[272,128]{1,0:T(8,128)(2,1)S(1)}, u32[]{:S(2)}, u32[]{:S(2)}) collective-permute-start(bf16[272,128]{1,0:T(8,128)(2,1)S(1)} %get-tuple-element.16), channel_id=1, source_target_pairs={{0,16},{4,20},{8,24},{12,28},{16,0},{20,4},{24,8},{28,12},{1,17},{... | collective-permute-start | bytes 208904 | tf_op jit(solution)/shard_map/ppermute | solution.py:72
  14.7 4.8 %collective-permute-start.4 = (bf16[272,128]{1,0:T(8,128)(2,1)S(1)}, bf16[272,128]{1,0:T(8,128)(2,1)S(1)}, u32[]{:S(2)}, u32[]{:S(2)}) collective-permute-start(bf16[272,128]{1,0:T(8,128)(2,1)S(1)} %get-tuple-element.17), channel_id=1, source_target_pairs={{0,8},{4,12},{8,0},{12,4},{16,24},{20,28},{24,16},{28,20},{1,9},{5... | collective-permute-start | bytes 208904 | tf_op jit(solution)/shard_map/ppermute | solution.py:72
  23.0 1.9 %collective-permute-start.7 = (bf16[272,128]{1,0:T(8,128)(2,1)S(1)}, bf16[272,128]{1,0:T(8,128)(2,1)S(1)}, u32[]{:S(2)}, u32[]{:S(2)}) collective-permute-start(bf16[272,128]{1,0:T(8,128)(2,1)S(1)} %near_swap.1), channel_id=1, source_target_pairs={{0,4},{4,0},{8,12},{12,8},{16,20},{20,16},{24,28},{28,24},{1,5},{5... | collective-permute-start | bytes 208904 | tf_op jit(solution)/shard_map/ppermute | solution.py:72
  23.4 5.4 %collective-permute-start.5 = (bf16[272,128]{1,0:T(8,128)(2,1)S(1)}, bf16[272,128]{1,0:T(8,128)(2,1)S(1)}, u32[]{:S(2)}, u32[]{:S(2)}) collective-permute-start(bf16[272,128]{1,0:T(8,128)(2,1)S(1)} %get-tuple-element.20), channel_id=1, source_target_pairs={{0,24},{4,28},{8,16},{12,20},{16,8},{20,12},{24,0},{28,4},{1,25},{... | collective-permute-start | bytes 208904 | tf_op jit(solution)/shard_map/ppermute | solution.py:72
  24.9 5.1 %collective-permute-start.8 = (bf16[272,128]{1,0:T(8,128)(2,1)S(1)}, bf16[272,128]{1,0:T(8,128)(2,1)S(1)}, u32[]{:S(2)}, u32[]{:S(2)}) collective-permute-start(bf16[272,128]{1,0:T(8,128)(2,1)S(1)} %get-tuple-element.24), channel_id=1, source_target_pairs={{0,16},{4,12},{8,24},{12,4},{16,0},{20,28},{24,8},{28,20},{1,17},{... | collective-permute-start | bytes 208904 | tf_op jit(solution)/shard_map/ppermute | solution.py:77
  26.4 4.3 %collective-permute-start.9 = (bf16[272,128]{1,0:T(8,128)(2,1)S(1)}, bf16[272,128]{1,0:T(8,128)(2,1)S(1)}, u32[]{:S(2)}, u32[]{:S(2)}) collective-permute-start(bf16[272,128]{1,0:T(8,128)(2,1)S(1)} %get-tuple-element.25), channel_id=1, source_target_pairs={{0,8},{4,20},{8,0},{12,28},{16,24},{20,4},{24,16},{28,12},{1,9},{5... | collective-permute-start | bytes 208904 | tf_op jit(solution)/shard_map/ppermute | solution.py:77
  29.4 1.4 %collective-permute-start.6 = (bf16[272,128]{1,0:T(8,128)(2,1)S(1)}, bf16[272,128]{1,0:T(8,128)(2,1)S(1)}, u32[]{:S(2)}, u32[]{:S(2)}) collective-permute-start(bf16[272,128]{1,0:T(8,128)(2,1)S(1)} %swap.1), channel_id=1, source_target_pairs={{0,4},{4,0},{8,12},{12,8},{16,20},{20,16},{24,28},{28,24},{1,5},{5... | collective-permute-start | bytes 208904 | tf_op jit(solution)/shard_map/ppermute | solution.py:72

commit v10 on v9

--- a/solution.py
+++ b/solution.py
@@ -142,15 +142,21 @@
         filt_ref[chip ^ bits] = jnp.where(low, first, pltpu.roll(second, taps_here, 1))
 
 
-def toeplitz_rows(filt_ref, toep_ref):
+def toeplitz_rows(filt_ref, toep_ref, rest_ref):
     chips, groups, _ = filt_ref.shape
-    reach = toep_ref.shape[1]
+    taps = chips * LANES
     tiles = [filt_ref[tile] for tile in range(chips)]
     filt = jnp.concatenate(tiles + [jnp.zeros((groups, LANES), jnp.float32)], axis=1)
+    low = lax.broadcasted_iota(jnp.int32, (SLAB, LANES), 1) < SLAB
+    outside = []
     for group in range(groups):
-        rows = jnp.broadcast_to(filt[group : group + 1], (SLAB, reach))
+        rows = jnp.broadcast_to(filt[group : group + 1], (SLAB, taps + LANES))
         rows = pltpu.roll(rows, 0, 1, stride=1, stride_axis=0)
-        toep_ref[group * SLAB : (group + 1) * SLAB] = rows.astype(jnp.bfloat16)
+        toep_ref[group * SLAB : (group + 1) * SLAB] = rows[:, :taps].astype(jnp.bfloat16)
+        outside.append(rows[:, taps:])
+    for pair in range(groups // 2):
+        both = jnp.where(low, outside[2 * pair], pltpu.roll(outside[2 * pair + 1], SLAB, 1))
+        rest_ref[:, pair * LANES : (pair + 1) * LANES] = both.astype(jnp.bfloat16)
 
 
 def group_of_lane(rows, width, groups):
@@ -158,36 +164,44 @@
     return (lane % LANES) // (LANES // groups)
 
 
-def filtered(dye_ref, start, toeplitz, groups):
-    reach = toeplitz.shape[1]
-    window = jnp.concatenate(
-        [
-            dye_ref[pl.ds(pl.multiple_of(start, SLAB), reach)],
-            dye_ref[pl.ds(pl.multiple_of(start + SLAB, SLAB), reach)],
-        ],
-        axis=1,
-    )
-    full = jnp.dot(toeplitz, window, preferred_element_type=jnp.float32)
+def filtered(dye_ref, start, toep_ref, rest_ref):
+    groups = toep_ref.shape[0] // SLAB
+    taps = toep_ref.shape[1]
+
+    def window(at, size):
+        return jnp.concatenate(
+            [
+                dye_ref[pl.ds(pl.multiple_of(start + at, SLAB), size)],
+                dye_ref[pl.ds(pl.multiple_of(start + at + SLAB, SLAB), size)],
+            ],
+            axis=1,
+        )
+
     group2 = group_of_lane(SLAB, 2 * LANES, groups)
+    after = window(taps, SLAB)
+    after = [jnp.where(group2 == group, after, jnp.zeros_like(after)) for group in range(groups)]
+    full = jnp.dot(toep_ref[...], window(0, taps), preferred_element_type=jnp.float32)
+    rest = jnp.dot(
+        rest_ref[...], jnp.concatenate(after, axis=0), preferred_element_type=jnp.float32
+    )
     total = full[:SLAB]
     for group in range(1, groups):
         total = jnp.where(group2 == group, full[group * SLAB : (group + 1) * SLAB], total)
+    total = total + rest
     return jnp.concatenate([total[:, :LANES], total[:, LANES:]], axis=0).astype(jnp.bfloat16)
 
 
-def tokens_of(seq, dye_ref, toep_ref, out_ref, at, block_len):
-    toeplitz = toep_ref[...]
-    groups = toeplitz.shape[0] // SLAB
+def tokens_of(seq, dye_ref, toep_ref, rest_ref, out_ref, at, block_len):
     for row in range(0, block_len, 2 * SLAB):
         out_ref[at + row : at + row + 2 * SLAB] = filtered(
-            dye_ref, seq * block_len + row, toeplitz, groups
+            dye_ref, seq * block_len + row, toep_ref, rest_ref
         )
 
 
 def first_kernel(n_seq, taps_here, far, dy_ref, *refs):
     chips = n_seq // 2
     in_refs = refs[:chips]
-    dye_ref, taps_ref, toep_ref, out_ref, x_ref, filt_ref, lag_ref = refs[chips:]
+    dye_ref, taps_ref, toep_ref, rest_ref, far_ref, x_ref, filt_ref, lag_ref = refs[chips:]
     tokens = dy_ref.shape[0]
     groups = EXTRA // 2
     taps = n_seq * taps_here
@@ -218,11 +232,16 @@
         else:
             lag_ref[:rows] += part
         if at == 0:
-            toeplitz_rows(filt_ref, toep_ref)
-
+            toeplitz_rows(filt_ref, toep_ref, rest_ref)
+
+    block_len = tokens // n_seq
+    blocks = [(2 * (chip ^ far) + (core ^ flip), flip * block_len) for flip in range(2)]
     lags = lag_ref[...].T
     eights = []
     for group in range(groups):
+        if group % 2 == 0 and blocks:
+            seq, at = blocks.pop(0)
+            tokens_of(seq, dye_ref, toep_ref, rest_ref, far_ref, at, block_len)
         at = group * STEP
         rows = lags[at : at + 8]
         for high in range(1, STEP // 8):
@@ -246,11 +265,7 @@
         other = jnp.where(core == 0, odd, even)
         taps_ref[to_chip] = jnp.concatenate([mine, other], axis=0).astype(jnp.bfloat16)
 
-    block_len = (out_ref.shape[0] - EXTRA) // 2
-    for flip in range(2):
-        seq = 2 * (chip ^ far) + (core ^ flip)
-        tokens_of(seq, dye_ref, toep_ref, out_ref, flip * block_len, block_len)
-    out_ref[2 * block_len :] = taps_ref[chip ^ far]
+    far_ref[2 * block_len :] = taps_ref[chip ^ far]
 
 
 def half_of(taps, flip):
@@ -262,12 +277,12 @@
     return jnp.concatenate(rows, axis=0).astype(jnp.bfloat16)
 
 
-def near_kernel(masks, flip, dye_ref, toep_ref, taps_ref, out_ref):
+def near_kernel(masks, flip, dye_ref, toep_ref, rest_ref, taps_ref, out_ref):
     chip, core, _ = place()
     block_len = (out_ref.shape[0] - len(masks) * EXTRA // 2) // len(masks)
     for index, bits in enumerate(masks):
         seq = 2 * (chip ^ bits) + (core ^ flip)
-        tokens_of(seq, dye_ref, toep_ref, out_ref, index * block_len, block_len)
+        tokens_of(seq, dye_ref, toep_ref, rest_ref, out_ref, index * block_len, block_len)
     out_ref[len(masks) * block_len :] = stacked(
         [half_of(taps_ref[chip ^ bits], flip) for bits in masks]
     )
@@ -293,12 +308,12 @@
         out_ref[2 * block_len :] = jnp.where(core == 0, taps[index], taps[other])
 
 
-def own_kernel(dye_ref, toep_ref, taps_ref, out_ref):
+def own_kernel(dye_ref, toep_ref, rest_ref, taps_ref, out_ref):
     chip, core, _ = place()
     block_len = (out_ref.shape[0] - EXTRA) // 2
     for flip in range(2):
         seq = 2 * chip + (core ^ flip)
-        tokens_of(seq, dye_ref, toep_ref, out_ref, flip * block_len, block_len)
+        tokens_of(seq, dye_ref, toep_ref, rest_ref, out_ref, flip * block_len, block_len)
     out_ref[2 * block_len :] = taps_ref[chip]
 
 
@@ -383,12 +398,15 @@
         "fan_inputs",
         [pltpu.VMEM((2, groups_here, LANES), jnp.float32)],
     )
-    dye, tap_parts, toeplitz, far = local_call(
+    near = masks[2:]
+    near_shape = half(len(near) * (block_len + EXTRA // 2), LANES)
+    dye, tap_parts, toeplitz, outside, far = local_call(
         functools.partial(first_kernel, n_seq, taps_here, masks[1]),
         [
             half(tokens + taps + LANES, LANES),
             half(chips, EXTRA, LANES),
-            half(groups * SLAB, taps + LANES),
+            half(groups * SLAB, taps),
+            half(SLAB, groups * SLAB),
             unit,
         ],
         (dy.reshape(tokens, LANES), *fan_out(pieces, "seq", 2)),
@@ -400,19 +418,17 @@
         ],
     )
     far = xor_permute(far, "seq", 2 * masks[1])
-    near = masks[2:]
-    near_shape = half(len(near) * (block_len + EXTRA // 2), LANES)
     (send,) = local_call(
         functools.partial(near_kernel, near, 1),
         [near_shape],
-        (dye, toeplitz, tap_parts),
+        (dye, toeplitz, outside, tap_parts),
         "near_swap",
     )
     got = xor_permute(send, "seq", 1)
     (keep,) = local_call(
         functools.partial(near_kernel, near, 0),
         [near_shape],
-        (dye, toeplitz, tap_parts),
+        (dye, toeplitz, outside, tap_parts),
         "near_keep",
     )
     pieces = local_call(near_pieces_kernel, [unit] * len(near), (keep, got), "near_pieces")
@@ -421,7 +437,7 @@
         for index, piece in enumerate(pieces)
     ]
     far, tap_parts = lax.optimization_barrier((far, tap_parts))
-    (own,) = local_call(own_kernel, [unit], (dye, toeplitz, tap_parts), "own")
+    (own,) = local_call(own_kernel, [unit], (dye, toeplitz, outside, tap_parts), "own")
     (send,) = local_call(
         swap_kernel, [half(2 * block_len + EXTRA, LANES)], (own, far), "swap"
     )

time: 31.8 us -> 31.7 us (level)
  no operation moved by 1% of the time
where the time goes in v10:
time: 31.7 us; the launch traced here: 31.4 us
  starting transfers between devices  15.4 us (49%)
  waiting for transfers between devices  8.6 us (27%)
  Pallas kernels  5.72 us (18%)
  local copies, waits for them, and re-layouts  0.95 us (3%)
  between operations  0.73 us (2%)
    all_to_all x1, starting transfers between devices, by_channels(): lax.all_to_all(dy, ('seq', 'chan'), split_axis=0, concat_axis=0, tiled=True)  7.3 us
    ppermute x8, waiting for transfers between devices, xor_permute(): return lax.ppermute(value, axis, pairs)  6.98 us
    pallas_call x9, Pallas kernels, local_call(): pl.pallas_call(kernel, out_shape=out_shape, in_specs=[whole] * len(operan...  5.72 us
    ppermute x8, starting transfers between devices, xor_permute(): return lax.ppermute(value, axis, pairs)  5.48 us
    ppermute x2, starting transfers between devices, turned_permute(): return lax.ppermute(value, axis, pairs)  2.66 us
    ppermute x2, waiting for transfers between devices, turned_permute(): return lax.ppermute(value, axis, pairs)  1.22 us
    unnamed x6, local copies, waits for them, and re-layouts  0.95 us
  transfers between devices with their start and end apart: 11, of which 7 were waited for; matrix products, arithmetic and copies ran while one was open for 0% of the time, Pallas kernels for 4%

profile of v10, /device:TPU:0, one launch (start us, length us, event | category | flops | bytes accessed | tf_op | source)
XLA Modules:
  0.0 31.4 jit_solution(18090498749401534356)
XLA Ops:
  0.6 0.9 %copy-done = bf16[32,4096]{1,0:T(8,128)(2,1)S(1)} copy-done((bf16[32,4096]{1,0:T(8,128)(2,1)S(1)}, bf16[32,4096]{1,0:T(8,128)(2,1)}, u32[]{:S(2)}) %copy-start) | copy-done | bytes 262168
  1.6 0.7 %fan_grads.1 = bf16[32,32,128]{2,1,0:T(8,128)(2,1)} custom-call(bf16[32,4096]{1,0:T(8,128)(2,1)S(1)} %copy-done), custom_call_target="tpu_custom_call" | custom-call | tf_op jit(solution)/shard_map/fan_grads/pallas_call | solution.py:360
  2.3 7.3 %all-to-all-start = ((bf16[32,32,128]{2,1,0:T(8,128)(2,1)}), bf16[32,32,128]{2,1,0:T(8,128)(2,1)S(1)}, u32[]{:S(2)}, u32[]{:S(2)}) async-start(bf16[32,32,128]{2,1,0:T(8,128)(2,1)} %fan_grads.1), calls=%async_computation | async-start | bytes 524288 | tf_op jit(solution)/shard_map/all_to_all | solution.py:393
  9.6 0.3 %collective-permute-start = (bf16[128,1024]{1,0:T(8,128)(2,1)S(1)}, bf16[128,1024]{1,0:T(8,128)(2,1)S(1)}, u32[]{:S(2)}, u32[]{:S(2)}) collective-permute-start(bf16[128,1024]{1,0:T(8,128)(2,1)S(1)} %copy-done.1), channel_id=1, source_target_pairs={{0,4},{4,0},{8,12},{12,8},{16,20},{20,16},{24,28},{28,24},{1,5},{5... | collective-permute-start | bytes 786440 | tf_op jit(solution)/shard_map/ppermute | solution.py:72
  10.0 0.3 collective-permute-start.1
  10.2 1.0 %collective-permute-done.1.f_other_ref = bf16[64,64]{1,0:T(8,128)(2,1)S(1)} collective-permute-done((bf16[64,64]{1,0:T(8,128)(2,1)S(1)}, bf16[64,64]{1,0:T(8,128)(2,1)S(1)}, u32[]{:S(2)}, u32[]{:S(2)}) %collective-permute-start.1) | collective-permute-done | bytes 8224 | tf_op jit(solution)/shard_map/ppermute | solution.py:72
  11.4 2.7 %collective-permute-start.2 = (bf16[272,128]{1,0:T(8,128)(2,1)S(1)}, bf16[272,128]{1,0:T(8,128)(2,1)S(1)}, u32[]{:S(2)}, u32[]{:S(2)}) collective-permute-start(bf16[272,128]{1,0:T(8,128)(2,1)S(1)} %get-tuple-element.16), channel_id=1, source_target_pairs={{0,24},{4,28},{8,16},{12,20},{16,8},{20,12},{24,0},{28,4},{1,25},{... | collective-permute-start | bytes 208904 | tf_op jit(solution)/shard_map/ppermute | solution.py:72
  14.1 0.6 %collective-permute-start.3 = (bf16[272,128]{1,0:T(8,128)(2,1)S(1)}, bf16[272,128]{1,0:T(8,128)(2,1)S(1)}, u32[]{:S(2)}, u32[]{:S(2)}) collective-permute-start(bf16[272,128]{1,0:T(8,128)(2,1)S(1)} %get-tuple-element.17), channel_id=1, source_target_pairs={{0,16},{4,20},{8,24},{12,28},{16,0},{20,4},{24,8},{28,12},{1,17},{... | collective-permute-start | bytes 208904 | tf_op jit(solution)/shard_map/ppermute | solution.py:72
  14.7 0.3 collective-permute-start.4
  14.9 2.8 %collective-permute-done.2.refs_1_ = bf16[272,128]{1,0:T(8,128)(2,1)S(1)} collective-permute-done((bf16[272,128]{1,0:T(8,128)(2,1)S(1)}, bf16[272,128]{1,0:T(8,128)(2,1)S(1)}, u32[]{:S(2)}, u32[]{:S(2)}) %collective-permute-start.2) | collective-permute-done | bytes 69664 | tf_op jit(solution)/shard_map/ppermute | solution.py:72
  17.8 1.7 %collective-permute-done.3.refs_2_ = bf16[272,128]{1,0:T(8,128)(2,1)S(1)} collective-permute-done((bf16[272,128]{1,0:T(8,128)(2,1)S(1)}, bf16[272,128]{1,0:T(8,128)(2,1)S(1)}, u32[]{:S(2)}, u32[]{:S(2)}) %collective-permute-start.3) | collective-permute-done | bytes 69664 | tf_op jit(solution)/shard_map/ppermute | solution.py:72
  19.5 0.4 %all-to-all-done = bf16[32,32,128]{2,1,0:T(8,128)(2,1)S(1)} async-done(((bf16[32,32,128]{2,1,0:T(8,128)(2,1)}), bf16[32,32,128]{2,1,0:T(8,128)(2,1)S(1)}, u32[]{:S(2)}, u32[]{:S(2)}) %all-to-all-start) | async-done | bytes 262176 | tf_op jit(solution)/shard_map/all_to_all | solution.py:393
  19.9 2.5 %first.1 = (bf16[1664,128]{1,0:T(8,128)(2,1)S(1)}, bf16[4,16,128]{2,1,0:T(8,128)(2,1)S(1)}, bf16[512,512]{1,0:T(8,128)(2,1)S(1)}, bf16[64,512]{1,0:T(8,128)(2,1)S(1)}, bf16[272,128]{1,0:T(8,128)(2,1)S(1)}) custom-call(bf16[1024,128]{1,0:T(8,128)(2,1)S(1)} %bitcast.1, bf16[272,128]{1,0:T(8,128)(2,1)S(1)} %get-tuple-element.15.refs_0_, ...), custom_call_target="tpu_custom_call" | custom-call | tf_op jit(solution)/shard_map/first/pallas_call | solution.py:360
  22.4 0.5 %near_swap.1 = bf16[272,128]{1,0:T(8,128)(2,1)S(1)} custom-call(bf16[1664,128]{1,0:T(8,128)(2,1)S(1)} %get-tuple-element.19.dye_ref, bf16[512,512]{1,0:T(8,128)(2,1)S(1)} %get-tuple-element.20.toep_ref, bf16[64,512]{1,0:T(8,128)(2,1)S(1)} %get-tuple-element.21.rest_ref, bf16[4,16,128]{2,1,0:T(8,128)(2,1)S(1)} %get-tuple-element.24.taps_ref), custom_call_target="tpu_custom_call" | custom-call | tf_op jit(solution)/shard_map/near_swap/pallas_call | solution.py:360
  22.9 0.4 %collective-permute-start.7 = (bf16[272,128]{1,0:T(8,128)(2,1)S(1)}, bf16[272,128]{1,0:T(8,128)(2,1)S(1)}, u32[]{:S(2)}, u32[]{:S(2)}) collective-permute-start(bf16[272,128]{1,0:T(8,128)(2,1)S(1)} %near_swap.1), channel_id=1, source_target_pairs={{0,4},{4,0},{8,12},{12,8},{16,20},{20,16},{24,28},{28,24},{1,5},{5... | collective-permute-start | bytes 208904 | tf_op jit(solution)/shard_map/ppermute | solution.py:72
  23.3 0.9 %collective-permute-start.5 = (bf16[272,128]{1,0:T(8,128)(2,1)S(1)}, bf16[272,128]{1,0:T(8,128)(2,1)S(1)}, u32[]{:S(2)}, u32[]{:S(2)}) collective-permute-start(bf16[272,128]{1,0:T(8,128)(2,1)S(1)} %get-tuple-element.22), channel_id=1, source_target_pairs={{0,24},{4,28},{8,16},{12,20},{16,8},{20,12},{24,0},{28,4},{1,25},{... | collective-permute-start | bytes 208904 | tf_op jit(solution)/shard_map/ppermute | solution.py:72
  24.2 0.5 %near_keep.1.keep_ref = bf16[272,128]{1,0:T(8,128)(2,1)S(1)} custom-call(bf16[1664,128]{1,0:T(8,128)(2,1)S(1)} %get-tuple-element.19.dye_ref, bf16[512,512]{1,0:T(8,128)(2,1)S(1)} %get-tuple-element.20.toep_ref, bf16[64,512]{1,0:T(8,128)(2,1)S(1)} %get-tuple-element.21.rest_ref, bf16[4,16,128]{2,1,0:T(8,128)(2,1)S(1)} %get-tuple-element.24.taps_ref), custom_call_target="tpu_custom_call" | custom-call | tf_op jit(solution)/shard_map/near_keep/pallas_call | solution.py:360
  24.8 1.5 %collective-permute-start.8 = (bf16[272,128]{1,0:T(8,128)(2,1)S(1)}, bf16[272,128]{1,0:T(8,128)(2,1)S(1)}, u32[]{:S(2)}, u32[]{:S(2)}) collective-permute-start(bf16[272,128]{1,0:T(8,128)(2,1)S(1)} %get-tuple-element.26), channel_id=1, source_target_pairs={{0,16},{4,12},{8,24},{12,4},{16,0},{20,28},{24,8},{28,20},{1,17},{... | collective-permute-start | bytes 208904 | tf_op jit(solution)/shard_map/ppermute | solution.py:77
  26.3 1.1 %collective-permute-start.9 = (bf16[272,128]{1,0:T(8,128)(2,1)S(1)}, bf16[272,128]{1,0:T(8,128)(2,1)S(1)}, u32[]{:S(2)}, u32[]{:S(2)}) collective-permute-start(bf16[272,128]{1,0:T(8,128)(2,1)S(1)} %get-tuple-element.27), channel_id=1, source_target_pairs={{0,8},{4,20},{8,0},{12,28},{16,24},{20,4},{24,16},{28,12},{1,9},{5... | collective-permute-start | bytes 208904 | tf_op jit(solution)/shard_map/ppermute | solution.py:77
  27.4 1.3 %collective-permute-done.5.refs_1_ = bf16[272,128]{1,0:T(8,128)(2,1)S(1)} collective-permute-done((bf16[272,128]{1,0:T(8,128)(2,1)S(1)}, bf16[272,128]{1,0:T(8,128)(2,1)S(1)}, u32[]{:S(2)}, u32[]{:S(2)}) %collective-permute-start.5) | collective-permute-done | bytes 69664 | tf_op jit(solution)/shard_map/ppermute | solution.py:72
  28.8 0.5 %own.1.refs_0_ = bf16[272,128]{1,0:T(8,128)(2,1)S(1)} custom-call(bf16[1664,128]{1,0:T(8,128)(2,1)S(1)} %get-tuple-element.19.dye_ref, bf16[512,512]{1,0:T(8,128)(2,1)S(1)} %get-tuple-element.20.toep_ref, bf16[64,512]{1,0:T(8,128)(2,1)S(1)} %get-tuple-element.21.rest_ref, bf16[4,16,128]{2,1,0:T(8,128)(2,1)S(1)} %get-tuple-element.24.taps_ref), custom_call_target="tpu_custom_call" | custom-call | tf_op jit(solution)/shard_map/own/pallas_call | solution.py:360
  29.4 0.6 %collective-permute-done.8.refs_3_ = bf16[272,128]{1,0:T(8,128)(2,1)S(1)} collective-permute-done((bf16[272,128]{1,0:T(8,128)(2,1)S(1)}, bf16[272,128]{1,0:T(8,128)(2,1)S(1)}, u32[]{:S(2)}, u32[]{:S(2)}) %collective-permute-start.8) | collective-permute-done | bytes 69664 | tf_op jit(solution)/shard_map/ppermute | solution.py:77
  30.0 0.6 %collective-permute-done.9.refs_4_ = bf16[272,128]{1,0:T(8,128)(2,1)S(1)} collective-permute-done((bf16[272,128]{1,0:T(8,128)(2,1)S(1)}, bf16[272,128]{1,0:T(8,128)(2,1)S(1)}, u32[]{:S(2)}, u32[]{:S(2)}) %collective-permute-start.9) | collective-permute-done | bytes 69664 | tf_op jit(solution)/shard_map/ppermute | solution.py:77
  30.7 0.8 %unpack.1 = (bf16[128,1024]{1,0:T(8,128)(2,1)}, f32[64,64]{1,0:T(8,128)}) custom-call(bf16[272,128]{1,0:T(8,128)(2,1)S(1)} %own.1.refs_0_, bf16[272,128]{1,0:T(8,128)(2,1)S(1)} %collective-permute-done.5.refs_1_, bf16[272,128]{1,0:T(8,128)(2,1)S(1)} %collective-permute-done.6.refs_2_, bf16[272,128]{1,0:T(8,128)(2,1)S(1)} %collective-permute-done.8.refs_3_, ...), custom_call_target="tpu_custom_call" | custom-call | tf_op jit(solution)/shard_map/unpack/pallas_call | solution.py:360
  (13 shorter events, 0.3 us)
Async XLA Ops:
  0.6 1.0 %copy-start = (bf16[32,4096]{1,0:T(8,128)(2,1)S(1)}, bf16[32,4096]{1,0:T(8,128)(2,1)}, u32[]{:S(2)}) copy-start(bf16[32,4096]{1,0:T(8,128)(2,1)} %in_ref.1) | copy-start | bytes 786436
  2.3 7.3 %copy-start.1 = (bf16[128,1024]{1,0:T(8,128)(2,1)S(1)}, bf16[128,1024]{1,0:T(8,128)(2,1)}, u32[]{:S(2)}) copy-start(bf16[128,1024]{1,0:T(8,128)(2,1)} %x_own_ref.1) | copy-start | bytes 786436
  2.3 7.6 %copy-start.2 = (bf16[64,64]{1,0:T(8,128)(2,1)S(1)}, bf16[64,64]{1,0:T(8,128)(2,1)}, u32[]{:S(2)}) copy-start(bf16[64,64]{1,0:T(8,128)(2,1)} %f_own_ref.1) | copy-start | bytes 24580
  2.3 17.6 %all-to-all-start = ((bf16[32,32,128]{2,1,0:T(8,128)(2,1)}), bf16[32,32,128]{2,1,0:T(8,128)(2,1)S(1)}, u32[]{:S(2)}, u32[]{:S(2)}) async-start(bf16[32,32,128]{2,1,0:T(8,128)(2,1)} %fan_grads.1), calls=%async_computation | async-start | bytes 524288 | tf_op jit(solution)/shard_map/all_to_all | solution.py:393
  9.6 1.6 %collective-permute-start = (bf16[128,1024]{1,0:T(8,128)(2,1)S(1)}, bf16[128,1024]{1,0:T(8,128)(2,1)S(1)}, u32[]{:S(2)}, u32[]{:S(2)}) collective-permute-start(bf16[128,1024]{1,0:T(8,128)(2,1)S(1)} %copy-done.1), channel_id=1, source_target_pairs={{0,4},{4,0},{8,12},{12,8},{16,20},{20,16},{24,28},{28,24},{1,5},{5... | collective-permute-start | bytes 786440 | tf_op jit(solution)/shard_map/ppermute | solution.py:72
  10.0 1.3 %collective-permute-start.1 = (bf16[64,64]{1,0:T(8,128)(2,1)S(1)}, bf16[64,64]{1,0:T(8,128)(2,1)S(1)}, u32[]{:S(2)}, u32[]{:S(2)}) collective-permute-start(bf16[64,64]{1,0:T(8,128)(2,1)S(1)} %copy-done.2), channel_id=1, source_target_pairs={{0,4},{4,0},{8,12},{12,8},{16,20},{20,16},{24,28},{28,24},{1,5},{5... | collective-permute-start | bytes 24584 | tf_op jit(solution)/shard_map/ppermute | solution.py:72
  11.4 6.4 %collective-permute-start.2 = (bf16[272,128]{1,0:T(8,128)(2,1)S(1)}, bf16[272,128]{1,0:T(8,128)(2,1)S(1)}, u32[]{:S(2)}, u32[]{:S(2)}) collective-permute-start(bf16[272,128]{1,0:T(8,128)(2,1)S(1)} %get-tuple-element.16), channel_id=1, source_target_pairs={{0,24},{4,28},{8,16},{12,20},{16,8},{20,12},{24,0},{28,4},{1,25},{... | collective-permute-start | bytes 208904 | tf_op jit(solution)/shard_map/ppermute | solution.py:72
  14.1 5.4 %collective-permute-start.3 = (bf16[272,128]{1,0:T(8,128)(2,1)S(1)}, bf16[272,128]{1,0:T(8,128)(2,1)S(1)}, u32[]{:S(2)}, u32[]{:S(2)}) collective-permute-start(bf16[272,128]{1,0:T(8,128)(2,1)S(1)} %get-tuple-element.17), channel_id=1, source_target_pairs={{0,16},{4,20},{8,24},{12,28},{16,0},{20,4},{24,8},{28,12},{1,17},{... | collective-permute-start | bytes 208904 | tf_op jit(solution)/shard_map/ppermute | solution.py:72
  14.7 4.8 %collective-permute-start.4 = (bf16[272,128]{1,0:T(8,128)(2,1)S(1)}, bf16[272,128]{1,0:T(8,128)(2,1)S(1)}, u32[]{:S(2)}, u32[]{:S(2)}) collective-permute-start(bf16[272,128]{1,0:T(8,128)(2,1)S(1)} %get-tuple-element.18), channel_id=1, source_target_pairs={{0,8},{4,12},{8,0},{12,4},{16,24},{20,28},{24,16},{28,20},{1,9},{5... | collective-permute-start | bytes 208904 | tf_op jit(solution)/shard_map/ppermute | solution.py:72
  22.9 1.8 %collective-permute-start.7 = (bf16[272,128]{1,0:T(8,128)(2,1)S(1)}, bf16[272,128]{1,0:T(8,128)(2,1)S(1)}, u32[]{:S(2)}, u32[]{:S(2)}) collective-permute-start(bf16[272,128]{1,0:T(8,128)(2,1)S(1)} %near_swap.1), channel_id=1, source_target_pairs={{0,4},{4,0},{8,12},{12,8},{16,20},{20,16},{24,28},{28,24},{1,5},{5... | collective-permute-start | bytes 208904 | tf_op jit(solution)/shard_map/ppermute | solution.py:72
  23.3 5.5 %collective-permute-start.5 = (bf16[272,128]{1,0:T(8,128)(2,1)S(1)}, bf16[272,128]{1,0:T(8,128)(2,1)S(1)}, u32[]{:S(2)}, u32[]{:S(2)}) collective-permute-start(bf16[272,128]{1,0:T(8,128)(2,1)S(1)} %get-tuple-element.22), channel_id=1, source_target_pairs={{0,24},{4,28},{8,16},{12,20},{16,8},{20,12},{24,0},{28,4},{1,25},{... | collective-permute-start | bytes 208904 | tf_op jit(solution)/shard_map/ppermute | solution.py:72
  24.8 5.2 %collective-permute-start.8 = (bf16[272,128]{1,0:T(8,128)(2,1)S(1)}, bf16[272,128]{1,0:T(8,128)(2,1)S(1)}, u32[]{:S(2)}, u32[]{:S(2)}) collective-permute-start(bf16[272,128]{1,0:T(8,128)(2,1)S(1)} %get-tuple-element.26), channel_id=1, source_target_pairs={{0,16},{4,12},{8,24},{12,4},{16,0},{20,28},{24,8},{28,20},{1,17},{... | collective-permute-start | bytes 208904 | tf_op jit(solution)/shard_map/ppermute | solution.py:77
  26.3 4.3 %collective-permute-start.9 = (bf16[272,128]{1,0:T(8,128)(2,1)S(1)}, bf16[272,128]{1,0:T(8,128)(2,1)S(1)}, u32[]{:S(2)}, u32[]{:S(2)}) collective-permute-start(bf16[272,128]{1,0:T(8,128)(2,1)S(1)} %get-tuple-element.27), channel_id=1, source_target_pairs={{0,8},{4,20},{8,0},{12,28},{16,24},{20,4},{24,16},{28,12},{1,9},{5... | collective-permute-start | bytes 208904 | tf_op jit(solution)/shard_map/ppermute | solution.py:77
  29.3 1.3 %collective-permute-start.6 = (bf16[272,128]{1,0:T(8,128)(2,1)S(1)}, bf16[272,128]{1,0:T(8,128)(2,1)S(1)}, u32[]{:S(2)}, u32[]{:S(2)}) collective-permute-start(bf16[272,128]{1,0:T(8,128)(2,1)S(1)} %swap.1), channel_id=1, source_target_pairs={{0,4},{4,0},{8,12},{12,8},{16,20},{20,16},{24,28},{28,24},{1,5},{5... | collective-permute-start | bytes 208904 | tf_op jit(solution)/shard_map/ppermute | solution.py:72

commit v11 on v10

--- a/solution.py
+++ b/solution.py
@@ -164,38 +164,30 @@
     return (lane % LANES) // (LANES // groups)
 
 
-def filtered(dye_ref, start, toep_ref, rest_ref):
+def tokens_of(seqs, dye_ref, toep_ref, rest_ref, out_ref, block_len):
     groups = toep_ref.shape[0] // SLAB
     taps = toep_ref.shape[1]
-
-    def window(at, size):
+    starts = [seq * block_len + row for seq in seqs for row in range(0, block_len, SLAB)]
+
+    def windows(at, size):
         return jnp.concatenate(
-            [
-                dye_ref[pl.ds(pl.multiple_of(start + at, SLAB), size)],
-                dye_ref[pl.ds(pl.multiple_of(start + at + SLAB, SLAB), size)],
-            ],
-            axis=1,
-        )
-
-    group2 = group_of_lane(SLAB, 2 * LANES, groups)
-    after = window(taps, SLAB)
-    after = [jnp.where(group2 == group, after, jnp.zeros_like(after)) for group in range(groups)]
-    full = jnp.dot(toep_ref[...], window(0, taps), preferred_element_type=jnp.float32)
+            [dye_ref[pl.ds(pl.multiple_of(start + at, SLAB), size)] for start in starts], axis=1
+        )
+
+    group_in = group_of_lane(SLAB, len(starts) * LANES, groups)
+    after = windows(taps, SLAB)
+    after = [jnp.where(group_in == group, after, jnp.zeros_like(after)) for group in range(groups)]
+    full = jnp.dot(toep_ref[...], windows(0, taps), preferred_element_type=jnp.float32)
     rest = jnp.dot(
         rest_ref[...], jnp.concatenate(after, axis=0), preferred_element_type=jnp.float32
     )
     total = full[:SLAB]
     for group in range(1, groups):
-        total = jnp.where(group2 == group, full[group * SLAB : (group + 1) * SLAB], total)
-    total = total + rest
-    return jnp.concatenate([total[:, :LANES], total[:, LANES:]], axis=0).astype(jnp.bfloat16)
-
-
-def tokens_of(seq, dye_ref, toep_ref, rest_ref, out_ref, at, block_len):
-    for row in range(0, block_len, 2 * SLAB):
-        out_ref[at + row : at + row + 2 * SLAB] = filtered(
-            dye_ref, seq * block_len + row, toep_ref, rest_ref
-        )
+        total = jnp.where(group_in == group, full[group * SLAB : (group + 1) * SLAB], total)
+    total = (total + rest).astype(jnp.bfloat16)
+    for index in range(len(starts)):
+        columns = slice(index * LANES, (index + 1) * LANES)
+        out_ref[index * SLAB : (index + 1) * SLAB] = total[:, columns]
 
 
 def first_kernel(n_seq, taps_here, far, dy_ref, *refs):
@@ -235,13 +227,11 @@
             toeplitz_rows(filt_ref, toep_ref, rest_ref)
 
     block_len = tokens // n_seq
-    blocks = [(2 * (chip ^ far) + (core ^ flip), flip * block_len) for flip in range(2)]
+    seqs = [2 * (chip ^ far) + (core ^ flip) for flip in range(2)]
+    tokens_of(seqs, dye_ref, toep_ref, rest_ref, far_ref, block_len)
     lags = lag_ref[...].T
     eights = []
     for group in range(groups):
-        if group % 2 == 0 and blocks:
-            seq, at = blocks.pop(0)
-            tokens_of(seq, dye_ref, toep_ref, rest_ref, far_ref, at, block_len)
         at = group * STEP
         rows = lags[at : at + 8]
         for high in range(1, STEP // 8):
@@ -280,9 +270,8 @@
 def near_kernel(masks, flip, dye_ref, toep_ref, rest_ref, taps_ref, out_ref):
     chip, core, _ = place()
     block_len = (out_ref.shape[0] - len(masks) * EXTRA // 2) // len(masks)
-    for index, bits in enumerate(masks):
-        seq = 2 * (chip ^ bits) + (core ^ flip)
-        tokens_of(seq, dye_ref, toep_ref, rest_ref, out_ref, index * block_len, block_len)
+    seqs = [2 * (chip ^ bits) + (core ^ flip) for bits in masks]
+    tokens_of(seqs, dye_ref, toep_ref, rest_ref, out_ref, block_len)
     out_ref[len(masks) * block_len :] = stacked(
         [half_of(taps_ref[chip ^ bits], flip) for bits in masks]
     )
@@ -311,9 +300,8 @@
 def own_kernel(dye_ref, toep_ref, rest_ref, taps_ref, out_ref):
     chip, core, _ = place()
     block_len = (out_ref.shape[0] - EXTRA) // 2
-    for flip in range(2):
-        seq = 2 * chip + (core ^ flip)
-        tokens_of(seq, dye_ref, toep_ref, rest_ref, out_ref, flip * block_len, block_len)
+    seqs = [2 * chip + (core ^ flip) for flip in range(2)]
+    tokens_of(seqs, dye_ref, toep_ref, rest_ref, out_ref, block_len)
     out_ref[2 * block_len :] = taps_ref[chip]
 
 
@@ -465,7 +453,7 @@
             and groups_here == 8 * n_seq
             and 2 * taps_here == LANES
             and out_grads.shape[0] % 16 == 0
-            and layer_inputs.shape[0] % (2 * SLAB) == 0
+            and layer_inputs.shape[0] % SLAB == 0
             and n_seq * layer_inputs.shape[0] % (STEP * DEPTH // LANES) == 0
             and n_seq * taps_here + LANES <= n_seq * layer_inputs.shape[0]
         )

time: 31.7 us -> 31.6 us (level)
  transfers between devices with their start and end apart: 11 -> 11, of which waited for: 7 -> 8; matrix products, arithmetic and copies ran while one was open for 0% -> 0% of each run, Pallas kernels for 4% -> 4%
where the time goes in v11:
time: 31.6 us; the launch traced here: 31.4 us
  starting transfers between devices  15.4 us (49%)
  waiting for transfers between devices  8.67 us (27%)
  Pallas kernels  5.62 us (18%)
  local copies, waits for them, and re-layouts  0.95 us (3%)
  between operations  0.73 us (2%)
    all_to_all x1, starting transfers between devices, by_channels(): lax.all_to_all(dy, ('seq', 'chan'), split_axis=0, concat_axis=0, tiled=True)  7.3 us
    ppermute x8, waiting for transfers between devices, xor_permute(): return lax.ppermute(value, axis, pairs)  7.07 us
    pallas_call x9, Pallas kernels, local_call(): pl.pallas_call(kernel, out_shape=out_shape, in_specs=[whole] * len(operan...  5.62 us
    ppermute x8, starting transfers between devices, xor_permute(): return lax.ppermute(value, axis, pairs)  5.49 us
    ppermute x2, starting transfers between devices, turned_permute(): return lax.ppermute(value, axis, pairs)  2.65 us
    ppermute x2, waiting for transfers between devices, turned_permute(): return lax.ppermute(value, axis, pairs)  1.19 us
    unnamed x6, local copies, waits for them, and re-layouts  0.95 us
  transfers between devices with their start and end apart: 11, of which 8 were waited for; matrix products, arithmetic and copies ran while one was open for 0% of the time, Pallas kernels for 4%

profile of v11, /device:TPU:0, one launch (start us, length us, event | category | flops | bytes accessed | tf_op | source)
XLA Modules:
  0.0 31.4 jit_solution(7346098848688182634)
XLA Ops:
  0.6 0.9 %copy-done = bf16[32,4096]{1,0:T(8,128)(2,1)S(1)} copy-done((bf16[32,4096]{1,0:T(8,128)(2,1)S(1)}, bf16[32,4096]{1,0:T(8,128)(2,1)}, u32[]{:S(2)}) %copy-start) | copy-done | bytes 262168
  1.6 0.7 %fan_grads.1 = bf16[32,32,128]{2,1,0:T(8,128)(2,1)} custom-call(bf16[32,4096]{1,0:T(8,128)(2,1)S(1)} %copy-done), custom_call_target="tpu_custom_call" | custom-call | tf_op jit(solution)/shard_map/fan_grads/pallas_call | solution.py:348
  2.3 7.3 %all-to-all-start = ((bf16[32,32,128]{2,1,0:T(8,128)(2,1)}), bf16[32,32,128]{2,1,0:T(8,128)(2,1)S(1)}, u32[]{:S(2)}, u32[]{:S(2)}) async-start(bf16[32,32,128]{2,1,0:T(8,128)(2,1)} %fan_grads.1), calls=%async_computation | async-start | bytes 524288 | tf_op jit(solution)/shard_map/all_to_all | solution.py:381
  9.6 0.3 %collective-permute-start = (bf16[128,1024]{1,0:T(8,128)(2,1)S(1)}, bf16[128,1024]{1,0:T(8,128)(2,1)S(1)}, u32[]{:S(2)}, u32[]{:S(2)}) collective-permute-start(bf16[128,1024]{1,0:T(8,128)(2,1)S(1)} %copy-done.1), channel_id=1, source_target_pairs={{0,4},{4,0},{8,12},{12,8},{16,20},{20,16},{24,28},{28,24},{1,5},{5... | collective-permute-start | bytes 786440 | tf_op jit(solution)/shard_map/ppermute | solution.py:72
  10.0 0.3 collective-permute-start.1
  10.2 1.0 %collective-permute-done.1.f_other_ref = bf16[64,64]{1,0:T(8,128)(2,1)S(1)} collective-permute-done((bf16[64,64]{1,0:T(8,128)(2,1)S(1)}, bf16[64,64]{1,0:T(8,128)(2,1)S(1)}, u32[]{:S(2)}, u32[]{:S(2)}) %collective-permute-start.1) | collective-permute-done | bytes 8224 | tf_op jit(solution)/shard_map/ppermute | solution.py:72
  11.4 2.7 %collective-permute-start.2 = (bf16[272,128]{1,0:T(8,128)(2,1)S(1)}, bf16[272,128]{1,0:T(8,128)(2,1)S(1)}, u32[]{:S(2)}, u32[]{:S(2)}) collective-permute-start(bf16[272,128]{1,0:T(8,128)(2,1)S(1)} %get-tuple-element.16), channel_id=1, source_target_pairs={{0,24},{4,28},{8,16},{12,20},{16,8},{20,12},{24,0},{28,4},{1,25},{... | collective-permute-start | bytes 208904 | tf_op jit(solution)/shard_map/ppermute | solution.py:72
  14.1 0.6 %collective-permute-start.3 = (bf16[272,128]{1,0:T(8,128)(2,1)S(1)}, bf16[272,128]{1,0:T(8,128)(2,1)S(1)}, u32[]{:S(2)}, u32[]{:S(2)}) collective-permute-start(bf16[272,128]{1,0:T(8,128)(2,1)S(1)} %get-tuple-element.17), channel_id=1, source_target_pairs={{0,16},{4,20},{8,24},{12,28},{16,0},{20,4},{24,8},{28,12},{1,17},{... | collective-permute-start | bytes 208904 | tf_op jit(solution)/shard_map/ppermute | solution.py:72
  14.7 0.3 collective-permute-start.4
  14.9 2.8 %collective-permute-done.2.refs_1_ = bf16[272,128]{1,0:T(8,128)(2,1)S(1)} collective-permute-done((bf16[272,128]{1,0:T(8,128)(2,1)S(1)}, bf16[272,128]{1,0:T(8,128)(2,1)S(1)}, u32[]{:S(2)}, u32[]{:S(2)}) %collective-permute-start.2) | collective-permute-done | bytes 69664 | tf_op jit(solution)/shard_map/ppermute | solution.py:72
  17.8 1.7 %collective-permute-done.3.refs_2_ = bf16[272,128]{1,0:T(8,128)(2,1)S(1)} collective-permute-done((bf16[272,128]{1,0:T(8,128)(2,1)S(1)}, bf16[272,128]{1,0:T(8,128)(2,1)S(1)}, u32[]{:S(2)}, u32[]{:S(2)}) %collective-permute-start.3) | collective-permute-done | bytes 69664 | tf_op jit(solution)/shard_map/ppermute | solution.py:72
  19.5 0.4 %all-to-all-done = bf16[32,32,128]{2,1,0:T(8,128)(2,1)S(1)} async-done(((bf16[32,32,128]{2,1,0:T(8,128)(2,1)}), bf16[32,32,128]{2,1,0:T(8,128)(2,1)S(1)}, u32[]{:S(2)}, u32[]{:S(2)}) %all-to-all-start) | async-done | bytes 262176 | tf_op jit(solution)/shard_map/all_to_all | solution.py:381
  19.9 2.4 %first.1 = (bf16[1664,128]{1,0:T(8,128)(2,1)S(1)}, bf16[4,16,128]{2,1,0:T(8,128)(2,1)S(1)}, bf16[512,512]{1,0:T(8,128)(2,1)S(1)}, bf16[64,512]{1,0:T(8,128)(2,1)S(1)}, bf16[272,128]{1,0:T(8,128)(2,1)S(1)}) custom-call(bf16[1024,128]{1,0:T(8,128)(2,1)S(1)} %bitcast.1, bf16[272,128]{1,0:T(8,128)(2,1)S(1)} %get-tuple-element.15.refs_0_, ...), custom_call_target="tpu_custom_call" | custom-call | tf_op jit(solution)/shard_map/first/pallas_call | solution.py:348
  22.3 0.5 %near_swap.1 = bf16[272,128]{1,0:T(8,128)(2,1)S(1)} custom-call(bf16[1664,128]{1,0:T(8,128)(2,1)S(1)} %get-tuple-element.19.dye_ref, bf16[512,512]{1,0:T(8,128)(2,1)S(1)} %get-tuple-element.20.toep_ref, bf16[64,512]{1,0:T(8,128)(2,1)S(1)} %get-tuple-element.21.rest_ref, bf16[4,16,128]{2,1,0:T(8,128)(2,1)S(1)} %get-tuple-element.24.taps_ref), custom_call_target="tpu_custom_call" | custom-call | tf_op jit(solution)/shard_map/near_swap/pallas_call | solution.py:348
  22.9 0.4 %collective-permute-start.7 = (bf16[272,128]{1,0:T(8,128)(2,1)S(1)}, bf16[272,128]{1,0:T(8,128)(2,1)S(1)}, u32[]{:S(2)}, u32[]{:S(2)}) collective-permute-start(bf16[272,128]{1,0:T(8,128)(2,1)S(1)} %near_swap.1), channel_id=1, source_target_pairs={{0,4},{4,0},{8,12},{12,8},{16,20},{20,16},{24,28},{28,24},{1,5},{5... | collective-permute-start | bytes 208904 | tf_op jit(solution)/shard_map/ppermute | solution.py:72
  23.3 0.9 %collective-permute-start.5 = (bf16[272,128]{1,0:T(8,128)(2,1)S(1)}, bf16[272,128]{1,0:T(8,128)(2,1)S(1)}, u32[]{:S(2)}, u32[]{:S(2)}) collective-permute-start(bf16[272,128]{1,0:T(8,128)(2,1)S(1)} %get-tuple-element.22), channel_id=1, source_target_pairs={{0,24},{4,28},{8,16},{12,20},{16,8},{20,12},{24,0},{28,4},{1,25},{... | collective-permute-start | bytes 208904 | tf_op jit(solution)/shard_map/ppermute | solution.py:72
  24.2 0.5 %near_keep.1.keep_ref = bf16[272,128]{1,0:T(8,128)(2,1)S(1)} custom-call(bf16[1664,128]{1,0:T(8,128)(2,1)S(1)} %get-tuple-element.19.dye_ref, bf16[512,512]{1,0:T(8,128)(2,1)S(1)} %get-tuple-element.20.toep_ref, bf16[64,512]{1,0:T(8,128)(2,1)S(1)} %get-tuple-element.21.rest_ref, bf16[4,16,128]{2,1,0:T(8,128)(2,1)S(1)} %get-tuple-element.24.taps_ref), custom_call_target="tpu_custom_call" | custom-call | tf_op jit(solution)/shard_map/near_keep/pallas_call | solution.py:348
  24.7 1.5 %collective-permute-start.8 = (bf16[272,128]{1,0:T(8,128)(2,1)S(1)}, bf16[272,128]{1,0:T(8,128)(2,1)S(1)}, u32[]{:S(2)}, u32[]{:S(2)}) collective-permute-start(bf16[272,128]{1,0:T(8,128)(2,1)S(1)} %get-tuple-element.26), channel_id=1, source_target_pairs={{0,16},{4,12},{8,24},{12,4},{16,0},{20,28},{24,8},{28,20},{1,17},{... | collective-permute-start | bytes 208904 | tf_op jit(solution)/shard_map/ppermute | solution.py:77
  26.2 1.1 %collective-permute-start.9 = (bf16[272,128]{1,0:T(8,128)(2,1)S(1)}, bf16[272,128]{1,0:T(8,128)(2,1)S(1)}, u32[]{:S(2)}, u32[]{:S(2)}) collective-permute-start(bf16[272,128]{1,0:T(8,128)(2,1)S(1)} %get-tuple-element.27), channel_id=1, source_target_pairs={{0,8},{4,20},{8,0},{12,28},{16,24},{20,4},{24,16},{28,12},{1,9},{5... | collective-permute-start | bytes 208904 | tf_op jit(solution)/shard_map/ppermute | solution.py:77
  27.4 1.4 %collective-permute-done.5.refs_1_ = bf16[272,128]{1,0:T(8,128)(2,1)S(1)} collective-permute-done((bf16[272,128]{1,0:T(8,128)(2,1)S(1)}, bf16[272,128]{1,0:T(8,128)(2,1)S(1)}, u32[]{:S(2)}, u32[]{:S(2)}) %collective-permute-start.5) | collective-permute-done | bytes 69664 | tf_op jit(solution)/shard_map/ppermute | solution.py:72
  28.8 0.5 %own.1.refs_0_ = bf16[272,128]{1,0:T(8,128)(2,1)S(1)} custom-call(bf16[1664,128]{1,0:T(8,128)(2,1)S(1)} %get-tuple-element.19.dye_ref, bf16[512,512]{1,0:T(8,128)(2,1)S(1)} %get-tuple-element.20.toep_ref, bf16[64,512]{1,0:T(8,128)(2,1)S(1)} %get-tuple-element.21.rest_ref, bf16[4,16,128]{2,1,0:T(8,128)(2,1)S(1)} %get-tuple-element.24.taps_ref), custom_call_target="tpu_custom_call" | custom-call | tf_op jit(solution)/shard_map/own/pallas_call | solution.py:348
  29.4 0.6 %collective-permute-done.8.refs_3_ = bf16[272,128]{1,0:T(8,128)(2,1)S(1)} collective-permute-done((bf16[272,128]{1,0:T(8,128)(2,1)S(1)}, bf16[272,128]{1,0:T(8,128)(2,1)S(1)}, u32[]{:S(2)}, u32[]{:S(2)}) %collective-permute-start.8) | collective-permute-done | bytes 69664 | tf_op jit(solution)/shard_map/ppermute | solution.py:77
  29.9 0.6 %collective-permute-done.9.refs_4_ = bf16[272,128]{1,0:T(8,128)(2,1)S(1)} collective-permute-done((bf16[272,128]{1,0:T(8,128)(2,1)S(1)}, bf16[272,128]{1,0:T(8,128)(2,1)S(1)}, u32[]{:S(2)}, u32[]{:S(2)}) %collective-permute-start.9) | collective-permute-done | bytes 69664 | tf_op jit(solution)/shard_map/ppermute | solution.py:77
  30.6 0.8 %unpack.1 = (bf16[128,1024]{1,0:T(8,128)(2,1)}, f32[64,64]{1,0:T(8,128)}) custom-call(bf16[272,128]{1,0:T(8,128)(2,1)S(1)} %own.1.refs_0_, bf16[272,128]{1,0:T(8,128)(2,1)S(1)} %collective-permute-done.5.refs_1_, bf16[272,128]{1,0:T(8,128)(2,1)S(1)} %collective-permute-done.6.refs_2_, bf16[272,128]{1,0:T(8,128)(2,1)S(1)} %collective-permute-done.8.refs_3_, ...), custom_call_target="tpu_custom_call" | custom-call | tf_op jit(solution)/shard_map/unpack/pallas_call | solution.py:348
  (13 shorter events, 0.3 us)
Async XLA Ops:
  0.6 1.0 %copy-start = (bf16[32,4096]{1,0:T(8,128)(2,1)S(1)}, bf16[32,4096]{1,0:T(8,128)(2,1)}, u32[]{:S(2)}) copy-start(bf16[32,4096]{1,0:T(8,128)(2,1)} %in_ref.1) | copy-start | bytes 786436
  2.3 7.3 %copy-start.1 = (bf16[128,1024]{1,0:T(8,128)(2,1)S(1)}, bf16[128,1024]{1,0:T(8,128)(2,1)}, u32[]{:S(2)}) copy-start(bf16[128,1024]{1,0:T(8,128)(2,1)} %x_own_ref.1) | copy-start | bytes 786436
  2.3 7.6 %copy-start.2 = (bf16[64,64]{1,0:T(8,128)(2,1)S(1)}, bf16[64,64]{1,0:T(8,128)(2,1)}, u32[]{:S(2)}) copy-start(bf16[64,64]{1,0:T(8,128)(2,1)} %f_own_ref.1) | copy-start | bytes 24580
  2.3 17.6 %all-to-all-start = ((bf16[32,32,128]{2,1,0:T(8,128)(2,1)}), bf16[32,32,128]{2,1,0:T(8,128)(2,1)S(1)}, u32[]{:S(2)}, u32[]{:S(2)}) async-start(bf16[32,32,128]{2,1,0:T(8,128)(2,1)} %fan_grads.1), calls=%async_computation | async-start | bytes 524288 | tf_op jit(solution)/shard_map/all_to_all | solution.py:381
  9.6 1.6 %collective-permute-start = (bf16[128,1024]{1,0:T(8,128)(2,1)S(1)}, bf16[128,1024]{1,0:T(8,128)(2,1)S(1)}, u32[]{:S(2)}, u32[]{:S(2)}) collective-permute-start(bf16[128,1024]{1,0:T(8,128)(2,1)S(1)} %copy-done.1), channel_id=1, source_target_pairs={{0,4},{4,0},{8,12},{12,8},{16,20},{20,16},{24,28},{28,24},{1,5},{5... | collective-permute-start | bytes 786440 | tf_op jit(solution)/shard_map/ppermute | solution.py:72
  10.0 1.3 %collective-permute-start.1 = (bf16[64,64]{1,0:T(8,128)(2,1)S(1)}, bf16[64,64]{1,0:T(8,128)(2,1)S(1)}, u32[]{:S(2)}, u32[]{:S(2)}) collective-permute-start(bf16[64,64]{1,0:T(8,128)(2,1)S(1)} %copy-done.2), channel_id=1, source_target_pairs={{0,4},{4,0},{8,12},{12,8},{16,20},{20,16},{24,28},{28,24},{1,5},{5... | collective-permute-start | bytes 24584 | tf_op jit(solution)/shard_map/ppermute | solution.py:72
  11.4 6.4 %collective-permute-start.2 = (bf16[272,128]{1,0:T(8,128)(2,1)S(1)}, bf16[272,128]{1,0:T(8,128)(2,1)S(1)}, u32[]{:S(2)}, u32[]{:S(2)}) collective-permute-start(bf16[272,128]{1,0:T(8,128)(2,1)S(1)} %get-tuple-element.16), channel_id=1, source_target_pairs={{0,24},{4,28},{8,16},{12,20},{16,8},{20,12},{24,0},{28,4},{1,25},{... | collective-permute-start | bytes 208904 | tf_op jit(solution)/shard_map/ppermute | solution.py:72
  14.1 5.4 %collective-permute-start.3 = (bf16[272,128]{1,0:T(8,128)(2,1)S(1)}, bf16[272,128]{1,0:T(8,128)(2,1)S(1)}, u32[]{:S(2)}, u32[]{:S(2)}) collective-permute-start(bf16[272,128]{1,0:T(8,128)(2,1)S(1)} %get-tuple-element.17), channel_id=1, source_target_pairs={{0,16},{4,20},{8,24},{12,28},{16,0},{20,4},{24,8},{28,12},{1,17},{... | collective-permute-start | bytes 208904 | tf_op jit(solution)/shard_map/ppermute | solution.py:72
  14.7 4.8 %collective-permute-start.4 = (bf16[272,128]{1,0:T(8,128)(2,1)S(1)}, bf16[272,128]{1,0:T(8,128)(2,1)S(1)}, u32[]{:S(2)}, u32[]{:S(2)}) collective-permute-start(bf16[272,128]{1,0:T(8,128)(2,1)S(1)} %get-tuple-element.18), channel_id=1, source_target_pairs={{0,8},{4,12},{8,0},{12,4},{16,24},{20,28},{24,16},{28,20},{1,9},{5... | collective-permute-start | bytes 208904 | tf_op jit(solution)/shard_map/ppermute | solution.py:72
  22.9 1.8 %collective-permute-start.7 = (bf16[272,128]{1,0:T(8,128)(2,1)S(1)}, bf16[272,128]{1,0:T(8,128)(2,1)S(1)}, u32[]{:S(2)}, u32[]{:S(2)}) collective-permute-start(bf16[272,128]{1,0:T(8,128)(2,1)S(1)} %near_swap.1), channel_id=1, source_target_pairs={{0,4},{4,0},{8,12},{12,8},{16,20},{20,16},{24,28},{28,24},{1,5},{5... | collective-permute-start | bytes 208904 | tf_op jit(solution)/shard_map/ppermute | solution.py:72
  23.3 5.5 %collective-permute-start.5 = (bf16[272,128]{1,0:T(8,128)(2,1)S(1)}, bf16[272,128]{1,0:T(8,128)(2,1)S(1)}, u32[]{:S(2)}, u32[]{:S(2)}) collective-permute-start(bf16[272,128]{1,0:T(8,128)(2,1)S(1)} %get-tuple-element.22), channel_id=1, source_target_pairs={{0,24},{4,28},{8,16},{12,20},{16,8},{20,12},{24,0},{28,4},{1,25},{... | collective-permute-start | bytes 208904 | tf_op jit(solution)/shard_map/ppermute | solution.py:72
  24.7 5.2 %collective-permute-start.8 = (bf16[272,128]{1,0:T(8,128)(2,1)S(1)}, bf16[272,128]{1,0:T(8,128)(2,1)S(1)}, u32[]{:S(2)}, u32[]{:S(2)}) collective-permute-start(bf16[272,128]{1,0:T(8,128)(2,1)S(1)} %get-tuple-element.26), channel_id=1, source_target_pairs={{0,16},{4,12},{8,24},{12,4},{16,0},{20,28},{24,8},{28,20},{1,17},{... | collective-permute-start | bytes 208904 | tf_op jit(solution)/shard_map/ppermute | solution.py:77
  26.2 4.3 %collective-permute-start.9 = (bf16[272,128]{1,0:T(8,128)(2,1)S(1)}, bf16[272,128]{1,0:T(8,128)(2,1)S(1)}, u32[]{:S(2)}, u32[]{:S(2)}) collective-permute-start(bf16[272,128]{1,0:T(8,128)(2,1)S(1)} %get-tuple-element.27), channel_id=1, source_target_pairs={{0,8},{4,20},{8,0},{12,28},{16,24},{20,4},{24,16},{28,12},{1,9},{5... | collective-permute-start | bytes 208904 | tf_op jit(solution)/shard_map/ppermute | solution.py:77
  29.3 1.3 %collective-permute-start.6 = (bf16[272,128]{1,0:T(8,128)(2,1)S(1)}, bf16[272,128]{1,0:T(8,128)(2,1)S(1)}, u32[]{:S(2)}, u32[]{:S(2)}) collective-permute-start(bf16[272,128]{1,0:T(8,128)(2,1)S(1)} %swap.1), channel_id=1, source_target_pairs={{0,4},{4,0},{8,12},{12,8},{16,20},{20,16},{24,28},{28,24},{1,5},{5... | collective-permute-start | bytes 208904 | tf_op jit(solution)/shard_map/ppermute | solution.py:72

commit v12 on v11

--- a/solution.py
+++ b/solution.py
@@ -190,10 +190,10 @@
         out_ref[index * SLAB : (index + 1) * SLAB] = total[:, columns]
 
 
-def first_kernel(n_seq, taps_here, far, dy_ref, *refs):
+def first_kernel(n_seq, taps_here, far, near, dy_ref, *refs):
     chips = n_seq // 2
     in_refs = refs[:chips]
-    dye_ref, taps_ref, toep_ref, rest_ref, far_ref, x_ref, filt_ref, lag_ref = refs[chips:]
+    dye_ref, taps_ref, toep_ref, rest_ref, far_ref, near_ref, x_ref, filt_ref, lag_ref = refs[chips:]
     tokens = dy_ref.shape[0]
     groups = EXTRA // 2
     taps = n_seq * taps_here
@@ -229,6 +229,8 @@
     block_len = tokens // n_seq
     seqs = [2 * (chip ^ far) + (core ^ flip) for flip in range(2)]
     tokens_of(seqs, dye_ref, toep_ref, rest_ref, far_ref, block_len)
+    seqs = [2 * (chip ^ bits) + (core ^ 1) for bits in near]
+    tokens_of(seqs, dye_ref, toep_ref, rest_ref, near_ref, block_len)
     lags = lag_ref[...].T
     eights = []
     for group in range(groups):
@@ -256,6 +258,7 @@
         taps_ref[to_chip] = jnp.concatenate([mine, other], axis=0).astype(jnp.bfloat16)
 
     far_ref[2 * block_len :] = taps_ref[chip ^ far]
+    near_ref[len(near) * block_len :] = stacked([half_of(taps_ref[chip ^ bits], 1) for bits in near])
 
 
 def half_of(taps, flip):
@@ -267,13 +270,13 @@
     return jnp.concatenate(rows, axis=0).astype(jnp.bfloat16)
 
 
-def near_kernel(masks, flip, dye_ref, toep_ref, rest_ref, taps_ref, out_ref):
+def near_kernel(masks, dye_ref, toep_ref, rest_ref, taps_ref, out_ref):
     chip, core, _ = place()
     block_len = (out_ref.shape[0] - len(masks) * EXTRA // 2) // len(masks)
-    seqs = [2 * (chip ^ bits) + (core ^ flip) for bits in masks]
+    seqs = [2 * (chip ^ bits) + core for bits in masks]
     tokens_of(seqs, dye_ref, toep_ref, rest_ref, out_ref, block_len)
     out_ref[len(masks) * block_len :] = stacked(
-        [half_of(taps_ref[chip ^ bits], flip) for bits in masks]
+        [half_of(taps_ref[chip ^ bits], 0) for bits in masks]
     )
 
 
@@ -316,7 +319,7 @@
 
 
 def unpack_kernel(masks, *refs):
-    own_ref, far_ref, swapped_ref, *near_refs, dx_ref, dh_ref, rows_ref = refs
+    *near_refs, own_ref, far_ref, swapped_ref, dx_ref, dh_ref, rows_ref = refs
     chip, core, _ = place()
     block_len = dx_ref.shape[0]
     taps_here, groups_here = dh_ref.shape
@@ -388,14 +391,15 @@
     )
     near = masks[2:]
     near_shape = half(len(near) * (block_len + EXTRA // 2), LANES)
-    dye, tap_parts, toeplitz, outside, far = local_call(
-        functools.partial(first_kernel, n_seq, taps_here, masks[1]),
+    dye, tap_parts, toeplitz, outside, far, send = local_call(
+        functools.partial(first_kernel, n_seq, taps_here, masks[1], near),
         [
             half(tokens + taps + LANES, LANES),
             half(chips, EXTRA, LANES),
             half(groups * SLAB, taps),
             half(SLAB, groups * SLAB),
             unit,
+            near_shape,
         ],
         (dy.reshape(tokens, LANES), *fan_out(pieces, "seq", 2)),
         "first",
@@ -406,15 +410,9 @@
         ],
     )
     far = xor_permute(far, "seq", 2 * masks[1])
-    (send,) = local_call(
-        functools.partial(near_kernel, near, 1),
-        [near_shape],
-        (dye, toeplitz, outside, tap_parts),
-        "near_swap",
-    )
     got = xor_permute(send, "seq", 1)
     (keep,) = local_call(
-        functools.partial(near_kernel, near, 0),
+        functools.partial(near_kernel, near),
         [near_shape],
         (dye, toeplitz, outside, tap_parts),
         "near_keep",
@@ -435,7 +433,7 @@
             half(block_len, n_seq * LANES),
             jax.ShapeDtypeStruct((taps_here, groups_here), jnp.float32),
         ],
-        (own, far, xor_permute(send, "seq", 1), *pieces),
+        (*pieces, own, far, xor_permute(send, "seq", 1)),
         "unpack",
         [pltpu.VMEM((groups_here, LANES), jnp.float32)],
     )

time: 31.6 us -> 31.4 us (level)
    pallas_call x9 -> x8, Pallas kernels: 5.62 us -> 5.42 us  [local_call(): pl.pallas_call(kernel, out_shape=out_shape, in_specs=[whole] * len(operan...]
where the time goes in v12:
time: 31.4 us; the launch traced here: 31.2 us
  starting transfers between devices  15.4 us (49%)
  waiting for transfers between devices  8.67 us (28%)
  Pallas kernels  5.42 us (17%)
  local copies, waits for them, and re-layouts  0.95 us (3%)
  between operations  0.72 us (2%)
    all_to_all x1, starting transfers between devices, by_channels(): lax.all_to_all(dy, ('seq', 'chan'), split_axis=0, concat_axis=0, tiled=True)  7.3 us
    ppermute x8, waiting for transfers between devices, xor_permute(): return lax.ppermute(value, axis, pairs)  7.07 us
    ppermute x8, starting transfers between devices, xor_permute(): return lax.ppermute(value, axis, pairs)  5.47 us
    pallas_call x8, Pallas kernels, local_call(): pl.pallas_call(kernel, out_shape=out_shape, in_specs=[whole] * len(operan...  5.42 us
    ppermute x2, starting transfers between devices, turned_permute(): return lax.ppermute(value, axis, pairs)  2.66 us
    ppermute x2, waiting for transfers between devices, turned_permute(): return lax.ppermute(value, axis, pairs)  1.19 us
    unnamed x6, local copies, waits for them, and re-layouts  0.95 us
  transfers between devices with their start and end apart: 11, of which 8 were waited for; matrix products, arithmetic and copies ran while one was open for 0% of the time, Pallas kernels for 4%

profile of v12, /device:TPU:0, one launch (start us, length us, event | category | flops | bytes accessed | tf_op | source)
XLA Modules:
  0.0 31.2 jit_solution(7101688522519265701)
XLA Ops:
  0.6 0.9 %copy-done = bf16[32,4096]{1,0:T(8,128)(2,1)S(1)} copy-done((bf16[32,4096]{1,0:T(8,128)(2,1)S(1)}, bf16[32,4096]{1,0:T(8,128)(2,1)}, u32[]{:S(2)}) %copy-start) | copy-done | bytes 262168
  1.6 0.7 %fan_grads.1 = bf16[32,32,128]{2,1,0:T(8,128)(2,1)} custom-call(bf16[32,4096]{1,0:T(8,128)(2,1)S(1)} %copy-done), custom_call_target="tpu_custom_call" | custom-call | tf_op jit(solution)/shard_map/fan_grads/pallas_call | solution.py:351
  2.3 7.3 %all-to-all-start = ((bf16[32,32,128]{2,1,0:T(8,128)(2,1)}), bf16[32,32,128]{2,1,0:T(8,128)(2,1)S(1)}, u32[]{:S(2)}, u32[]{:S(2)}) async-start(bf16[32,32,128]{2,1,0:T(8,128)(2,1)} %fan_grads.1), calls=%async_computation | async-start | bytes 524288 | tf_op jit(solution)/shard_map/all_to_all | solution.py:384
  9.6 0.3 %collective-permute-start = (bf16[128,1024]{1,0:T(8,128)(2,1)S(1)}, bf16[128,1024]{1,0:T(8,128)(2,1)S(1)}, u32[]{:S(2)}, u32[]{:S(2)}) collective-permute-start(bf16[128,1024]{1,0:T(8,128)(2,1)S(1)} %copy-done.1), channel_id=1, source_target_pairs={{0,4},{4,0},{8,12},{12,8},{16,20},{20,16},{24,28},{28,24},{1,5},{5... | collective-permute-start | bytes 786440 | tf_op jit(solution)/shard_map/ppermute | solution.py:72
  10.0 0.3 collective-permute-start.1
  10.2 1.0 %collective-permute-done.1.f_other_ref = bf16[64,64]{1,0:T(8,128)(2,1)S(1)} collective-permute-done((bf16[64,64]{1,0:T(8,128)(2,1)S(1)}, bf16[64,64]{1,0:T(8,128)(2,1)S(1)}, u32[]{:S(2)}, u32[]{:S(2)}) %collective-permute-start.1) | collective-permute-done | bytes 8224 | tf_op jit(solution)/shard_map/ppermute | solution.py:72
  11.3 0.1 fan_inputs.1
  11.4 2.7 %collective-permute-start.2 = (bf16[272,128]{1,0:T(8,128)(2,1)S(1)}, bf16[272,128]{1,0:T(8,128)(2,1)S(1)}, u32[]{:S(2)}, u32[]{:S(2)}) collective-permute-start(bf16[272,128]{1,0:T(8,128)(2,1)S(1)} %get-tuple-element.17), channel_id=1, source_target_pairs={{0,24},{4,28},{8,16},{12,20},{16,8},{20,12},{24,0},{28,4},{1,25},{... | collective-permute-start | bytes 208904 | tf_op jit(solution)/shard_map/ppermute | solution.py:72
  14.1 0.6 %collective-permute-start.3 = (bf16[272,128]{1,0:T(8,128)(2,1)S(1)}, bf16[272,128]{1,0:T(8,128)(2,1)S(1)}, u32[]{:S(2)}, u32[]{:S(2)}) collective-permute-start(bf16[272,128]{1,0:T(8,128)(2,1)S(1)} %get-tuple-element.18), channel_id=1, source_target_pairs={{0,16},{4,20},{8,24},{12,28},{16,0},{20,4},{24,8},{28,12},{1,17},{... | collective-permute-start | bytes 208904 | tf_op jit(solution)/shard_map/ppermute | solution.py:72
  14.7 0.3 collective-permute-start.4
  14.9 2.8 %collective-permute-done.2.refs_1_ = bf16[272,128]{1,0:T(8,128)(2,1)S(1)} collective-permute-done((bf16[272,128]{1,0:T(8,128)(2,1)S(1)}, bf16[272,128]{1,0:T(8,128)(2,1)S(1)}, u32[]{:S(2)}, u32[]{:S(2)}) %collective-permute-start.2) | collective-permute-done | bytes 69664 | tf_op jit(solution)/shard_map/ppermute | solution.py:72
  17.8 1.7 %collective-permute-done.3.refs_2_ = bf16[272,128]{1,0:T(8,128)(2,1)S(1)} collective-permute-done((bf16[272,128]{1,0:T(8,128)(2,1)S(1)}, bf16[272,128]{1,0:T(8,128)(2,1)S(1)}, u32[]{:S(2)}, u32[]{:S(2)}) %collective-permute-start.3) | collective-permute-done | bytes 69664 | tf_op jit(solution)/shard_map/ppermute | solution.py:72
  19.5 0.4 %all-to-all-done = bf16[32,32,128]{2,1,0:T(8,128)(2,1)S(1)} async-done(((bf16[32,32,128]{2,1,0:T(8,128)(2,1)}), bf16[32,32,128]{2,1,0:T(8,128)(2,1)S(1)}, u32[]{:S(2)}, u32[]{:S(2)}) %all-to-all-start) | async-done | bytes 262176 | tf_op jit(solution)/shard_map/all_to_all | solution.py:384
  19.9 2.8 %first.1 = (bf16[1664,128]{1,0:T(8,128)(2,1)S(1)}, bf16[4,16,128]{2,1,0:T(8,128)(2,1)S(1)}, bf16[512,512]{1,0:T(8,128)(2,1)S(1)}, bf16[64,512]{1,0:T(8,128)(2,1)...) custom-call(bf16[1024,128]{1,0:T(8,128)(2,1)S(1)} %bitcast.1, ...), custom_call_target="tpu_custom_call" | custom-call | tf_op jit(solution)/shard_map/first/pallas_call | solution.py:351
  22.7 0.4 %collective-permute-start.5 = (bf16[272,128]{1,0:T(8,128)(2,1)S(1)}, bf16[272,128]{1,0:T(8,128)(2,1)S(1)}, u32[]{:S(2)}, u32[]{:S(2)}) collective-permute-start(bf16[272,128]{1,0:T(8,128)(2,1)S(1)} %get-tuple-element.24), channel_id=1, source_target_pairs={{0,4},{4,0},{8,12},{12,8},{16,20},{20,16},{24,28},{28,24},{1,5},{5... | collective-permute-start | bytes 208904 | tf_op jit(solution)/shard_map/ppermute | solution.py:72
  23.1 0.9 %collective-permute-start.8 = (bf16[272,128]{1,0:T(8,128)(2,1)S(1)}, bf16[272,128]{1,0:T(8,128)(2,1)S(1)}, u32[]{:S(2)}, u32[]{:S(2)}) collective-permute-start(bf16[272,128]{1,0:T(8,128)(2,1)S(1)} %get-tuple-element.27), channel_id=1, source_target_pairs={{0,24},{4,28},{8,16},{12,20},{16,8},{20,12},{24,0},{28,4},{1,25},{... | collective-permute-start | bytes 208904 | tf_op jit(solution)/shard_map/ppermute | solution.py:72
  23.9 0.5 %near_keep.1.keep_ref = bf16[272,128]{1,0:T(8,128)(2,1)S(1)} custom-call(bf16[1664,128]{1,0:T(8,128)(2,1)S(1)} %get-tuple-element.20.dye_ref, bf16[512,512]{1,0:T(8,128)(2,1)S(1)} %get-tuple-element.21.toep_ref, bf16[64,512]{1,0:T(8,128)(2,1)S(1)} %get-tuple-element.22.rest_ref, bf16[4,16,128]{2,1,0:T(8,128)(2,1)S(1)} %get-tuple-element.28.taps_ref), custom_call_target="tpu_custom_call" | custom-call | tf_op jit(solution)/shard_map/near_keep/pallas_call | solution.py:351
  24.5 1.5 %collective-permute-start.6 = (bf16[272,128]{1,0:T(8,128)(2,1)S(1)}, bf16[272,128]{1,0:T(8,128)(2,1)S(1)}, u32[]{:S(2)}, u32[]{:S(2)}) collective-permute-start(bf16[272,128]{1,0:T(8,128)(2,1)S(1)} %get-tuple-element.25), channel_id=1, source_target_pairs={{0,16},{4,12},{8,24},{12,4},{16,0},{20,28},{24,8},{28,20},{1,17},{... | collective-permute-start | bytes 208904 | tf_op jit(solution)/shard_map/ppermute | solution.py:77
  26.0 1.1 %collective-permute-start.7 = (bf16[272,128]{1,0:T(8,128)(2,1)S(1)}, bf16[272,128]{1,0:T(8,128)(2,1)S(1)}, u32[]{:S(2)}, u32[]{:S(2)}) collective-permute-start(bf16[272,128]{1,0:T(8,128)(2,1)S(1)} %get-tuple-element.26), channel_id=1, source_target_pairs={{0,8},{4,20},{8,0},{12,28},{16,24},{20,4},{24,16},{28,12},{1,9},{5... | collective-permute-start | bytes 208904 | tf_op jit(solution)/shard_map/ppermute | solution.py:77
  27.2 1.4 %collective-permute-done.8.refs_1_.refs_3_ = bf16[272,128]{1,0:T(8,128)(2,1)S(1)} collective-permute-done((bf16[272,128]{1,0:T(8,128)(2,1)S(1)}, bf16[272,128]{1,0:T(8,128)(2,1)S(1)}, u32[]{:S(2)}, u32[]{:S(2)}) %collective-permute-start.8) | collective-permute-done | bytes 69664 | tf_op jit(solution)/shard_map/ppermute | solution.py:72
  28.6 0.5 %own.1.refs_0_.refs_2_ = bf16[272,128]{1,0:T(8,128)(2,1)S(1)} custom-call(bf16[1664,128]{1,0:T(8,128)(2,1)S(1)} %get-tuple-element.20.dye_ref, bf16[512,512]{1,0:T(8,128)(2,1)S(1)} %get-tuple-element.21.toep_ref, bf16[64,512]{1,0:T(8,128)(2,1)S(1)} %get-tuple-element.22.rest_ref, bf16[4,16,128]{2,1,0:T(8,128)(2,1)S(1)} %get-tuple-element.28.taps_ref), custom_call_target="tpu_custom_call" | custom-call | tf_op jit(solution)/shard_map/own/pallas_call | solution.py:351
  29.2 0.6 %collective-permute-done.6.refs_0_ = bf16[272,128]{1,0:T(8,128)(2,1)S(1)} collective-permute-done((bf16[272,128]{1,0:T(8,128)(2,1)S(1)}, bf16[272,128]{1,0:T(8,128)(2,1)S(1)}, u32[]{:S(2)}, u32[]{:S(2)}) %collective-permute-start.6) | collective-permute-done | bytes 69664 | tf_op jit(solution)/shard_map/ppermute | solution.py:77
  29.7 0.6 %collective-permute-done.7.refs_1_ = bf16[272,128]{1,0:T(8,128)(2,1)S(1)} collective-permute-done((bf16[272,128]{1,0:T(8,128)(2,1)S(1)}, bf16[272,128]{1,0:T(8,128)(2,1)S(1)}, u32[]{:S(2)}, u32[]{:S(2)}) %collective-permute-start.7) | collective-permute-done | bytes 69664 | tf_op jit(solution)/shard_map/ppermute | solution.py:77
  30.4 0.8 %unpack.1 = (bf16[128,1024]{1,0:T(8,128)(2,1)}, f32[64,64]{1,0:T(8,128)}) custom-call(bf16[272,128]{1,0:T(8,128)(2,1)S(1)} %collective-permute-done.6.refs_0_, bf16[272,128]{1,0:T(8,128)(2,1)S(1)} %collective-permute-done.7.refs_1_, bf16[272,128]{1,0:T(8,128)(2,1)S(1)} %own.1.refs_0_.refs_2_, bf16[272,128]{1,0:T(8,128)(2,1)S(1)} %collective-permute-done.8.refs_1_.refs_3_, ...), custom_call_target="tpu_custom_call" | custom-call | tf_op jit(solution)/shard_map/unpack/pallas_call | solution.py:351
  (12 shorter events, 0.2 us)
Async XLA Ops:
  0.6 1.0 %copy-start = (bf16[32,4096]{1,0:T(8,128)(2,1)S(1)}, bf16[32,4096]{1,0:T(8,128)(2,1)}, u32[]{:S(2)}) copy-start(bf16[32,4096]{1,0:T(8,128)(2,1)} %in_ref.1) | copy-start | bytes 786436
  2.3 7.3 %copy-start.1 = (bf16[128,1024]{1,0:T(8,128)(2,1)S(1)}, bf16[128,1024]{1,0:T(8,128)(2,1)}, u32[]{:S(2)}) copy-start(bf16[128,1024]{1,0:T(8,128)(2,1)} %x_own_ref.1) | copy-start | bytes 786436
  2.3 7.6 %copy-start.2 = (bf16[64,64]{1,0:T(8,128)(2,1)S(1)}, bf16[64,64]{1,0:T(8,128)(2,1)}, u32[]{:S(2)}) copy-start(bf16[64,64]{1,0:T(8,128)(2,1)} %f_own_ref.1) | copy-start | bytes 24580
  2.3 17.6 %all-to-all-start = ((bf16[32,32,128]{2,1,0:T(8,128)(2,1)}), bf16[32,32,128]{2,1,0:T(8,128)(2,1)S(1)}, u32[]{:S(2)}, u32[]{:S(2)}) async-start(bf16[32,32,128]{2,1,0:T(8,128)(2,1)} %fan_grads.1), calls=%async_computation | async-start | bytes 524288 | tf_op jit(solution)/shard_map/all_to_all | solution.py:384
  9.6 1.6 %collective-permute-start = (bf16[128,1024]{1,0:T(8,128)(2,1)S(1)}, bf16[128,1024]{1,0:T(8,128)(2,1)S(1)}, u32[]{:S(2)}, u32[]{:S(2)}) collective-permute-start(bf16[128,1024]{1,0:T(8,128)(2,1)S(1)} %copy-done.1), channel_id=1, source_target_pairs={{0,4},{4,0},{8,12},{12,8},{16,20},{20,16},{24,28},{28,24},{1,5},{5... | collective-permute-start | bytes 786440 | tf_op jit(solution)/shard_map/ppermute | solution.py:72
  10.0 1.3 %collective-permute-start.1 = (bf16[64,64]{1,0:T(8,128)(2,1)S(1)}, bf16[64,64]{1,0:T(8,128)(2,1)S(1)}, u32[]{:S(2)}, u32[]{:S(2)}) collective-permute-start(bf16[64,64]{1,0:T(8,128)(2,1)S(1)} %copy-done.2), channel_id=1, source_target_pairs={{0,4},{4,0},{8,12},{12,8},{16,20},{20,16},{24,28},{28,24},{1,5},{5... | collective-permute-start | bytes 24584 | tf_op jit(solution)/shard_map/ppermute | solution.py:72
  11.4 6.4 %collective-permute-start.2 = (bf16[272,128]{1,0:T(8,128)(2,1)S(1)}, bf16[272,128]{1,0:T(8,128)(2,1)S(1)}, u32[]{:S(2)}, u32[]{:S(2)}) collective-permute-start(bf16[272,128]{1,0:T(8,128)(2,1)S(1)} %get-tuple-element.17), channel_id=1, source_target_pairs={{0,24},{4,28},{8,16},{12,20},{16,8},{20,12},{24,0},{28,4},{1,25},{... | collective-permute-start | bytes 208904 | tf_op jit(solution)/shard_map/ppermute | solution.py:72
  14.1 5.4 %collective-permute-start.3 = (bf16[272,128]{1,0:T(8,128)(2,1)S(1)}, bf16[272,128]{1,0:T(8,128)(2,1)S(1)}, u32[]{:S(2)}, u32[]{:S(2)}) collective-permute-start(bf16[272,128]{1,0:T(8,128)(2,1)S(1)} %get-tuple-element.18), channel_id=1, source_target_pairs={{0,16},{4,20},{8,24},{12,28},{16,0},{20,4},{24,8},{28,12},{1,17},{... | collective-permute-start | bytes 208904 | tf_op jit(solution)/shard_map/ppermute | solution.py:72
  14.7 4.8 %collective-permute-start.4 = (bf16[272,128]{1,0:T(8,128)(2,1)S(1)}, bf16[272,128]{1,0:T(8,128)(2,1)S(1)}, u32[]{:S(2)}, u32[]{:S(2)}) collective-permute-start(bf16[272,128]{1,0:T(8,128)(2,1)S(1)} %get-tuple-element.19), channel_id=1, source_target_pairs={{0,8},{4,12},{8,0},{12,4},{16,24},{20,28},{24,16},{28,20},{1,9},{5... | collective-permute-start | bytes 208904 | tf_op jit(solution)/shard_map/ppermute | solution.py:72
  22.7 1.8 %collective-permute-start.5 = (bf16[272,128]{1,0:T(8,128)(2,1)S(1)}, bf16[272,128]{1,0:T(8,128)(2,1)S(1)}, u32[]{:S(2)}, u32[]{:S(2)}) collective-permute-start(bf16[272,128]{1,0:T(8,128)(2,1)S(1)} %get-tuple-element.24), channel_id=1, source_target_pairs={{0,4},{4,0},{8,12},{12,8},{16,20},{20,16},{24,28},{28,24},{1,5},{5... | collective-permute-start | bytes 208904 | tf_op jit(solution)/shard_map/ppermute | solution.py:72
  23.1 5.5 %collective-permute-start.8 = (bf16[272,128]{1,0:T(8,128)(2,1)S(1)}, bf16[272,128]{1,0:T(8,128)(2,1)S(1)}, u32[]{:S(2)}, u32[]{:S(2)}) collective-permute-start(bf16[272,128]{1,0:T(8,128)(2,1)S(1)} %get-tuple-element.27), channel_id=1, source_target_pairs={{0,24},{4,28},{8,16},{12,20},{16,8},{20,12},{24,0},{28,4},{1,25},{... | collective-permute-start | bytes 208904 | tf_op jit(solution)/shard_map/ppermute | solution.py:72
  24.5 5.2 %collective-permute-start.6 = (bf16[272,128]{1,0:T(8,128)(2,1)S(1)}, bf16[272,128]{1,0:T(8,128)(2,1)S(1)}, u32[]{:S(2)}, u32[]{:S(2)}) collective-permute-start(bf16[272,128]{1,0:T(8,128)(2,1)S(1)} %get-tuple-element.25), channel_id=1, source_target_pairs={{0,16},{4,12},{8,24},{12,4},{16,0},{20,28},{24,8},{28,20},{1,17},{... | collective-permute-start | bytes 208904 | tf_op jit(solution)/shard_map/ppermute | solution.py:77
  26.0 4.3 %collective-permute-start.7 = (bf16[272,128]{1,0:T(8,128)(2,1)S(1)}, bf16[272,128]{1,0:T(8,128)(2,1)S(1)}, u32[]{:S(2)}, u32[]{:S(2)}) collective-permute-start(bf16[272,128]{1,0:T(8,128)(2,1)S(1)} %get-tuple-element.26), channel_id=1, source_target_pairs={{0,8},{4,20},{8,0},{12,28},{16,24},{20,4},{24,16},{28,12},{1,9},{5... | collective-permute-start | bytes 208904 | tf_op jit(solution)/shard_map/ppermute | solution.py:77
  29.1 1.3 %collective-permute-start.9 = (bf16[272,128]{1,0:T(8,128)(2,1)S(1)}, bf16[272,128]{1,0:T(8,128)(2,1)S(1)}, u32[]{:S(2)}, u32[]{:S(2)}) collective-permute-start(bf16[272,128]{1,0:T(8,128)(2,1)S(1)} %swap.1), channel_id=1, source_target_pairs={{0,4},{4,0},{8,12},{12,8},{16,20},{20,16},{24,28},{28,24},{1,5},{5... | collective-permute-start | bytes 208904 | tf_op jit(solution)/shard_map/ppermute | solution.py:72

commit v13 on v12

--- a/solution.py
+++ b/solution.py
@@ -11,7 +11,7 @@
 STEP = 32
 SLAB = 64
 EXTRA = 16
-DEPTH = 1024
+DEPTH = 4096
 VMEM_LIMIT = 40 * 1024 * 1024
 
 

time: 31.4 us -> 31.4 us (level)
  transfers between devices with their start and end apart: 11 -> 11, of which waited for: 8 -> 7; matrix products, arithmetic and copies ran while one was open for 0% -> 0% of each run, Pallas kernels for 4% -> 4%
where the time goes in v13:
time: 31.4 us; the launch traced here: 31.2 us
  starting transfers between devices  15.4 us (49%)
  waiting for transfers between devices  8.66 us (28%)
  Pallas kernels  5.42 us (17%)
  local copies, waits for them, and re-layouts  0.95 us (3%)
  between operations  0.72 us (2%)
    all_to_all x1, starting transfers between devices, by_channels(): lax.all_to_all(dy, ('seq', 'chan'), split_axis=0, concat_axis=0, tiled=True)  7.3 us
    ppermute x8, waiting for transfers between devices, xor_permute(): return lax.ppermute(value, axis, pairs)  7.06 us
    ppermute x8, starting transfers between devices, xor_permute(): return lax.ppermute(value, axis, pairs)  5.48 us
    pallas_call x8, Pallas kernels, local_call(): pl.pallas_call(kernel, out_shape=out_shape, in_specs=[whole] * len(operan...  5.42 us
    ppermute x2, starting transfers between devices, turned_permute(): return lax.ppermute(value, axis, pairs)  2.65 us
    ppermute x2, waiting for transfers between devices, turned_permute(): return lax.ppermute(value, axis, pairs)  1.2 us
    unnamed x6, local copies, waits for them, and re-layouts  0.95 us
  transfers between devices with their start and end apart: 11, of which 7 were waited for; matrix products, arithmetic and copies ran while one was open for 0% of the time, Pallas kernels for 4%

profile of v13, /device:TPU:0, one launch (start us, length us, event | category | flops | bytes accessed | tf_op | source)
XLA Modules:
  0.0 31.2 jit_solution(10980599941351657173)
XLA Ops:
  0.6 0.9 %copy-done = bf16[32,4096]{1,0:T(8,128)(2,1)S(1)} copy-done((bf16[32,4096]{1,0:T(8,128)(2,1)S(1)}, bf16[32,4096]{1,0:T(8,128)(2,1)}, u32[]{:S(2)}) %copy-start) | copy-done | bytes 262168
  1.6 0.7 %fan_grads.1 = bf16[32,32,128]{2,1,0:T(8,128)(2,1)} custom-call(bf16[32,4096]{1,0:T(8,128)(2,1)S(1)} %copy-done), custom_call_target="tpu_custom_call" | custom-call | tf_op jit(solution)/shard_map/fan_grads/pallas_call | solution.py:351
  2.3 7.3 %all-to-all-start = ((bf16[32,32,128]{2,1,0:T(8,128)(2,1)}), bf16[32,32,128]{2,1,0:T(8,128)(2,1)S(1)}, u32[]{:S(2)}, u32[]{:S(2)}) async-start(bf16[32,32,128]{2,1,0:T(8,128)(2,1)} %fan_grads.1), calls=%async_computation | async-start | bytes 524288 | tf_op jit(solution)/shard_map/all_to_all | solution.py:384
  9.6 0.3 %collective-permute-start = (bf16[128,1024]{1,0:T(8,128)(2,1)S(1)}, bf16[128,1024]{1,0:T(8,128)(2,1)S(1)}, u32[]{:S(2)}, u32[]{:S(2)}) collective-permute-start(bf16[128,1024]{1,0:T(8,128)(2,1)S(1)} %copy-done.1), channel_id=1, source_target_pairs={{0,4},{4,0},{8,12},{12,8},{16,20},{20,16},{24,28},{28,24},{1,5},{5... | collective-permute-start | bytes 786440 | tf_op jit(solution)/shard_map/ppermute | solution.py:72
  10.0 0.3 collective-permute-start.1
  10.2 1.0 %collective-permute-done.1.f_other_ref = bf16[64,64]{1,0:T(8,128)(2,1)S(1)} collective-permute-done((bf16[64,64]{1,0:T(8,128)(2,1)S(1)}, bf16[64,64]{1,0:T(8,128)(2,1)S(1)}, u32[]{:S(2)}, u32[]{:S(2)}) %collective-permute-start.1) | collective-permute-done | bytes 8224 | tf_op jit(solution)/shard_map/ppermute | solution.py:72
  11.3 0.1 fan_inputs.1
  11.4 2.7 %collective-permute-start.2 = (bf16[272,128]{1,0:T(8,128)(2,1)S(1)}, bf16[272,128]{1,0:T(8,128)(2,1)S(1)}, u32[]{:S(2)}, u32[]{:S(2)}) collective-permute-start(bf16[272,128]{1,0:T(8,128)(2,1)S(1)} %get-tuple-element.17), channel_id=1, source_target_pairs={{0,24},{4,28},{8,16},{12,20},{16,8},{20,12},{24,0},{28,4},{1,25},{... | collective-permute-start | bytes 208904 | tf_op jit(solution)/shard_map/ppermute | solution.py:72
  14.1 0.6 %collective-permute-start.3 = (bf16[272,128]{1,0:T(8,128)(2,1)S(1)}, bf16[272,128]{1,0:T(8,128)(2,1)S(1)}, u32[]{:S(2)}, u32[]{:S(2)}) collective-permute-start(bf16[272,128]{1,0:T(8,128)(2,1)S(1)} %get-tuple-element.18), channel_id=1, source_target_pairs={{0,16},{4,20},{8,24},{12,28},{16,0},{20,4},{24,8},{28,12},{1,17},{... | collective-permute-start | bytes 208904 | tf_op jit(solution)/shard_map/ppermute | solution.py:72
  14.7 0.3 collective-permute-start.4
  14.9 2.8 %collective-permute-done.2.refs_1_ = bf16[272,128]{1,0:T(8,128)(2,1)S(1)} collective-permute-done((bf16[272,128]{1,0:T(8,128)(2,1)S(1)}, bf16[272,128]{1,0:T(8,128)(2,1)S(1)}, u32[]{:S(2)}, u32[]{:S(2)}) %collective-permute-start.2) | collective-permute-done | bytes 69664 | tf_op jit(solution)/shard_map/ppermute | solution.py:72
  17.8 1.7 %collective-permute-done.3.refs_2_ = bf16[272,128]{1,0:T(8,128)(2,1)S(1)} collective-permute-done((bf16[272,128]{1,0:T(8,128)(2,1)S(1)}, bf16[272,128]{1,0:T(8,128)(2,1)S(1)}, u32[]{:S(2)}, u32[]{:S(2)}) %collective-permute-start.3) | collective-permute-done | bytes 69664 | tf_op jit(solution)/shard_map/ppermute | solution.py:72
  19.5 0.4 %all-to-all-done = bf16[32,32,128]{2,1,0:T(8,128)(2,1)S(1)} async-done(((bf16[32,32,128]{2,1,0:T(8,128)(2,1)}), bf16[32,32,128]{2,1,0:T(8,128)(2,1)S(1)}, u32[]{:S(2)}, u32[]{:S(2)}) %all-to-all-start) | async-done | bytes 262176 | tf_op jit(solution)/shard_map/all_to_all | solution.py:384
  19.9 2.8 %first.1 = (bf16[1664,128]{1,0:T(8,128)(2,1)S(1)}, bf16[4,16,128]{2,1,0:T(8,128)(2,1)S(1)}, bf16[512,512]{1,0:T(8,128)(2,1)S(1)}, bf16[64,512]{1,0:T(8,128)(2,1)...) custom-call(bf16[1024,128]{1,0:T(8,128)(2,1)S(1)} %bitcast.1, ...), custom_call_target="tpu_custom_call" | custom-call | tf_op jit(solution)/shard_map/first/pallas_call | solution.py:351
  22.7 0.4 %collective-permute-start.5 = (bf16[272,128]{1,0:T(8,128)(2,1)S(1)}, bf16[272,128]{1,0:T(8,128)(2,1)S(1)}, u32[]{:S(2)}, u32[]{:S(2)}) collective-permute-start(bf16[272,128]{1,0:T(8,128)(2,1)S(1)} %get-tuple-element.24), channel_id=1, source_target_pairs={{0,4},{4,0},{8,12},{12,8},{16,20},{20,16},{24,28},{28,24},{1,5},{5... | collective-permute-start | bytes 208904 | tf_op jit(solution)/shard_map/ppermute | solution.py:72
  23.1 0.9 %collective-permute-start.8 = (bf16[272,128]{1,0:T(8,128)(2,1)S(1)}, bf16[272,128]{1,0:T(8,128)(2,1)S(1)}, u32[]{:S(2)}, u32[]{:S(2)}) collective-permute-start(bf16[272,128]{1,0:T(8,128)(2,1)S(1)} %get-tuple-element.27), channel_id=1, source_target_pairs={{0,24},{4,28},{8,16},{12,20},{16,8},{20,12},{24,0},{28,4},{1,25},{... | collective-permute-start | bytes 208904 | tf_op jit(solution)/shard_map/ppermute | solution.py:72
  24.0 0.5 %near_keep.1.keep_ref = bf16[272,128]{1,0:T(8,128)(2,1)S(1)} custom-call(bf16[1664,128]{1,0:T(8,128)(2,1)S(1)} %get-tuple-element.20.dye_ref, bf16[512,512]{1,0:T(8,128)(2,1)S(1)} %get-tuple-element.21.toep_ref, bf16[64,512]{1,0:T(8,128)(2,1)S(1)} %get-tuple-element.22.rest_ref, bf16[4,16,128]{2,1,0:T(8,128)(2,1)S(1)} %get-tuple-element.28.taps_ref), custom_call_target="tpu_custom_call" | custom-call | tf_op jit(solution)/shard_map/near_keep/pallas_call | solution.py:351
  24.5 1.5 %collective-permute-start.6 = (bf16[272,128]{1,0:T(8,128)(2,1)S(1)}, bf16[272,128]{1,0:T(8,128)(2,1)S(1)}, u32[]{:S(2)}, u32[]{:S(2)}) collective-permute-start(bf16[272,128]{1,0:T(8,128)(2,1)S(1)} %get-tuple-element.25), channel_id=1, source_target_pairs={{0,16},{4,12},{8,24},{12,4},{16,0},{20,28},{24,8},{28,20},{1,17},{... | collective-permute-start | bytes 208904 | tf_op jit(solution)/shard_map/ppermute | solution.py:77
  26.0 1.1 %collective-permute-start.7 = (bf16[272,128]{1,0:T(8,128)(2,1)S(1)}, bf16[272,128]{1,0:T(8,128)(2,1)S(1)}, u32[]{:S(2)}, u32[]{:S(2)}) collective-permute-start(bf16[272,128]{1,0:T(8,128)(2,1)S(1)} %get-tuple-element.26), channel_id=1, source_target_pairs={{0,8},{4,20},{8,0},{12,28},{16,24},{20,4},{24,16},{28,12},{1,9},{5... | collective-permute-start | bytes 208904 | tf_op jit(solution)/shard_map/ppermute | solution.py:77
  27.2 1.4 %collective-permute-done.8.refs_1_.refs_3_ = bf16[272,128]{1,0:T(8,128)(2,1)S(1)} collective-permute-done((bf16[272,128]{1,0:T(8,128)(2,1)S(1)}, bf16[272,128]{1,0:T(8,128)(2,1)S(1)}, u32[]{:S(2)}, u32[]{:S(2)}) %collective-permute-start.8) | collective-permute-done | bytes 69664 | tf_op jit(solution)/shard_map/ppermute | solution.py:72
  28.5 0.5 %own.1.refs_0_.refs_2_ = bf16[272,128]{1,0:T(8,128)(2,1)S(1)} custom-call(bf16[1664,128]{1,0:T(8,128)(2,1)S(1)} %get-tuple-element.20.dye_ref, bf16[512,512]{1,0:T(8,128)(2,1)S(1)} %get-tuple-element.21.toep_ref, bf16[64,512]{1,0:T(8,128)(2,1)S(1)} %get-tuple-element.22.rest_ref, bf16[4,16,128]{2,1,0:T(8,128)(2,1)S(1)} %get-tuple-element.28.taps_ref), custom_call_target="tpu_custom_call" | custom-call | tf_op jit(solution)/shard_map/own/pallas_call | solution.py:351
  29.1 0.6 %collective-permute-done.6.refs_0_ = bf16[272,128]{1,0:T(8,128)(2,1)S(1)} collective-permute-done((bf16[272,128]{1,0:T(8,128)(2,1)S(1)}, bf16[272,128]{1,0:T(8,128)(2,1)S(1)}, u32[]{:S(2)}, u32[]{:S(2)}) %collective-permute-start.6) | collective-permute-done | bytes 69664 | tf_op jit(solution)/shard_map/ppermute | solution.py:77
  29.7 0.6 %collective-permute-done.7.refs_1_ = bf16[272,128]{1,0:T(8,128)(2,1)S(1)} collective-permute-done((bf16[272,128]{1,0:T(8,128)(2,1)S(1)}, bf16[272,128]{1,0:T(8,128)(2,1)S(1)}, u32[]{:S(2)}, u32[]{:S(2)}) %collective-permute-start.7) | collective-permute-done | bytes 69664 | tf_op jit(solution)/shard_map/ppermute | solution.py:77
  30.4 0.8 %unpack.1 = (bf16[128,1024]{1,0:T(8,128)(2,1)}, f32[64,64]{1,0:T(8,128)}) custom-call(bf16[272,128]{1,0:T(8,128)(2,1)S(1)} %collective-permute-done.6.refs_0_, bf16[272,128]{1,0:T(8,128)(2,1)S(1)} %collective-permute-done.7.refs_1_, bf16[272,128]{1,0:T(8,128)(2,1)S(1)} %own.1.refs_0_.refs_2_, bf16[272,128]{1,0:T(8,128)(2,1)S(1)} %collective-permute-done.8.refs_1_.refs_3_, ...), custom_call_target="tpu_custom_call" | custom-call | tf_op jit(solution)/shard_map/unpack/pallas_call | solution.py:351
  (12 shorter events, 0.2 us)
Async XLA Ops:
  0.6 1.0 %copy-start = (bf16[32,4096]{1,0:T(8,128)(2,1)S(1)}, bf16[32,4096]{1,0:T(8,128)(2,1)}, u32[]{:S(2)}) copy-start(bf16[32,4096]{1,0:T(8,128)(2,1)} %in_ref.1) | copy-start | bytes 786436
  2.3 7.3 %copy-start.1 = (bf16[128,1024]{1,0:T(8,128)(2,1)S(1)}, bf16[128,1024]{1,0:T(8,128)(2,1)}, u32[]{:S(2)}) copy-start(bf16[128,1024]{1,0:T(8,128)(2,1)} %x_own_ref.1) | copy-start | bytes 786436
  2.3 7.6 %copy-start.2 = (bf16[64,64]{1,0:T(8,128)(2,1)S(1)}, bf16[64,64]{1,0:T(8,128)(2,1)}, u32[]{:S(2)}) copy-start(bf16[64,64]{1,0:T(8,128)(2,1)} %f_own_ref.1) | copy-start | bytes 24580
  2.3 17.6 %all-to-all-start = ((bf16[32,32,128]{2,1,0:T(8,128)(2,1)}), bf16[32,32,128]{2,1,0:T(8,128)(2,1)S(1)}, u32[]{:S(2)}, u32[]{:S(2)}) async-start(bf16[32,32,128]{2,1,0:T(8,128)(2,1)} %fan_grads.1), calls=%async_computation | async-start | bytes 524288 | tf_op jit(solution)/shard_map/all_to_all | solution.py:384
  9.6 1.6 %collective-permute-start = (bf16[128,1024]{1,0:T(8,128)(2,1)S(1)}, bf16[128,1024]{1,0:T(8,128)(2,1)S(1)}, u32[]{:S(2)}, u32[]{:S(2)}) collective-permute-start(bf16[128,1024]{1,0:T(8,128)(2,1)S(1)} %copy-done.1), channel_id=1, source_target_pairs={{0,4},{4,0},{8,12},{12,8},{16,20},{20,16},{24,28},{28,24},{1,5},{5... | collective-permute-start | bytes 786440 | tf_op jit(solution)/shard_map/ppermute | solution.py:72
  10.0 1.3 %collective-permute-start.1 = (bf16[64,64]{1,0:T(8,128)(2,1)S(1)}, bf16[64,64]{1,0:T(8,128)(2,1)S(1)}, u32[]{:S(2)}, u32[]{:S(2)}) collective-permute-start(bf16[64,64]{1,0:T(8,128)(2,1)S(1)} %copy-done.2), channel_id=1, source_target_pairs={{0,4},{4,0},{8,12},{12,8},{16,20},{20,16},{24,28},{28,24},{1,5},{5... | collective-permute-start | bytes 24584 | tf_op jit(solution)/shard_map/ppermute | solution.py:72
  11.4 6.4 %collective-permute-start.2 = (bf16[272,128]{1,0:T(8,128)(2,1)S(1)}, bf16[272,128]{1,0:T(8,128)(2,1)S(1)}, u32[]{:S(2)}, u32[]{:S(2)}) collective-permute-start(bf16[272,128]{1,0:T(8,128)(2,1)S(1)} %get-tuple-element.17), channel_id=1, source_target_pairs={{0,24},{4,28},{8,16},{12,20},{16,8},{20,12},{24,0},{28,4},{1,25},{... | collective-permute-start | bytes 208904 | tf_op jit(solution)/shard_map/ppermute | solution.py:72
  14.1 5.4 %collective-permute-start.3 = (bf16[272,128]{1,0:T(8,128)(2,1)S(1)}, bf16[272,128]{1,0:T(8,128)(2,1)S(1)}, u32[]{:S(2)}, u32[]{:S(2)}) collective-permute-start(bf16[272,128]{1,0:T(8,128)(2,1)S(1)} %get-tuple-element.18), channel_id=1, source_target_pairs={{0,16},{4,20},{8,24},{12,28},{16,0},{20,4},{24,8},{28,12},{1,17},{... | collective-permute-start | bytes 208904 | tf_op jit(solution)/shard_map/ppermute | solution.py:72
  14.7 4.8 %collective-permute-start.4 = (bf16[272,128]{1,0:T(8,128)(2,1)S(1)}, bf16[272,128]{1,0:T(8,128)(2,1)S(1)}, u32[]{:S(2)}, u32[]{:S(2)}) collective-permute-start(bf16[272,128]{1,0:T(8,128)(2,1)S(1)} %get-tuple-element.19), channel_id=1, source_target_pairs={{0,8},{4,12},{8,0},{12,4},{16,24},{20,28},{24,16},{28,20},{1,9},{5... | collective-permute-start | bytes 208904 | tf_op jit(solution)/shard_map/ppermute | solution.py:72
  22.7 1.8 %collective-permute-start.5 = (bf16[272,128]{1,0:T(8,128)(2,1)S(1)}, bf16[272,128]{1,0:T(8,128)(2,1)S(1)}, u32[]{:S(2)}, u32[]{:S(2)}) collective-permute-start(bf16[272,128]{1,0:T(8,128)(2,1)S(1)} %get-tuple-element.24), channel_id=1, source_target_pairs={{0,4},{4,0},{8,12},{12,8},{16,20},{20,16},{24,28},{28,24},{1,5},{5... | collective-permute-start | bytes 208904 | tf_op jit(solution)/shard_map/ppermute | solution.py:72
  23.1 5.5 %collective-permute-start.8 = (bf16[272,128]{1,0:T(8,128)(2,1)S(1)}, bf16[272,128]{1,0:T(8,128)(2,1)S(1)}, u32[]{:S(2)}, u32[]{:S(2)}) collective-permute-start(bf16[272,128]{1,0:T(8,128)(2,1)S(1)} %get-tuple-element.27), channel_id=1, source_target_pairs={{0,24},{4,28},{8,16},{12,20},{16,8},{20,12},{24,0},{28,4},{1,25},{... | collective-permute-start | bytes 208904 | tf_op jit(solution)/shard_map/ppermute | solution.py:72
  24.5 5.2 %collective-permute-start.6 = (bf16[272,128]{1,0:T(8,128)(2,1)S(1)}, bf16[272,128]{1,0:T(8,128)(2,1)S(1)}, u32[]{:S(2)}, u32[]{:S(2)}) collective-permute-start(bf16[272,128]{1,0:T(8,128)(2,1)S(1)} %get-tuple-element.25), channel_id=1, source_target_pairs={{0,16},{4,12},{8,24},{12,4},{16,0},{20,28},{24,8},{28,20},{1,17},{... | collective-permute-start | bytes 208904 | tf_op jit(solution)/shard_map/ppermute | solution.py:77
  26.0 4.3 %collective-permute-start.7 = (bf16[272,128]{1,0:T(8,128)(2,1)S(1)}, bf16[272,128]{1,0:T(8,128)(2,1)S(1)}, u32[]{:S(2)}, u32[]{:S(2)}) collective-permute-start(bf16[272,128]{1,0:T(8,128)(2,1)S(1)} %get-tuple-element.26), channel_id=1, source_target_pairs={{0,8},{4,20},{8,0},{12,28},{16,24},{20,4},{24,16},{28,12},{1,9},{5... | collective-permute-start | bytes 208904 | tf_op jit(solution)/shard_map/ppermute | solution.py:77
  29.1 1.3 %collective-permute-start.9 = (bf16[272,128]{1,0:T(8,128)(2,1)S(1)}, bf16[272,128]{1,0:T(8,128)(2,1)S(1)}, u32[]{:S(2)}, u32[]{:S(2)}) collective-permute-start(bf16[272,128]{1,0:T(8,128)(2,1)S(1)} %swap.1), channel_id=1, source_target_pairs={{0,4},{4,0},{8,12},{12,8},{16,20},{20,16},{24,28},{28,24},{1,5},{5... | collective-permute-start | bytes 208904 | tf_op jit(solution)/shard_map/ppermute | solution.py:72

commit v14 on v13

--- a/solution.py
+++ b/solution.py
@@ -100,12 +100,11 @@
     return pl.ds(pl.multiple_of(index * size, 16), size)
 
 
-def fan_grads_kernel(n_seq, in_ref, out_ref):
+def fan_grads_kernel(n_seq, order, in_ref, out_ref):
     n_chan = out_ref.shape[0] // n_seq
-    for seq in range(n_seq):
-        for chan in range(n_chan):
-            start = (chan * n_seq + seq) * LANES
-            out_ref[seq * n_chan + chan] = in_ref[:, start : start + LANES]
+    for index, device in enumerate(order):
+        start = (device % n_chan * n_seq + device // n_chan) * LANES
+        out_ref[index] = in_ref[:, start : start + LANES]
 
 
 def fan_inputs_kernel(x_own_ref, x_other_ref, f_own_ref, f_other_ref, *refs):
@@ -190,7 +189,7 @@
         out_ref[index * SLAB : (index + 1) * SLAB] = total[:, columns]
 
 
-def first_kernel(n_seq, taps_here, far, near, dy_ref, *refs):
+def first_kernel(n_seq, taps_here, far, near, ahead, dy_ref, *refs):
     chips = n_seq // 2
     in_refs = refs[:chips]
     dye_ref, taps_ref, toep_ref, rest_ref, far_ref, near_ref, x_ref, filt_ref, lag_ref = refs[chips:]
@@ -201,8 +200,9 @@
     chip, core, _ = place()
 
     place_inputs(in_refs, taps_here, x_ref, filt_ref)
-    dye_ref[:tokens] = dy_ref[...]
-    dye_ref[tokens:] = dy_ref[:reach]
+    dye_ref[ahead:tokens] = dy_ref[: tokens - ahead]
+    dye_ref[:ahead] = dy_ref[tokens - ahead :]
+    dye_ref[tokens:] = dye_ref[:reach]
 
     rows = taps + STEP
     deep = DEPTH // LANES
@@ -373,15 +373,18 @@
         return jax.ShapeDtypeStruct(shape, jnp.bfloat16)
 
     unit = half(2 * block_len + EXTRA, LANES)
+    order = [(n_chan // 2 + index) % (n_seq * n_chan) for index in range(n_seq * n_chan)]
     x_other = xor_permute(layer_inputs, "seq", 1)
     f_other = xor_permute(filters, "seq", 1)
     (dy,) = local_call(
-        functools.partial(fan_grads_kernel, n_seq),
+        functools.partial(fan_grads_kernel, n_seq, order),
         [half(n_seq * n_chan, rows, LANES)],
         (out_grads,),
         "fan_grads",
     )
-    dy = lax.all_to_all(dy, ("seq", "chan"), split_axis=0, concat_axis=0, tiled=True)
+    dy = lax.all_to_all(
+        dy, ("seq", "chan"), split_axis=0, concat_axis=0, axis_index_groups=[order], tiled=True
+    )
     pieces = local_call(
         fan_inputs_kernel,
         [unit] * chips,
@@ -392,7 +395,7 @@
     near = masks[2:]
     near_shape = half(len(near) * (block_len + EXTRA // 2), LANES)
     dye, tap_parts, toeplitz, outside, far, send = local_call(
-        functools.partial(first_kernel, n_seq, taps_here, masks[1], near),
+        functools.partial(first_kernel, n_seq, taps_here, masks[1], near, order[0] * rows),
         [
             half(tokens + taps + LANES, LANES),
             half(chips, EXTRA, LANES),

time: 31.4 us -> 31.4 us (level)
  transfers between devices with their start and end apart: 11 -> 11, of which waited for: 7 -> 8; matrix products, arithmetic and copies ran while one was open for 0% -> 0% of each run, Pallas kernels for 4% -> 4%
where the time goes in v14:
time: 31.4 us; the launch traced here: 31.2 us
  starting transfers between devices  15.4 us (49%)
  waiting for transfers between devices  8.67 us (28%)
  Pallas kernels  5.41 us (17%)
  local copies, waits for them, and re-layouts  0.95 us (3%)
  between operations  0.72 us (2%)
    all_to_all x1, starting transfers between devices, by_channels(): lax.all_to_all(dy, ('seq', 'chan'), split_axis=0, concat_axis=0, axis_ind...  7.3 us
    ppermute x8, waiting for transfers between devices, xor_permute(): return lax.ppermute(value, axis, pairs)  7.08 us
    ppermute x8, starting transfers between devices, xor_permute(): return lax.ppermute(value, axis, pairs)  5.48 us
    pallas_call x8, Pallas kernels, local_call(): pl.pallas_call(kernel, out_shape=out_shape, in_specs=[whole] * len(operan...  5.41 us
    ppermute x2, starting transfers between devices, turned_permute(): return lax.ppermute(value, axis, pairs)  2.66 us
    ppermute x2, waiting for transfers between devices, turned_permute(): return lax.ppermute(value, axis, pairs)  1.18 us
    unnamed x6, local copies, waits for them, and re-layouts  0.95 us
  transfers between devices with their start and end apart: 11, of which 8 were waited for; matrix products, arithmetic and copies ran while one was open for 0% of the time, Pallas kernels for 4%

profile of v14, /device:TPU:0, one launch (start us, length us, event | category | flops | bytes accessed | tf_op | source)
XLA Modules:
  0.0 31.2 jit_solution(8718714237349608844)
XLA Ops:
  0.6 0.9 %copy-done = bf16[32,4096]{1,0:T(8,128)(2,1)S(1)} copy-done((bf16[32,4096]{1,0:T(8,128)(2,1)S(1)}, bf16[32,4096]{1,0:T(8,128)(2,1)}, u32[]{:S(2)}) %copy-start) | copy-done | bytes 262168
  1.6 0.7 %fan_grads.1 = bf16[32,32,128]{2,1,0:T(8,128)(2,1)} custom-call(bf16[32,4096]{1,0:T(8,128)(2,1)S(1)} %copy-done), custom_call_target="tpu_custom_call" | custom-call | tf_op jit(solution)/shard_map/fan_grads/pallas_call | solution.py:351
  2.3 7.3 %all-to-all-start = ((bf16[32,32,128]{2,1,0:T(8,128)(2,1)}), bf16[32,32,128]{2,1,0:T(8,128)(2,1)S(1)}, u32[]{:S(2)}, u32[]{:S(2)}) async-start(bf16[32,32,128]{2,1,0:T(8,128)(2,1)} %fan_grads.1), calls=%async_computation | async-start | bytes 524288 | tf_op jit(solution)/shard_map/all_to_all | solution.py:385
  9.6 0.3 %collective-permute-start = (bf16[128,1024]{1,0:T(8,128)(2,1)S(1)}, bf16[128,1024]{1,0:T(8,128)(2,1)S(1)}, u32[]{:S(2)}, u32[]{:S(2)}) collective-permute-start(bf16[128,1024]{1,0:T(8,128)(2,1)S(1)} %copy-done.1), channel_id=1, source_target_pairs={{0,4},{4,0},{8,12},{12,8},{16,20},{20,16},{24,28},{28,24},{1,5},{5... | collective-permute-start | bytes 786440 | tf_op jit(solution)/shard_map/ppermute | solution.py:72
  10.0 0.3 collective-permute-start.1
  10.2 1.0 %collective-permute-done.1.f_other_ref = bf16[64,64]{1,0:T(8,128)(2,1)S(1)} collective-permute-done((bf16[64,64]{1,0:T(8,128)(2,1)S(1)}, bf16[64,64]{1,0:T(8,128)(2,1)S(1)}, u32[]{:S(2)}, u32[]{:S(2)}) %collective-permute-start.1) | collective-permute-done | bytes 8224 | tf_op jit(solution)/shard_map/ppermute | solution.py:72
  11.3 0.1 fan_inputs.1
  11.4 2.7 %collective-permute-start.2 = (bf16[272,128]{1,0:T(8,128)(2,1)S(1)}, bf16[272,128]{1,0:T(8,128)(2,1)S(1)}, u32[]{:S(2)}, u32[]{:S(2)}) collective-permute-start(bf16[272,128]{1,0:T(8,128)(2,1)S(1)} %get-tuple-element.17), channel_id=1, source_target_pairs={{0,24},{4,28},{8,16},{12,20},{16,8},{20,12},{24,0},{28,4},{1,25},{... | collective-permute-start | bytes 208904 | tf_op jit(solution)/shard_map/ppermute | solution.py:72
  14.1 0.6 %collective-permute-start.3 = (bf16[272,128]{1,0:T(8,128)(2,1)S(1)}, bf16[272,128]{1,0:T(8,128)(2,1)S(1)}, u32[]{:S(2)}, u32[]{:S(2)}) collective-permute-start(bf16[272,128]{1,0:T(8,128)(2,1)S(1)} %get-tuple-element.18), channel_id=1, source_target_pairs={{0,16},{4,20},{8,24},{12,28},{16,0},{20,4},{24,8},{28,12},{1,17},{... | collective-permute-start | bytes 208904 | tf_op jit(solution)/shard_map/ppermute | solution.py:72
  14.7 0.3 collective-permute-start.4
  14.9 2.8 %collective-permute-done.2.refs_1_ = bf16[272,128]{1,0:T(8,128)(2,1)S(1)} collective-permute-done((bf16[272,128]{1,0:T(8,128)(2,1)S(1)}, bf16[272,128]{1,0:T(8,128)(2,1)S(1)}, u32[]{:S(2)}, u32[]{:S(2)}) %collective-permute-start.2) | collective-permute-done | bytes 69664 | tf_op jit(solution)/shard_map/ppermute | solution.py:72
  17.8 1.7 %collective-permute-done.3.refs_2_ = bf16[272,128]{1,0:T(8,128)(2,1)S(1)} collective-permute-done((bf16[272,128]{1,0:T(8,128)(2,1)S(1)}, bf16[272,128]{1,0:T(8,128)(2,1)S(1)}, u32[]{:S(2)}, u32[]{:S(2)}) %collective-permute-start.3) | collective-permute-done | bytes 69664 | tf_op jit(solution)/shard_map/ppermute | solution.py:72
  19.5 0.4 %all-to-all-done = bf16[32,32,128]{2,1,0:T(8,128)(2,1)S(1)} async-done(((bf16[32,32,128]{2,1,0:T(8,128)(2,1)}), bf16[32,32,128]{2,1,0:T(8,128)(2,1)S(1)}, u32[]{:S(2)}, u32[]{:S(2)}) %all-to-all-start) | async-done | bytes 262176 | tf_op jit(solution)/shard_map/all_to_all | solution.py:385
  19.9 2.8 %first.1 = (bf16[1664,128]{1,0:T(8,128)(2,1)S(1)}, bf16[4,16,128]{2,1,0:T(8,128)(2,1)S(1)}, bf16[512,512]{1,0:T(8,128)(2,1)S(1)}, bf16[64,512]{1,0:T(8,128)(2,1)...) custom-call(bf16[1024,128]{1,0:T(8,128)(2,1)S(1)} %bitcast.1, ...), custom_call_target="tpu_custom_call" | custom-call | tf_op jit(solution)/shard_map/first/pallas_call | solution.py:351
  22.7 0.4 %collective-permute-start.5 = (bf16[272,128]{1,0:T(8,128)(2,1)S(1)}, bf16[272,128]{1,0:T(8,128)(2,1)S(1)}, u32[]{:S(2)}, u32[]{:S(2)}) collective-permute-start(bf16[272,128]{1,0:T(8,128)(2,1)S(1)} %get-tuple-element.24), channel_id=1, source_target_pairs={{0,4},{4,0},{8,12},{12,8},{16,20},{20,16},{24,28},{28,24},{1,5},{5... | collective-permute-start | bytes 208904 | tf_op jit(solution)/shard_map/ppermute | solution.py:72
  23.1 0.9 %collective-permute-start.8 = (bf16[272,128]{1,0:T(8,128)(2,1)S(1)}, bf16[272,128]{1,0:T(8,128)(2,1)S(1)}, u32[]{:S(2)}, u32[]{:S(2)}) collective-permute-start(bf16[272,128]{1,0:T(8,128)(2,1)S(1)} %get-tuple-element.27), channel_id=1, source_target_pairs={{0,24},{4,28},{8,16},{12,20},{16,8},{20,12},{24,0},{28,4},{1,25},{... | collective-permute-start | bytes 208904 | tf_op jit(solution)/shard_map/ppermute | solution.py:72
  24.0 0.5 %near_keep.1.keep_ref = bf16[272,128]{1,0:T(8,128)(2,1)S(1)} custom-call(bf16[1664,128]{1,0:T(8,128)(2,1)S(1)} %get-tuple-element.20.dye_ref, bf16[512,512]{1,0:T(8,128)(2,1)S(1)} %get-tuple-element.21.toep_ref, bf16[64,512]{1,0:T(8,128)(2,1)S(1)} %get-tuple-element.22.rest_ref, bf16[4,16,128]{2,1,0:T(8,128)(2,1)S(1)} %get-tuple-element.28.taps_ref), custom_call_target="tpu_custom_call" | custom-call | tf_op jit(solution)/shard_map/near_keep/pallas_call | solution.py:351
  24.5 1.5 %collective-permute-start.6 = (bf16[272,128]{1,0:T(8,128)(2,1)S(1)}, bf16[272,128]{1,0:T(8,128)(2,1)S(1)}, u32[]{:S(2)}, u32[]{:S(2)}) collective-permute-start(bf16[272,128]{1,0:T(8,128)(2,1)S(1)} %get-tuple-element.25), channel_id=1, source_target_pairs={{0,16},{4,12},{8,24},{12,4},{16,0},{20,28},{24,8},{28,20},{1,17},{... | collective-permute-start | bytes 208904 | tf_op jit(solution)/shard_map/ppermute | solution.py:77
  26.0 1.1 %collective-permute-start.7 = (bf16[272,128]{1,0:T(8,128)(2,1)S(1)}, bf16[272,128]{1,0:T(8,128)(2,1)S(1)}, u32[]{:S(2)}, u32[]{:S(2)}) collective-permute-start(bf16[272,128]{1,0:T(8,128)(2,1)S(1)} %get-tuple-element.26), channel_id=1, source_target_pairs={{0,8},{4,20},{8,0},{12,28},{16,24},{20,4},{24,16},{28,12},{1,9},{5... | collective-permute-start | bytes 208904 | tf_op jit(solution)/shard_map/ppermute | solution.py:77
  27.2 1.4 %collective-permute-done.8.refs_1_.refs_3_ = bf16[272,128]{1,0:T(8,128)(2,1)S(1)} collective-permute-done((bf16[272,128]{1,0:T(8,128)(2,1)S(1)}, bf16[272,128]{1,0:T(8,128)(2,1)S(1)}, u32[]{:S(2)}, u32[]{:S(2)}) %collective-permute-start.8) | collective-permute-done | bytes 69664 | tf_op jit(solution)/shard_map/ppermute | solution.py:72
  28.6 0.5 %own.1.refs_0_.refs_2_ = bf16[272,128]{1,0:T(8,128)(2,1)S(1)} custom-call(bf16[1664,128]{1,0:T(8,128)(2,1)S(1)} %get-tuple-element.20.dye_ref, bf16[512,512]{1,0:T(8,128)(2,1)S(1)} %get-tuple-element.21.toep_ref, bf16[64,512]{1,0:T(8,128)(2,1)S(1)} %get-tuple-element.22.rest_ref, bf16[4,16,128]{2,1,0:T(8,128)(2,1)S(1)} %get-tuple-element.28.taps_ref), custom_call_target="tpu_custom_call" | custom-call | tf_op jit(solution)/shard_map/own/pallas_call | solution.py:351
  29.2 0.6 %collective-permute-done.6.refs_0_ = bf16[272,128]{1,0:T(8,128)(2,1)S(1)} collective-permute-done((bf16[272,128]{1,0:T(8,128)(2,1)S(1)}, bf16[272,128]{1,0:T(8,128)(2,1)S(1)}, u32[]{:S(2)}, u32[]{:S(2)}) %collective-permute-start.6) | collective-permute-done | bytes 69664 | tf_op jit(solution)/shard_map/ppermute | solution.py:77
  29.7 0.6 %collective-permute-done.7.refs_1_ = bf16[272,128]{1,0:T(8,128)(2,1)S(1)} collective-permute-done((bf16[272,128]{1,0:T(8,128)(2,1)S(1)}, bf16[272,128]{1,0:T(8,128)(2,1)S(1)}, u32[]{:S(2)}, u32[]{:S(2)}) %collective-permute-start.7) | collective-permute-done | bytes 69664 | tf_op jit(solution)/shard_map/ppermute | solution.py:77
  30.4 0.8 %unpack.1 = (bf16[128,1024]{1,0:T(8,128)(2,1)}, f32[64,64]{1,0:T(8,128)}) custom-call(bf16[272,128]{1,0:T(8,128)(2,1)S(1)} %collective-permute-done.6.refs_0_, bf16[272,128]{1,0:T(8,128)(2,1)S(1)} %collective-permute-done.7.refs_1_, bf16[272,128]{1,0:T(8,128)(2,1)S(1)} %own.1.refs_0_.refs_2_, bf16[272,128]{1,0:T(8,128)(2,1)S(1)} %collective-permute-done.8.refs_1_.refs_3_, ...), custom_call_target="tpu_custom_call" | custom-call | tf_op jit(solution)/shard_map/unpack/pallas_call | solution.py:351
  (12 shorter events, 0.2 us)
Async XLA Ops:
  0.6 1.0 %copy-start = (bf16[32,4096]{1,0:T(8,128)(2,1)S(1)}, bf16[32,4096]{1,0:T(8,128)(2,1)}, u32[]{:S(2)}) copy-start(bf16[32,4096]{1,0:T(8,128)(2,1)} %in_ref.1) | copy-start | bytes 786436
  2.3 7.3 %copy-start.1 = (bf16[128,1024]{1,0:T(8,128)(2,1)S(1)}, bf16[128,1024]{1,0:T(8,128)(2,1)}, u32[]{:S(2)}) copy-start(bf16[128,1024]{1,0:T(8,128)(2,1)} %x_own_ref.1) | copy-start | bytes 786436
  2.3 7.6 %copy-start.2 = (bf16[64,64]{1,0:T(8,128)(2,1)S(1)}, bf16[64,64]{1,0:T(8,128)(2,1)}, u32[]{:S(2)}) copy-start(bf16[64,64]{1,0:T(8,128)(2,1)} %f_own_ref.1) | copy-start | bytes 24580
  2.3 17.6 %all-to-all-start = ((bf16[32,32,128]{2,1,0:T(8,128)(2,1)}), bf16[32,32,128]{2,1,0:T(8,128)(2,1)S(1)}, u32[]{:S(2)}, u32[]{:S(2)}) async-start(bf16[32,32,128]{2,1,0:T(8,128)(2,1)} %fan_grads.1), calls=%async_computation | async-start | bytes 524288 | tf_op jit(solution)/shard_map/all_to_all | solution.py:385
  9.6 1.6 %collective-permute-start = (bf16[128,1024]{1,0:T(8,128)(2,1)S(1)}, bf16[128,1024]{1,0:T(8,128)(2,1)S(1)}, u32[]{:S(2)}, u32[]{:S(2)}) collective-permute-start(bf16[128,1024]{1,0:T(8,128)(2,1)S(1)} %copy-done.1), channel_id=1, source_target_pairs={{0,4},{4,0},{8,12},{12,8},{16,20},{20,16},{24,28},{28,24},{1,5},{5... | collective-permute-start | bytes 786440 | tf_op jit(solution)/shard_map/ppermute | solution.py:72
  10.0 1.3 %collective-permute-start.1 = (bf16[64,64]{1,0:T(8,128)(2,1)S(1)}, bf16[64,64]{1,0:T(8,128)(2,1)S(1)}, u32[]{:S(2)}, u32[]{:S(2)}) collective-permute-start(bf16[64,64]{1,0:T(8,128)(2,1)S(1)} %copy-done.2), channel_id=1, source_target_pairs={{0,4},{4,0},{8,12},{12,8},{16,20},{20,16},{24,28},{28,24},{1,5},{5... | collective-permute-start | bytes 24584 | tf_op jit(solution)/shard_map/ppermute | solution.py:72
  11.4 6.4 %collective-permute-start.2 = (bf16[272,128]{1,0:T(8,128)(2,1)S(1)}, bf16[272,128]{1,0:T(8,128)(2,1)S(1)}, u32[]{:S(2)}, u32[]{:S(2)}) collective-permute-start(bf16[272,128]{1,0:T(8,128)(2,1)S(1)} %get-tuple-element.17), channel_id=1, source_target_pairs={{0,24},{4,28},{8,16},{12,20},{16,8},{20,12},{24,0},{28,4},{1,25},{... | collective-permute-start | bytes 208904 | tf_op jit(solution)/shard_map/ppermute | solution.py:72
  14.1 5.4 %collective-permute-start.3 = (bf16[272,128]{1,0:T(8,128)(2,1)S(1)}, bf16[272,128]{1,0:T(8,128)(2,1)S(1)}, u32[]{:S(2)}, u32[]{:S(2)}) collective-permute-start(bf16[272,128]{1,0:T(8,128)(2,1)S(1)} %get-tuple-element.18), channel_id=1, source_target_pairs={{0,16},{4,20},{8,24},{12,28},{16,0},{20,4},{24,8},{28,12},{1,17},{... | collective-permute-start | bytes 208904 | tf_op jit(solution)/shard_map/ppermute | solution.py:72
  14.7 4.8 %collective-permute-start.4 = (bf16[272,128]{1,0:T(8,128)(2,1)S(1)}, bf16[272,128]{1,0:T(8,128)(2,1)S(1)}, u32[]{:S(2)}, u32[]{:S(2)}) collective-permute-start(bf16[272,128]{1,0:T(8,128)(2,1)S(1)} %get-tuple-element.19), channel_id=1, source_target_pairs={{0,8},{4,12},{8,0},{12,4},{16,24},{20,28},{24,16},{28,20},{1,9},{5... | collective-permute-start | bytes 208904 | tf_op jit(solution)/shard_map/ppermute | solution.py:72
  22.7 1.8 %collective-permute-start.5 = (bf16[272,128]{1,0:T(8,128)(2,1)S(1)}, bf16[272,128]{1,0:T(8,128)(2,1)S(1)}, u32[]{:S(2)}, u32[]{:S(2)}) collective-permute-start(bf16[272,128]{1,0:T(8,128)(2,1)S(1)} %get-tuple-element.24), channel_id=1, source_target_pairs={{0,4},{4,0},{8,12},{12,8},{16,20},{20,16},{24,28},{28,24},{1,5},{5... | collective-permute-start | bytes 208904 | tf_op jit(solution)/shard_map/ppermute | solution.py:72
  23.1 5.5 %collective-permute-start.8 = (bf16[272,128]{1,0:T(8,128)(2,1)S(1)}, bf16[272,128]{1,0:T(8,128)(2,1)S(1)}, u32[]{:S(2)}, u32[]{:S(2)}) collective-permute-start(bf16[272,128]{1,0:T(8,128)(2,1)S(1)} %get-tuple-element.27), channel_id=1, source_target_pairs={{0,24},{4,28},{8,16},{12,20},{16,8},{20,12},{24,0},{28,4},{1,25},{... | collective-permute-start | bytes 208904 | tf_op jit(solution)/shard_map/ppermute | solution.py:72
  24.5 5.2 %collective-permute-start.6 = (bf16[272,128]{1,0:T(8,128)(2,1)S(1)}, bf16[272,128]{1,0:T(8,128)(2,1)S(1)}, u32[]{:S(2)}, u32[]{:S(2)}) collective-permute-start(bf16[272,128]{1,0:T(8,128)(2,1)S(1)} %get-tuple-element.25), channel_id=1, source_target_pairs={{0,16},{4,12},{8,24},{12,4},{16,0},{20,28},{24,8},{28,20},{1,17},{... | collective-permute-start | bytes 208904 | tf_op jit(solution)/shard_map/ppermute | solution.py:77
  26.0 4.3 %collective-permute-start.7 = (bf16[272,128]{1,0:T(8,128)(2,1)S(1)}, bf16[272,128]{1,0:T(8,128)(2,1)S(1)}, u32[]{:S(2)}, u32[]{:S(2)}) collective-permute-start(bf16[272,128]{1,0:T(8,128)(2,1)S(1)} %get-tuple-element.26), channel_id=1, source_target_pairs={{0,8},{4,20},{8,0},{12,28},{16,24},{20,4},{24,16},{28,12},{1,9},{5... | collective-permute-start | bytes 208904 | tf_op jit(solution)/shard_map/ppermute | solution.py:77
  29.1 1.3 %collective-permute-start.9 = (bf16[272,128]{1,0:T(8,128)(2,1)S(1)}, bf16[272,128]{1,0:T(8,128)(2,1)S(1)}, u32[]{:S(2)}, u32[]{:S(2)}) collective-permute-start(bf16[272,128]{1,0:T(8,128)(2,1)S(1)} %swap.1), channel_id=1, source_target_pairs={{0,4},{4,0},{8,12},{12,8},{16,20},{20,16},{24,28},{28,24},{1,5},{5... | collective-permute-start | bytes 208904 | tf_op jit(solution)/shard_map/ppermute | solution.py:72

commit v15 on v13

--- a/solution.py
+++ b/solution.py
@@ -418,11 +418,11 @@
         "near_keep",
     )
     pieces = local_call(near_pieces_kernel, [unit] * len(near), (keep, got), "near_pieces")
+    tap_parts, _ = lax.optimization_barrier((tap_parts, pieces[0]))
     pieces = [
         turned_permute(piece, "seq", [2 * bits for bits in near[index:] + near[:index]])
         for index, piece in enumerate(pieces)
     ]
-    far, tap_parts = lax.optimization_barrier((far, tap_parts))
     (own,) = local_call(own_kernel, [unit], (dye, toeplitz, outside, tap_parts), "own")
     (send,) = local_call(
         swap_kernel, [half(2 * block_len + EXTRA, LANES)], (own, far), "swap"

time: 31.4 us -> 31.9 us (1.016)
  waiting for transfers between devices: 8.66 us -> 9.2 us
    ppermute x2, waiting for transfers between devices: 1.2 us -> 2.34 us  [turned_permute(): return lax.ppermute(value, axis, pairs)]
    ppermute x8, waiting for transfers between devices: 7.06 us -> 6.45 us  [xor_permute(): return lax.ppermute(value, axis, pairs)]
  transfers between devices with their start and end apart: 11 -> 11, of which waited for: 7 -> 6; matrix products, arithmetic and copies ran while one was open for 0% -> 0% of each run, Pallas kernels for 4% -> 4%
where the time goes in v15:
time: 31.9 us; the launch traced here: 31.7 us
  starting transfers between devices  15.4 us (48%)
  waiting for transfers between devices  9.2 us (29%)
  Pallas kernels  5.41 us (17%)
  local copies, waits for them, and re-layouts  0.95 us (3%)
  between operations  0.71 us (2%)
    all_to_all x1, starting transfers between devices, by_channels(): lax.all_to_all(dy, ('seq', 'chan'), split_axis=0, concat_axis=0, tiled=True)  7.3 us
    ppermute x8, waiting for transfers between devices, xor_permute(): return lax.ppermute(value, axis, pairs)  6.45 us
    ppermute x8, starting transfers between devices, xor_permute(): return lax.ppermute(value, axis, pairs)  5.42 us
    pallas_call x8, Pallas kernels, local_call(): pl.pallas_call(kernel, out_shape=out_shape, in_specs=[whole] * len(operan...  5.41 us
    ppermute x2, starting transfers between devices, turned_permute(): return lax.ppermute(value, axis, pairs)  2.72 us
    ppermute x2, waiting for transfers between devices, turned_permute(): return lax.ppermute(value, axis, pairs)  2.34 us
    unnamed x6, local copies, waits for them, and re-layouts  0.95 us
  transfers between devices with their start and end apart: 11, of which 6 were waited for; matrix products, arithmetic and copies ran while one was open for 0% of the time, Pallas kernels for 4%

profile of v15, /device:TPU:0, one launch (start us, length us, event | category | flops | bytes accessed | tf_op | source)
XLA Modules:
  0.0 31.7 jit_solution(177140617671615074)
XLA Ops:
  0.6 0.9 %copy-done = bf16[32,4096]{1,0:T(8,128)(2,1)S(1)} copy-done((bf16[32,4096]{1,0:T(8,128)(2,1)S(1)}, bf16[32,4096]{1,0:T(8,128)(2,1)}, u32[]{:S(2)}) %copy-start) | copy-done | bytes 262168
  1.6 0.7 %fan_grads.1 = bf16[32,32,128]{2,1,0:T(8,128)(2,1)} custom-call(bf16[32,4096]{1,0:T(8,128)(2,1)S(1)} %copy-done), custom_call_target="tpu_custom_call" | custom-call | tf_op jit(solution)/shard_map/fan_grads/pallas_call | solution.py:351
  2.3 7.3 %all-to-all-start = ((bf16[32,32,128]{2,1,0:T(8,128)(2,1)}), bf16[32,32,128]{2,1,0:T(8,128)(2,1)S(1)}, u32[]{:S(2)}, u32[]{:S(2)}) async-start(bf16[32,32,128]{2,1,0:T(8,128)(2,1)} %fan_grads.1), calls=%async_computation | async-start | bytes 524288 | tf_op jit(solution)/shard_map/all_to_all | solution.py:384
  9.6 0.3 collective-permute-start
  10.0 0.3 collective-permute-start.1
  10.2 1.0 %collective-permute-done.1.f_other_ref = bf16[64,64]{1,0:T(8,128)(2,1)S(1)} collective-permute-done((bf16[64,64]{1,0:T(8,128)(2,1)S(1)}, bf16[64,64]{1,0:T(8,128)(2,1)S(1)}, u32[]{:S(2)}, u32[]{:S(2)}) %collective-permute-start.1) | collective-permute-done | bytes 8224 | tf_op jit(solution)/shard_map/ppermute | solution.py:72
  11.3 0.0 collective-permute-done.x_other_ref
  11.3 0.1 fan_inputs.1
  11.4 2.7 %collective-permute-start.2 = (bf16[272,128]{1,0:T(8,128)(2,1)S(1)}, bf16[272,128]{1,0:T(8,128)(2,1)S(1)}, u32[]{:S(2)}, u32[]{:S(2)}) collective-permute-start(bf16[272,128]{1,0:T(8,128)(2,1)S(1)} %get-tuple-element.16), channel_id=1, source_target_pairs={{0,24},{4,28},{8,16},{12,20},{16,8},{20,12},{24,0},{28,4},{1,25},{... | collective-permute-start | bytes 208904 | tf_op jit(solution)/shard_map/ppermute | solution.py:72
  14.1 0.6 %collective-permute-start.3 = (bf16[272,128]{1,0:T(8,128)(2,1)S(1)}, bf16[272,128]{1,0:T(8,128)(2,1)S(1)}, u32[]{:S(2)}, u32[]{:S(2)}) collective-permute-start(bf16[272,128]{1,0:T(8,128)(2,1)S(1)} %get-tuple-element.17), channel_id=1, source_target_pairs={{0,16},{4,20},{8,24},{12,28},{16,0},{20,4},{24,8},{28,12},{1,17},{... | collective-permute-start | bytes 208904 | tf_op jit(solution)/shard_map/ppermute | solution.py:72
  14.7 0.3 collective-permute-start.4
  14.9 2.8 %collective-permute-done.2.refs_1_ = bf16[272,128]{1,0:T(8,128)(2,1)S(1)} collective-permute-done((bf16[272,128]{1,0:T(8,128)(2,1)S(1)}, bf16[272,128]{1,0:T(8,128)(2,1)S(1)}, u32[]{:S(2)}, u32[]{:S(2)}) %collective-permute-start.2) | collective-permute-done | bytes 69664 | tf_op jit(solution)/shard_map/ppermute | solution.py:72
  17.8 1.7 %collective-permute-done.3.refs_2_ = bf16[272,128]{1,0:T(8,128)(2,1)S(1)} collective-permute-done((bf16[272,128]{1,0:T(8,128)(2,1)S(1)}, bf16[272,128]{1,0:T(8,128)(2,1)S(1)}, u32[]{:S(2)}, u32[]{:S(2)}) %collective-permute-start.3) | collective-permute-done | bytes 69664 | tf_op jit(solution)/shard_map/ppermute | solution.py:72
  19.5 0.4 %all-to-all-done = bf16[32,32,128]{2,1,0:T(8,128)(2,1)S(1)} async-done(((bf16[32,32,128]{2,1,0:T(8,128)(2,1)}), bf16[32,32,128]{2,1,0:T(8,128)(2,1)S(1)}, u32[]{:S(2)}, u32[]{:S(2)}) %all-to-all-start) | async-done | bytes 262176 | tf_op jit(solution)/shard_map/all_to_all | solution.py:384
  19.9 2.8 %first.1 = (bf16[1664,128]{1,0:T(8,128)(2,1)S(1)}, bf16[4,16,128]{2,1,0:T(8,128)(2,1)S(1)}, bf16[512,512]{1,0:T(8,128)(2,1)S(1)}, bf16[64,512]{1,0:T(8,128)(2,1)...) custom-call(bf16[1024,128]{1,0:T(8,128)(2,1)S(1)} %bitcast.1, ...), custom_call_target="tpu_custom_call" | custom-call | tf_op jit(solution)/shard_map/first/pallas_call | solution.py:351
  22.7 0.4 %collective-permute-start.5 = (bf16[272,128]{1,0:T(8,128)(2,1)S(1)}, bf16[272,128]{1,0:T(8,128)(2,1)S(1)}, u32[]{:S(2)}, u32[]{:S(2)}) collective-permute-start(bf16[272,128]{1,0:T(8,128)(2,1)S(1)} %get-tuple-element.23), channel_id=1, source_target_pairs={{0,4},{4,0},{8,12},{12,8},{16,20},{20,16},{24,28},{28,24},{1,5},{5... | collective-permute-start | bytes 208904 | tf_op jit(solution)/shard_map/ppermute | solution.py:72
  23.1 0.9 %collective-permute-start.8 = (bf16[272,128]{1,0:T(8,128)(2,1)S(1)}, bf16[272,128]{1,0:T(8,128)(2,1)S(1)}, u32[]{:S(2)}, u32[]{:S(2)}) collective-permute-start(bf16[272,128]{1,0:T(8,128)(2,1)S(1)} %get-tuple-element.27), channel_id=1, source_target_pairs={{0,24},{4,28},{8,16},{12,20},{16,8},{20,12},{24,0},{28,4},{1,25},{... | collective-permute-start | bytes 208904 | tf_op jit(solution)/shard_map/ppermute | solution.py:72
  24.0 0.5 %near_keep.1.keep_ref = bf16[272,128]{1,0:T(8,128)(2,1)S(1)} custom-call(bf16[1664,128]{1,0:T(8,128)(2,1)S(1)} %get-tuple-element.19.dye_ref, bf16[512,512]{1,0:T(8,128)(2,1)S(1)} %get-tuple-element.20.toep_ref, bf16[64,512]{1,0:T(8,128)(2,1)S(1)} %get-tuple-element.21.rest_ref, bf16[4,16,128]{2,1,0:T(8,128)(2,1)S(1)} %get-tuple-element.26.taps_ref), custom_call_target="tpu_custom_call" | custom-call | tf_op jit(solution)/shard_map/near_keep/pallas_call | solution.py:351
  24.5 1.5 %collective-permute-start.6 = (bf16[272,128]{1,0:T(8,128)(2,1)S(1)}, bf16[272,128]{1,0:T(8,128)(2,1)S(1)}, u32[]{:S(2)}, u32[]{:S(2)}) collective-permute-start(bf16[272,128]{1,0:T(8,128)(2,1)S(1)} %get-tuple-element.24), channel_id=1, source_target_pairs={{0,16},{4,12},{8,24},{12,4},{16,0},{20,28},{24,8},{28,20},{1,17},{... | collective-permute-start | bytes 208904 | tf_op jit(solution)/shard_map/ppermute | solution.py:77
  26.0 0.5 %own.1.refs_0_.refs_2_ = bf16[272,128]{1,0:T(8,128)(2,1)S(1)} custom-call(bf16[1664,128]{1,0:T(8,128)(2,1)S(1)} %get-tuple-element.19.dye_ref, bf16[512,512]{1,0:T(8,128)(2,1)S(1)} %get-tuple-element.20.toep_ref, bf16[64,512]{1,0:T(8,128)(2,1)S(1)} %get-tuple-element.21.rest_ref, bf16[4,16,128]{2,1,0:T(8,128)(2,1)S(1)} %get-tuple-element.26.taps_ref), custom_call_target="tpu_custom_call" | custom-call | tf_op jit(solution)/shard_map/own/pallas_call | solution.py:351
  26.5 1.2 %collective-permute-start.7 = (bf16[272,128]{1,0:T(8,128)(2,1)S(1)}, bf16[272,128]{1,0:T(8,128)(2,1)S(1)}, u32[]{:S(2)}, u32[]{:S(2)}) collective-permute-start(bf16[272,128]{1,0:T(8,128)(2,1)S(1)} %get-tuple-element.25), channel_id=1, source_target_pairs={{0,8},{4,20},{8,0},{12,28},{16,24},{20,4},{24,16},{28,12},{1,9},{5... | collective-permute-start | bytes 208904 | tf_op jit(solution)/shard_map/ppermute | solution.py:77
  27.7 0.8 %collective-permute-done.8.refs_1_.refs_3_ = bf16[272,128]{1,0:T(8,128)(2,1)S(1)} collective-permute-done((bf16[272,128]{1,0:T(8,128)(2,1)S(1)}, bf16[272,128]{1,0:T(8,128)(2,1)S(1)}, u32[]{:S(2)}, u32[]{:S(2)}) %collective-permute-start.8) | collective-permute-done | bytes 69664 | tf_op jit(solution)/shard_map/ppermute | solution.py:72
  28.6 2.3 %collective-permute-done.7.refs_1_ = bf16[272,128]{1,0:T(8,128)(2,1)S(1)} collective-permute-done((bf16[272,128]{1,0:T(8,128)(2,1)S(1)}, bf16[272,128]{1,0:T(8,128)(2,1)S(1)}, u32[]{:S(2)}, u32[]{:S(2)}) %collective-permute-start.7) | collective-permute-done | bytes 69664 | tf_op jit(solution)/shard_map/ppermute | solution.py:77
  30.9 0.8 %unpack.1 = (bf16[128,1024]{1,0:T(8,128)(2,1)}, f32[64,64]{1,0:T(8,128)}) custom-call(bf16[272,128]{1,0:T(8,128)(2,1)S(1)} %collective-permute-done.6.refs_0_, bf16[272,128]{1,0:T(8,128)(2,1)S(1)} %collective-permute-done.7.refs_1_, bf16[272,128]{1,0:T(8,128)(2,1)S(1)} %own.1.refs_0_.refs_2_, bf16[272,128]{1,0:T(8,128)(2,1)S(1)} %collective-permute-done.8.refs_1_.refs_3_, ...), custom_call_target="tpu_custom_call" | custom-call | tf_op jit(solution)/shard_map/unpack/pallas_call | solution.py:351
  (12 shorter events, 0.1 us)
Async XLA Ops:
  0.6 1.0 %copy-start = (bf16[32,4096]{1,0:T(8,128)(2,1)S(1)}, bf16[32,4096]{1,0:T(8,128)(2,1)}, u32[]{:S(2)}) copy-start(bf16[32,4096]{1,0:T(8,128)(2,1)} %in_ref.1) | copy-start | bytes 786436
  2.3 7.3 %copy-start.1 = (bf16[128,1024]{1,0:T(8,128)(2,1)S(1)}, bf16[128,1024]{1,0:T(8,128)(2,1)}, u32[]{:S(2)}) copy-start(bf16[128,1024]{1,0:T(8,128)(2,1)} %x_own_ref.1) | copy-start | bytes 786436
  2.3 7.6 %copy-start.2 = (bf16[64,64]{1,0:T(8,128)(2,1)S(1)}, bf16[64,64]{1,0:T(8,128)(2,1)}, u32[]{:S(2)}) copy-start(bf16[64,64]{1,0:T(8,128)(2,1)} %f_own_ref.1) | copy-start | bytes 24580
  2.3 17.6 %all-to-all-start = ((bf16[32,32,128]{2,1,0:T(8,128)(2,1)}), bf16[32,32,128]{2,1,0:T(8,128)(2,1)S(1)}, u32[]{:S(2)}, u32[]{:S(2)}) async-start(bf16[32,32,128]{2,1,0:T(8,128)(2,1)} %fan_grads.1), calls=%async_computation | async-start | bytes 524288 | tf_op jit(solution)/shard_map/all_to_all | solution.py:384
  9.6 1.6 %collective-permute-start = (bf16[128,1024]{1,0:T(8,128)(2,1)S(1)}, bf16[128,1024]{1,0:T(8,128)(2,1)S(1)}, u32[]{:S(2)}, u32[]{:S(2)}) collective-permute-start(bf16[128,1024]{1,0:T(8,128)(2,1)S(1)} %copy-done.1), channel_id=1, source_target_pairs={{0,4},{4,0},{8,12},{12,8},{16,20},{20,16},{24,28},{28,24},{1,5},{5... | collective-permute-start | bytes 786440 | tf_op jit(solution)/shard_map/ppermute | solution.py:72
  10.0 1.3 %collective-permute-start.1 = (bf16[64,64]{1,0:T(8,128)(2,1)S(1)}, bf16[64,64]{1,0:T(8,128)(2,1)S(1)}, u32[]{:S(2)}, u32[]{:S(2)}) collective-permute-start(bf16[64,64]{1,0:T(8,128)(2,1)S(1)} %copy-done.2), channel_id=1, source_target_pairs={{0,4},{4,0},{8,12},{12,8},{16,20},{20,16},{24,28},{28,24},{1,5},{5... | collective-permute-start | bytes 24584 | tf_op jit(solution)/shard_map/ppermute | solution.py:72
  11.4 6.4 %collective-permute-start.2 = (bf16[272,128]{1,0:T(8,128)(2,1)S(1)}, bf16[272,128]{1,0:T(8,128)(2,1)S(1)}, u32[]{:S(2)}, u32[]{:S(2)}) collective-permute-start(bf16[272,128]{1,0:T(8,128)(2,1)S(1)} %get-tuple-element.16), channel_id=1, source_target_pairs={{0,24},{4,28},{8,16},{12,20},{16,8},{20,12},{24,0},{28,4},{1,25},{... | collective-permute-start | bytes 208904 | tf_op jit(solution)/shard_map/ppermute | solution.py:72
  14.1 5.4 %collective-permute-start.3 = (bf16[272,128]{1,0:T(8,128)(2,1)S(1)}, bf16[272,128]{1,0:T(8,128)(2,1)S(1)}, u32[]{:S(2)}, u32[]{:S(2)}) collective-permute-start(bf16[272,128]{1,0:T(8,128)(2,1)S(1)} %get-tuple-element.17), channel_id=1, source_target_pairs={{0,16},{4,20},{8,24},{12,28},{16,0},{20,4},{24,8},{28,12},{1,17},{... | collective-permute-start | bytes 208904 | tf_op jit(solution)/shard_map/ppermute | solution.py:72
  14.7 4.8 %collective-permute-start.4 = (bf16[272,128]{1,0:T(8,128)(2,1)S(1)}, bf16[272,128]{1,0:T(8,128)(2,1)S(1)}, u32[]{:S(2)}, u32[]{:S(2)}) collective-permute-start(bf16[272,128]{1,0:T(8,128)(2,1)S(1)} %get-tuple-element.18), channel_id=1, source_target_pairs={{0,8},{4,12},{8,0},{12,4},{16,24},{20,28},{24,16},{28,20},{1,9},{5... | collective-permute-start | bytes 208904 | tf_op jit(solution)/shard_map/ppermute | solution.py:72
  22.7 1.8 %collective-permute-start.5 = (bf16[272,128]{1,0:T(8,128)(2,1)S(1)}, bf16[272,128]{1,0:T(8,128)(2,1)S(1)}, u32[]{:S(2)}, u32[]{:S(2)}) collective-permute-start(bf16[272,128]{1,0:T(8,128)(2,1)S(1)} %get-tuple-element.23), channel_id=1, source_target_pairs={{0,4},{4,0},{8,12},{12,8},{16,20},{20,16},{24,28},{28,24},{1,5},{5... | collective-permute-start | bytes 208904 | tf_op jit(solution)/shard_map/ppermute | solution.py:72
  23.1 5.5 %collective-permute-start.8 = (bf16[272,128]{1,0:T(8,128)(2,1)S(1)}, bf16[272,128]{1,0:T(8,128)(2,1)S(1)}, u32[]{:S(2)}, u32[]{:S(2)}) collective-permute-start(bf16[272,128]{1,0:T(8,128)(2,1)S(1)} %get-tuple-element.27), channel_id=1, source_target_pairs={{0,24},{4,28},{8,16},{12,20},{16,8},{20,12},{24,0},{28,4},{1,25},{... | collective-permute-start | bytes 208904 | tf_op jit(solution)/shard_map/ppermute | solution.py:72
  24.5 6.4 %collective-permute-start.6 = (bf16[272,128]{1,0:T(8,128)(2,1)S(1)}, bf16[272,128]{1,0:T(8,128)(2,1)S(1)}, u32[]{:S(2)}, u32[]{:S(2)}) collective-permute-start(bf16[272,128]{1,0:T(8,128)(2,1)S(1)} %get-tuple-element.24), channel_id=1, source_target_pairs={{0,16},{4,12},{8,24},{12,4},{16,0},{20,28},{24,8},{28,20},{1,17},{... | collective-permute-start | bytes 208904 | tf_op jit(solution)/shard_map/ppermute | solution.py:77
  26.5 4.4 %collective-permute-start.7 = (bf16[272,128]{1,0:T(8,128)(2,1)S(1)}, bf16[272,128]{1,0:T(8,128)(2,1)S(1)}, u32[]{:S(2)}, u32[]{:S(2)}) collective-permute-start(bf16[272,128]{1,0:T(8,128)(2,1)S(1)} %get-tuple-element.25), channel_id=1, source_target_pairs={{0,8},{4,20},{8,0},{12,28},{16,24},{20,4},{24,16},{28,12},{1,9},{5... | collective-permute-start | bytes 208904 | tf_op jit(solution)/shard_map/ppermute | solution.py:77
  28.6 2.4 %collective-permute-start.9 = (bf16[272,128]{1,0:T(8,128)(2,1)S(1)}, bf16[272,128]{1,0:T(8,128)(2,1)S(1)}, u32[]{:S(2)}, u32[]{:S(2)}) collective-permute-start(bf16[272,128]{1,0:T(8,128)(2,1)S(1)} %swap.1), channel_id=1, source_target_pairs={{0,4},{4,0},{8,12},{12,8},{16,20},{20,16},{24,28},{28,24},{1,5},{5... | collective-permute-start | bytes 208904 | tf_op jit(solution)/shard_map/ppermute | solution.py:72

commit v16 on v13

--- a/solution.py
+++ b/solution.py
@@ -8,10 +8,9 @@
 from jax.sharding import PartitionSpec as P
 
 LANES = 128
-STEP = 32
+STEP = 64
 SLAB = 64
 EXTRA = 16
-DEPTH = 4096
 VMEM_LIMIT = 40 * 1024 * 1024
 
 
@@ -193,51 +192,51 @@
 def first_kernel(n_seq, taps_here, far, near, dy_ref, *refs):
     chips = n_seq // 2
     in_refs = refs[:chips]
-    dye_ref, taps_ref, toep_ref, rest_ref, far_ref, near_ref, x_ref, filt_ref, lag_ref = refs[chips:]
+    dye_ref, taps_ref, toep_ref, rest_ref, far_ref, near_ref, x_ref, filt_ref, turned_ref = refs[chips:]
     tokens = dy_ref.shape[0]
     groups = EXTRA // 2
     taps = n_seq * taps_here
     reach = taps + LANES
+    per_group = LANES // groups
     chip, core, _ = place()
 
     place_inputs(in_refs, taps_here, x_ref, filt_ref)
     dye_ref[:tokens] = dy_ref[...]
     dye_ref[tokens:] = dy_ref[:reach]
 
-    rows = taps + STEP
-    deep = DEPTH // LANES
-    group_in = group_of_lane(STEP, DEPTH, groups)
-    lag_ref[rows:] = jnp.zeros((reach - rows, groups * STEP), jnp.float32)
-    for at in range(0, tokens, STEP * deep):
-        starts = range(at, at + STEP * deep, STEP)
-        windows = jnp.concatenate([dye_ref[row : row + rows] for row in starts], axis=1)
-        inputs = jnp.concatenate([x_ref[row : row + STEP] for row in starts], axis=1)
-        masked = jnp.concatenate(
-            [jnp.where(group_in == group, inputs, jnp.zeros_like(inputs)) for group in range(groups)],
+    pairs = tokens // (2 * STEP)
+    wide = (pairs - 1) * LANES + reach
+    for odd in range(2):
+        turned_ref[odd] = dye_ref[odd * STEP : odd * STEP + wide].T
+    inputs = x_ref[...].T
+    toeplitz_rows(filt_ref, toep_ref, rest_ref)
+    products = []
+    for group in range(groups):
+        own = slice(group * per_group, (group + 1) * per_group)
+        sides = jnp.concatenate(
+            [inputs[own, pair * LANES : (pair + 1) * LANES] for pair in range(pairs)], axis=0
+        ).T
+        sides = jnp.concatenate([sides[:STEP], sides[STEP:]], axis=1)
+        windows = jnp.concatenate(
+            [
+                turned_ref[odd, own, pair * LANES : pair * LANES + reach]
+                for odd in range(2)
+                for pair in range(pairs)
+            ],
             axis=0,
         )
-        part = lax.dot_general(
-            windows, masked, (((1,), (1,)), ((), ())), preferred_element_type=jnp.float32
-        )
-        if at == 0:
-            lag_ref[:rows] = part
-        else:
-            lag_ref[:rows] += part
-        if at == 0:
-            toeplitz_rows(filt_ref, toep_ref, rest_ref)
+        products.append(jnp.dot(sides, windows, preferred_element_type=jnp.float32))
 
     block_len = tokens // n_seq
     seqs = [2 * (chip ^ far) + (core ^ flip) for flip in range(2)]
     tokens_of(seqs, dye_ref, toep_ref, rest_ref, far_ref, block_len)
     seqs = [2 * (chip ^ bits) + (core ^ 1) for bits in near]
     tokens_of(seqs, dye_ref, toep_ref, rest_ref, near_ref, block_len)
-    lags = lag_ref[...].T
     eights = []
-    for group in range(groups):
-        at = group * STEP
-        rows = lags[at : at + 8]
+    for lags in products:
+        rows = lags[:8]
         for high in range(1, STEP // 8):
-            rows = rows + roll_left(lags[at + 8 * high : at + 8 * high + 8], 8 * high)
+            rows = rows + roll_left(lags[8 * high : 8 * high + 8], 8 * high)
         eights.append(rows)
     skew = jnp.concatenate(eights, axis=0)
     row_in = lax.broadcasted_iota(jnp.int32, skew.shape, 0) % 8
@@ -406,7 +405,7 @@
         [
             pltpu.VMEM((tokens, LANES), jnp.bfloat16),
             pltpu.VMEM((chips, groups, LANES), jnp.float32),
-            pltpu.VMEM((taps + LANES, groups * STEP), jnp.float32),
+            pltpu.VMEM((2, LANES, tokens + taps), jnp.bfloat16),
         ],
     )
     far = xor_permute(far, "seq", 2 * masks[1])
@@ -452,7 +451,7 @@
             and 2 * taps_here == LANES
             and out_grads.shape[0] % 16 == 0
             and layer_inputs.shape[0] % SLAB == 0
-            and n_seq * layer_inputs.shape[0] % (STEP * DEPTH // LANES) == 0
+            and layer_inputs.shape[0] == 2 * STEP
             and n_seq * taps_here + LANES <= n_seq * layer_inputs.shape[0]
         )
         if fits:

time: 31.4 us -> 30.3 us (0.965)
  Pallas kernels: 5.42 us -> 4.32 us
    pallas_call x8, Pallas kernels: 5.42 us -> 4.32 us  [local_call(): pl.pallas_call(kernel, out_shape=out_shape, in_specs=[whole] * len(operan...]
  transfers between devices with their start and end apart: 11 -> 11, of which waited for: 7 -> 8; matrix products, arithmetic and copies ran while one was open for 0% -> 0% of each run, Pallas kernels for 4% -> 4%
where the time goes in v16:
time: 30.3 us; the launch traced here: 30.1 us
  starting transfers between devices  15.4 us (51%)
  waiting for transfers between devices  8.66 us (29%)
  Pallas kernels  4.32 us (14%)
  local copies, waits for them, and re-layouts  0.95 us (3%)
  between operations  0.72 us (2%)
    all_to_all x1, starting transfers between devices, by_channels(): lax.all_to_all(dy, ('seq', 'chan'), split_axis=0, concat_axis=0, tiled=True)  7.3 us
    ppermute x8, waiting for transfers between devices, xor_permute(): return lax.ppermute(value, axis, pairs)  7.06 us
    ppermute x8, starting transfers between devices, xor_permute(): return lax.ppermute(value, axis, pairs)  5.47 us
    pallas_call x8, Pallas kernels, local_call(): pl.pallas_call(kernel, out_shape=out_shape, in_specs=[whole] * len(operan...  4.32 us
    ppermute x2, starting transfers between devices, turned_permute(): return lax.ppermute(value, axis, pairs)  2.66 us
    ppermute x2, waiting for transfers between devices, turned_permute(): return lax.ppermute(value, axis, pairs)  1.19 us
    unnamed x6, local copies, waits for them, and re-layouts  0.95 us
  transfers between devices with their start and end apart: 11, of which 8 were waited for; matrix products, arithmetic and copies ran while one was open for 0% of the time, Pallas kernels for 4%

profile of v16, /device:TPU:0, one launch (start us, length us, event | category | flops | bytes accessed | tf_op | source)
XLA Modules:
  0.0 30.1 jit_solution(11407502799999059356)
XLA Ops:
  0.6 0.9 %copy-done = bf16[32,4096]{1,0:T(8,128)(2,1)S(1)} copy-done((bf16[32,4096]{1,0:T(8,128)(2,1)S(1)}, bf16[32,4096]{1,0:T(8,128)(2,1)}, u32[]{:S(2)}) %copy-start) | copy-done | bytes 262168
  1.6 0.7 %fan_grads.1 = bf16[32,32,128]{2,1,0:T(8,128)(2,1)} custom-call(bf16[32,4096]{1,0:T(8,128)(2,1)S(1)} %copy-done), custom_call_target="tpu_custom_call" | custom-call | tf_op jit(solution)/shard_map/fan_grads/pallas_call | solution.py:350
  2.3 7.3 %all-to-all-start = ((bf16[32,32,128]{2,1,0:T(8,128)(2,1)}), bf16[32,32,128]{2,1,0:T(8,128)(2,1)S(1)}, u32[]{:S(2)}, u32[]{:S(2)}) async-start(bf16[32,32,128]{2,1,0:T(8,128)(2,1)} %fan_grads.1), calls=%async_computation | async-start | bytes 524288 | tf_op jit(solution)/shard_map/all_to_all | solution.py:383
  9.6 0.3 %collective-permute-start = (bf16[128,1024]{1,0:T(8,128)(2,1)S(1)}, bf16[128,1024]{1,0:T(8,128)(2,1)S(1)}, u32[]{:S(2)}, u32[]{:S(2)}) collective-permute-start(bf16[128,1024]{1,0:T(8,128)(2,1)S(1)} %copy-done.1), channel_id=1, source_target_pairs={{0,4},{4,0},{8,12},{12,8},{16,20},{20,16},{24,28},{28,24},{1,5},{5... | collective-permute-start | bytes 786440 | tf_op jit(solution)/shard_map/ppermute | solution.py:71
  10.0 0.3 collective-permute-start.1
  10.2 1.0 %collective-permute-done.1.f_other_ref = bf16[64,64]{1,0:T(8,128)(2,1)S(1)} collective-permute-done((bf16[64,64]{1,0:T(8,128)(2,1)S(1)}, bf16[64,64]{1,0:T(8,128)(2,1)S(1)}, u32[]{:S(2)}, u32[]{:S(2)}) %collective-permute-start.1) | collective-permute-done | bytes 8224 | tf_op jit(solution)/shard_map/ppermute | solution.py:71
  11.3 0.1 fan_inputs.1
  11.4 2.7 %collective-permute-start.2 = (bf16[272,128]{1,0:T(8,128)(2,1)S(1)}, bf16[272,128]{1,0:T(8,128)(2,1)S(1)}, u32[]{:S(2)}, u32[]{:S(2)}) collective-permute-start(bf16[272,128]{1,0:T(8,128)(2,1)S(1)} %get-tuple-element.17), channel_id=1, source_target_pairs={{0,24},{4,28},{8,16},{12,20},{16,8},{20,12},{24,0},{28,4},{1,25},{... | collective-permute-start | bytes 208904 | tf_op jit(solution)/shard_map/ppermute | solution.py:71
  14.1 0.6 %collective-permute-start.3 = (bf16[272,128]{1,0:T(8,128)(2,1)S(1)}, bf16[272,128]{1,0:T(8,128)(2,1)S(1)}, u32[]{:S(2)}, u32[]{:S(2)}) collective-permute-start(bf16[272,128]{1,0:T(8,128)(2,1)S(1)} %get-tuple-element.18), channel_id=1, source_target_pairs={{0,16},{4,20},{8,24},{12,28},{16,0},{20,4},{24,8},{28,12},{1,17},{... | collective-permute-start | bytes 208904 | tf_op jit(solution)/shard_map/ppermute | solution.py:71
  14.7 0.3 collective-permute-start.4
  14.9 2.8 %collective-permute-done.2.refs_1_ = bf16[272,128]{1,0:T(8,128)(2,1)S(1)} collective-permute-done((bf16[272,128]{1,0:T(8,128)(2,1)S(1)}, bf16[272,128]{1,0:T(8,128)(2,1)S(1)}, u32[]{:S(2)}, u32[]{:S(2)}) %collective-permute-start.2) | collective-permute-done | bytes 69664 | tf_op jit(solution)/shard_map/ppermute | solution.py:71
  17.8 1.7 %collective-permute-done.3.refs_2_ = bf16[272,128]{1,0:T(8,128)(2,1)S(1)} collective-permute-done((bf16[272,128]{1,0:T(8,128)(2,1)S(1)}, bf16[272,128]{1,0:T(8,128)(2,1)S(1)}, u32[]{:S(2)}, u32[]{:S(2)}) %collective-permute-start.3) | collective-permute-done | bytes 69664 | tf_op jit(solution)/shard_map/ppermute | solution.py:71
  19.5 0.4 %all-to-all-done = bf16[32,32,128]{2,1,0:T(8,128)(2,1)S(1)} async-done(((bf16[32,32,128]{2,1,0:T(8,128)(2,1)}), bf16[32,32,128]{2,1,0:T(8,128)(2,1)S(1)}, u32[]{:S(2)}, u32[]{:S(2)}) %all-to-all-start) | async-done | bytes 262176 | tf_op jit(solution)/shard_map/all_to_all | solution.py:383
  19.9 1.7 %first.1 = (bf16[1664,128]{1,0:T(8,128)(2,1)S(1)}, bf16[4,16,128]{2,1,0:T(8,128)(2,1)S(1)}, bf16[512,512]{1,0:T(8,128)(2,1)S(1)}, bf16[64,512]{1,0:T(8,128)(2,1)...) custom-call(bf16[1024,128]{1,0:T(8,128)(2,1)S(1)} %bitcast.1, ...), custom_call_target="tpu_custom_call" | custom-call | tf_op jit(solution)/shard_map/first/pallas_call | solution.py:350
  21.6 0.4 %collective-permute-start.5 = (bf16[272,128]{1,0:T(8,128)(2,1)S(1)}, bf16[272,128]{1,0:T(8,128)(2,1)S(1)}, u32[]{:S(2)}, u32[]{:S(2)}) collective-permute-start(bf16[272,128]{1,0:T(8,128)(2,1)S(1)} %get-tuple-element.24), channel_id=1, source_target_pairs={{0,4},{4,0},{8,12},{12,8},{16,20},{20,16},{24,28},{28,24},{1,5},{5... | collective-permute-start | bytes 208904 | tf_op jit(solution)/shard_map/ppermute | solution.py:71
  22.0 0.9 %collective-permute-start.8 = (bf16[272,128]{1,0:T(8,128)(2,1)S(1)}, bf16[272,128]{1,0:T(8,128)(2,1)S(1)}, u32[]{:S(2)}, u32[]{:S(2)}) collective-permute-start(bf16[272,128]{1,0:T(8,128)(2,1)S(1)} %get-tuple-element.27), channel_id=1, source_target_pairs={{0,24},{4,28},{8,16},{12,20},{16,8},{20,12},{24,0},{28,4},{1,25},{... | collective-permute-start | bytes 208904 | tf_op jit(solution)/shard_map/ppermute | solution.py:71
  22.9 0.5 %near_keep.1.keep_ref = bf16[272,128]{1,0:T(8,128)(2,1)S(1)} custom-call(bf16[1664,128]{1,0:T(8,128)(2,1)S(1)} %get-tuple-element.20.dye_ref, bf16[512,512]{1,0:T(8,128)(2,1)S(1)} %get-tuple-element.21.toep_ref, bf16[64,512]{1,0:T(8,128)(2,1)S(1)} %get-tuple-element.22.rest_ref, bf16[4,16,128]{2,1,0:T(8,128)(2,1)S(1)} %get-tuple-element.28.taps_ref), custom_call_target="tpu_custom_call" | custom-call | tf_op jit(solution)/shard_map/near_keep/pallas_call | solution.py:350
  23.4 1.5 %collective-permute-start.6 = (bf16[272,128]{1,0:T(8,128)(2,1)S(1)}, bf16[272,128]{1,0:T(8,128)(2,1)S(1)}, u32[]{:S(2)}, u32[]{:S(2)}) collective-permute-start(bf16[272,128]{1,0:T(8,128)(2,1)S(1)} %get-tuple-element.25), channel_id=1, source_target_pairs={{0,16},{4,12},{8,24},{12,4},{16,0},{20,28},{24,8},{28,20},{1,17},{... | collective-permute-start | bytes 208904 | tf_op jit(solution)/shard_map/ppermute | solution.py:76
  24.9 1.1 %collective-permute-start.7 = (bf16[272,128]{1,0:T(8,128)(2,1)S(1)}, bf16[272,128]{1,0:T(8,128)(2,1)S(1)}, u32[]{:S(2)}, u32[]{:S(2)}) collective-permute-start(bf16[272,128]{1,0:T(8,128)(2,1)S(1)} %get-tuple-element.26), channel_id=1, source_target_pairs={{0,8},{4,20},{8,0},{12,28},{16,24},{20,4},{24,16},{28,12},{1,9},{5... | collective-permute-start | bytes 208904 | tf_op jit(solution)/shard_map/ppermute | solution.py:76
  26.1 1.4 %collective-permute-done.8.refs_1_.refs_3_ = bf16[272,128]{1,0:T(8,128)(2,1)S(1)} collective-permute-done((bf16[272,128]{1,0:T(8,128)(2,1)S(1)}, bf16[272,128]{1,0:T(8,128)(2,1)S(1)}, u32[]{:S(2)}, u32[]{:S(2)}) %collective-permute-start.8) | collective-permute-done | bytes 69664 | tf_op jit(solution)/shard_map/ppermute | solution.py:71
  27.5 0.5 %own.1.refs_0_.refs_2_ = bf16[272,128]{1,0:T(8,128)(2,1)S(1)} custom-call(bf16[1664,128]{1,0:T(8,128)(2,1)S(1)} %get-tuple-element.20.dye_ref, bf16[512,512]{1,0:T(8,128)(2,1)S(1)} %get-tuple-element.21.toep_ref, bf16[64,512]{1,0:T(8,128)(2,1)S(1)} %get-tuple-element.22.rest_ref, bf16[4,16,128]{2,1,0:T(8,128)(2,1)S(1)} %get-tuple-element.28.taps_ref), custom_call_target="tpu_custom_call" | custom-call | tf_op jit(solution)/shard_map/own/pallas_call | solution.py:350
  28.0 0.6 %collective-permute-done.6.refs_0_ = bf16[272,128]{1,0:T(8,128)(2,1)S(1)} collective-permute-done((bf16[272,128]{1,0:T(8,128)(2,1)S(1)}, bf16[272,128]{1,0:T(8,128)(2,1)S(1)}, u32[]{:S(2)}, u32[]{:S(2)}) %collective-permute-start.6) | collective-permute-done | bytes 69664 | tf_op jit(solution)/shard_map/ppermute | solution.py:76
  28.6 0.6 %collective-permute-done.7.refs_1_ = bf16[272,128]{1,0:T(8,128)(2,1)S(1)} collective-permute-done((bf16[272,128]{1,0:T(8,128)(2,1)S(1)}, bf16[272,128]{1,0:T(8,128)(2,1)S(1)}, u32[]{:S(2)}, u32[]{:S(2)}) %collective-permute-start.7) | collective-permute-done | bytes 69664 | tf_op jit(solution)/shard_map/ppermute | solution.py:76
  29.3 0.8 %unpack.1 = (bf16[128,1024]{1,0:T(8,128)(2,1)}, f32[64,64]{1,0:T(8,128)}) custom-call(bf16[272,128]{1,0:T(8,128)(2,1)S(1)} %collective-permute-done.6.refs_0_, bf16[272,128]{1,0:T(8,128)(2,1)S(1)} %collective-permute-done.7.refs_1_, bf16[272,128]{1,0:T(8,128)(2,1)S(1)} %own.1.refs_0_.refs_2_, bf16[272,128]{1,0:T(8,128)(2,1)S(1)} %collective-permute-done.8.refs_1_.refs_3_, ...), custom_call_target="tpu_custom_call" | custom-call | tf_op jit(solution)/shard_map/unpack/pallas_call | solution.py:350
  (12 shorter events, 0.2 us)
Async XLA Ops:
  0.6 1.0 %copy-start = (bf16[32,4096]{1,0:T(8,128)(2,1)S(1)}, bf16[32,4096]{1,0:T(8,128)(2,1)}, u32[]{:S(2)}) copy-start(bf16[32,4096]{1,0:T(8,128)(2,1)} %in_ref.1) | copy-start | bytes 786436
  2.3 7.3 %copy-start.1 = (bf16[128,1024]{1,0:T(8,128)(2,1)S(1)}, bf16[128,1024]{1,0:T(8,128)(2,1)}, u32[]{:S(2)}) copy-start(bf16[128,1024]{1,0:T(8,128)(2,1)} %x_own_ref.1) | copy-start | bytes 786436
  2.3 7.6 %copy-start.2 = (bf16[64,64]{1,0:T(8,128)(2,1)S(1)}, bf16[64,64]{1,0:T(8,128)(2,1)}, u32[]{:S(2)}) copy-start(bf16[64,64]{1,0:T(8,128)(2,1)} %f_own_ref.1) | copy-start | bytes 24580
  2.3 17.6 %all-to-all-start = ((bf16[32,32,128]{2,1,0:T(8,128)(2,1)}), bf16[32,32,128]{2,1,0:T(8,128)(2,1)S(1)}, u32[]{:S(2)}, u32[]{:S(2)}) async-start(bf16[32,32,128]{2,1,0:T(8,128)(2,1)} %fan_grads.1), calls=%async_computation | async-start | bytes 524288 | tf_op jit(solution)/shard_map/all_to_all | solution.py:383
  9.6 1.6 %collective-permute-start = (bf16[128,1024]{1,0:T(8,128)(2,1)S(1)}, bf16[128,1024]{1,0:T(8,128)(2,1)S(1)}, u32[]{:S(2)}, u32[]{:S(2)}) collective-permute-start(bf16[128,1024]{1,0:T(8,128)(2,1)S(1)} %copy-done.1), channel_id=1, source_target_pairs={{0,4},{4,0},{8,12},{12,8},{16,20},{20,16},{24,28},{28,24},{1,5},{5... | collective-permute-start | bytes 786440 | tf_op jit(solution)/shard_map/ppermute | solution.py:71
  10.0 1.3 %collective-permute-start.1 = (bf16[64,64]{1,0:T(8,128)(2,1)S(1)}, bf16[64,64]{1,0:T(8,128)(2,1)S(1)}, u32[]{:S(2)}, u32[]{:S(2)}) collective-permute-start(bf16[64,64]{1,0:T(8,128)(2,1)S(1)} %copy-done.2), channel_id=1, source_target_pairs={{0,4},{4,0},{8,12},{12,8},{16,20},{20,16},{24,28},{28,24},{1,5},{5... | collective-permute-start | bytes 24584 | tf_op jit(solution)/shard_map/ppermute | solution.py:71
  11.4 6.4 %collective-permute-start.2 = (bf16[272,128]{1,0:T(8,128)(2,1)S(1)}, bf16[272,128]{1,0:T(8,128)(2,1)S(1)}, u32[]{:S(2)}, u32[]{:S(2)}) collective-permute-start(bf16[272,128]{1,0:T(8,128)(2,1)S(1)} %get-tuple-element.17), channel_id=1, source_target_pairs={{0,24},{4,28},{8,16},{12,20},{16,8},{20,12},{24,0},{28,4},{1,25},{... | collective-permute-start | bytes 208904 | tf_op jit(solution)/shard_map/ppermute | solution.py:71
  14.1 5.4 %collective-permute-start.3 = (bf16[272,128]{1,0:T(8,128)(2,1)S(1)}, bf16[272,128]{1,0:T(8,128)(2,1)S(1)}, u32[]{:S(2)}, u32[]{:S(2)}) collective-permute-start(bf16[272,128]{1,0:T(8,128)(2,1)S(1)} %get-tuple-element.18), channel_id=1, source_target_pairs={{0,16},{4,20},{8,24},{12,28},{16,0},{20,4},{24,8},{28,12},{1,17},{... | collective-permute-start | bytes 208904 | tf_op jit(solution)/shard_map/ppermute | solution.py:71
  14.7 4.8 %collective-permute-start.4 = (bf16[272,128]{1,0:T(8,128)(2,1)S(1)}, bf16[272,128]{1,0:T(8,128)(2,1)S(1)}, u32[]{:S(2)}, u32[]{:S(2)}) collective-permute-start(bf16[272,128]{1,0:T(8,128)(2,1)S(1)} %get-tuple-element.19), channel_id=1, source_target_pairs={{0,8},{4,12},{8,0},{12,4},{16,24},{20,28},{24,16},{28,20},{1,9},{5... | collective-permute-start | bytes 208904 | tf_op jit(solution)/shard_map/ppermute | solution.py:71
  21.6 1.8 %collective-permute-start.5 = (bf16[272,128]{1,0:T(8,128)(2,1)S(1)}, bf16[272,128]{1,0:T(8,128)(2,1)S(1)}, u32[]{:S(2)}, u32[]{:S(2)}) collective-permute-start(bf16[272,128]{1,0:T(8,128)(2,1)S(1)} %get-tuple-element.24), channel_id=1, source_target_pairs={{0,4},{4,0},{8,12},{12,8},{16,20},{20,16},{24,28},{28,24},{1,5},{5... | collective-permute-start | bytes 208904 | tf_op jit(solution)/shard_map/ppermute | solution.py:71
  22.0 5.5 %collective-permute-start.8 = (bf16[272,128]{1,0:T(8,128)(2,1)S(1)}, bf16[272,128]{1,0:T(8,128)(2,1)S(1)}, u32[]{:S(2)}, u32[]{:S(2)}) collective-permute-start(bf16[272,128]{1,0:T(8,128)(2,1)S(1)} %get-tuple-element.27), channel_id=1, source_target_pairs={{0,24},{4,28},{8,16},{12,20},{16,8},{20,12},{24,0},{28,4},{1,25},{... | collective-permute-start | bytes 208904 | tf_op jit(solution)/shard_map/ppermute | solution.py:71
  23.4 5.2 %collective-permute-start.6 = (bf16[272,128]{1,0:T(8,128)(2,1)S(1)}, bf16[272,128]{1,0:T(8,128)(2,1)S(1)}, u32[]{:S(2)}, u32[]{:S(2)}) collective-permute-start(bf16[272,128]{1,0:T(8,128)(2,1)S(1)} %get-tuple-element.25), channel_id=1, source_target_pairs={{0,16},{4,12},{8,24},{12,4},{16,0},{20,28},{24,8},{28,20},{1,17},{... | collective-permute-start | bytes 208904 | tf_op jit(solution)/shard_map/ppermute | solution.py:76
  24.9 4.3 %collective-permute-start.7 = (bf16[272,128]{1,0:T(8,128)(2,1)S(1)}, bf16[272,128]{1,0:T(8,128)(2,1)S(1)}, u32[]{:S(2)}, u32[]{:S(2)}) collective-permute-start(bf16[272,128]{1,0:T(8,128)(2,1)S(1)} %get-tuple-element.26), channel_id=1, source_target_pairs={{0,8},{4,20},{8,0},{12,28},{16,24},{20,4},{24,16},{28,12},{1,9},{5... | collective-permute-start | bytes 208904 | tf_op jit(solution)/shard_map/ppermute | solution.py:76
  28.0 1.3 %collective-permute-start.9 = (bf16[272,128]{1,0:T(8,128)(2,1)S(1)}, bf16[272,128]{1,0:T(8,128)(2,1)S(1)}, u32[]{:S(2)}, u32[]{:S(2)}) collective-permute-start(bf16[272,128]{1,0:T(8,128)(2,1)S(1)} %swap.1), channel_id=1, source_target_pairs={{0,4},{4,0},{8,12},{12,8},{16,20},{20,16},{24,28},{28,24},{1,5},{5... | collective-permute-start | bytes 208904 | tf_op jit(solution)/shard_map/ppermute | solution.py:71

commit v17 on v16

--- a/solution.py
+++ b/solution.py
@@ -9,7 +9,6 @@
 
 LANES = 128
 STEP = 64
-SLAB = 64
 EXTRA = 16
 VMEM_LIMIT = 40 * 1024 * 1024
 
@@ -141,59 +140,19 @@
         filt_ref[chip ^ bits] = jnp.where(low, first, pltpu.roll(second, taps_here, 1))
 
 
-def toeplitz_rows(filt_ref, toep_ref, rest_ref):
-    chips, groups, _ = filt_ref.shape
-    taps = chips * LANES
-    tiles = [filt_ref[tile] for tile in range(chips)]
-    filt = jnp.concatenate(tiles + [jnp.zeros((groups, LANES), jnp.float32)], axis=1)
-    low = lax.broadcasted_iota(jnp.int32, (SLAB, LANES), 1) < SLAB
-    outside = []
-    for group in range(groups):
-        rows = jnp.broadcast_to(filt[group : group + 1], (SLAB, taps + LANES))
-        rows = pltpu.roll(rows, 0, 1, stride=1, stride_axis=0)
-        toep_ref[group * SLAB : (group + 1) * SLAB] = rows[:, :taps].astype(jnp.bfloat16)
-        outside.append(rows[:, taps:])
-    for pair in range(groups // 2):
-        both = jnp.where(low, outside[2 * pair], pltpu.roll(outside[2 * pair + 1], SLAB, 1))
-        rest_ref[:, pair * LANES : (pair + 1) * LANES] = both.astype(jnp.bfloat16)
-
-
-def group_of_lane(rows, width, groups):
-    lane = lax.broadcasted_iota(jnp.int32, (rows, width), 1)
-    return (lane % LANES) // (LANES // groups)
-
-
-def tokens_of(seqs, dye_ref, toep_ref, rest_ref, out_ref, block_len):
-    groups = toep_ref.shape[0] // SLAB
-    taps = toep_ref.shape[1]
-    starts = [seq * block_len + row for seq in seqs for row in range(0, block_len, SLAB)]
-
-    def windows(at, size):
-        return jnp.concatenate(
-            [dye_ref[pl.ds(pl.multiple_of(start + at, SLAB), size)] for start in starts], axis=1
-        )
-
-    group_in = group_of_lane(SLAB, len(starts) * LANES, groups)
-    after = windows(taps, SLAB)
-    after = [jnp.where(group_in == group, after, jnp.zeros_like(after)) for group in range(groups)]
-    full = jnp.dot(toep_ref[...], windows(0, taps), preferred_element_type=jnp.float32)
-    rest = jnp.dot(
-        rest_ref[...], jnp.concatenate(after, axis=0), preferred_element_type=jnp.float32
-    )
-    total = full[:SLAB]
-    for group in range(1, groups):
-        total = jnp.where(group_in == group, full[group * SLAB : (group + 1) * SLAB], total)
-    total = (total + rest).astype(jnp.bfloat16)
-    for index in range(len(starts)):
-        columns = slice(index * LANES, (index + 1) * LANES)
-        out_ref[index * SLAB : (index + 1) * SLAB] = total[:, columns]
-
-
-def first_kernel(n_seq, taps_here, far, near, dy_ref, *refs):
+def toeplitz_rows(taps):
+    rows = jnp.broadcast_to(taps, (LANES, taps.shape[1]))
+    return pltpu.roll(rows, 0, 1, stride=1, stride_axis=0).astype(jnp.bfloat16)
+
+
+def first_kernel(n_seq, taps_here, masks, dy_ref, *refs):
     chips = n_seq // 2
     in_refs = refs[:chips]
-    dye_ref, taps_ref, toep_ref, rest_ref, far_ref, near_ref, x_ref, filt_ref, turned_ref = refs[chips:]
+    own_ref, far_ref, send_ref, keep_ref, x_ref, filt_ref, dye_ref, turned_ref, dx_ref, taps_ref = refs[
+        chips:
+    ]
     tokens = dy_ref.shape[0]
+    block_len = tokens // n_seq
     groups = EXTRA // 2
     taps = n_seq * taps_here
     reach = taps + LANES
@@ -209,7 +168,13 @@
     for odd in range(2):
         turned_ref[odd] = dye_ref[odd * STEP : odd * STEP + wide].T
     inputs = x_ref[...].T
-    toeplitz_rows(filt_ref, toep_ref, rest_ref)
+    tiles = [filt_ref[tile] for tile in range(chips)]
+    filt = jnp.concatenate(tiles + [jnp.zeros((groups, LANES), jnp.float32)], axis=1)
+    far, near = masks[1], masks[2:]
+    blocks = [(masks[0], flip, own_ref, flip) for flip in range(2)]
+    blocks += [(far, flip, far_ref, flip) for flip in range(2)]
+    blocks += [(bits, 1, send_ref, index) for index, bits in enumerate(near)]
+    blocks += [(bits, 0, keep_ref, index) for index, bits in enumerate(near)]
     products = []
     for group in range(groups):
         own = slice(group * per_group, (group + 1) * per_group)
@@ -226,12 +191,21 @@
             axis=0,
         )
         products.append(jnp.dot(sides, windows, preferred_element_type=jnp.float32))
-
-    block_len = tokens // n_seq
-    seqs = [2 * (chip ^ far) + (core ^ flip) for flip in range(2)]
-    tokens_of(seqs, dye_ref, toep_ref, rest_ref, far_ref, block_len)
-    seqs = [2 * (chip ^ bits) + (core ^ 1) for bits in near]
-    tokens_of(seqs, dye_ref, toep_ref, rest_ref, near_ref, block_len)
+        windows = []
+        for bits, flip, _, _ in blocks:
+            start = (2 * (chip ^ bits) + (core ^ flip)) * block_len
+            windows.append(turned_ref[0, own, pl.ds(pl.multiple_of(start, LANES), reach)])
+        grads = lax.dot_general(
+            jnp.concatenate(windows, axis=0),
+            toeplitz_rows(filt[group : group + 1]),
+            (((1,), (1,)), ((), ())),
+            preferred_element_type=jnp.float32,
+        )
+        for index in range(len(blocks)):
+            dx_ref[index, own] = grads[index * per_group : (index + 1) * per_group]
+
+    for index, (_, _, out_ref, at) in enumerate(blocks):
+        out_ref[at * block_len : (at + 1) * block_len] = dx_ref[index].T.astype(jnp.bfloat16)
     eights = []
     for lags in products:
         rows = lags[:8]
@@ -256,8 +230,12 @@
         other = jnp.where(core == 0, odd, even)
         taps_ref[to_chip] = jnp.concatenate([mine, other], axis=0).astype(jnp.bfloat16)
 
+    own_ref[2 * block_len :] = taps_ref[chip]
     far_ref[2 * block_len :] = taps_ref[chip ^ far]
-    near_ref[len(near) * block_len :] = stacked([half_of(taps_ref[chip ^ bits], 1) for bits in near])
+    for flip, out_ref in ((1, send_ref), (0, keep_ref)):
+        out_ref[len(near) * block_len :] = stacked(
+            [half_of(taps_ref[chip ^ bits], flip) for bits in near]
+        )
 
 
 def half_of(taps, flip):
@@ -267,16 +245,6 @@
 
 def stacked(rows):
     return jnp.concatenate(rows, axis=0).astype(jnp.bfloat16)
-
-
-def near_kernel(masks, dye_ref, toep_ref, rest_ref, taps_ref, out_ref):
-    chip, core, _ = place()
-    block_len = (out_ref.shape[0] - len(masks) * EXTRA // 2) // len(masks)
-    seqs = [2 * (chip ^ bits) + core for bits in masks]
-    tokens_of(seqs, dye_ref, toep_ref, rest_ref, out_ref, block_len)
-    out_ref[len(masks) * block_len :] = stacked(
-        [half_of(taps_ref[chip ^ bits], 0) for bits in masks]
-    )
 
 
 def near_pieces_kernel(keep_ref, got_ref, *out_refs):
@@ -297,14 +265,6 @@
         out_ref[:block_len] = keep_ref[rows_at((index + core) % count, block_len)]
         out_ref[block_len : 2 * block_len] = got_ref[rows_at((index + core) % count, block_len)]
         out_ref[2 * block_len :] = jnp.where(core == 0, taps[index], taps[other])
-
-
-def own_kernel(dye_ref, toep_ref, rest_ref, taps_ref, out_ref):
-    chip, core, _ = place()
-    block_len = (out_ref.shape[0] - EXTRA) // 2
-    seqs = [2 * chip + (core ^ flip) for flip in range(2)]
-    tokens_of(seqs, dye_ref, toep_ref, rest_ref, out_ref, block_len)
-    out_ref[2 * block_len :] = taps_ref[chip]
 
 
 def swap_kernel(*refs):
@@ -390,39 +350,27 @@
     )
     near = masks[2:]
     near_shape = half(len(near) * (block_len + EXTRA // 2), LANES)
-    dye, tap_parts, toeplitz, outside, far, send = local_call(
-        functools.partial(first_kernel, n_seq, taps_here, masks[1], near),
-        [
-            half(tokens + taps + LANES, LANES),
-            half(chips, EXTRA, LANES),
-            half(groups * SLAB, taps),
-            half(SLAB, groups * SLAB),
-            unit,
-            near_shape,
-        ],
+    own, far, send, keep = local_call(
+        functools.partial(first_kernel, n_seq, taps_here, masks),
+        [unit, unit, near_shape, near_shape],
         (dy.reshape(tokens, LANES), *fan_out(pieces, "seq", 2)),
         "first",
         [
             pltpu.VMEM((tokens, LANES), jnp.bfloat16),
             pltpu.VMEM((chips, groups, LANES), jnp.float32),
+            pltpu.VMEM((tokens + taps + LANES, LANES), jnp.bfloat16),
             pltpu.VMEM((2, LANES, tokens + taps), jnp.bfloat16),
+            pltpu.VMEM((n_seq, LANES, block_len), jnp.float32),
+            pltpu.VMEM((chips, EXTRA, LANES), jnp.bfloat16),
         ],
     )
     far = xor_permute(far, "seq", 2 * masks[1])
     got = xor_permute(send, "seq", 1)
-    (keep,) = local_call(
-        functools.partial(near_kernel, near),
-        [near_shape],
-        (dye, toeplitz, outside, tap_parts),
-        "near_keep",
-    )
     pieces = local_call(near_pieces_kernel, [unit] * len(near), (keep, got), "near_pieces")
     pieces = [
         turned_permute(piece, "seq", [2 * bits for bits in near[index:] + near[:index]])
         for index, piece in enumerate(pieces)
     ]
-    far, tap_parts = lax.optimization_barrier((far, tap_parts))
-    (own,) = local_call(own_kernel, [unit], (dye, toeplitz, outside, tap_parts), "own")
     (send,) = local_call(
         swap_kernel, [half(2 * block_len + EXTRA, LANES)], (own, far), "swap"
     )
@@ -450,7 +398,6 @@
             and groups_here == 8 * n_seq
             and 2 * taps_here == LANES
             and out_grads.shape[0] % 16 == 0
-            and layer_inputs.shape[0] % SLAB == 0
             and layer_inputs.shape[0] == 2 * STEP
             and n_seq * taps_here + LANES <= n_seq * layer_inputs.shape[0]
         )

time: 30.3 us -> 30.5 us (level)
  waiting for transfers between devices: 8.66 us -> 9.69 us
  Pallas kernels: 4.32 us -> 3.62 us
    ppermute x8, waiting for transfers between devices: 7.06 us -> 8.49 us  [xor_permute(): return lax.ppermute(value, axis, pairs)]
    pallas_call x8 -> x6, Pallas kernels: 4.32 us -> 3.62 us  [local_call(): pl.pallas_call(kernel, out_shape=out_shape, in_specs=[whole] * len(operan...]
    ppermute x2, waiting for transfers between devices: 1.19 us -> 0.79 us  [turned_permute(): return lax.ppermute(value, axis, pairs)]
  transfers between devices with their start and end apart: 11 -> 11, of which waited for: 8 -> 8; matrix products, arithmetic and copies ran while one was open for 0% -> 0% of each run, Pallas kernels for 4% -> 0%
where the time goes in v17:
time: 30.5 us; the launch traced here: 30.3 us
  starting transfers between devices  15.3 us (50%)
  waiting for transfers between devices  9.69 us (32%)
  Pallas kernels  3.62 us (12%)
  local copies, waits for them, and re-layouts  0.95 us (3%)
  between operations  0.68 us (2%)
    ppermute x8, waiting for transfers between devices, xor_permute(): return lax.ppermute(value, axis, pairs)  8.49 us
    all_to_all x1, starting transfers between devices, by_channels(): lax.all_to_all(dy, ('seq', 'chan'), split_axis=0, concat_axis=0, tiled=True)  7.3 us
    ppermute x8, starting transfers between devices, xor_permute(): return lax.ppermute(value, axis, pairs)  5.42 us
    pallas_call x6, Pallas kernels, local_call(): pl.pallas_call(kernel, out_shape=out_shape, in_specs=[whole] * len(operan...  3.62 us
    ppermute x2, starting transfers between devices, turned_permute(): return lax.ppermute(value, axis, pairs)  2.62 us
    unnamed x6, local copies, waits for them, and re-layouts  0.95 us
    ppermute x2, waiting for transfers between devices, turned_permute(): return lax.ppermute(value, axis, pairs)  0.79 us
  transfers between devices with their start and end apart: 11, of which 8 were waited for; matrix products, arithmetic and copies ran while one was open for 0% of the time, Pallas kernels for 0%

profile of v17, /device:TPU:0, one launch (start us, length us, event | category | flops | bytes accessed | tf_op | source)
XLA Modules:
  0.0 30.3 jit_solution(952813447984949440)
XLA Ops:
  0.6 0.9 %copy-done = bf16[32,4096]{1,0:T(8,128)(2,1)S(1)} copy-done((bf16[32,4096]{1,0:T(8,128)(2,1)S(1)}, bf16[32,4096]{1,0:T(8,128)(2,1)}, u32[]{:S(2)}) %copy-start) | copy-done | bytes 262168
  1.6 0.7 %fan_grads.1 = bf16[32,32,128]{2,1,0:T(8,128)(2,1)} custom-call(bf16[32,4096]{1,0:T(8,128)(2,1)S(1)} %copy-done), custom_call_target="tpu_custom_call" | custom-call | tf_op jit(solution)/shard_map/fan_grads/pallas_call | solution.py:310
  2.3 7.3 %all-to-all-start = ((bf16[32,32,128]{2,1,0:T(8,128)(2,1)}), bf16[32,32,128]{2,1,0:T(8,128)(2,1)S(1)}, u32[]{:S(2)}, u32[]{:S(2)}) async-start(bf16[32,32,128]{2,1,0:T(8,128)(2,1)} %fan_grads.1), calls=%async_computation | async-start | bytes 524288 | tf_op jit(solution)/shard_map/all_to_all | solution.py:343
  9.6 0.3 %collective-permute-start = (bf16[128,1024]{1,0:T(8,128)(2,1)S(1)}, bf16[128,1024]{1,0:T(8,128)(2,1)S(1)}, u32[]{:S(2)}, u32[]{:S(2)}) collective-permute-start(bf16[128,1024]{1,0:T(8,128)(2,1)S(1)} %copy-done.1), channel_id=1, source_target_pairs={{0,4},{4,0},{8,12},{12,8},{16,20},{20,16},{24,28},{28,24},{1,5},{5... | collective-permute-start | bytes 786440 | tf_op jit(solution)/shard_map/ppermute | solution.py:70
  10.0 0.3 collective-permute-start.1
  10.2 1.0 %collective-permute-done.1.f_other_ref = bf16[64,64]{1,0:T(8,128)(2,1)S(1)} collective-permute-done((bf16[64,64]{1,0:T(8,128)(2,1)S(1)}, bf16[64,64]{1,0:T(8,128)(2,1)S(1)}, u32[]{:S(2)}, u32[]{:S(2)}) %collective-permute-start.1) | collective-permute-done | bytes 8224 | tf_op jit(solution)/shard_map/ppermute | solution.py:70
  11.3 0.1 fan_inputs.1
  11.4 2.7 %collective-permute-start.2 = (bf16[272,128]{1,0:T(8,128)(2,1)S(1)}, bf16[272,128]{1,0:T(8,128)(2,1)S(1)}, u32[]{:S(2)}, u32[]{:S(2)}) collective-permute-start(bf16[272,128]{1,0:T(8,128)(2,1)S(1)} %get-tuple-element.13), channel_id=1, source_target_pairs={{0,24},{4,28},{8,16},{12,20},{16,8},{20,12},{24,0},{28,4},{1,25},{... | collective-permute-start | bytes 208904 | tf_op jit(solution)/shard_map/ppermute | solution.py:70
  14.1 0.6 %collective-permute-start.3 = (bf16[272,128]{1,0:T(8,128)(2,1)S(1)}, bf16[272,128]{1,0:T(8,128)(2,1)S(1)}, u32[]{:S(2)}, u32[]{:S(2)}) collective-permute-start(bf16[272,128]{1,0:T(8,128)(2,1)S(1)} %get-tuple-element.14), channel_id=1, source_target_pairs={{0,16},{4,20},{8,24},{12,28},{16,0},{20,4},{24,8},{28,12},{1,17},{... | collective-permute-start | bytes 208904 | tf_op jit(solution)/shard_map/ppermute | solution.py:70
  14.7 0.3 collective-permute-start.4
  14.9 2.8 %collective-permute-done.2.refs_1_ = bf16[272,128]{1,0:T(8,128)(2,1)S(1)} collective-permute-done((bf16[272,128]{1,0:T(8,128)(2,1)S(1)}, bf16[272,128]{1,0:T(8,128)(2,1)S(1)}, u32[]{:S(2)}, u32[]{:S(2)}) %collective-permute-start.2) | collective-permute-done | bytes 69664 | tf_op jit(solution)/shard_map/ppermute | solution.py:70
  17.8 1.7 %collective-permute-done.3.refs_2_ = bf16[272,128]{1,0:T(8,128)(2,1)S(1)} collective-permute-done((bf16[272,128]{1,0:T(8,128)(2,1)S(1)}, bf16[272,128]{1,0:T(8,128)(2,1)S(1)}, u32[]{:S(2)}, u32[]{:S(2)}) %collective-permute-start.3) | collective-permute-done | bytes 69664 | tf_op jit(solution)/shard_map/ppermute | solution.py:70
  19.5 0.4 %all-to-all-done = bf16[32,32,128]{2,1,0:T(8,128)(2,1)S(1)} async-done(((bf16[32,32,128]{2,1,0:T(8,128)(2,1)}), bf16[32,32,128]{2,1,0:T(8,128)(2,1)S(1)}, u32[]{:S(2)}, u32[]{:S(2)}) %all-to-all-start) | async-done | bytes 262176 | tf_op jit(solution)/shard_map/all_to_all | solution.py:343
  19.9 2.0 %first.1 = (bf16[272,128]{1,0:T(8,128)(2,1)S(1)}, bf16[272,128]{1,0:T(8,128)(2,1)S(1)}, bf16[272,128]{1,0:T(8,128)(2,1)S(1)}, bf16[272,128]{1,0:T(8,128)(2,1)S(1)}) custom-call(bf16[1024,128]{1,0:T(8,128)(2,1)S(1)} %bitcast.1, bf16[272,128]{1,0:T(8,128)(2,1)S(1)} %get-tuple-element.12.refs_0_, bf16[272,128]{1,0:T(8,128)(2,1)S(1)} %collective-permute-done.2.refs_1_, ...), custom_call_target="tpu_custom_call" | custom-call | tf_op jit(solution)/shard_map/first/pallas_call | solution.py:310
  21.9 0.4 %collective-permute-start.5 = (bf16[272,128]{1,0:T(8,128)(2,1)S(1)}, bf16[272,128]{1,0:T(8,128)(2,1)S(1)}, u32[]{:S(2)}, u32[]{:S(2)}) collective-permute-start(bf16[272,128]{1,0:T(8,128)(2,1)S(1)} %get-tuple-element.17), channel_id=1, source_target_pairs={{0,4},{4,0},{8,12},{12,8},{16,20},{20,16},{24,28},{28,24},{1,5},{5... | collective-permute-start | bytes 208904 | tf_op jit(solution)/shard_map/ppermute | solution.py:70
  22.3 0.9 %collective-permute-start.8 = (bf16[272,128]{1,0:T(8,128)(2,1)S(1)}, bf16[272,128]{1,0:T(8,128)(2,1)S(1)}, u32[]{:S(2)}, u32[]{:S(2)}) collective-permute-start(bf16[272,128]{1,0:T(8,128)(2,1)S(1)} %get-tuple-element.21), channel_id=1, source_target_pairs={{0,24},{4,28},{8,16},{12,20},{16,8},{20,12},{24,0},{28,4},{1,25},{... | collective-permute-start | bytes 208904 | tf_op jit(solution)/shard_map/ppermute | solution.py:70
  23.2 0.0 collective-permute-done.5.got_ref
  23.2 1.5 %collective-permute-start.6 = (bf16[272,128]{1,0:T(8,128)(2,1)S(1)}, bf16[272,128]{1,0:T(8,128)(2,1)S(1)}, u32[]{:S(2)}, u32[]{:S(2)}) collective-permute-start(bf16[272,128]{1,0:T(8,128)(2,1)S(1)} %get-tuple-element.18), channel_id=1, source_target_pairs={{0,16},{4,12},{8,24},{12,4},{16,0},{20,28},{24,8},{28,20},{1,17},{... | collective-permute-start | bytes 208904 | tf_op jit(solution)/shard_map/ppermute | solution.py:75
  24.7 1.1 %collective-permute-start.7 = (bf16[272,128]{1,0:T(8,128)(2,1)S(1)}, bf16[272,128]{1,0:T(8,128)(2,1)S(1)}, u32[]{:S(2)}, u32[]{:S(2)}) collective-permute-start(bf16[272,128]{1,0:T(8,128)(2,1)S(1)} %get-tuple-element.19), channel_id=1, source_target_pairs={{0,8},{4,20},{8,0},{12,28},{16,24},{20,4},{24,16},{28,12},{1,9},{5... | collective-permute-start | bytes 208904 | tf_op jit(solution)/shard_map/ppermute | solution.py:75
  25.8 2.4 %collective-permute-done.8.refs_1_.refs_3_ = bf16[272,128]{1,0:T(8,128)(2,1)S(1)} collective-permute-done((bf16[272,128]{1,0:T(8,128)(2,1)S(1)}, bf16[272,128]{1,0:T(8,128)(2,1)S(1)}, u32[]{:S(2)}, u32[]{:S(2)}) %collective-permute-start.8) | collective-permute-done | bytes 69664 | tf_op jit(solution)/shard_map/ppermute | solution.py:70
  28.2 0.7 %collective-permute-done.6.refs_0_ = bf16[272,128]{1,0:T(8,128)(2,1)S(1)} collective-permute-done((bf16[272,128]{1,0:T(8,128)(2,1)S(1)}, bf16[272,128]{1,0:T(8,128)(2,1)S(1)}, u32[]{:S(2)}, u32[]{:S(2)}) %collective-permute-start.6) | collective-permute-done | bytes 69664 | tf_op jit(solution)/shard_map/ppermute | solution.py:75
  28.9 0.1 collective-permute-done.7.refs_1_
  29.0 0.5 %collective-permute-done.9.refs_4_ = bf16[272,128]{1,0:T(8,128)(2,1)S(1)} collective-permute-done((bf16[272,128]{1,0:T(8,128)(2,1)S(1)}, bf16[272,128]{1,0:T(8,128)(2,1)S(1)}, u32[]{:S(2)}, u32[]{:S(2)}) %collective-permute-start.9) | collective-permute-done | bytes 69664 | tf_op jit(solution)/shard_map/ppermute | solution.py:70
  29.5 0.8 %unpack.1 = (bf16[128,1024]{1,0:T(8,128)(2,1)}, f32[64,64]{1,0:T(8,128)}) custom-call(bf16[272,128]{1,0:T(8,128)(2,1)S(1)} %collective-permute-done.6.refs_0_, bf16[272,128]{1,0:T(8,128)(2,1)S(1)} %collective-permute-done.7.refs_1_, bf16[272,128]{1,0:T(8,128)(2,1)S(1)} %get-tuple-element.20.refs_0_.refs_2_, ...), custom_call_target="tpu_custom_call" | custom-call | tf_op jit(solution)/shard_map/unpack/pallas_call | solution.py:310
  (10 shorter events, 0.0 us)
Async XLA Ops:
  0.6 1.0 %copy-start = (bf16[32,4096]{1,0:T(8,128)(2,1)S(1)}, bf16[32,4096]{1,0:T(8,128)(2,1)}, u32[]{:S(2)}) copy-start(bf16[32,4096]{1,0:T(8,128)(2,1)} %in_ref.1) | copy-start | bytes 786436
  2.3 7.3 %copy-start.1 = (bf16[128,1024]{1,0:T(8,128)(2,1)S(1)}, bf16[128,1024]{1,0:T(8,128)(2,1)}, u32[]{:S(2)}) copy-start(bf16[128,1024]{1,0:T(8,128)(2,1)} %x_own_ref.1) | copy-start | bytes 786436
  2.3 7.6 %copy-start.2 = (bf16[64,64]{1,0:T(8,128)(2,1)S(1)}, bf16[64,64]{1,0:T(8,128)(2,1)}, u32[]{:S(2)}) copy-start(bf16[64,64]{1,0:T(8,128)(2,1)} %f_own_ref.1) | copy-start | bytes 24580
  2.3 17.6 %all-to-all-start = ((bf16[32,32,128]{2,1,0:T(8,128)(2,1)}), bf16[32,32,128]{2,1,0:T(8,128)(2,1)S(1)}, u32[]{:S(2)}, u32[]{:S(2)}) async-start(bf16[32,32,128]{2,1,0:T(8,128)(2,1)} %fan_grads.1), calls=%async_computation | async-start | bytes 524288 | tf_op jit(solution)/shard_map/all_to_all | solution.py:343
  9.6 1.6 %collective-permute-start = (bf16[128,1024]{1,0:T(8,128)(2,1)S(1)}, bf16[128,1024]{1,0:T(8,128)(2,1)S(1)}, u32[]{:S(2)}, u32[]{:S(2)}) collective-permute-start(bf16[128,1024]{1,0:T(8,128)(2,1)S(1)} %copy-done.1), channel_id=1, source_target_pairs={{0,4},{4,0},{8,12},{12,8},{16,20},{20,16},{24,28},{28,24},{1,5},{5... | collective-permute-start | bytes 786440 | tf_op jit(solution)/shard_map/ppermute | solution.py:70
  10.0 1.3 %collective-permute-start.1 = (bf16[64,64]{1,0:T(8,128)(2,1)S(1)}, bf16[64,64]{1,0:T(8,128)(2,1)S(1)}, u32[]{:S(2)}, u32[]{:S(2)}) collective-permute-start(bf16[64,64]{1,0:T(8,128)(2,1)S(1)} %copy-done.2), channel_id=1, source_target_pairs={{0,4},{4,0},{8,12},{12,8},{16,20},{20,16},{24,28},{28,24},{1,5},{5... | collective-permute-start | bytes 24584 | tf_op jit(solution)/shard_map/ppermute | solution.py:70
  11.4 6.4 %collective-permute-start.2 = (bf16[272,128]{1,0:T(8,128)(2,1)S(1)}, bf16[272,128]{1,0:T(8,128)(2,1)S(1)}, u32[]{:S(2)}, u32[]{:S(2)}) collective-permute-start(bf16[272,128]{1,0:T(8,128)(2,1)S(1)} %get-tuple-element.13), channel_id=1, source_target_pairs={{0,24},{4,28},{8,16},{12,20},{16,8},{20,12},{24,0},{28,4},{1,25},{... | collective-permute-start | bytes 208904 | tf_op jit(solution)/shard_map/ppermute | solution.py:70
  14.1 5.4 %collective-permute-start.3 = (bf16[272,128]{1,0:T(8,128)(2,1)S(1)}, bf16[272,128]{1,0:T(8,128)(2,1)S(1)}, u32[]{:S(2)}, u32[]{:S(2)}) collective-permute-start(bf16[272,128]{1,0:T(8,128)(2,1)S(1)} %get-tuple-element.14), channel_id=1, source_target_pairs={{0,16},{4,20},{8,24},{12,28},{16,0},{20,4},{24,8},{28,12},{1,17},{... | collective-permute-start | bytes 208904 | tf_op jit(solution)/shard_map/ppermute | solution.py:70
  14.7 4.8 %collective-permute-start.4 = (bf16[272,128]{1,0:T(8,128)(2,1)S(1)}, bf16[272,128]{1,0:T(8,128)(2,1)S(1)}, u32[]{:S(2)}, u32[]{:S(2)}) collective-permute-start(bf16[272,128]{1,0:T(8,128)(2,1)S(1)} %get-tuple-element.15), channel_id=1, source_target_pairs={{0,8},{4,12},{8,0},{12,4},{16,24},{20,28},{24,16},{28,20},{1,9},{5... | collective-permute-start | bytes 208904 | tf_op jit(solution)/shard_map/ppermute | solution.py:70
  21.9 1.3 %collective-permute-start.5 = (bf16[272,128]{1,0:T(8,128)(2,1)S(1)}, bf16[272,128]{1,0:T(8,128)(2,1)S(1)}, u32[]{:S(2)}, u32[]{:S(2)}) collective-permute-start(bf16[272,128]{1,0:T(8,128)(2,1)S(1)} %get-tuple-element.17), channel_id=1, source_target_pairs={{0,4},{4,0},{8,12},{12,8},{16,20},{20,16},{24,28},{28,24},{1,5},{5... | collective-permute-start | bytes 208904 | tf_op jit(solution)/shard_map/ppermute | solution.py:70
  22.3 6.0 %collective-permute-start.8 = (bf16[272,128]{1,0:T(8,128)(2,1)S(1)}, bf16[272,128]{1,0:T(8,128)(2,1)S(1)}, u32[]{:S(2)}, u32[]{:S(2)}) collective-permute-start(bf16[272,128]{1,0:T(8,128)(2,1)S(1)} %get-tuple-element.21), channel_id=1, source_target_pairs={{0,24},{4,28},{8,16},{12,20},{16,8},{20,12},{24,0},{28,4},{1,25},{... | collective-permute-start | bytes 208904 | tf_op jit(solution)/shard_map/ppermute | solution.py:70
  23.2 5.7 %collective-permute-start.6 = (bf16[272,128]{1,0:T(8,128)(2,1)S(1)}, bf16[272,128]{1,0:T(8,128)(2,1)S(1)}, u32[]{:S(2)}, u32[]{:S(2)}) collective-permute-start(bf16[272,128]{1,0:T(8,128)(2,1)S(1)} %get-tuple-element.18), channel_id=1, source_target_pairs={{0,16},{4,12},{8,24},{12,4},{16,0},{20,28},{24,8},{28,20},{1,17},{... | collective-permute-start | bytes 208904 | tf_op jit(solution)/shard_map/ppermute | solution.py:75
  24.7 4.3 %collective-permute-start.7 = (bf16[272,128]{1,0:T(8,128)(2,1)S(1)}, bf16[272,128]{1,0:T(8,128)(2,1)S(1)}, u32[]{:S(2)}, u32[]{:S(2)}) collective-permute-start(bf16[272,128]{1,0:T(8,128)(2,1)S(1)} %get-tuple-element.19), channel_id=1, source_target_pairs={{0,8},{4,20},{8,0},{12,28},{16,24},{20,4},{24,16},{28,12},{1,9},{5... | collective-permute-start | bytes 208904 | tf_op jit(solution)/shard_map/ppermute | solution.py:75
  28.2 1.3 %collective-permute-start.9 = (bf16[272,128]{1,0:T(8,128)(2,1)S(1)}, bf16[272,128]{1,0:T(8,128)(2,1)S(1)}, u32[]{:S(2)}, u32[]{:S(2)}) collective-permute-start(bf16[272,128]{1,0:T(8,128)(2,1)S(1)} %swap.1), channel_id=1, source_target_pairs={{0,4},{4,0},{8,12},{12,8},{16,20},{20,16},{24,28},{28,24},{1,5},{5... | collective-permute-start | bytes 208904 | tf_op jit(solution)/shard_map/ppermute | solution.py:70

commit v18 on v16

--- a/solution.py
+++ b/solution.py
@@ -189,10 +189,27 @@
         out_ref[index * SLAB : (index + 1) * SLAB] = total[:, columns]
 
 
-def first_kernel(n_seq, taps_here, far, near, dy_ref, *refs):
+def inputs_kernel(n_seq, taps_here, *refs):
     chips = n_seq // 2
     in_refs = refs[:chips]
-    dye_ref, taps_ref, toep_ref, rest_ref, far_ref, near_ref, x_ref, filt_ref, turned_ref = refs[chips:]
+    toep_ref, rest_ref, sides_ref, x_ref, filt_ref = refs[chips:]
+    groups = sides_ref.shape[0]
+    per_group = LANES // groups
+    place_inputs(in_refs, taps_here, x_ref, filt_ref)
+    pairs = x_ref.shape[0] // (2 * STEP)
+    inputs = x_ref[...].T
+    toeplitz_rows(filt_ref, toep_ref, rest_ref)
+    for group in range(groups):
+        own = slice(group * per_group, (group + 1) * per_group)
+        sides = jnp.concatenate(
+            [inputs[own, pair * LANES : (pair + 1) * LANES] for pair in range(pairs)], axis=0
+        ).T
+        sides_ref[group] = jnp.concatenate([sides[:STEP], sides[STEP:]], axis=1)
+
+
+def first_kernel(n_seq, taps_here, far, near, dy_ref, toep_ref, rest_ref, sides_ref, *refs):
+    chips = n_seq // 2
+    dye_ref, taps_ref, far_ref, near_ref, turned_ref = refs
     tokens = dy_ref.shape[0]
     groups = EXTRA // 2
     taps = n_seq * taps_here
@@ -200,7 +217,6 @@
     per_group = LANES // groups
     chip, core, _ = place()
 
-    place_inputs(in_refs, taps_here, x_ref, filt_ref)
     dye_ref[:tokens] = dy_ref[...]
     dye_ref[tokens:] = dy_ref[:reach]
 
@@ -208,15 +224,9 @@
     wide = (pairs - 1) * LANES + reach
     for odd in range(2):
         turned_ref[odd] = dye_ref[odd * STEP : odd * STEP + wide].T
-    inputs = x_ref[...].T
-    toeplitz_rows(filt_ref, toep_ref, rest_ref)
     products = []
     for group in range(groups):
         own = slice(group * per_group, (group + 1) * per_group)
-        sides = jnp.concatenate(
-            [inputs[own, pair * LANES : (pair + 1) * LANES] for pair in range(pairs)], axis=0
-        ).T
-        sides = jnp.concatenate([sides[:STEP], sides[STEP:]], axis=1)
         windows = jnp.concatenate(
             [
                 turned_ref[odd, own, pair * LANES : pair * LANES + reach]
@@ -225,7 +235,7 @@
             ],
             axis=0,
         )
-        products.append(jnp.dot(sides, windows, preferred_element_type=jnp.float32))
+        products.append(jnp.dot(sides_ref[group], windows, preferred_element_type=jnp.float32))
 
     block_len = tokens // n_seq
     seqs = [2 * (chip ^ far) + (core ^ flip) for flip in range(2)]
@@ -390,23 +400,26 @@
     )
     near = masks[2:]
     near_shape = half(len(near) * (block_len + EXTRA // 2), LANES)
-    dye, tap_parts, toeplitz, outside, far, send = local_call(
-        functools.partial(first_kernel, n_seq, taps_here, masks[1], near),
+    toeplitz, outside, sides = local_call(
+        functools.partial(inputs_kernel, n_seq, taps_here),
         [
-            half(tokens + taps + LANES, LANES),
-            half(chips, EXTRA, LANES),
             half(groups * SLAB, taps),
             half(SLAB, groups * SLAB),
-            unit,
-            near_shape,
+            half(groups, STEP, tokens * LANES // (groups * STEP)),
         ],
-        (dy.reshape(tokens, LANES), *fan_out(pieces, "seq", 2)),
-        "first",
+        fan_out(pieces, "seq", 2),
+        "inputs",
         [
             pltpu.VMEM((tokens, LANES), jnp.bfloat16),
             pltpu.VMEM((chips, groups, LANES), jnp.float32),
-            pltpu.VMEM((2, LANES, tokens + taps), jnp.bfloat16),
         ],
+    )
+    dye, tap_parts, far, send = local_call(
+        functools.partial(first_kernel, n_seq, taps_here, masks[1], near),
+        [half(tokens + taps + LANES, LANES), half(chips, EXTRA, LANES), unit, near_shape],
+        (dy.reshape(tokens, LANES), toeplitz, outside, sides),
+        "first",
+        [pltpu.VMEM((2, LANES, tokens + taps), jnp.bfloat16)],
     )
     far = xor_permute(far, "seq", 2 * masks[1])
     got = xor_permute(send, "seq", 1)

time: 30.3 us -> 30.4 us (level)
  Pallas kernels: 4.32 us -> 4.68 us
    ppermute x2, waiting for transfers between devices: 1.19 us -> 1.67 us  [turned_permute(): return lax.ppermute(value, axis, pairs)]
    ppermute x2, starting transfers between devices: 2.66 us -> 2.21 us  [turned_permute(): return lax.ppermute(value, axis, pairs)]
    all_to_all x1, waiting for transfers between devices: 0.41 us -> 0.01 us  [by_channels(): lax.all_to_all(dy, ('seq', 'chan'), split_axis=0, concat_axis=0, tiled=True)]
    pallas_call x8 -> x9, Pallas kernels: 4.32 us -> 4.68 us  [local_call(): pl.pallas_call(kernel, out_shape=out_shape, in_specs=[whole] * len(operan...]
    ppermute x8, starting transfers between devices: 5.47 us -> 5.78 us  [xor_permute(): return lax.ppermute(value, axis, pairs)]
  transfers between devices with their start and end apart: 11 -> 11, of which waited for: 8 -> 6; matrix products, arithmetic and copies ran while one was open for 0% -> 0% of each run, Pallas kernels for 4% -> 6%
where the time goes in v18:
time: 30.4 us; the launch traced here: 30.2 us
  starting transfers between devices  15.3 us (50%)
  waiting for transfers between devices  8.53 us (28%)
  Pallas kernels  4.68 us (15%)
  local copies, waits for them, and re-layouts  0.95 us (3%)
  between operations  0.74 us (2%)
    all_to_all x1, starting transfers between devices, by_channels(): lax.all_to_all(dy, ('seq', 'chan'), split_axis=0, concat_axis=0, tiled=True)  7.3 us
    ppermute x8, waiting for transfers between devices, xor_permute(): return lax.ppermute(value, axis, pairs)  6.85 us
    ppermute x8, starting transfers between devices, xor_permute(): return lax.ppermute(value, axis, pairs)  5.78 us
    pallas_call x9, Pallas kernels, local_call(): pl.pallas_call(kernel, out_shape=out_shape, in_specs=[whole] * len(operan...  4.68 us
    ppermute x2, starting transfers between devices, turned_permute(): return lax.ppermute(value, axis, pairs)  2.21 us
    ppermute x2, waiting for transfers between devices, turned_permute(): return lax.ppermute(value, axis, pairs)  1.67 us
    unnamed x6, local copies, waits for them, and re-layouts  0.95 us
  transfers between devices with their start and end apart: 11, of which 6 were waited for; matrix products, arithmetic and copies ran while one was open for 0% of the time, Pallas kernels for 6%

profile of v18, /device:TPU:0, one launch (start us, length us, event | category | flops | bytes accessed | tf_op | source)
XLA Modules:
  0.0 30.2 jit_solution(11372232442673838485)
XLA Ops:
  0.6 0.9 %copy-done = bf16[32,4096]{1,0:T(8,128)(2,1)S(1)} copy-done((bf16[32,4096]{1,0:T(8,128)(2,1)S(1)}, bf16[32,4096]{1,0:T(8,128)(2,1)}, u32[]{:S(2)}) %copy-start) | copy-done | bytes 262168
  1.6 0.7 %fan_grads.1 = bf16[32,32,128]{2,1,0:T(8,128)(2,1)} custom-call(bf16[32,4096]{1,0:T(8,128)(2,1)S(1)} %copy-done), custom_call_target="tpu_custom_call" | custom-call | tf_op jit(solution)/shard_map/fan_grads/pallas_call | solution.py:360
  2.3 7.3 %all-to-all-start = ((bf16[32,32,128]{2,1,0:T(8,128)(2,1)}), bf16[32,32,128]{2,1,0:T(8,128)(2,1)S(1)}, u32[]{:S(2)}, u32[]{:S(2)}) async-start(bf16[32,32,128]{2,1,0:T(8,128)(2,1)} %fan_grads.1), calls=%async_computation | async-start | bytes 524288 | tf_op jit(solution)/shard_map/all_to_all | solution.py:393
  9.6 0.3 %collective-permute-start = (bf16[128,1024]{1,0:T(8,128)(2,1)S(1)}, bf16[128,1024]{1,0:T(8,128)(2,1)S(1)}, u32[]{:S(2)}, u32[]{:S(2)}) collective-permute-start(bf16[128,1024]{1,0:T(8,128)(2,1)S(1)} %copy-done.1), channel_id=1, source_target_pairs={{0,4},{4,0},{8,12},{12,8},{16,20},{20,16},{24,28},{28,24},{1,5},{5... | collective-permute-start | bytes 786440 | tf_op jit(solution)/shard_map/ppermute | solution.py:71
  10.0 0.3 collective-permute-start.1
  10.2 1.0 %collective-permute-done.1.f_other_ref = bf16[64,64]{1,0:T(8,128)(2,1)S(1)} collective-permute-done((bf16[64,64]{1,0:T(8,128)(2,1)S(1)}, bf16[64,64]{1,0:T(8,128)(2,1)S(1)}, u32[]{:S(2)}, u32[]{:S(2)}) %collective-permute-start.1) | collective-permute-done | bytes 8224 | tf_op jit(solution)/shard_map/ppermute | solution.py:71
  11.3 0.1 fan_inputs.1
  11.4 2.7 %collective-permute-start.2 = (bf16[272,128]{1,0:T(8,128)(2,1)S(1)}, bf16[272,128]{1,0:T(8,128)(2,1)S(1)}, u32[]{:S(2)}, u32[]{:S(2)}) collective-permute-start(bf16[272,128]{1,0:T(8,128)(2,1)S(1)} %get-tuple-element.18), channel_id=1, source_target_pairs={{0,24},{4,28},{8,16},{12,20},{16,8},{20,12},{24,0},{28,4},{1,25},{... | collective-permute-start | bytes 208904 | tf_op jit(solution)/shard_map/ppermute | solution.py:71
  14.1 0.6 %collective-permute-start.3 = (bf16[272,128]{1,0:T(8,128)(2,1)S(1)}, bf16[272,128]{1,0:T(8,128)(2,1)S(1)}, u32[]{:S(2)}, u32[]{:S(2)}) collective-permute-start(bf16[272,128]{1,0:T(8,128)(2,1)S(1)} %get-tuple-element.19), channel_id=1, source_target_pairs={{0,16},{4,20},{8,24},{12,28},{16,0},{20,4},{24,8},{28,12},{1,17},{... | collective-permute-start | bytes 208904 | tf_op jit(solution)/shard_map/ppermute | solution.py:71
  14.7 0.3 collective-permute-start.4
  14.9 2.8 %collective-permute-done.2.refs_1_ = bf16[272,128]{1,0:T(8,128)(2,1)S(1)} collective-permute-done((bf16[272,128]{1,0:T(8,128)(2,1)S(1)}, bf16[272,128]{1,0:T(8,128)(2,1)S(1)}, u32[]{:S(2)}, u32[]{:S(2)}) %collective-permute-start.2) | collective-permute-done | bytes 69664 | tf_op jit(solution)/shard_map/ppermute | solution.py:71
  17.8 1.7 %collective-permute-done.3.refs_2_ = bf16[272,128]{1,0:T(8,128)(2,1)S(1)} collective-permute-done((bf16[272,128]{1,0:T(8,128)(2,1)S(1)}, bf16[272,128]{1,0:T(8,128)(2,1)S(1)}, u32[]{:S(2)}, u32[]{:S(2)}) %collective-permute-start.3) | collective-permute-done | bytes 69664 | tf_op jit(solution)/shard_map/ppermute | solution.py:71
  19.5 0.6 %inputs.1 = (bf16[512,512]{1,0:T(8,128)(2,1)S(1)}, bf16[64,512]{1,0:T(8,128)(2,1)S(1)}, bf16[8,64,256]{2,1,0:T(8,128)(2,1)S(1)}) custom-call(bf16[272,128]{1,0:T(8,128)(2,1)S(1)} %get-tuple-element.17.refs_0_, bf16[272,128]{1,0:T(8,128)(2,1)S(1)} %collective-permute-done.2.refs_1_, bf16[272,128]{1,0:T(8,128)(2,1)S(1)} %collective-permute-done.3.refs_2_, ...), custom_call_target="tpu_custom_call" | custom-call | tf_op jit(solution)/shard_map/inputs/pallas_call | solution.py:360
  20.1 1.5 %first.1 = (bf16[1664,128]{1,0:T(8,128)(2,1)S(1)}, bf16[4,16,128]{2,1,0:T(8,128)(2,1)S(1)}, bf16[272,128]{1,0:T(8,128)(2,1)S(1)}, bf16[272,128]{1,0:T(8,128)(2,1)S(1)}) custom-call(bf16[1024,128]{1,0:T(8,128)(2,1)S(1)} %bitcast.1, bf16[512,512]{1,0:T(8,128)(2,1)S(1)} %get-tuple-element.21.toep_ref, bf16[64,512]{1,0:T(8,128)(2,1)S(1)} %get-tuple-element.22.rest_ref, ...), custom_call_target="tpu_custom_call" | custom-call | tf_op jit(solution)/shard_map/first/pallas_call | solution.py:360
  21.6 0.2 collective-permute-start.5
  21.8 1.4 %collective-permute-start.8 = (bf16[272,128]{1,0:T(8,128)(2,1)S(1)}, bf16[272,128]{1,0:T(8,128)(2,1)S(1)}, u32[]{:S(2)}, u32[]{:S(2)}) collective-permute-start(bf16[272,128]{1,0:T(8,128)(2,1)S(1)} %get-tuple-element.29), channel_id=1, source_target_pairs={{0,24},{4,28},{8,16},{12,20},{16,8},{20,12},{24,0},{28,4},{1,25},{... | collective-permute-start | bytes 208904 | tf_op jit(solution)/shard_map/ppermute | solution.py:71
  23.1 0.5 %near_keep.1.keep_ref = bf16[272,128]{1,0:T(8,128)(2,1)S(1)} custom-call(bf16[1664,128]{1,0:T(8,128)(2,1)S(1)} %get-tuple-element.24.dye_ref, bf16[512,512]{1,0:T(8,128)(2,1)S(1)} %get-tuple-element.21.toep_ref, bf16[64,512]{1,0:T(8,128)(2,1)S(1)} %get-tuple-element.22.rest_ref, bf16[4,16,128]{2,1,0:T(8,128)(2,1)S(1)} %get-tuple-element.30.taps_ref), custom_call_target="tpu_custom_call" | custom-call | tf_op jit(solution)/shard_map/near_keep/pallas_call | solution.py:360
  23.7 1.4 %collective-permute-start.6 = (bf16[272,128]{1,0:T(8,128)(2,1)S(1)}, bf16[272,128]{1,0:T(8,128)(2,1)S(1)}, u32[]{:S(2)}, u32[]{:S(2)}) collective-permute-start(bf16[272,128]{1,0:T(8,128)(2,1)S(1)} %get-tuple-element.27), channel_id=1, source_target_pairs={{0,16},{4,12},{8,24},{12,4},{16,0},{20,28},{24,8},{28,20},{1,17},{... | collective-permute-start | bytes 208904 | tf_op jit(solution)/shard_map/ppermute | solution.py:76
  25.1 0.8 %collective-permute-start.7 = (bf16[272,128]{1,0:T(8,128)(2,1)S(1)}, bf16[272,128]{1,0:T(8,128)(2,1)S(1)}, u32[]{:S(2)}, u32[]{:S(2)}) collective-permute-start(bf16[272,128]{1,0:T(8,128)(2,1)S(1)} %get-tuple-element.28), channel_id=1, source_target_pairs={{0,8},{4,20},{8,0},{12,28},{16,24},{20,4},{24,16},{28,12},{1,9},{5... | collective-permute-start | bytes 208904 | tf_op jit(solution)/shard_map/ppermute | solution.py:76
  25.9 1.2 %collective-permute-done.8.refs_1_.refs_3_ = bf16[272,128]{1,0:T(8,128)(2,1)S(1)} collective-permute-done((bf16[272,128]{1,0:T(8,128)(2,1)S(1)}, bf16[272,128]{1,0:T(8,128)(2,1)S(1)}, u32[]{:S(2)}, u32[]{:S(2)}) %collective-permute-start.8) | collective-permute-done | bytes 69664 | tf_op jit(solution)/shard_map/ppermute | solution.py:71
  27.1 0.5 %own.1.refs_0_.refs_2_ = bf16[272,128]{1,0:T(8,128)(2,1)S(1)} custom-call(bf16[1664,128]{1,0:T(8,128)(2,1)S(1)} %get-tuple-element.24.dye_ref, bf16[512,512]{1,0:T(8,128)(2,1)S(1)} %get-tuple-element.21.toep_ref, bf16[64,512]{1,0:T(8,128)(2,1)S(1)} %get-tuple-element.22.rest_ref, bf16[4,16,128]{2,1,0:T(8,128)(2,1)S(1)} %get-tuple-element.30.taps_ref), custom_call_target="tpu_custom_call" | custom-call | tf_op jit(solution)/shard_map/own/pallas_call | solution.py:360
  27.7 1.0 %collective-permute-done.6.refs_0_ = bf16[272,128]{1,0:T(8,128)(2,1)S(1)} collective-permute-done((bf16[272,128]{1,0:T(8,128)(2,1)S(1)}, bf16[272,128]{1,0:T(8,128)(2,1)S(1)}, u32[]{:S(2)}, u32[]{:S(2)}) %collective-permute-start.6) | collective-permute-done | bytes 69664 | tf_op jit(solution)/shard_map/ppermute | solution.py:76
  28.7 0.7 %collective-permute-done.7.refs_1_ = bf16[272,128]{1,0:T(8,128)(2,1)S(1)} collective-permute-done((bf16[272,128]{1,0:T(8,128)(2,1)S(1)}, bf16[272,128]{1,0:T(8,128)(2,1)S(1)}, u32[]{:S(2)}, u32[]{:S(2)}) %collective-permute-start.7) | collective-permute-done | bytes 69664 | tf_op jit(solution)/shard_map/ppermute | solution.py:76
  29.4 0.8 %unpack.1 = (bf16[128,1024]{1,0:T(8,128)(2,1)}, f32[64,64]{1,0:T(8,128)}) custom-call(bf16[272,128]{1,0:T(8,128)(2,1)S(1)} %collective-permute-done.6.refs_0_, bf16[272,128]{1,0:T(8,128)(2,1)S(1)} %collective-permute-done.7.refs_1_, bf16[272,128]{1,0:T(8,128)(2,1)S(1)} %own.1.refs_0_.refs_2_, bf16[272,128]{1,0:T(8,128)(2,1)S(1)} %collective-permute-done.8.refs_1_.refs_3_, ...), custom_call_target="tpu_custom_call" | custom-call | tf_op jit(solution)/shard_map/unpack/pallas_call | solution.py:360
  (13 shorter events, 0.1 us)
Async XLA Ops:
  0.6 1.0 %copy-start = (bf16[32,4096]{1,0:T(8,128)(2,1)S(1)}, bf16[32,4096]{1,0:T(8,128)(2,1)}, u32[]{:S(2)}) copy-start(bf16[32,4096]{1,0:T(8,128)(2,1)} %in_ref.1) | copy-start | bytes 786436
  2.3 7.3 %copy-start.1 = (bf16[128,1024]{1,0:T(8,128)(2,1)S(1)}, bf16[128,1024]{1,0:T(8,128)(2,1)}, u32[]{:S(2)}) copy-start(bf16[128,1024]{1,0:T(8,128)(2,1)} %x_own_ref.1) | copy-start | bytes 786436
  2.3 7.6 %copy-start.2 = (bf16[64,64]{1,0:T(8,128)(2,1)S(1)}, bf16[64,64]{1,0:T(8,128)(2,1)}, u32[]{:S(2)}) copy-start(bf16[64,64]{1,0:T(8,128)(2,1)} %f_own_ref.1) | copy-start | bytes 24580
  2.3 17.7 %all-to-all-start = ((bf16[32,32,128]{2,1,0:T(8,128)(2,1)}), bf16[32,32,128]{2,1,0:T(8,128)(2,1)S(1)}, u32[]{:S(2)}, u32[]{:S(2)}) async-start(bf16[32,32,128]{2,1,0:T(8,128)(2,1)} %fan_grads.1), calls=%async_computation | async-start | bytes 524288 | tf_op jit(solution)/shard_map/all_to_all | solution.py:393
  9.6 1.6 %collective-permute-start = (bf16[128,1024]{1,0:T(8,128)(2,1)S(1)}, bf16[128,1024]{1,0:T(8,128)(2,1)S(1)}, u32[]{:S(2)}, u32[]{:S(2)}) collective-permute-start(bf16[128,1024]{1,0:T(8,128)(2,1)S(1)} %copy-done.1), channel_id=1, source_target_pairs={{0,4},{4,0},{8,12},{12,8},{16,20},{20,16},{24,28},{28,24},{1,5},{5... | collective-permute-start | bytes 786440 | tf_op jit(solution)/shard_map/ppermute | solution.py:71
  10.0 1.3 %collective-permute-start.1 = (bf16[64,64]{1,0:T(8,128)(2,1)S(1)}, bf16[64,64]{1,0:T(8,128)(2,1)S(1)}, u32[]{:S(2)}, u32[]{:S(2)}) collective-permute-start(bf16[64,64]{1,0:T(8,128)(2,1)S(1)} %copy-done.2), channel_id=1, source_target_pairs={{0,4},{4,0},{8,12},{12,8},{16,20},{20,16},{24,28},{28,24},{1,5},{5... | collective-permute-start | bytes 24584 | tf_op jit(solution)/shard_map/ppermute | solution.py:71
  11.4 6.4 %collective-permute-start.2 = (bf16[272,128]{1,0:T(8,128)(2,1)S(1)}, bf16[272,128]{1,0:T(8,128)(2,1)S(1)}, u32[]{:S(2)}, u32[]{:S(2)}) collective-permute-start(bf16[272,128]{1,0:T(8,128)(2,1)S(1)} %get-tuple-element.18), channel_id=1, source_target_pairs={{0,24},{4,28},{8,16},{12,20},{16,8},{20,12},{24,0},{28,4},{1,25},{... | collective-permute-start | bytes 208904 | tf_op jit(solution)/shard_map/ppermute | solution.py:71
  14.1 5.4 %collective-permute-start.3 = (bf16[272,128]{1,0:T(8,128)(2,1)S(1)}, bf16[272,128]{1,0:T(8,128)(2,1)S(1)}, u32[]{:S(2)}, u32[]{:S(2)}) collective-permute-start(bf16[272,128]{1,0:T(8,128)(2,1)S(1)} %get-tuple-element.19), channel_id=1, source_target_pairs={{0,16},{4,20},{8,24},{12,28},{16,0},{20,4},{24,8},{28,12},{1,17},{... | collective-permute-start | bytes 208904 | tf_op jit(solution)/shard_map/ppermute | solution.py:71
  14.7 4.8 %collective-permute-start.4 = (bf16[272,128]{1,0:T(8,128)(2,1)S(1)}, bf16[272,128]{1,0:T(8,128)(2,1)S(1)}, u32[]{:S(2)}, u32[]{:S(2)}) collective-permute-start(bf16[272,128]{1,0:T(8,128)(2,1)S(1)} %get-tuple-element.20), channel_id=1, source_target_pairs={{0,8},{4,12},{8,0},{12,4},{16,24},{20,28},{24,16},{28,20},{1,9},{5... | collective-permute-start | bytes 208904 | tf_op jit(solution)/shard_map/ppermute | solution.py:71
  21.6 2.1 %collective-permute-start.5 = (bf16[272,128]{1,0:T(8,128)(2,1)S(1)}, bf16[272,128]{1,0:T(8,128)(2,1)S(1)}, u32[]{:S(2)}, u32[]{:S(2)}) collective-permute-start(bf16[272,128]{1,0:T(8,128)(2,1)S(1)} %get-tuple-element.26), channel_id=1, source_target_pairs={{0,4},{4,0},{8,12},{12,8},{16,20},{20,16},{24,28},{28,24},{1,5},{5... | collective-permute-start | bytes 208904 | tf_op jit(solution)/shard_map/ppermute | solution.py:71
  21.8 5.3 %collective-permute-start.8 = (bf16[272,128]{1,0:T(8,128)(2,1)S(1)}, bf16[272,128]{1,0:T(8,128)(2,1)S(1)}, u32[]{:S(2)}, u32[]{:S(2)}) collective-permute-start(bf16[272,128]{1,0:T(8,128)(2,1)S(1)} %get-tuple-element.29), channel_id=1, source_target_pairs={{0,24},{4,28},{8,16},{12,20},{16,8},{20,12},{24,0},{28,4},{1,25},{... | collective-permute-start | bytes 208904 | tf_op jit(solution)/shard_map/ppermute | solution.py:71
  23.7 5.0 %collective-permute-start.6 = (bf16[272,128]{1,0:T(8,128)(2,1)S(1)}, bf16[272,128]{1,0:T(8,128)(2,1)S(1)}, u32[]{:S(2)}, u32[]{:S(2)}) collective-permute-start(bf16[272,128]{1,0:T(8,128)(2,1)S(1)} %get-tuple-element.27), channel_id=1, source_target_pairs={{0,16},{4,12},{8,24},{12,4},{16,0},{20,28},{24,8},{28,20},{1,17},{... | collective-permute-start | bytes 208904 | tf_op jit(solution)/shard_map/ppermute | solution.py:76
  25.1 4.3 %collective-permute-start.7 = (bf16[272,128]{1,0:T(8,128)(2,1)S(1)}, bf16[272,128]{1,0:T(8,128)(2,1)S(1)}, u32[]{:S(2)}, u32[]{:S(2)}) collective-permute-start(bf16[272,128]{1,0:T(8,128)(2,1)S(1)} %get-tuple-element.28), channel_id=1, source_target_pairs={{0,8},{4,20},{8,0},{12,28},{16,24},{20,4},{24,16},{28,12},{1,9},{5... | collective-permute-start | bytes 208904 | tf_op jit(solution)/shard_map/ppermute | solution.py:76
  27.6 1.8 %collective-permute-start.9 = (bf16[272,128]{1,0:T(8,128)(2,1)S(1)}, bf16[272,128]{1,0:T(8,128)(2,1)S(1)}, u32[]{:S(2)}, u32[]{:S(2)}) collective-permute-start(bf16[272,128]{1,0:T(8,128)(2,1)S(1)} %swap.1), channel_id=1, source_target_pairs={{0,4},{4,0},{8,12},{12,8},{16,20},{20,16},{24,28},{28,24},{1,5},{5... | collective-permute-start | bytes 208904 | tf_op jit(solution)/shard_map/ppermute | solution.py:71

commit v19 on v16

--- a/solution.py
+++ b/solution.py
@@ -209,7 +209,6 @@
     for odd in range(2):
         turned_ref[odd] = dye_ref[odd * STEP : odd * STEP + wide].T
     inputs = x_ref[...].T
-    toeplitz_rows(filt_ref, toep_ref, rest_ref)
     products = []
     for group in range(groups):
         own = slice(group * per_group, (group + 1) * per_group)
@@ -226,6 +225,7 @@
             axis=0,
         )
         products.append(jnp.dot(sides, windows, preferred_element_type=jnp.float32))
+    toeplitz_rows(filt_ref, toep_ref, rest_ref)
 
     block_len = tokens // n_seq
     seqs = [2 * (chip ^ far) + (core ^ flip) for flip in range(2)]

time: 30.3 us -> 30.3 us (level)
  no operation moved by 1% of the time
where the time goes in v19:
time: 30.3 us; the launch traced here: 30.1 us
  starting transfers between devices  15.4 us (51%)
  waiting for transfers between devices  8.66 us (29%)
  Pallas kernels  4.34 us (14%)
  local copies, waits for them, and re-layouts  0.95 us (3%)
  between operations  0.72 us (2%)
    all_to_all x1, starting transfers between devices, by_channels(): lax.all_to_all(dy, ('seq', 'chan'), split_axis=0, concat_axis=0, tiled=True)  7.3 us
    ppermute x8, waiting for transfers between devices, xor_permute(): return lax.ppermute(value, axis, pairs)  7.07 us
    ppermute x8, starting transfers between devices, xor_permute(): return lax.ppermute(value, axis, pairs)  5.46 us
    pallas_call x8, Pallas kernels, local_call(): pl.pallas_call(kernel, out_shape=out_shape, in_specs=[whole] * len(operan...  4.34 us
    ppermute x2, starting transfers between devices, turned_permute(): return lax.ppermute(value, axis, pairs)  2.68 us
    ppermute x2, waiting for transfers between devices, turned_permute(): return lax.ppermute(value, axis, pairs)  1.18 us
    unnamed x6, local copies, waits for them, and re-layouts  0.95 us
  transfers between devices with their start and end apart: 11, of which 8 were waited for; matrix products, arithmetic and copies ran while one was open for 0% of the time, Pallas kernels for 4%

profile of v19, /device:TPU:0, one launch (start us, length us, event | category | flops | bytes accessed | tf_op | source)
XLA Modules:
  0.0 30.1 jit_solution(5910936585067276782)
XLA Ops:
  0.6 0.9 %copy-done = bf16[32,4096]{1,0:T(8,128)(2,1)S(1)} copy-done((bf16[32,4096]{1,0:T(8,128)(2,1)S(1)}, bf16[32,4096]{1,0:T(8,128)(2,1)}, u32[]{:S(2)}) %copy-start) | copy-done | bytes 262168
  1.6 0.7 %fan_grads.1 = bf16[32,32,128]{2,1,0:T(8,128)(2,1)} custom-call(bf16[32,4096]{1,0:T(8,128)(2,1)S(1)} %copy-done), custom_call_target="tpu_custom_call" | custom-call | tf_op jit(solution)/shard_map/fan_grads/pallas_call | solution.py:350
  2.3 7.3 %all-to-all-start = ((bf16[32,32,128]{2,1,0:T(8,128)(2,1)}), bf16[32,32,128]{2,1,0:T(8,128)(2,1)S(1)}, u32[]{:S(2)}, u32[]{:S(2)}) async-start(bf16[32,32,128]{2,1,0:T(8,128)(2,1)} %fan_grads.1), calls=%async_computation | async-start | bytes 524288 | tf_op jit(solution)/shard_map/all_to_all | solution.py:383
  9.6 0.3 %collective-permute-start = (bf16[128,1024]{1,0:T(8,128)(2,1)S(1)}, bf16[128,1024]{1,0:T(8,128)(2,1)S(1)}, u32[]{:S(2)}, u32[]{:S(2)}) collective-permute-start(bf16[128,1024]{1,0:T(8,128)(2,1)S(1)} %copy-done.1), channel_id=1, source_target_pairs={{0,4},{4,0},{8,12},{12,8},{16,20},{20,16},{24,28},{28,24},{1,5},{5... | collective-permute-start | bytes 786440 | tf_op jit(solution)/shard_map/ppermute | solution.py:71
  10.0 0.3 collective-permute-start.1
  10.2 1.0 %collective-permute-done.1.f_other_ref = bf16[64,64]{1,0:T(8,128)(2,1)S(1)} collective-permute-done((bf16[64,64]{1,0:T(8,128)(2,1)S(1)}, bf16[64,64]{1,0:T(8,128)(2,1)S(1)}, u32[]{:S(2)}, u32[]{:S(2)}) %collective-permute-start.1) | collective-permute-done | bytes 8224 | tf_op jit(solution)/shard_map/ppermute | solution.py:71
  11.3 0.1 fan_inputs.1
  11.4 2.7 %collective-permute-start.2 = (bf16[272,128]{1,0:T(8,128)(2,1)S(1)}, bf16[272,128]{1,0:T(8,128)(2,1)S(1)}, u32[]{:S(2)}, u32[]{:S(2)}) collective-permute-start(bf16[272,128]{1,0:T(8,128)(2,1)S(1)} %get-tuple-element.17), channel_id=1, source_target_pairs={{0,24},{4,28},{8,16},{12,20},{16,8},{20,12},{24,0},{28,4},{1,25},{... | collective-permute-start | bytes 208904 | tf_op jit(solution)/shard_map/ppermute | solution.py:71
  14.1 0.6 %collective-permute-start.3 = (bf16[272,128]{1,0:T(8,128)(2,1)S(1)}, bf16[272,128]{1,0:T(8,128)(2,1)S(1)}, u32[]{:S(2)}, u32[]{:S(2)}) collective-permute-start(bf16[272,128]{1,0:T(8,128)(2,1)S(1)} %get-tuple-element.18), channel_id=1, source_target_pairs={{0,16},{4,20},{8,24},{12,28},{16,0},{20,4},{24,8},{28,12},{1,17},{... | collective-permute-start | bytes 208904 | tf_op jit(solution)/shard_map/ppermute | solution.py:71
  14.7 0.3 collective-permute-start.4
  14.9 2.8 %collective-permute-done.2.refs_1_ = bf16[272,128]{1,0:T(8,128)(2,1)S(1)} collective-permute-done((bf16[272,128]{1,0:T(8,128)(2,1)S(1)}, bf16[272,128]{1,0:T(8,128)(2,1)S(1)}, u32[]{:S(2)}, u32[]{:S(2)}) %collective-permute-start.2) | collective-permute-done | bytes 69664 | tf_op jit(solution)/shard_map/ppermute | solution.py:71
  17.8 1.7 %collective-permute-done.3.refs_2_ = bf16[272,128]{1,0:T(8,128)(2,1)S(1)} collective-permute-done((bf16[272,128]{1,0:T(8,128)(2,1)S(1)}, bf16[272,128]{1,0:T(8,128)(2,1)S(1)}, u32[]{:S(2)}, u32[]{:S(2)}) %collective-permute-start.3) | collective-permute-done | bytes 69664 | tf_op jit(solution)/shard_map/ppermute | solution.py:71
  19.5 0.4 %all-to-all-done = bf16[32,32,128]{2,1,0:T(8,128)(2,1)S(1)} async-done(((bf16[32,32,128]{2,1,0:T(8,128)(2,1)}), bf16[32,32,128]{2,1,0:T(8,128)(2,1)S(1)}, u32[]{:S(2)}, u32[]{:S(2)}) %all-to-all-start) | async-done | bytes 262176 | tf_op jit(solution)/shard_map/all_to_all | solution.py:383
  19.9 1.7 %first.1 = (bf16[1664,128]{1,0:T(8,128)(2,1)S(1)}, bf16[4,16,128]{2,1,0:T(8,128)(2,1)S(1)}, bf16[512,512]{1,0:T(8,128)(2,1)S(1)}, bf16[64,512]{1,0:T(8,128)(2,1)...) custom-call(bf16[1024,128]{1,0:T(8,128)(2,1)S(1)} %bitcast.1, ...), custom_call_target="tpu_custom_call" | custom-call | tf_op jit(solution)/shard_map/first/pallas_call | solution.py:350
  21.6 0.4 %collective-permute-start.5 = (bf16[272,128]{1,0:T(8,128)(2,1)S(1)}, bf16[272,128]{1,0:T(8,128)(2,1)S(1)}, u32[]{:S(2)}, u32[]{:S(2)}) collective-permute-start(bf16[272,128]{1,0:T(8,128)(2,1)S(1)} %get-tuple-element.24), channel_id=1, source_target_pairs={{0,4},{4,0},{8,12},{12,8},{16,20},{20,16},{24,28},{28,24},{1,5},{5... | collective-permute-start | bytes 208904 | tf_op jit(solution)/shard_map/ppermute | solution.py:71
  22.0 0.9 %collective-permute-start.8 = (bf16[272,128]{1,0:T(8,128)(2,1)S(1)}, bf16[272,128]{1,0:T(8,128)(2,1)S(1)}, u32[]{:S(2)}, u32[]{:S(2)}) collective-permute-start(bf16[272,128]{1,0:T(8,128)(2,1)S(1)} %get-tuple-element.27), channel_id=1, source_target_pairs={{0,24},{4,28},{8,16},{12,20},{16,8},{20,12},{24,0},{28,4},{1,25},{... | collective-permute-start | bytes 208904 | tf_op jit(solution)/shard_map/ppermute | solution.py:71
  22.9 0.5 %near_keep.1.keep_ref = bf16[272,128]{1,0:T(8,128)(2,1)S(1)} custom-call(bf16[1664,128]{1,0:T(8,128)(2,1)S(1)} %get-tuple-element.20.dye_ref, bf16[512,512]{1,0:T(8,128)(2,1)S(1)} %get-tuple-element.21.toep_ref, bf16[64,512]{1,0:T(8,128)(2,1)S(1)} %get-tuple-element.22.rest_ref, bf16[4,16,128]{2,1,0:T(8,128)(2,1)S(1)} %get-tuple-element.28.taps_ref), custom_call_target="tpu_custom_call" | custom-call | tf_op jit(solution)/shard_map/near_keep/pallas_call | solution.py:350
  23.4 1.5 %collective-permute-start.6 = (bf16[272,128]{1,0:T(8,128)(2,1)S(1)}, bf16[272,128]{1,0:T(8,128)(2,1)S(1)}, u32[]{:S(2)}, u32[]{:S(2)}) collective-permute-start(bf16[272,128]{1,0:T(8,128)(2,1)S(1)} %get-tuple-element.25), channel_id=1, source_target_pairs={{0,16},{4,12},{8,24},{12,4},{16,0},{20,28},{24,8},{28,20},{1,17},{... | collective-permute-start | bytes 208904 | tf_op jit(solution)/shard_map/ppermute | solution.py:76
  24.9 1.1 %collective-permute-start.7 = (bf16[272,128]{1,0:T(8,128)(2,1)S(1)}, bf16[272,128]{1,0:T(8,128)(2,1)S(1)}, u32[]{:S(2)}, u32[]{:S(2)}) collective-permute-start(bf16[272,128]{1,0:T(8,128)(2,1)S(1)} %get-tuple-element.26), channel_id=1, source_target_pairs={{0,8},{4,20},{8,0},{12,28},{16,24},{20,4},{24,16},{28,12},{1,9},{5... | collective-permute-start | bytes 208904 | tf_op jit(solution)/shard_map/ppermute | solution.py:76
  26.1 1.4 %collective-permute-done.8.refs_1_.refs_3_ = bf16[272,128]{1,0:T(8,128)(2,1)S(1)} collective-permute-done((bf16[272,128]{1,0:T(8,128)(2,1)S(1)}, bf16[272,128]{1,0:T(8,128)(2,1)S(1)}, u32[]{:S(2)}, u32[]{:S(2)}) %collective-permute-start.8) | collective-permute-done | bytes 69664 | tf_op jit(solution)/shard_map/ppermute | solution.py:71
  27.5 0.5 %own.1.refs_0_.refs_2_ = bf16[272,128]{1,0:T(8,128)(2,1)S(1)} custom-call(bf16[1664,128]{1,0:T(8,128)(2,1)S(1)} %get-tuple-element.20.dye_ref, bf16[512,512]{1,0:T(8,128)(2,1)S(1)} %get-tuple-element.21.toep_ref, bf16[64,512]{1,0:T(8,128)(2,1)S(1)} %get-tuple-element.22.rest_ref, bf16[4,16,128]{2,1,0:T(8,128)(2,1)S(1)} %get-tuple-element.28.taps_ref), custom_call_target="tpu_custom_call" | custom-call | tf_op jit(solution)/shard_map/own/pallas_call | solution.py:350
  28.1 0.6 %collective-permute-done.6.refs_0_ = bf16[272,128]{1,0:T(8,128)(2,1)S(1)} collective-permute-done((bf16[272,128]{1,0:T(8,128)(2,1)S(1)}, bf16[272,128]{1,0:T(8,128)(2,1)S(1)}, u32[]{:S(2)}, u32[]{:S(2)}) %collective-permute-start.6) | collective-permute-done | bytes 69664 | tf_op jit(solution)/shard_map/ppermute | solution.py:76
  28.6 0.6 %collective-permute-done.7.refs_1_ = bf16[272,128]{1,0:T(8,128)(2,1)S(1)} collective-permute-done((bf16[272,128]{1,0:T(8,128)(2,1)S(1)}, bf16[272,128]{1,0:T(8,128)(2,1)S(1)}, u32[]{:S(2)}, u32[]{:S(2)}) %collective-permute-start.7) | collective-permute-done | bytes 69664 | tf_op jit(solution)/shard_map/ppermute | solution.py:76
  29.3 0.8 %unpack.1 = (bf16[128,1024]{1,0:T(8,128)(2,1)}, f32[64,64]{1,0:T(8,128)}) custom-call(bf16[272,128]{1,0:T(8,128)(2,1)S(1)} %collective-permute-done.6.refs_0_, bf16[272,128]{1,0:T(8,128)(2,1)S(1)} %collective-permute-done.7.refs_1_, bf16[272,128]{1,0:T(8,128)(2,1)S(1)} %own.1.refs_0_.refs_2_, bf16[272,128]{1,0:T(8,128)(2,1)S(1)} %collective-permute-done.8.refs_1_.refs_3_, ...), custom_call_target="tpu_custom_call" | custom-call | tf_op jit(solution)/shard_map/unpack/pallas_call | solution.py:350
  (12 shorter events, 0.2 us)
Async XLA Ops:
  0.6 1.0 %copy-start = (bf16[32,4096]{1,0:T(8,128)(2,1)S(1)}, bf16[32,4096]{1,0:T(8,128)(2,1)}, u32[]{:S(2)}) copy-start(bf16[32,4096]{1,0:T(8,128)(2,1)} %in_ref.1) | copy-start | bytes 786436
  2.3 7.3 %copy-start.1 = (bf16[128,1024]{1,0:T(8,128)(2,1)S(1)}, bf16[128,1024]{1,0:T(8,128)(2,1)}, u32[]{:S(2)}) copy-start(bf16[128,1024]{1,0:T(8,128)(2,1)} %x_own_ref.1) | copy-start | bytes 786436
  2.3 7.6 %copy-start.2 = (bf16[64,64]{1,0:T(8,128)(2,1)S(1)}, bf16[64,64]{1,0:T(8,128)(2,1)}, u32[]{:S(2)}) copy-start(bf16[64,64]{1,0:T(8,128)(2,1)} %f_own_ref.1) | copy-start | bytes 24580
  2.3 17.6 %all-to-all-start = ((bf16[32,32,128]{2,1,0:T(8,128)(2,1)}), bf16[32,32,128]{2,1,0:T(8,128)(2,1)S(1)}, u32[]{:S(2)}, u32[]{:S(2)}) async-start(bf16[32,32,128]{2,1,0:T(8,128)(2,1)} %fan_grads.1), calls=%async_computation | async-start | bytes 524288 | tf_op jit(solution)/shard_map/all_to_all | solution.py:383
  9.6 1.6 %collective-permute-start = (bf16[128,1024]{1,0:T(8,128)(2,1)S(1)}, bf16[128,1024]{1,0:T(8,128)(2,1)S(1)}, u32[]{:S(2)}, u32[]{:S(2)}) collective-permute-start(bf16[128,1024]{1,0:T(8,128)(2,1)S(1)} %copy-done.1), channel_id=1, source_target_pairs={{0,4},{4,0},{8,12},{12,8},{16,20},{20,16},{24,28},{28,24},{1,5},{5... | collective-permute-start | bytes 786440 | tf_op jit(solution)/shard_map/ppermute | solution.py:71
  10.0 1.3 %collective-permute-start.1 = (bf16[64,64]{1,0:T(8,128)(2,1)S(1)}, bf16[64,64]{1,0:T(8,128)(2,1)S(1)}, u32[]{:S(2)}, u32[]{:S(2)}) collective-permute-start(bf16[64,64]{1,0:T(8,128)(2,1)S(1)} %copy-done.2), channel_id=1, source_target_pairs={{0,4},{4,0},{8,12},{12,8},{16,20},{20,16},{24,28},{28,24},{1,5},{5... | collective-permute-start | bytes 24584 | tf_op jit(solution)/shard_map/ppermute | solution.py:71
  11.4 6.4 %collective-permute-start.2 = (bf16[272,128]{1,0:T(8,128)(2,1)S(1)}, bf16[272,128]{1,0:T(8,128)(2,1)S(1)}, u32[]{:S(2)}, u32[]{:S(2)}) collective-permute-start(bf16[272,128]{1,0:T(8,128)(2,1)S(1)} %get-tuple-element.17), channel_id=1, source_target_pairs={{0,24},{4,28},{8,16},{12,20},{16,8},{20,12},{24,0},{28,4},{1,25},{... | collective-permute-start | bytes 208904 | tf_op jit(solution)/shard_map/ppermute | solution.py:71
  14.1 5.4 %collective-permute-start.3 = (bf16[272,128]{1,0:T(8,128)(2,1)S(1)}, bf16[272,128]{1,0:T(8,128)(2,1)S(1)}, u32[]{:S(2)}, u32[]{:S(2)}) collective-permute-start(bf16[272,128]{1,0:T(8,128)(2,1)S(1)} %get-tuple-element.18), channel_id=1, source_target_pairs={{0,16},{4,20},{8,24},{12,28},{16,0},{20,4},{24,8},{28,12},{1,17},{... | collective-permute-start | bytes 208904 | tf_op jit(solution)/shard_map/ppermute | solution.py:71
  14.7 4.8 %collective-permute-start.4 = (bf16[272,128]{1,0:T(8,128)(2,1)S(1)}, bf16[272,128]{1,0:T(8,128)(2,1)S(1)}, u32[]{:S(2)}, u32[]{:S(2)}) collective-permute-start(bf16[272,128]{1,0:T(8,128)(2,1)S(1)} %get-tuple-element.19), channel_id=1, source_target_pairs={{0,8},{4,12},{8,0},{12,4},{16,24},{20,28},{24,16},{28,20},{1,9},{5... | collective-permute-start | bytes 208904 | tf_op jit(solution)/shard_map/ppermute | solution.py:71
  21.6 1.8 %collective-permute-start.5 = (bf16[272,128]{1,0:T(8,128)(2,1)S(1)}, bf16[272,128]{1,0:T(8,128)(2,1)S(1)}, u32[]{:S(2)}, u32[]{:S(2)}) collective-permute-start(bf16[272,128]{1,0:T(8,128)(2,1)S(1)} %get-tuple-element.24), channel_id=1, source_target_pairs={{0,4},{4,0},{8,12},{12,8},{16,20},{20,16},{24,28},{28,24},{1,5},{5... | collective-permute-start | bytes 208904 | tf_op jit(solution)/shard_map/ppermute | solution.py:71
  22.0 5.5 %collective-permute-start.8 = (bf16[272,128]{1,0:T(8,128)(2,1)S(1)}, bf16[272,128]{1,0:T(8,128)(2,1)S(1)}, u32[]{:S(2)}, u32[]{:S(2)}) collective-permute-start(bf16[272,128]{1,0:T(8,128)(2,1)S(1)} %get-tuple-element.27), channel_id=1, source_target_pairs={{0,24},{4,28},{8,16},{12,20},{16,8},{20,12},{24,0},{28,4},{1,25},{... | collective-permute-start | bytes 208904 | tf_op jit(solution)/shard_map/ppermute | solution.py:71
  23.4 5.2 %collective-permute-start.6 = (bf16[272,128]{1,0:T(8,128)(2,1)S(1)}, bf16[272,128]{1,0:T(8,128)(2,1)S(1)}, u32[]{:S(2)}, u32[]{:S(2)}) collective-permute-start(bf16[272,128]{1,0:T(8,128)(2,1)S(1)} %get-tuple-element.25), channel_id=1, source_target_pairs={{0,16},{4,12},{8,24},{12,4},{16,0},{20,28},{24,8},{28,20},{1,17},{... | collective-permute-start | bytes 208904 | tf_op jit(solution)/shard_map/ppermute | solution.py:76
  24.9 4.3 %collective-permute-start.7 = (bf16[272,128]{1,0:T(8,128)(2,1)S(1)}, bf16[272,128]{1,0:T(8,128)(2,1)S(1)}, u32[]{:S(2)}, u32[]{:S(2)}) collective-permute-start(bf16[272,128]{1,0:T(8,128)(2,1)S(1)} %get-tuple-element.26), channel_id=1, source_target_pairs={{0,8},{4,20},{8,0},{12,28},{16,24},{20,4},{24,16},{28,12},{1,9},{5... | collective-permute-start | bytes 208904 | tf_op jit(solution)/shard_map/ppermute | solution.py:76
  28.0 1.3 %collective-permute-start.9 = (bf16[272,128]{1,0:T(8,128)(2,1)S(1)}, bf16[272,128]{1,0:T(8,128)(2,1)S(1)}, u32[]{:S(2)}, u32[]{:S(2)}) collective-permute-start(bf16[272,128]{1,0:T(8,128)(2,1)S(1)} %swap.1), channel_id=1, source_target_pairs={{0,4},{4,0},{8,12},{12,8},{16,20},{20,16},{24,28},{28,24},{1,5},{5... | collective-permute-start | bytes 208904 | tf_op jit(solution)/shard_map/ppermute | solution.py:71

commit v20 on v18

--- a/solution.py
+++ b/solution.py
@@ -192,13 +192,12 @@
 def inputs_kernel(n_seq, taps_here, *refs):
     chips = n_seq // 2
     in_refs = refs[:chips]
-    toep_ref, rest_ref, sides_ref, x_ref, filt_ref = refs[chips:]
+    filt_ref, sides_ref, x_ref = refs[chips:]
     groups = sides_ref.shape[0]
     per_group = LANES // groups
     place_inputs(in_refs, taps_here, x_ref, filt_ref)
     pairs = x_ref.shape[0] // (2 * STEP)
     inputs = x_ref[...].T
-    toeplitz_rows(filt_ref, toep_ref, rest_ref)
     for group in range(groups):
         own = slice(group * per_group, (group + 1) * per_group)
         sides = jnp.concatenate(
@@ -207,9 +206,9 @@
         sides_ref[group] = jnp.concatenate([sides[:STEP], sides[STEP:]], axis=1)
 
 
-def first_kernel(n_seq, taps_here, far, near, dy_ref, toep_ref, rest_ref, sides_ref, *refs):
+def first_kernel(n_seq, taps_here, far, near, dy_ref, filt_ref, sides_ref, *refs):
     chips = n_seq // 2
-    dye_ref, taps_ref, far_ref, near_ref, turned_ref = refs
+    dye_ref, taps_ref, toep_ref, rest_ref, far_ref, near_ref, turned_ref = refs
     tokens = dy_ref.shape[0]
     groups = EXTRA // 2
     taps = n_seq * taps_here
@@ -224,6 +223,7 @@
     wide = (pairs - 1) * LANES + reach
     for odd in range(2):
         turned_ref[odd] = dye_ref[odd * STEP : odd * STEP + wide].T
+    toeplitz_rows(filt_ref, toep_ref, rest_ref)
     products = []
     for group in range(groups):
         own = slice(group * per_group, (group + 1) * per_group)
@@ -400,24 +400,27 @@
     )
     near = masks[2:]
     near_shape = half(len(near) * (block_len + EXTRA // 2), LANES)
-    toeplitz, outside, sides = local_call(
+    by_chip, sides = local_call(
         functools.partial(inputs_kernel, n_seq, taps_here),
         [
-            half(groups * SLAB, taps),
-            half(SLAB, groups * SLAB),
+            jax.ShapeDtypeStruct((chips, groups, LANES), jnp.float32),
             half(groups, STEP, tokens * LANES // (groups * STEP)),
         ],
         fan_out(pieces, "seq", 2),
         "inputs",
+        [pltpu.VMEM((tokens, LANES), jnp.bfloat16)],
+    )
+    dye, tap_parts, toeplitz, outside, far, send = local_call(
+        functools.partial(first_kernel, n_seq, taps_here, masks[1], near),
         [
-            pltpu.VMEM((tokens, LANES), jnp.bfloat16),
-            pltpu.VMEM((chips, groups, LANES), jnp.float32),
+            half(tokens + taps + LANES, LANES),
+            half(chips, EXTRA, LANES),
+            half(groups * SLAB, taps),
+            half(SLAB, groups * SLAB),
+            unit,
+            near_shape,
         ],
-    )
-    dye, tap_parts, far, send = local_call(
-        functools.partial(first_kernel, n_seq, taps_here, masks[1], near),
-        [half(tokens + taps + LANES, LANES), half(chips, EXTRA, LANES), unit, near_shape],
-        (dy.reshape(tokens, LANES), toeplitz, outside, sides),
+        (dy.reshape(tokens, LANES), by_chip, sides),
         "first",
         [pltpu.VMEM((2, LANES, tokens + taps), jnp.bfloat16)],
     )

time: 30.4 us -> 30.1 us (level)
  transfers between devices with their start and end apart: 11 -> 11, of which waited for: 6 -> 7; matrix products, arithmetic and copies ran while one was open for 0% -> 0% of each run, Pallas kernels for 6% -> 5%
where the time goes in v20:
time: 30.1 us; the launch traced here: 29.9 us
  starting transfers between devices  15.4 us (51%)
  waiting for transfers between devices  8.39 us (28%)
  Pallas kernels  4.39 us (15%)
  local copies, waits for them, and re-layouts  0.95 us (3%)
  between operations  0.73 us (2%)
    all_to_all x1, starting transfers between devices, by_channels(): lax.all_to_all(dy, ('seq', 'chan'), split_axis=0, concat_axis=0, tiled=True)  7.3 us
    ppermute x8, waiting for transfers between devices, xor_permute(): return lax.ppermute(value, axis, pairs)  6.78 us
    ppermute x8, starting transfers between devices, xor_permute(): return lax.ppermute(value, axis, pairs)  5.65 us
    pallas_call x9, Pallas kernels, local_call(): pl.pallas_call(kernel, out_shape=out_shape, in_specs=[whole] * len(operan...  4.39 us
    ppermute x2, starting transfers between devices, turned_permute(): return lax.ppermute(value, axis, pairs)  2.49 us
    ppermute x2, waiting for transfers between devices, turned_permute(): return lax.ppermute(value, axis, pairs)  1.46 us
    unnamed x6, local copies, waits for them, and re-layouts  0.95 us
  transfers between devices with their start and end apart: 11, of which 7 were waited for; matrix products, arithmetic and copies ran while one was open for 0% of the time, Pallas kernels for 5%

profile of v20, /device:TPU:0, one launch (start us, length us, event | category | flops | bytes accessed | tf_op | source)
XLA Modules:
  0.0 29.9 jit_solution(14885257169147669773)
XLA Ops:
  0.6 0.9 %copy-done = bf16[32,4096]{1,0:T(8,128)(2,1)S(1)} copy-done((bf16[32,4096]{1,0:T(8,128)(2,1)S(1)}, bf16[32,4096]{1,0:T(8,128)(2,1)}, u32[]{:S(2)}) %copy-start) | copy-done | bytes 262168
  1.6 0.7 %fan_grads.1 = bf16[32,32,128]{2,1,0:T(8,128)(2,1)} custom-call(bf16[32,4096]{1,0:T(8,128)(2,1)S(1)} %copy-done), custom_call_target="tpu_custom_call" | custom-call | tf_op jit(solution)/shard_map/fan_grads/pallas_call | solution.py:360
  2.3 7.3 %all-to-all-start = ((bf16[32,32,128]{2,1,0:T(8,128)(2,1)}), bf16[32,32,128]{2,1,0:T(8,128)(2,1)S(1)}, u32[]{:S(2)}, u32[]{:S(2)}) async-start(bf16[32,32,128]{2,1,0:T(8,128)(2,1)} %fan_grads.1), calls=%async_computation | async-start | bytes 524288 | tf_op jit(solution)/shard_map/all_to_all | solution.py:393
  9.6 0.3 %collective-permute-start = (bf16[128,1024]{1,0:T(8,128)(2,1)S(1)}, bf16[128,1024]{1,0:T(8,128)(2,1)S(1)}, u32[]{:S(2)}, u32[]{:S(2)}) collective-permute-start(bf16[128,1024]{1,0:T(8,128)(2,1)S(1)} %copy-done.1), channel_id=1, source_target_pairs={{0,4},{4,0},{8,12},{12,8},{16,20},{20,16},{24,28},{28,24},{1,5},{5... | collective-permute-start | bytes 786440 | tf_op jit(solution)/shard_map/ppermute | solution.py:71
  10.0 0.3 collective-permute-start.1
  10.2 1.0 %collective-permute-done.1.f_other_ref = bf16[64,64]{1,0:T(8,128)(2,1)S(1)} collective-permute-done((bf16[64,64]{1,0:T(8,128)(2,1)S(1)}, bf16[64,64]{1,0:T(8,128)(2,1)S(1)}, u32[]{:S(2)}, u32[]{:S(2)}) %collective-permute-start.1) | collective-permute-done | bytes 8224 | tf_op jit(solution)/shard_map/ppermute | solution.py:71
  11.4 2.7 %collective-permute-start.2 = (bf16[272,128]{1,0:T(8,128)(2,1)S(1)}, bf16[272,128]{1,0:T(8,128)(2,1)S(1)}, u32[]{:S(2)}, u32[]{:S(2)}) collective-permute-start(bf16[272,128]{1,0:T(8,128)(2,1)S(1)} %get-tuple-element.19), channel_id=1, source_target_pairs={{0,24},{4,28},{8,16},{12,20},{16,8},{20,12},{24,0},{28,4},{1,25},{... | collective-permute-start | bytes 208904 | tf_op jit(solution)/shard_map/ppermute | solution.py:71
  14.1 0.6 %collective-permute-start.3 = (bf16[272,128]{1,0:T(8,128)(2,1)S(1)}, bf16[272,128]{1,0:T(8,128)(2,1)S(1)}, u32[]{:S(2)}, u32[]{:S(2)}) collective-permute-start(bf16[272,128]{1,0:T(8,128)(2,1)S(1)} %get-tuple-element.20), channel_id=1, source_target_pairs={{0,16},{4,20},{8,24},{12,28},{16,0},{20,4},{24,8},{28,12},{1,17},{... | collective-permute-start | bytes 208904 | tf_op jit(solution)/shard_map/ppermute | solution.py:71
  14.7 0.3 collective-permute-start.4
  14.9 2.8 %collective-permute-done.2.refs_1_ = bf16[272,128]{1,0:T(8,128)(2,1)S(1)} collective-permute-done((bf16[272,128]{1,0:T(8,128)(2,1)S(1)}, bf16[272,128]{1,0:T(8,128)(2,1)S(1)}, u32[]{:S(2)}, u32[]{:S(2)}) %collective-permute-start.2) | collective-permute-done | bytes 69664 | tf_op jit(solution)/shard_map/ppermute | solution.py:71
  17.8 1.7 %collective-permute-done.3.refs_2_ = bf16[272,128]{1,0:T(8,128)(2,1)S(1)} collective-permute-done((bf16[272,128]{1,0:T(8,128)(2,1)S(1)}, bf16[272,128]{1,0:T(8,128)(2,1)S(1)}, u32[]{:S(2)}, u32[]{:S(2)}) %collective-permute-start.3) | collective-permute-done | bytes 69664 | tf_op jit(solution)/shard_map/ppermute | solution.py:71
  19.5 0.3 inputs.1
  19.8 0.1 all-to-all-done
  19.9 1.5 %first.1 = (bf16[1664,128]{1,0:T(8,128)(2,1)S(1)}, bf16[4,16,128]{2,1,0:T(8,128)(2,1)S(1)}, bf16[512,512]{1,0:T(8,128)(2,1)S(1)}, bf16[64,512]{1,0:T(8,128)(2,1)...) custom-call(bf16[1024,128]{1,0:T(8,128)(2,1)S(1)} %bitcast.1, ...), custom_call_target="tpu_custom_call" | custom-call | tf_op jit(solution)/shard_map/first/pallas_call | solution.py:360
  21.4 0.4 %collective-permute-start.5 = (bf16[272,128]{1,0:T(8,128)(2,1)S(1)}, bf16[272,128]{1,0:T(8,128)(2,1)S(1)}, u32[]{:S(2)}, u32[]{:S(2)}) collective-permute-start(bf16[272,128]{1,0:T(8,128)(2,1)S(1)} %get-tuple-element.28), channel_id=1, source_target_pairs={{0,4},{4,0},{8,12},{12,8},{16,20},{20,16},{24,28},{28,24},{1,5},{5... | collective-permute-start | bytes 208904 | tf_op jit(solution)/shard_map/ppermute | solution.py:71
  21.8 1.1 %collective-permute-start.8 = (bf16[272,128]{1,0:T(8,128)(2,1)S(1)}, bf16[272,128]{1,0:T(8,128)(2,1)S(1)}, u32[]{:S(2)}, u32[]{:S(2)}) collective-permute-start(bf16[272,128]{1,0:T(8,128)(2,1)S(1)} %get-tuple-element.31), channel_id=1, source_target_pairs={{0,24},{4,28},{8,16},{12,20},{16,8},{20,12},{24,0},{28,4},{1,25},{... | collective-permute-start | bytes 208904 | tf_op jit(solution)/shard_map/ppermute | solution.py:71
  22.9 0.5 %near_keep.1.keep_ref = bf16[272,128]{1,0:T(8,128)(2,1)S(1)} custom-call(bf16[1664,128]{1,0:T(8,128)(2,1)S(1)} %get-tuple-element.24.dye_ref, bf16[512,512]{1,0:T(8,128)(2,1)S(1)} %get-tuple-element.25.toep_ref, bf16[64,512]{1,0:T(8,128)(2,1)S(1)} %get-tuple-element.26.rest_ref, bf16[4,16,128]{2,1,0:T(8,128)(2,1)S(1)} %get-tuple-element.32.taps_ref), custom_call_target="tpu_custom_call" | custom-call | tf_op jit(solution)/shard_map/near_keep/pallas_call | solution.py:360
  23.4 1.4 %collective-permute-start.6 = (bf16[272,128]{1,0:T(8,128)(2,1)S(1)}, bf16[272,128]{1,0:T(8,128)(2,1)S(1)}, u32[]{:S(2)}, u32[]{:S(2)}) collective-permute-start(bf16[272,128]{1,0:T(8,128)(2,1)S(1)} %get-tuple-element.29), channel_id=1, source_target_pairs={{0,16},{4,12},{8,24},{12,4},{16,0},{20,28},{24,8},{28,20},{1,17},{... | collective-permute-start | bytes 208904 | tf_op jit(solution)/shard_map/ppermute | solution.py:76
  24.8 1.1 %collective-permute-start.7 = (bf16[272,128]{1,0:T(8,128)(2,1)S(1)}, bf16[272,128]{1,0:T(8,128)(2,1)S(1)}, u32[]{:S(2)}, u32[]{:S(2)}) collective-permute-start(bf16[272,128]{1,0:T(8,128)(2,1)S(1)} %get-tuple-element.30), channel_id=1, source_target_pairs={{0,8},{4,20},{8,0},{12,28},{16,24},{20,4},{24,16},{28,12},{1,9},{5... | collective-permute-start | bytes 208904 | tf_op jit(solution)/shard_map/ppermute | solution.py:76
  25.9 1.2 %collective-permute-done.8.refs_1_.refs_3_ = bf16[272,128]{1,0:T(8,128)(2,1)S(1)} collective-permute-done((bf16[272,128]{1,0:T(8,128)(2,1)S(1)}, bf16[272,128]{1,0:T(8,128)(2,1)S(1)}, u32[]{:S(2)}, u32[]{:S(2)}) %collective-permute-start.8) | collective-permute-done | bytes 69664 | tf_op jit(solution)/shard_map/ppermute | solution.py:71
  27.1 0.5 %own.1.refs_0_.refs_2_ = bf16[272,128]{1,0:T(8,128)(2,1)S(1)} custom-call(bf16[1664,128]{1,0:T(8,128)(2,1)S(1)} %get-tuple-element.24.dye_ref, bf16[512,512]{1,0:T(8,128)(2,1)S(1)} %get-tuple-element.25.toep_ref, bf16[64,512]{1,0:T(8,128)(2,1)S(1)} %get-tuple-element.26.rest_ref, bf16[4,16,128]{2,1,0:T(8,128)(2,1)S(1)} %get-tuple-element.32.taps_ref), custom_call_target="tpu_custom_call" | custom-call | tf_op jit(solution)/shard_map/own/pallas_call | solution.py:360
  27.6 0.8 %collective-permute-done.6.refs_0_ = bf16[272,128]{1,0:T(8,128)(2,1)S(1)} collective-permute-done((bf16[272,128]{1,0:T(8,128)(2,1)S(1)}, bf16[272,128]{1,0:T(8,128)(2,1)S(1)}, u32[]{:S(2)}, u32[]{:S(2)}) %collective-permute-start.6) | collective-permute-done | bytes 69664 | tf_op jit(solution)/shard_map/ppermute | solution.py:76
  28.5 0.6 %collective-permute-done.7.refs_1_ = bf16[272,128]{1,0:T(8,128)(2,1)S(1)} collective-permute-done((bf16[272,128]{1,0:T(8,128)(2,1)S(1)}, bf16[272,128]{1,0:T(8,128)(2,1)S(1)}, u32[]{:S(2)}, u32[]{:S(2)}) %collective-permute-start.7) | collective-permute-done | bytes 69664 | tf_op jit(solution)/shard_map/ppermute | solution.py:76
  29.1 0.8 %unpack.1 = (bf16[128,1024]{1,0:T(8,128)(2,1)}, f32[64,64]{1,0:T(8,128)}) custom-call(bf16[272,128]{1,0:T(8,128)(2,1)S(1)} %collective-permute-done.6.refs_0_, bf16[272,128]{1,0:T(8,128)(2,1)S(1)} %collective-permute-done.7.refs_1_, bf16[272,128]{1,0:T(8,128)(2,1)S(1)} %own.1.refs_0_.refs_2_, bf16[272,128]{1,0:T(8,128)(2,1)S(1)} %collective-permute-done.8.refs_1_.refs_3_, ...), custom_call_target="tpu_custom_call" | custom-call | tf_op jit(solution)/shard_map/unpack/pallas_call | solution.py:360
  (13 shorter events, 0.2 us)
Async XLA Ops:
  0.6 1.0 %copy-start = (bf16[32,4096]{1,0:T(8,128)(2,1)S(1)}, bf16[32,4096]{1,0:T(8,128)(2,1)}, u32[]{:S(2)}) copy-start(bf16[32,4096]{1,0:T(8,128)(2,1)} %in_ref.1) | copy-start | bytes 786436
  2.3 7.3 %copy-start.1 = (bf16[128,1024]{1,0:T(8,128)(2,1)S(1)}, bf16[128,1024]{1,0:T(8,128)(2,1)}, u32[]{:S(2)}) copy-start(bf16[128,1024]{1,0:T(8,128)(2,1)} %x_own_ref.1) | copy-start | bytes 786436
  2.3 7.6 %copy-start.2 = (bf16[64,64]{1,0:T(8,128)(2,1)S(1)}, bf16[64,64]{1,0:T(8,128)(2,1)}, u32[]{:S(2)}) copy-start(bf16[64,64]{1,0:T(8,128)(2,1)} %f_own_ref.1) | copy-start | bytes 24580
  2.3 17.6 %all-to-all-start = ((bf16[32,32,128]{2,1,0:T(8,128)(2,1)}), bf16[32,32,128]{2,1,0:T(8,128)(2,1)S(1)}, u32[]{:S(2)}, u32[]{:S(2)}) async-start(bf16[32,32,128]{2,1,0:T(8,128)(2,1)} %fan_grads.1), calls=%async_computation | async-start | bytes 524288 | tf_op jit(solution)/shard_map/all_to_all | solution.py:393
  9.6 1.6 %collective-permute-start = (bf16[128,1024]{1,0:T(8,128)(2,1)S(1)}, bf16[128,1024]{1,0:T(8,128)(2,1)S(1)}, u32[]{:S(2)}, u32[]{:S(2)}) collective-permute-start(bf16[128,1024]{1,0:T(8,128)(2,1)S(1)} %copy-done.1), channel_id=1, source_target_pairs={{0,4},{4,0},{8,12},{12,8},{16,20},{20,16},{24,28},{28,24},{1,5},{5... | collective-permute-start | bytes 786440 | tf_op jit(solution)/shard_map/ppermute | solution.py:71
  10.0 1.3 %collective-permute-start.1 = (bf16[64,64]{1,0:T(8,128)(2,1)S(1)}, bf16[64,64]{1,0:T(8,128)(2,1)S(1)}, u32[]{:S(2)}, u32[]{:S(2)}) collective-permute-start(bf16[64,64]{1,0:T(8,128)(2,1)S(1)} %copy-done.2), channel_id=1, source_target_pairs={{0,4},{4,0},{8,12},{12,8},{16,20},{20,16},{24,28},{28,24},{1,5},{5... | collective-permute-start | bytes 24584 | tf_op jit(solution)/shard_map/ppermute | solution.py:71
  11.4 6.4 %collective-permute-start.2 = (bf16[272,128]{1,0:T(8,128)(2,1)S(1)}, bf16[272,128]{1,0:T(8,128)(2,1)S(1)}, u32[]{:S(2)}, u32[]{:S(2)}) collective-permute-start(bf16[272,128]{1,0:T(8,128)(2,1)S(1)} %get-tuple-element.19), channel_id=1, source_target_pairs={{0,24},{4,28},{8,16},{12,20},{16,8},{20,12},{24,0},{28,4},{1,25},{... | collective-permute-start | bytes 208904 | tf_op jit(solution)/shard_map/ppermute | solution.py:71
  14.1 5.4 %collective-permute-start.3 = (bf16[272,128]{1,0:T(8,128)(2,1)S(1)}, bf16[272,128]{1,0:T(8,128)(2,1)S(1)}, u32[]{:S(2)}, u32[]{:S(2)}) collective-permute-start(bf16[272,128]{1,0:T(8,128)(2,1)S(1)} %get-tuple-element.20), channel_id=1, source_target_pairs={{0,16},{4,20},{8,24},{12,28},{16,0},{20,4},{24,8},{28,12},{1,17},{... | collective-permute-start | bytes 208904 | tf_op jit(solution)/shard_map/ppermute | solution.py:71
  14.7 4.8 %collective-permute-start.4 = (bf16[272,128]{1,0:T(8,128)(2,1)S(1)}, bf16[272,128]{1,0:T(8,128)(2,1)S(1)}, u32[]{:S(2)}, u32[]{:S(2)}) collective-permute-start(bf16[272,128]{1,0:T(8,128)(2,1)S(1)} %get-tuple-element.21), channel_id=1, source_target_pairs={{0,8},{4,12},{8,0},{12,4},{16,24},{20,28},{24,16},{28,20},{1,9},{5... | collective-permute-start | bytes 208904 | tf_op jit(solution)/shard_map/ppermute | solution.py:71
  21.4 2.0 %collective-permute-start.5 = (bf16[272,128]{1,0:T(8,128)(2,1)S(1)}, bf16[272,128]{1,0:T(8,128)(2,1)S(1)}, u32[]{:S(2)}, u32[]{:S(2)}) collective-permute-start(bf16[272,128]{1,0:T(8,128)(2,1)S(1)} %get-tuple-element.28), channel_id=1, source_target_pairs={{0,4},{4,0},{8,12},{12,8},{16,20},{20,16},{24,28},{28,24},{1,5},{5... | collective-permute-start | bytes 208904 | tf_op jit(solution)/shard_map/ppermute | solution.py:71
  21.8 5.3 %collective-permute-start.8 = (bf16[272,128]{1,0:T(8,128)(2,1)S(1)}, bf16[272,128]{1,0:T(8,128)(2,1)S(1)}, u32[]{:S(2)}, u32[]{:S(2)}) collective-permute-start(bf16[272,128]{1,0:T(8,128)(2,1)S(1)} %get-tuple-element.31), channel_id=1, source_target_pairs={{0,24},{4,28},{8,16},{12,20},{16,8},{20,12},{24,0},{28,4},{1,25},{... | collective-permute-start | bytes 208904 | tf_op jit(solution)/shard_map/ppermute | solution.py:71
  23.4 5.1 %collective-permute-start.6 = (bf16[272,128]{1,0:T(8,128)(2,1)S(1)}, bf16[272,128]{1,0:T(8,128)(2,1)S(1)}, u32[]{:S(2)}, u32[]{:S(2)}) collective-permute-start(bf16[272,128]{1,0:T(8,128)(2,1)S(1)} %get-tuple-element.29), channel_id=1, source_target_pairs={{0,16},{4,12},{8,24},{12,4},{16,0},{20,28},{24,8},{28,20},{1,17},{... | collective-permute-start | bytes 208904 | tf_op jit(solution)/shard_map/ppermute | solution.py:76
  24.8 4.3 %collective-permute-start.7 = (bf16[272,128]{1,0:T(8,128)(2,1)S(1)}, bf16[272,128]{1,0:T(8,128)(2,1)S(1)}, u32[]{:S(2)}, u32[]{:S(2)}) collective-permute-start(bf16[272,128]{1,0:T(8,128)(2,1)S(1)} %get-tuple-element.30), channel_id=1, source_target_pairs={{0,8},{4,20},{8,0},{12,28},{16,24},{20,4},{24,16},{28,12},{1,9},{5... | collective-permute-start | bytes 208904 | tf_op jit(solution)/shard_map/ppermute | solution.py:76
  27.6 1.5 %collective-permute-start.9 = (bf16[272,128]{1,0:T(8,128)(2,1)S(1)}, bf16[272,128]{1,0:T(8,128)(2,1)S(1)}, u32[]{:S(2)}, u32[]{:S(2)}) collective-permute-start(bf16[272,128]{1,0:T(8,128)(2,1)S(1)} %swap.1), channel_id=1, source_target_pairs={{0,4},{4,0},{8,12},{12,8},{16,20},{20,16},{24,28},{28,24},{1,5},{5... | collective-permute-start | bytes 208904 | tf_op jit(solution)/shard_map/ppermute | solution.py:71
